TPU v7x, 32 devices: a whole 2x2x4 slice. The times are simulated.
32 devices in a mesh: batch: 8 (over z, y), band: 4 (over x, core).
Axes of the slice: x: 2, y: 2, z: 4, core: 2. Of those that a mesh axis runs over, the one named last changes fastest.
Arguments:
- tokens: bfloat16 [24, 256, 768], P('batch', 'band'), may hold values from -32 to 32
- cotangent: bfloat16 [24, 256, 768], P('batch', 'band'), may hold values from -17 to 17
- visible: int32 [24, 256], P('batch', 'band'), may hold values from 0 to 1, as said below
- first_gain: float32 [768], replicated, may hold values from 0.1 to 1.9
- first_bias: float32 [768], replicated, may hold values from -3 to 3
- qkv_weight: bfloat16 [768, 2304], replicated, may hold values from -0.21875 to 0.21875
- qv_bias: float32 [2, 768], replicated, may hold values from -3 to 3
- proj_weight: bfloat16 [768, 768], replicated, may hold values from -0.625 to 0.625
- proj_bias: float32 [768], replicated, may hold values from -2 to 2
- attn_scale: float32 [768], replicated, may hold values from 0.5 to 2
- second_gain: float32 [768], replicated, may hold values from 0.1 to 1.9
- second_bias: float32 [768], replicated, may hold values from -3 to 3
- expand_weight: bfloat16 [768, 3072], replicated, may hold values from -0.21875 to 0.21875
- expand_bias: float32 [3072], replicated, may hold values from -3 to 3
- reduce_weight: bfloat16 [3072, 768], replicated, may hold values from -0.109375 to 0.109375
- reduce_bias: float32 [768], replicated, may hold values from -2 to 2
- mlp_scale: float32 [768], replicated, may hold values from 0.5 to 2
Outputs:
- layer_out: bfloat16 [24, 256, 768], P('batch', 'band')
- grad_tokens: bfloat16 [24, 256, 768], P('batch', 'band')
- grad_first_gain: float32 [768], P(('batch', 'band'))
- grad_first_bias: float32 [768], P(('batch', 'band'))
- grad_qkv_weight: float32 [768, 2304], P(('batch', 'band'))
- grad_qv_bias: float32 [2, 768], P(None, ('batch', 'band'))
- grad_proj_weight: float32 [768, 768], P(('batch', 'band'))
- grad_proj_bias: float32 [768], P(('batch', 'band'))
- grad_attn_scale: float32 [768], P(('batch', 'band'))
- grad_second_gain: float32 [768], P(('batch', 'band'))
- grad_second_bias: float32 [768], P(('batch', 'band'))
- grad_expand_weight: float32 [768, 3072], P(('batch', 'band'))
- grad_expand_bias: float32 [3072], P(('batch', 'band'))
- grad_reduce_weight: float32 [3072, 768], P(('batch', 'band'))
- grad_reduce_bias: float32 [768], P(('batch', 'band'))
- grad_mlp_scale: float32 [768], P(('batch', 'band'))
Inputs may be any that keep to these rules, and one draw needn't show every extreme that they name: Patch (r, c) of the 14 x 14 grid sits in slot r * 16 + c; in all other slots (columns from 14 on, rows from 14 on) visible is 0; tokens and cotangent there may hold any values. Each image has 78 to 137 visible patches, and in every draw some image has exactly 78 and some exactly 137.
All inputs are finite; a program needn't handle non-finite values.
Results may differ from a plain program's by a relative error of at most 0.012.
Values may be sent and summed in bfloat16 or wider, within the bound.
No kernel may reach another device: no remote copies, remote signals or barrier semaphores. Data moves between devices by JAX's collectives and lax.ppermute only.
A program may use at most 192 MiB of HBM per device.

v0:
```python
import math

import jax
import jax.numpy as jnp
from jax import lax
from jax.sharding import PartitionSpec as P

HD = 64


NORM_EPS = 1e-06


def layer_norm(values, norm_gain, norm_shift):
    center = values - jnp.mean(values, axis=-1, keepdims=True)
    spread = jnp.mean(center * center, axis=-1, keepdims=True)
    return center * lax.rsqrt(spread + NORM_EPS) * norm_gain + norm_shift


def gelu_exact(values):
    return jax.nn.gelu(values, approximate=False)


def split_rows(packed_rows, mask_rows):
    item_count = packed_rows.shape[0]
    slot_count = packed_rows.shape[1]
    heads_here = packed_rows.shape[4] // HD
    unpacked = packed_rows.reshape(item_count, slot_count, 3, heads_here, HD)
    queries = unpacked[:, :, 0]
    key_rows = unpacked[:, :, 1]
    value_rows = unpacked[:, :, 2]
    key_valid = mask_rows.reshape(item_count, slot_count) > 0
    score_scale = 1.0 / math.sqrt(HD)
    scores = (
        jnp.einsum("bqhe,bkhe->bhqk", queries, key_rows, preferred_element_type=jnp.float32)
        * score_scale
    )
    scores = jnp.where(key_valid[:, None, None, :], scores, -1e30)
    return (queries, key_rows, value_rows, scores)


def attend_plain(inputs):
    packed_rows, mask_rows = inputs
    queries, key_rows, value_rows, scores = split_rows(packed_rows, mask_rows)
    row_top = jnp.max(scores, axis=-1, keepdims=True)
    raised = jnp.exp(scores - row_top)
    row_total = jnp.sum(raised, axis=-1, keepdims=True)
    attn_prob = raised / row_total
    log_total = (row_top + jnp.log(row_total))[..., 0]
    mixed_rows = jnp.einsum(
        "bhqk,bkhe->bqhe",
        attn_prob.astype(jnp.bfloat16),
        value_rows,
        preferred_element_type=jnp.float32,
    ).astype(jnp.bfloat16)
    mixed_rows = mixed_rows.reshape(
        packed_rows.shape[0], packed_rows.shape[1], packed_rows.shape[4]
    )
    return (mixed_rows, log_total)


def backward_rows(score_parts, log_total, grad_rows):
    queries, key_rows, value_rows, scores = score_parts
    item_count, slot_count, heads_here, head_size = queries.shape
    score_scale = 1.0 / math.sqrt(HD)
    attn_prob = jnp.exp(scores - log_total[..., None])
    grad_heads = grad_rows.reshape(item_count, slot_count, heads_here, head_size)
    grad_prob = jnp.einsum(
        "bqhe,bkhe->bhqk", grad_heads, value_rows, preferred_element_type=jnp.float32
    )
    row_delta = jnp.sum(attn_prob * grad_prob, axis=-1, keepdims=True)
    grad_score = (attn_prob * (grad_prob - row_delta)).astype(jnp.bfloat16)
    grad_query = (
        jnp.einsum("bhqk,bkhe->bqhe", grad_score, key_rows, preferred_element_type=jnp.float32)
        * score_scale
    )
    grad_key = (
        jnp.einsum("bhqk,bqhe->bkhe", grad_score, queries, preferred_element_type=jnp.float32)
        * score_scale
    )
    grad_value = jnp.einsum(
        "bhqk,bqhe->bkhe",
        attn_prob.astype(jnp.bfloat16),
        grad_heads,
        preferred_element_type=jnp.float32,
    )
    stacked = jnp.stack([grad_query, grad_key, grad_value], axis=2)
    return stacked.reshape(item_count, slot_count, 3, 1, heads_here * head_size).astype(
        jnp.bfloat16
    )


def attend_again(inputs):
    packed_rows, mask_rows, grad_rows = inputs
    score_parts = split_rows(packed_rows, mask_rows)
    scores = score_parts[3]
    row_top = jnp.max(scores, axis=-1, keepdims=True)
    log_total = (row_top + jnp.log(jnp.sum(jnp.exp(scores - row_top), axis=-1, keepdims=True)))[
        ..., 0
    ]
    return backward_rows(score_parts, log_total, grad_rows)


def body(
    tokens,
    cotangent,
    visible,
    first_gain,
    first_bias,
    qkv_weight,
    qv_bias,
    proj_weight,
    proj_bias,
    attn_scale,
    second_gain,
    second_bias,
    expand_weight,
    expand_bias,
    reduce_weight,
    reduce_bias,
    mlp_scale,
):
    images, slot_count, model_width = tokens.shape
    groups = lax.axis_size("band")
    local_width = model_width // groups
    inputs_full = tokens.astype(jnp.float32)
    shown_mask = visible.astype(jnp.float32)
    normed, first_pull = jax.vjp(layer_norm, inputs_full, first_gain, first_bias)
    normed_low = normed.astype(jnp.bfloat16)
    qkv_bias = jnp.concatenate([qv_bias[0], jnp.zeros((model_width,), jnp.float32), qv_bias[1]])

    def project_qkv():
        product = jnp.einsum(
            "isd,de->ise", normed_low, qkv_weight, preferred_element_type=jnp.float32
        )
        return (
            (product + qkv_bias)
            .astype(jnp.bfloat16)
            .reshape(images, slot_count, 3, groups, local_width)
        )

    packed = project_qkv()
    mask_part = jnp.broadcast_to(
        shown_mask.astype(jnp.bfloat16)[:, :, None, None, None], (images, slot_count, 1, groups, 1)
    )
    results = attend_plain(
        (
            lax.all_to_all(packed, "band", split_axis=3, concat_axis=1, tiled=True),
            lax.all_to_all(mask_part, "band", split_axis=3, concat_axis=1, tiled=True),
        )
    )
    mixed_heads = results[0].reshape(images, groups * slot_count, 1, local_width)
    back_rows = lax.all_to_all(mixed_heads, "band", split_axis=1, concat_axis=2, tiled=True)
    mixed_rows = back_rows.reshape(images, slot_count, model_width)
    branch_one = (
        jnp.einsum("isd,de->ise", mixed_rows, proj_weight, preferred_element_type=jnp.float32)
        + proj_bias
    )
    residual = inputs_full + attn_scale * branch_one
    normed_two, second_pull = jax.vjp(layer_norm, residual, second_gain, second_bias)
    normed_two_low = normed_two.astype(jnp.bfloat16)
    hidden = (
        jnp.einsum("isd,df->isf", normed_two_low, expand_weight, preferred_element_type=jnp.float32)
        + expand_bias
    )
    activated, gelu_pull = jax.vjp(gelu_exact, hidden)
    activated_low = activated.astype(jnp.bfloat16)
    branch_two = (
        jnp.einsum("isf,fd->isd", activated_low, reduce_weight, preferred_element_type=jnp.float32)
        + reduce_bias
    )
    layer_out = (shown_mask[..., None] * (residual + mlp_scale * branch_two)).astype(jnp.bfloat16)
    grad_pre = shown_mask[..., None] * cotangent.astype(jnp.float32)
    grad_mlp_scale = jnp.sum(grad_pre * branch_two, axis=(0, 1))
    grad_branch_two = (mlp_scale * grad_pre).astype(jnp.bfloat16)
    grad_reduce_weight = jnp.einsum(
        "isf,isd->fd", activated_low, grad_branch_two, preferred_element_type=jnp.float32
    )
    grad_reduce_bias = jnp.sum(grad_branch_two.astype(jnp.float32), axis=(0, 1))
    grad_activated = jnp.einsum(
        "isd,fd->isf", grad_branch_two, reduce_weight, preferred_element_type=jnp.float32
    )
    grad_hidden = gelu_pull(grad_activated)[0].astype(jnp.bfloat16)
    grad_expand_weight = jnp.einsum(
        "isd,isf->df", normed_two_low, grad_hidden, preferred_element_type=jnp.float32
    )
    grad_expand_bias = jnp.sum(grad_hidden.astype(jnp.float32), axis=(0, 1))
    grad_normed_two = jnp.einsum(
        "isf,df->isd", grad_hidden, expand_weight, preferred_element_type=jnp.float32
    )
    grad_resid_norm, grad_second_gain, grad_second_bias = second_pull(grad_normed_two)
    grad_residual = grad_pre + grad_resid_norm
    grad_attn_scale = jnp.sum(grad_residual * branch_one, axis=(0, 1))
    grad_branch_one = (attn_scale * grad_residual).astype(jnp.bfloat16)
    grad_proj_weight = jnp.einsum(
        "isd,ise->de", mixed_rows, grad_branch_one, preferred_element_type=jnp.float32
    )
    grad_proj_bias = jnp.sum(grad_branch_one.astype(jnp.float32), axis=(0, 1))
    grad_mixed = jnp.einsum(
        "ise,de->isd", grad_branch_one, proj_weight, preferred_element_type=jnp.float32
    )
    grad_mixed = grad_mixed.astype(jnp.bfloat16).reshape(images, slot_count, 1, groups, local_width)
    repacked = project_qkv()
    grad_packed = attend_again(
        (
            lax.all_to_all(repacked, "band", split_axis=3, concat_axis=1, tiled=True),
            lax.all_to_all(mask_part, "band", split_axis=3, concat_axis=1, tiled=True),
            lax.all_to_all(grad_mixed, "band", split_axis=3, concat_axis=1, tiled=True),
        )
    )
    grad_bands = lax.all_to_all(grad_packed, "band", split_axis=1, concat_axis=3, tiled=True)
    grad_qkv = grad_bands.reshape(images, slot_count, 3 * model_width)
    grad_qkv_weight = jnp.einsum(
        "isd,ise->de", normed_low, grad_qkv, preferred_element_type=jnp.float32
    )
    column_sums = jnp.sum(grad_qkv.astype(jnp.float32), axis=(0, 1))
    grad_qv_bias = jnp.stack([column_sums[:model_width], column_sums[2 * model_width :]])
    grad_normed = jnp.einsum(
        "ise,de->isd", grad_qkv, qkv_weight, preferred_element_type=jnp.float32
    )
    grad_input_norm, grad_first_gain, grad_first_bias = first_pull(grad_normed)
    grad_tokens = (grad_residual + grad_input_norm).astype(jnp.bfloat16)
    all_sums = (
        lax.psum_scatter(grad_first_gain, ("batch", "band"), scatter_dimension=0, tiled=True),
        lax.psum_scatter(grad_first_bias, ("batch", "band"), scatter_dimension=0, tiled=True),
        lax.psum_scatter(grad_qkv_weight, ("batch", "band"), scatter_dimension=0, tiled=True),
        lax.psum_scatter(grad_qv_bias, ("batch", "band"), scatter_dimension=1, tiled=True),
        lax.psum_scatter(grad_proj_weight, ("batch", "band"), scatter_dimension=0, tiled=True),
        lax.psum_scatter(grad_proj_bias, ("batch", "band"), scatter_dimension=0, tiled=True),
        lax.psum_scatter(grad_attn_scale, ("batch", "band"), scatter_dimension=0, tiled=True),
        lax.psum_scatter(grad_second_gain, ("batch", "band"), scatter_dimension=0, tiled=True),
        lax.psum_scatter(grad_second_bias, ("batch", "band"), scatter_dimension=0, tiled=True),
        lax.psum_scatter(grad_expand_weight, ("batch", "band"), scatter_dimension=0, tiled=True),
        lax.psum_scatter(grad_expand_bias, ("batch", "band"), scatter_dimension=0, tiled=True),
        lax.psum_scatter(grad_reduce_weight, ("batch", "band"), scatter_dimension=0, tiled=True),
        lax.psum_scatter(grad_reduce_bias, ("batch", "band"), scatter_dimension=0, tiled=True),
        lax.psum_scatter(grad_mlp_scale, ("batch", "band"), scatter_dimension=0, tiled=True),
    )
    (
        sum_first_gain,
        sum_first_bias,
        sum_qkv_weight,
        sum_qv_bias,
        sum_proj_weight,
        sum_proj_bias,
        sum_attn_scale,
        sum_second_gain,
        sum_second_bias,
        sum_expand_weight,
        sum_expand_bias,
        sum_reduce_weight,
        sum_reduce_bias,
        sum_mlp_scale,
    ) = all_sums
    return (
        layer_out,
        grad_tokens,
        sum_first_gain,
        sum_first_bias,
        sum_qkv_weight,
        sum_qv_bias,
        sum_proj_weight,
        sum_proj_bias,
        sum_attn_scale,
        sum_second_gain,
        sum_second_bias,
        sum_expand_weight,
        sum_expand_bias,
        sum_reduce_weight,
        sum_reduce_bias,
        sum_mlp_scale,
    )


def solution(mesh):
    placed = (
        P("batch", "band", None),
        P("batch", "band", None),
        P("batch", "band"),
        P(),
        P(),
        P(),
        P(),
        P(),
        P(),
        P(),
        P(),
        P(),
        P(),
        P(),
        P(),
        P(),
        P(),
    )
    return jax.shard_map(
        body,
        mesh=mesh,
        in_specs=placed,
        out_specs=(
            P("batch", "band", None),
            P("batch", "band", None),
            P(("batch", "band")),
            P(("batch", "band")),
            P(("batch", "band"), None),
            P(None, ("batch", "band")),
            P(("batch", "band"), None),
            P(("batch", "band")),
            P(("batch", "band")),
            P(("batch", "band")),
            P(("batch", "band")),
            P(("batch", "band"), None),
            P(("batch", "band")),
            P(("batch", "band"), None),
            P(("batch", "band")),
            P(("batch", "band")),
        ),
        check_vma=False,
    )
```

profile of v0, /device:TPU:0, one launch (start us, length us, event | category | flops | bytes accessed | tf_op | source)
XLA Modules:
  0.0 615.8 jit_solution(7927623597454723844)
XLA Ops:
  7.2 1.4 fusion.58
  9.2 4.2 all-to-all-start.1
  17.2 2.9 fusion.11
  20.1 3.7 reshape.217
  23.7 2.5 copy.75
  26.2 4.3 all-to-all-start
  30.7 15.8 %all-to-all-done = bf16[3,64,3,4,192]{4,1,2,0,3:T(8,128)(2,1)} async-done(((bf16[3,64,3,4,192]{4,1,2,0,3:T(8,128)(2,1)}), bf16[3,64,3,4,192]{4,1,2,0,3:T(8,128)(2,1)}, u32[]{:S(2)}, u32[]{:S(2)}) %all-to-all-start) | async-done | bytes 884768 | tf_op jit(solution)/shard_map/all_to_all | solution.py:148
  46.5 3.7 copy.101
  50.2 3.9 reshape.233
  54.0 1.7 fusion.59
  56.1 2.4 convolution_convert_fusion.2
  58.5 2.0 copy.82
  60.6 12.3 %all_to_all.79 = bf16[3,256,1,192]{3,0,2,1:T(4,128)(2,1)S(1)} all-to-all(bf16[3,256,1,192]{3,0,2,1:T(4,128)(2,1)} %copy.82), channel_id=1, replica_groups=mesh['batch'=8,'band'=4] {'band'}, dimensions={1} | all-to-all | bytes 589824 | tf_op jit(solution)/shard_map/all_to_all | solution.py:153
  74.0 2.0 reshape.219
  76.0 2.8 fusion.56
  79.1 4.3 fusion.46
  83.4 6.1 multiply_convert_fusion.1
  89.5 2.7 convert_reduce_fusion
  92.2 2.3 multiply_reduce_fusion.2
  97.3 2.0 convolution_bitcast_fusion.3
  99.3 2.6 convolution_convert_fusion.1
  101.9 2.1 reshape.220
  104.0 1.8 copy.85
  105.9 4.1 all-to-all-start.3
  111.0 6.5 %all-to-all-done.3 = bf16[3,64,1,4,192]{4,1,2,0,3:T(8,128)(2,1)} async-done(((bf16[3,64,1,4,192]{4,1,2,0,3:T(8,128)(2,1)}), bf16[3,64,1,4,192]{4,1,2,0,3:T(8,128)(2,1)}, u32[]{:S(2)}, u32[]{:S(2)}) %all-to-all-start.3) | async-done | bytes 294944 | tf_op jit(solution)/shard_map/all_to_all | solution.py:208
  117.5 2.1 copy.86
  119.6 2.2 reshape.221
  121.8 3.0 convolution_convert_fusion
  124.9 3.0 copy.92
  127.8 2.7 multiply_reduce_fusion
  132.1 2.2 fusion.29
  134.3 3.0 copy.91
  137.2 2.4 fusion.28
  139.7 3.0 copy.90
  142.6 4.2 pad_maximum_fusion
  146.9 24.5 %all_to_all.80 = bf16[3,256,3,1,192]{4,2,0,3,1:T(4,128)(2,1)S(1)} all-to-all(bf16[3,256,3,1,192]{4,2,0,3,1:T(4,128)(2,1)S(1)} %pad_maximum_fusion), channel_id=1, replica_groups=mesh['batch'=8,'band'=4] {'band'}, dimensions={1} | all-to-all | bytes 1769472 | tf_op jit(solution)/shard_map/all_to_all | solution.py:211
  172.7 1.9 copy.94
  174.6 3.2 reshape.222
  177.8 5.4 convolution_bitcast_fusion.2
  183.9 6.6 %convolution_bitcast_fusion.1 = f32[768,3072]{1,0:T(8,128)} fusion(bf16[3,64,3072]{2,1,0:T(8,128)(2,1)} %copy-done.12, f32[3,64,768]{2,1,0:T(8,128)} %copy-done.5, f32[768]{0:T(1024)S(1)} %copy-done.20, f32[768]{0:T(1024)S(1)} %copy-done.18, f32[3,64]{1,0:T(4,128)S(1)} %copy-done.25, f32[3,64]{1,0:T(4,128)S(1)} %copy-done.22), kind=kOutput, calls=%fused_computation.1 | convolution fusion | flops 906706944 | bytes 11214336 | tf_op jit(solution)/shard_map/isd,isf->df/dot_general | solution.py:184
  191.3 6.5 %convolution_bitcast_fusion = f32[3072,768]{1,0:T(8,128)} fusion(bf16[3,64,3072]{2,1,0:T(8,128)(2,1)} %get-tuple-element.44, bf16[3,64,768]{2,1,0:T(8,128)(2,1)} %param.18, f32[768]{0:T(1024)S(1)} %copy-done.45, f32[3,64]{1,0:T(4,128)S(1)} %copy-done.35), kind=kOutput, calls=%fused_computation | convolution fusion | flops 906559488 | bytes 10915584 | tf_op jit(solution)/shard_map/isf,isd->fd/dot_general | solution.py:176
  197.8 1.5 convert_reduce_fusion.1
  200.9 3.4 fusion.53
  205.2 5.1 multiply_reduce_fusion.1
  210.3 41.0 %all-reduce.10 = (f32[768]{0:T(1024)}, f32[768]{0:T(1024)}, f32[2,768]{1,0:T(2,128)}, f32[768]{0:T(1024)}, f32[768]{0:T(1024)}, /*index=5*/f32[768]{0:T(1024)}, ...) all-reduce(f32[768]{0:T(1024)} %get-tuple-element.20, ...), channel_id=2, replica_groups=mesh['batch'=8,'band'=4] {'batch','band'}, use_global_device_ids=true, to_apply=%region_12.13.clone | all-reduce | flops 10752 | bytes 86016
  263.3 62.6 %reduce-scatter.6.cloned.1.call-done = f32[24,2304]{1,0:T(8,128)} async-done(((f32[768,2304]{1,0:T(8,128)}), f32[24,2304]{1,0:T(8,128)}) %reduce-scatter.6.cloned.1.call-update) | async-done | bytes 221200 | tf_op jit(solution)/shard_map/reduce_scatter | solution.py:226
  325.9 141.5 %reduce-scatter.10.cloned.1.call-done = f32[24,3072]{1,0:T(8,128)} async-done(((f32[768,3072]{1,0:T(8,128)}), f32[24,3072]{1,0:T(8,128)}) %reduce-scatter.10.cloned.1.call-update) | async-done | bytes 294928 | tf_op jit(solution)/shard_map/reduce_scatter | solution.py:233
  467.4 141.8 %reduce-scatter.12.cloned.1.call-done = f32[96,768]{1,0:T(8,128)} async-done(((f32[3072,768]{1,0:T(8,128)}), f32[96,768]{1,0:T(8,128)}) %reduce-scatter.12.cloned.1.call-update) | async-done | bytes 294928 | tf_op jit(solution)/shard_map/reduce_scatter | solution.py:235
  (157 shorter events, 28.4 us)
Async XLA Ops:
  7.2 10.0 %copy-start = (bf16[768,2304]{1,0:T(8,128)(2,1)S(1)}, bf16[768,2304]{1,0:T(8,128)(2,1)}, u32[]{:S(2)}) copy-start(bf16[768,2304]{1,0:T(8,128)(2,1)} %param.22) | copy-start | bytes 10616836
  9.2 17.0 %all-to-all-start.1 = ((bf16[3,64,1,4,1]{1,0,4,2,3:T(4,128)(2,1)}), bf16[3,64,1,4,1]{1,0,4,2,3:T(4,128)(2,1)S(1)}, u32[]{:S(2)}, u32[]{:S(2)}) async-start(bf16[3,64,1,4,1]{1,0,4,2,3:T(4,128)(2,1)} %broadcast_in_dim.29), calls=%async_computation.1 | async-start | bytes 8192 | tf_op jit(solution)/shard_map/all_to_all | solution.py:149
  14.5 2.6 copy-start.26
  26.2 20.2 %all-to-all-start = ((bf16[3,64,3,4,192]{4,1,2,0,3:T(8,128)(2,1)}), bf16[3,64,3,4,192]{4,1,2,0,3:T(8,128)(2,1)}, u32[]{:S(2)}, u32[]{:S(2)}) async-start(bf16[3,64,3,4,192]{4,1,2,0,3:T(8,128)(2,1)} %copy.75), calls=%async_computation | async-start | bytes 2359296 | tf_op jit(solution)/shard_map/all_to_all | solution.py:148
  30.5 232.8 %reduce-scatter.8.cloned.1.call-start = ((), (), s32[]{:S(2)}) async-start(), calls=%async_computation.10 | async-start | bytes 2433024 | tf_op jit(solution)/shard_map/reduce_scatter | solution.py:228
  55.7 2.8 copy-start.1
  55.7 2.8 copy-start.17
  56.1 2.5 copy-start.23
  58.5 17.5 %copy-start.31 = (f32[768]{0:T(1024)S(1)}, f32[768]{0:T(1024)}, u32[]{:S(2)}) copy-start(f32[768]{0:T(1024)} %param.26) | copy-start | bytes 9220
  72.9 6.2 %copy-start.18 = (f32[768]{0:T(1024)S(1)}, f32[768]{0:T(1024)}, u32[]{:S(2)}) copy-start(f32[768]{0:T(1024)} %param.27) | copy-start | bytes 9220
  72.9 6.2 %copy-start.19 = (f32[768]{0:T(1024)S(1)}, f32[768]{0:T(1024)}, u32[]{:S(2)}) copy-start(f32[768]{0:T(1024)} %param.28) | copy-start | bytes 9220
  76.0 13.5 %slice-start.2 = ((s8[4718592]{0:T(1024)(128)(4,1)}), s8[4194304]{0:T(1024)(128)(4,1)S(1)}, s32[]{:S(2)}) async-start(s8[4718592]{0:T(1024)(128)(4,1)} %bitcast.127), calls=%async_computation.15 | async-start | bytes 8388608
  78.8 15.8 %copy-start.5 = (f32[3,64,768]{2,1,0:T(8,128)}, f32[3,64,768]{2,1,0:T(8,128)S(1)}, u32[]{:S(2)}) copy-start(f32[3,64,768]{2,1,0:T(8,128)S(1)} %get-tuple-element.47) | copy-start | bytes 1769476
  78.8 15.8 %copy-start.21 = (f32[3,64]{1,0:T(4,128)}, f32[3,64]{1,0:T(4,128)S(1)}, u32[]{:S(2)}) copy-start(f32[3,64]{1,0:T(4,128)S(1)} %broadcast_multiply_fusion) | copy-start | bytes 2308
  79.1 15.6 %copy-start.24 = (f32[3,64]{1,0:T(4,128)}, f32[3,64]{1,0:T(4,128)S(1)}, u32[]{:S(2)}) copy-start(f32[3,64]{1,0:T(4,128)S(1)} %fusion.52) | copy-start | bytes 2308
  79.1 10.4 %slice-start.3 = ((s8[4718592]{0:T(1024)(128)(4,1)}), s8[524288]{0:T(1024)(128)(4,1)S(1)}, s32[]{:S(2)}) async-start(s8[4718592]{0:T(1024)(128)(4,1)} %bitcast.127), calls=%async_computation.16 | async-start | bytes 1048576
  83.4 6.1 copy-start.15
  83.4 6.1 copy-start.34
  83.4 6.1 copy-start.44
  83.4 8.8 %slice-start = ((s8[4718592]{0:T(1024)(128)(4,1)}), s8[4194304]{0:T(1024)(128)(4,1)S(1)}, s32[]{:S(2)}) async-start(s8[4718592]{0:T(1024)(128)(4,1)} %bitcast.125), calls=%async_computation.13 | async-start | bytes 8388608
  89.5 2.7 slice-start.1
  92.2 2.4 copy-start.12
  92.2 3.5 copy-start.32
  94.6 2.7 copy-start.8
  94.9 1.6 copy-start.40
  105.9 11.6 %all-to-all-start.3 = ((bf16[3,64,1,4,192]{4,1,2,0,3:T(8,128)(2,1)}), bf16[3,64,1,4,192]{4,1,2,0,3:T(8,128)(2,1)}, u32[]{:S(2)}, u32[]{:S(2)}) async-start(bf16[3,64,1,4,192]{4,1,2,0,3:T(8,128)(2,1)} %copy.85), calls=%async_computation.3 | async-start | bytes 786432 | tf_op jit(solution)/shard_map/all_to_all | solution.py:208
  110.0 215.9 %reduce-scatter.6.cloned.1.call-start = ((), (), s32[]{:S(2)}) async-start(), calls=%async_computation.9 | async-start | bytes 7299072 | tf_op jit(solution)/shard_map/reduce_scatter | solution.py:226
  127.8 2.7 copy-start.2
  171.6 6.2 %copy-start.27 = (f32[3,64]{1,0:T(4,128)S(1)}, f32[3,64]{1,0:T(4,128)}, u32[]{:S(2)}) copy-start(f32[3,64]{1,0:T(4,128)} %copy-done.26) | copy-start | bytes 2308
  171.6 6.2 %copy-start.38 = (f32[3,64]{1,0:T(4,128)S(1)}, f32[3,64]{1,0:T(4,128)}, u32[]{:S(2)}) copy-start(f32[3,64]{1,0:T(4,128)} %copy-done.37) | copy-start | bytes 2308
  171.6 6.2 %copy-start.42 = (f32[768]{0:T(1024)S(1)}, f32[768]{0:T(1024)}, u32[]{:S(2)}) copy-start(f32[768]{0:T(1024)} %param.20) | copy-start | bytes 9220
  183.3 284.2 %reduce-scatter.10.cloned.1.call-start = ((), (), s32[]{:S(2)}) async-start(), calls=%async_computation.11 | async-start | bytes 9732096 | tf_op jit(solution)/shard_map/reduce_scatter | solution.py:233
  190.6 418.6 %reduce-scatter.12.cloned.1.call-start = ((), (), s32[]{:S(2)}) async-start(), calls=%async_computation.12 | async-start | bytes 9732096 | tf_op jit(solution)/shard_map/reduce_scatter | solution.py:235
  197.7 3.0 copy-start.28
  200.7 3.5 copy-start.30
  200.7 3.5 copy-start.7
  200.7 3.5 copy-start.39
  200.7 3.5 copy-start.43
  200.8 4.4 copy-start.6
  200.8 4.4 copy-start.11
  200.8 4.4 copy-start.13
  200.8 4.4 copy-start.14
  200.8 4.4 copy-start.16
  200.8 4.4 copy-start.36
  200.8 4.4 copy-start.41
  200.8 4.4 copy-start.46
  200.8 4.4 copy-start.47
  205.2 5.1 copy-start.33
  (11 other events, 8.5 us)
Sparse Core Ops, SparseCore 0:
  99.4 101.1 reduce-scatter.7
  207.8 118.0 reduce-scatter.5
  332.4 134.9 reduce-scatter.9
  474.8 134.4 reduce-scatter.11
where the time goes:
time: 618 us; the launch traced here: 616 us
  waiting for transfers between devices  368 us (60%)
  blocking collectives  77.8 us (13%)
  matrix products  61.1 us (10%)
  local copies, waits for them, and re-layouts  60.9 us (10%)
  other arithmetic  20 us (3%)
  between operations  14.4 us (2%)
  starting transfers between devices  13.3 us (2%)
    reduce_scatter x1, waiting for transfers between devices, body(): lax.psum_scatter(grad_reduce_weight, ('batch', 'band'), scatter_dimension...  142 us
    reduce_scatter x1, waiting for transfers between devices, body(): lax.psum_scatter(grad_expand_weight, ('batch', 'band'), scatter_dimension...  141 us
    reduce_scatter x1, waiting for transfers between devices, body(): lax.psum_scatter(grad_qkv_weight, ('batch', 'band'), scatter_dimension=0,...  62.6 us
    unnamed x1, blocking collectives  41 us
    all_to_all x1, blocking collectives, body(): lax.all_to_all(grad_packed, 'band', split_axis=1, concat_axis=3, tiled=True)  24.5 us
    unnamed x114, local copies, waits for them, and re-layouts  17.4 us
    all_to_all x1, waiting for transfers between devices, body(): lax.all_to_all(packed, 'band', split_axis=3, concat_axis=1, tiled=True)  15.8 us
  transfers between devices with their start and end apart: 7, of which 5 were waited for; matrix products, arithmetic and copies ran while one was open for 16% of the time, Pallas kernels for 0%

commit v1 on v0

--- a/solution.py
+++ b/solution.py
@@ -1,14 +1,539 @@
+import functools
 import math
 
 import jax
 import jax.numpy as jnp
 from jax import lax
+from jax.experimental import pallas as pl
+from jax.experimental.pallas import tpu as pltpu
 from jax.sharding import PartitionSpec as P
 
 HD = 64
-
-
 NORM_EPS = 1e-06
+PACK = 144
+SLOTS = 256
+BAND = 64
+IMGS = 3
+ROWS = IMGS * PACK
+D = 768
+HALF = D // 2
+FF = 3072
+FH = FF // 2
+SMALL = 128
+MIB = 1024 * 1024
+F32 = jnp.float32
+BF = jnp.bfloat16
+ANY = pl.BlockSpec(memory_space=pl.ANY)
+VM = pl.BlockSpec(memory_space=pltpu.VMEM)
+
+
+def dot(a, b):
+    return jnp.dot(a, b, preferred_element_type=F32)
+
+
+def dot_nt(a, b):
+    return lax.dot_general(a, b, (((1,), (1,)), ((), ())), preferred_element_type=F32)
+
+
+def dot_tn(a, b):
+    return lax.dot_general(a, b, (((0,), (0,)), ((), ())), preferred_element_type=F32)
+
+
+def sds(shape, dtype):
+    return jax.ShapeDtypeStruct(shape, dtype)
+
+
+def place():
+    band = lax.axis_index("band")
+    batch = lax.axis_index("batch")
+    return band >> 1, band & 1, batch >> 1, batch & 1
+
+
+def one_hot_pack(pos, image):
+    rows = lax.broadcasted_iota(jnp.int32, (PACK, SLOTS), 0).astype(F32)
+    return jnp.where(rows == pos[image : image + 1, :], 1.0, 0.0).astype(BF)
+
+
+def feature_pick():
+    x, _, z, y = place()
+    lane = lax.broadcasted_iota(jnp.int32, (D, HALF), 1)
+    row = lax.broadcasted_iota(jnp.int32, (D, HALF), 0)
+    want = jnp.zeros((D, HALF), jnp.int32)
+    for q in range(8):
+        dy, dz = q // 4, q % 4
+        base = 96 * ((z ^ dz) * 2 + (y ^ dy)) + 48 * x - 48 * q
+        want = jnp.where((lane >= 48 * q) & (lane < 48 * q + 48), lane + base, want)
+    return jnp.where(row == want, 1.0, 0.0).astype(BF)
+
+
+def statistics(values):
+    center = values - jnp.mean(values, axis=-1, keepdims=True)
+    rstd = lax.rsqrt(jnp.mean(center * center, axis=-1, keepdims=True) + NORM_EPS)
+    return center * rstd, rstd
+
+
+def norm_back(grad, z, rstd):
+    return rstd * (
+        grad
+        - jnp.mean(grad, axis=-1, keepdims=True)
+        - z * jnp.mean(grad * z, axis=-1, keepdims=True)
+    )
+
+
+def gather_bands(blocks, dst, sems):
+    band = lax.axis_index("band")
+    copies = []
+    for k, block in enumerate(blocks):
+        at = pl.multiple_of((band ^ k) * BAND, BAND)
+        copy = pltpu.make_async_copy(block, dst.at[:, pl.ds(at, BAND), :], sems.at[k])
+        copy.start()
+        copies.append(copy)
+    return copies
+
+
+def head_probs(q2, k2, e, key_ok):
+    lane = lax.broadcasted_iota(jnp.int32, (PACK, 128), 1)
+    mine = (lane < HD) if e == 0 else (lane >= HD)
+    qm = jnp.where(mine, q2, jnp.zeros_like(q2))
+    scores = jnp.where(key_ok, dot_nt(qm, k2) * (1.0 / math.sqrt(HD)), -1e30)
+    raised = jnp.exp(scores - jnp.max(scores, axis=-1, keepdims=True))
+    return raised / jnp.sum(raised, axis=-1, keepdims=True)
+
+
+def keys_shown(pos, image):
+    shown = jnp.sum(jnp.where(pos[image : image + 1, :] >= 0, 1.0, 0.0), axis=-1, keepdims=True)
+    return lax.broadcasted_iota(jnp.int32, (1, PACK), 1).astype(F32) < shown
+
+
+def first_kernel(
+    t0, t1, t2, t3, va, vb, gain, bias, wqkv, qvb,
+    tok_o, norm_o, qkv_o, mix_o, pos_o,
+    xs, w, sems,
+):
+    _, c, _, _ = place()
+    copies = gather_bands((t0, t1, t2, t3), xs, sems)
+    heads = pl.multiple_of(c * HALF, 128)
+    loads = []
+    for m in range(3):
+        src = wqkv.at[:, pl.ds(pl.multiple_of(m * D + c * HALF, 128), HALF)]
+        loads.append(pltpu.make_async_copy(src, w.at[m], sems.at[4 + m]))
+        loads[-1].start()
+    vis = va[...] + vb[...]
+    upto = lax.broadcasted_iota(jnp.int32, (SLOTS, SLOTS), 0)
+    slot = lax.broadcasted_iota(jnp.int32, (SLOTS, SLOTS), 1)
+    before = jnp.where(upto < slot, 1.0, 0.0).astype(BF)
+    pos = jnp.where(vis > 0, dot(vis.astype(BF), before), -1.0)
+    pos_o[...] = pos
+    for copy in copies:
+        copy.wait()
+    for i in range(IMGS):
+        rows = slice(i * PACK, (i + 1) * PACK)
+        tok = dot(one_hot_pack(pos, i), xs[i])
+        tok_o[rows, :] = tok.astype(BF)
+        z, _ = statistics(tok)
+        norm_o[rows, :] = (z * gain[...] + bias[...]).astype(BF)
+    normed = norm_o[...]
+    for m in range(3):
+        loads[m].wait()
+        part = dot(normed, w[m])
+        if m != 1:
+            part = part + qvb[m // 2 : m // 2 + 1, pl.ds(heads, HALF)]
+        qkv_o[m] = part.astype(BF)
+    lane = lax.broadcasted_iota(jnp.int32, (PACK, 128), 1)
+    for i in range(IMGS):
+        rows = slice(i * PACK, (i + 1) * PACK)
+        key_ok = keys_shown(pos, i)
+        for hp in range(3):
+            cols = slice(hp * 128, (hp + 1) * 128)
+            q2, k2, v2 = (qkv_o[m, rows, cols] for m in range(3))
+            outs = [dot(head_probs(q2, k2, e, key_ok).astype(BF), v2) for e in range(2)]
+            mix_o[rows, cols] = jnp.where(lane < HD, outs[0], outs[1]).astype(BF)
+
+
+def second_kernel(
+    mix_a, mix_b, tok, c0, c1, c2, c3, pos_r, wp, bp, a_scale, gain, bias, we, be, wr, br, m_scale,
+    res_o, one_o, pre_o, gb2_o, n2_o, mix_o, act_o, gh_o, gn2_o, bt2_o, small_o,
+    xs, we_v, wr_v, act_v, sems,
+):
+    x, c, _, _ = place()
+    mine, other = pl.multiple_of(c * HALF, 128), pl.multiple_of((1 - c) * HALF, 128)
+    copy_a = pltpu.make_async_copy(mix_a, mix_o.at[:, pl.ds(mine, HALF)], sems.at[6])
+    copy_b = pltpu.make_async_copy(mix_b, mix_o.at[:, pl.ds(other, HALF)], sems.at[7])
+    copy_a.start()
+    copy_b.start()
+    copies = gather_bands((c0, c1, c2, c3), xs, sems)
+    units = pl.multiple_of(c * FH, 128)
+    load_e = pltpu.make_async_copy(we.at[:, pl.ds(units, FH)], we_v, sems.at[4])
+    load_r = pltpu.make_async_copy(wr.at[pl.ds(units, FH), :], wr_v, sems.at[5])
+    load_e.start()
+    load_r.start()
+    pos = pos_r[...]
+    copy_a.wait()
+    copy_b.wait()
+    one = dot(mix_o[...], wp[...]) + bp[...]
+    one_o[...] = one
+    residual = tok[...].astype(F32) + a_scale[...] * one
+    res_o[...] = residual
+    z, _ = statistics(residual)
+    n2_o[...] = (z * gain[...] + bias[...]).astype(BF)
+    for copy in copies:
+        copy.wait()
+    for i in range(IMGS):
+        rows = slice(i * PACK, (i + 1) * PACK)
+        pre = dot(one_hot_pack(pos, i), xs[i])
+        pre_o[rows, :] = pre.astype(BF)
+        gb2_o[rows, :] = (m_scale[...] * pre).astype(BF)
+    load_e.wait()
+    load_r.wait()
+    step = 256
+    for f in range(FH // step):
+        cols = slice(f * step, (f + 1) * step)
+        shift = be[:, pl.ds(pl.multiple_of(c * FH + f * step, 128), step)]
+        hidden = dot(n2_o[...], we_v[:, cols]) + shift
+        phi = 0.5 * (1.0 + lax.erf(hidden * math.sqrt(0.5)))
+        act_v[:, cols] = (hidden * phi).astype(BF)
+        slope = phi + hidden * (jnp.exp(-0.5 * hidden * hidden) * (1.0 / math.sqrt(2.0 * math.pi)))
+        back = dot_nt(gb2_o[...], wr_v[cols, :])
+        gh_o[:, cols] = (back * slope).astype(BF)
+    gn2_o[...] = dot_nt(gh_o[...], we_v[...]).astype(BF)
+    act_o[...] = act_v[:, pl.ds(pl.multiple_of(x * D, 128), D)]
+    two = dot(act_v[...], wr_v[...])
+    bt2_o[...] = two.astype(BF)
+    pre = pre_o[...].astype(F32)
+    first = jnp.where(c == 0, 1.0, 0.0)
+    small_o[...] = jnp.zeros_like(small_o)
+    small_o[0:1, :] = first * jnp.sum(gb2_o[...].astype(F32), axis=0, keepdims=True)
+    small_o[1:2, :] = jnp.sum(pre * (two + first * br[...]), axis=0, keepdims=True)
+
+
+def mlp_grads_kernel(n2, gh, act, gb2, wr_send, wr_keep, we_send, we_keep, eb_o, full, sums):
+    x, c, z, y = place()
+    full[...] = dot_tn(act[...], gb2[...])
+    for dy, out in ((1, wr_send), (0, wr_keep)):
+        for dz in range(4):
+            k = 4 * (y ^ dy) + (z ^ dz)
+            out[dz] = full[pl.ds(pl.multiple_of(96 * k, 96), 96), :].astype(BF)
+    picked = dot(n2[...], feature_pick()).astype(BF)
+    for dy, out in ((1, we_send), (0, we_keep)):
+        for dz in range(4):
+            lo = 192 * dy + 48 * dz
+            out[dz] = dot_tn(picked[:, lo : lo + 48], gh[...]).astype(BF)
+    sums[...] = dot_tn(gh[...], jnp.ones((ROWS, 128), BF))
+    lane = lax.broadcasted_iota(jnp.int32, (48, SMALL), 1)
+    for q in range(8):
+        b = (z ^ (q % 4)) * 2 + (y ^ (q // 4))
+        here = (b >> 2) == c
+        block = jnp.zeros((48, SMALL), F32)
+        for k in range(4):
+            at = pl.multiple_of(384 * (b & 3) + 192 * x + 48 * k, 48)
+            block = jnp.where((lane == 10 + k) & here, sums[pl.ds(at, 48), :], block)
+        eb_o[q] = block
+
+
+def third_kernel(
+    gn2_a, gn2_b, res, one, pre, tok, normed, qkv, mix, pos_r, small2, eb, wp, wqkv, a_scale, gain2, gain1,
+    gres_o, gnp_o, send_o, keep_o,
+    w, wp_v, gp, vecs, sems,
+):
+    x, c, z, y = place()
+    heads = pl.multiple_of(c * HALF, 128)
+    loads = []
+    for m in range(3):
+        src = wqkv.at[:, pl.ds(pl.multiple_of(m * D + c * HALF, 128), HALF)]
+        loads.append(pltpu.make_async_copy(src, w.at[m], sems.at[m]))
+        loads[-1].start()
+    load_p = pltpu.make_async_copy(wp.at[pl.ds(heads, HALF), :], wp_v, sems.at[3])
+    load_p.start()
+    first = jnp.where(c == 0, 1.0, 0.0)
+
+    def total(v):
+        return jnp.sum(v, axis=0, keepdims=True)
+
+    vecs[...] = jnp.zeros_like(vecs)
+    gn2 = gn2_a[...].astype(F32) + gn2_b[...].astype(F32)
+    z2, rstd2 = statistics(res[...])
+    vecs[6:7, :] = first * total(gn2 * z2)
+    vecs[7:8, :] = first * total(gn2)
+    gres = pre[...].astype(F32) + norm_back(gn2 * gain2[...], z2, rstd2)
+    gres_o[...] = gres
+    vecs[5:6, :] = first * total(gres * one[...])
+    gb1 = (a_scale[...] * gres).astype(BF)
+    vecs[4:5, :] = first * total(gb1.astype(F32))
+    vecs[8:10, :] = small2[0:2, :]
+    load_p.wait()
+    gm = dot_nt(gb1, wp_v[...]).astype(BF)
+    pos = pos_r[...]
+    lane = lax.broadcasted_iota(jnp.int32, (PACK, 128), 1)
+    scale = 1.0 / math.sqrt(HD)
+    for i in range(IMGS):
+        rows = slice(i * PACK, (i + 1) * PACK)
+        key_ok = keys_shown(pos, i)
+        for hp in range(3):
+            cols = slice(hp * 128, (hp + 1) * 128)
+            q2, k2, v2 = (qkv[m, rows, cols] for m in range(3))
+            g2 = gm[rows, cols]
+            grads = []
+            for e in range(2):
+                probs = head_probs(q2, k2, e, key_ok)
+                gmine = jnp.where((lane < HD) if e == 0 else (lane >= HD), g2, jnp.zeros_like(g2))
+                gprob = dot_nt(gmine, v2)
+                delta = jnp.sum(probs * gprob, axis=-1, keepdims=True)
+                gscore = (probs * (gprob - delta)).astype(BF)
+                grads.append(
+                    (
+                        dot(gscore, k2) * scale,
+                        dot_tn(gscore, q2) * scale,
+                        dot_tn(probs.astype(BF), g2),
+                    )
+                )
+            for m in range(3):
+                both = jnp.where(lane < HD, grads[0][m], grads[1][m])
+                gp[rows, m * HALF + hp * 128 : m * HALF + (hp + 1) * 128] = both.astype(BF)
+    gnp = jnp.zeros((ROWS, D), F32)
+    for m in range(3):
+        loads[m].wait()
+        gnp = gnp + dot_nt(gp[:, m * HALF : (m + 1) * HALF], w[m])
+    gnp_o[...] = gnp.astype(BF)
+    z1, _ = statistics(tok[...].astype(F32))
+    vecs[0:1, :] = total(gnp * z1)
+    vecs[1:2, :] = total(gnp)
+    vecs[2:3, pl.ds(heads, HALF)] = total(gp[:, 0:HALF].astype(F32))
+    vecs[3:4, pl.ds(heads, HALF)] = total(gp[:, 2 * HALF : 3 * HALF].astype(F32))
+    pick = feature_pick()
+    picked = dot(normed[...], pick).astype(BF)
+    rowl = lax.broadcasted_iota(jnp.int32, (D, 256), 0)
+    colr = lax.broadcasted_iota(jnp.int32, (D, 256), 1)
+    want = jnp.full((D, 256), -1, jnp.int32)
+    for q in range(8):
+        base = 96 * ((z ^ (q % 4)) * 2 + (y ^ (q // 4))) + 48 * x + 24 * c - 32 * q
+        want = jnp.where((colr >= 32 * q) & (colr < 32 * q + 24), colr + base, want)
+    pick_p = jnp.where(rowl == want, 1.0, 0.0).astype(BF)
+    mixed = dot(mix[...], pick_p).astype(BF)
+    vec_cols = lax.dot_general(
+        pick, vecs[...].astype(BF), (((0,), (1,)), ((), ())), preferred_element_type=F32
+    )
+    for dy, out in ((1, send_o), (0, keep_o)):
+        for dz in range(4):
+            q = 4 * dy + dz
+            lo = 48 * q
+            out[dz, :, 0 : 3 * HALF] = dot_tn(picked[:, lo : lo + 48], gp[...]).astype(BF)
+            out[dz, :, 3 * HALF : 3 * HALF + SMALL] = (vec_cols[lo : lo + 48] + eb[q]).astype(BF)
+            proj = dot_tn(mixed[:, 32 * q : 32 * q + 32], gb1).astype(BF)
+            out[dz, 0:32, 1280:1792] = proj[:, 0:512]
+            out[dz, 32:48, 1280:1536] = proj[0:16, 512:768]
+            out[dz, 32:48, 1536:1792] = proj[16:32, 512:768]
+
+
+def last_kernel(gnp_a, gnp_b, tok, gres, bt2_a, bt2_b, res, pos_r, gain1, m_scale, br, out_o, gtok_o, wide):
+    band = lax.axis_index("band")
+    at = pl.multiple_of(band * BAND, BAND)
+    pos = pos_r[...]
+    for i in range(IMGS):
+        rows = slice(i * PACK, (i + 1) * PACK)
+        z1, rstd1 = statistics(tok[rows, :].astype(F32))
+        gnp = gnp_a[rows, :].astype(F32) + gnp_b[rows, :].astype(F32)
+        gtok = (gres[rows, :] + norm_back(gnp * gain1[...], z1, rstd1)).astype(BF)
+        two = bt2_a[rows, :].astype(F32) + bt2_b[rows, :].astype(F32) + br[...]
+        out = (res[rows, :] + m_scale[...] * two).astype(BF)
+        pack = one_hot_pack(pos, i)
+        for value, dst in ((gtok, gtok_o), (out, out_o)):
+            wide[...] = dot_tn(pack, value)
+            dst[i] = wide[pl.ds(at, BAND), :].astype(BF)
+
+
+def call(kernel, outs, specs, scratch=(), flops=0, nbytes=0, vmem=40):
+    return pl.pallas_call(
+        kernel,
+        out_shape=outs,
+        in_specs=specs,
+        out_specs=jax.tree.map(lambda _: VM, outs),
+        scratch_shapes=list(scratch),
+        compiler_params=pltpu.CompilerParams(vmem_limit_bytes=vmem * MIB),
+        cost_estimate=pl.CostEstimate(flops=flops, bytes_accessed=nbytes, transcendentals=0),
+    )
+
+
+def by_core(value):
+    return lax.ppermute(value, "band", [(i, i ^ 1) for i in range(4)])
+
+
+def by_x(value):
+    return lax.ppermute(value, "band", [(i, i ^ 2) for i in range(4)])
+
+
+def by_y(value):
+    return lax.ppermute(value, "batch", [(i, i ^ 1) for i in range(8)])
+
+
+def by_z(value, dz):
+    return lax.ppermute(value, "batch", [(i, i ^ (2 * dz)) for i in range(8)])
+
+
+def reduce_shards(send, keep):
+    arrived = by_y(send)
+    both = keep.astype(F32) + arrived.astype(F32)
+    parts = [by_z(both[dz].astype(BF), dz) for dz in (1, 2, 3)]
+    return both[0] + parts[0].astype(F32) + parts[1].astype(F32) + parts[2].astype(F32)
+
+
+def packed_body(
+    tokens, cotangent, visible, first_gain, first_bias, qkv_weight, qv_bias, proj_weight, proj_bias,
+    attn_scale, second_gain, second_bias, expand_weight, expand_bias, reduce_weight, reduce_bias, mlp_scale,
+):
+    band = lax.axis_index("band")
+    core = band & 1
+    row = lambda v: v.reshape(1, -1)
+    g1, b1, g2, b2 = row(first_gain), row(first_bias), row(second_gain), row(second_bias)
+    bp, asc, br, msc, be = row(proj_bias), row(attn_scale), row(reduce_bias), row(mlp_scale), row(expand_bias)
+
+    tok_x = by_x(tokens)
+    spread = lax.dynamic_update_slice(
+        jnp.zeros((8, SLOTS), F32), visible.astype(F32), (jnp.int32(0), band * BAND)
+    )
+    vis_x = by_x(spread)
+    cot_x = by_x(cotangent)
+    tok_c = by_core(tokens)
+    vis_chip = spread + vis_x
+    vis_c = by_core(vis_chip)
+    tok_d = by_core(tok_x)
+    cot_c = by_core(cotangent)
+    cot_d = by_core(cot_x)
+
+    tok, normed, qkv, mix_own, pos = call(
+        first_kernel,
+        (
+            sds((ROWS, D), BF),
+            sds((ROWS, D), BF),
+            sds((3, ROWS, HALF), BF),
+            sds((ROWS, HALF), BF),
+            sds((8, SLOTS), F32),
+        ),
+        [ANY] * 4 + [VM] * 4 + [ANY, VM],
+        [
+            pltpu.VMEM((IMGS, SLOTS, D), BF),
+            pltpu.VMEM((3, D, HALF), BF),
+            pltpu.SemaphoreType.DMA((7,)),
+        ],
+        flops=int(1.5e9),
+        nbytes=int(6e6),
+    )(tokens, tok_c, tok_x, tok_d, vis_chip, vis_c, g1, b1, qkv_weight, qv_bias)
+    mix_other = by_core(mix_own)
+    res, one, pre, gb2, n2, mix, act, gh, gn2, bt2, small2 = call(
+        second_kernel,
+        (
+            sds((ROWS, D), F32),
+            sds((ROWS, D), F32),
+            sds((ROWS, D), BF),
+            sds((ROWS, D), BF),
+            sds((ROWS, D), BF),
+            sds((ROWS, D), BF),
+            sds((ROWS, D), BF),
+            sds((ROWS, FH), BF),
+            sds((ROWS, D), BF),
+            sds((ROWS, D), BF),
+            sds((8, D), F32),
+        ),
+        [ANY] * 2 + [VM] + [ANY] * 4 + [VM] * 6 + [ANY, VM, ANY] + [VM] * 2,
+        [
+            pltpu.VMEM((IMGS, SLOTS, D), BF),
+            pltpu.VMEM((D, FH), BF),
+            pltpu.VMEM((FH, D), BF),
+            pltpu.VMEM((ROWS, FH), BF),
+            pltpu.SemaphoreType.DMA((8,)),
+        ],
+        flops=int(5e9),
+        nbytes=int(15e6),
+    )(
+        mix_own, mix_other, tok, cotangent, cot_c, cot_x, cot_d, pos, proj_weight, bp, asc, g2, b2,
+        expand_weight, be, reduce_weight, br, msc,
+    )
+    gn2_other = by_core(gn2)
+    wr_send, wr_keep, we_send, we_keep, eb = call(
+        mlp_grads_kernel,
+        (
+            sds((4, 96, D), BF),
+            sds((4, 96, D), BF),
+            sds((4, 48, FH), BF),
+            sds((4, 48, FH), BF),
+            sds((8, 48, SMALL), F32),
+        ),
+        [VM] * 4,
+        [pltpu.VMEM((D, D), F32), pltpu.VMEM((FH, 128), F32)],
+        flops=int(2e9),
+        nbytes=int(6e6),
+    )(n2, gh, act, gb2)
+    wr_sum = reduce_shards(wr_send, wr_keep)
+    we_sum = reduce_shards(we_send, we_keep)
+    gres, gnp, qp_send, qp_keep = call(
+        third_kernel,
+        (
+            sds((ROWS, D), F32),
+            sds((ROWS, D), BF),
+            sds((4, 48, 1792), BF),
+            sds((4, 48, 1792), BF),
+        ),
+        [VM] * 12 + [ANY] * 2 + [VM] * 3,
+        [
+            pltpu.VMEM((3, D, HALF), BF),
+            pltpu.VMEM((HALF, D), BF),
+            pltpu.VMEM((ROWS, 3 * HALF), BF),
+            pltpu.VMEM((SMALL, D), F32),
+            pltpu.SemaphoreType.DMA((4,)),
+        ],
+        flops=int(4e9),
+        nbytes=int(12e6),
+    )(
+        gn2, gn2_other, res, one, pre, tok, normed, qkv, mix, pos, small2, eb, proj_weight, qkv_weight,
+        asc, g2, g1,
+    )
+    qp_sum = reduce_shards(qp_send, qp_keep)
+    bt2_other = by_core(bt2)
+    gnp_other = by_core(gnp)
+    layer_out, grad_tokens = call(
+        last_kernel,
+        (sds((IMGS, BAND, D), BF), sds((IMGS, BAND, D), BF)),
+        [VM] * 11,
+        [pltpu.VMEM((SLOTS, D), F32)],
+        flops=int(1e9),
+        nbytes=int(8e6),
+    )(gnp, gnp_other, tok, gres, bt2, bt2_other, res, pos, g1, msc, br)
+
+    moves = []
+    for b in range(8):
+        for g in range(4):
+            z, y, x, c = b >> 1, b & 1, g >> 1, g & 1
+            moves.append((b * 4 + g, ((2 * c + x) * 2 + y) * 4 + z))
+    grad_reduce = lax.ppermute(wr_sum, ("batch", "band"), moves)
+
+    def swap(mine):
+        keep = jnp.where(core == 0, mine[0:24], mine[24:48])
+        other = by_core(jnp.where(core == 0, mine[24:48], mine[0:24]))
+        first = jnp.where(core == 0, keep, other)
+        second = jnp.where(core == 0, other, keep)
+        return first, second
+
+    grad_expand = jnp.concatenate(swap(we_sum), axis=1)
+    qkv_first, qkv_second = swap(qp_sum[:, 0 : 3 * HALF])
+    pieces = []
+    for m in range(3):
+        cols = slice(m * HALF, (m + 1) * HALF)
+        pieces += [qkv_first[:, cols], qkv_second[:, cols]]
+    grad_qkv = jnp.concatenate(pieces, axis=1)
+    vec = qp_sum[:, 3 * HALF : 3 * HALF + SMALL]
+    vec = vec + by_core(vec)
+    own = jnp.where(core == 0, vec[0:24], vec[24:48]).T
+    grad_expand_bias = jnp.where(core == 0, vec[:, 10:12], vec[:, 12:14]).T.reshape(96)
+    proj = jnp.concatenate(
+        [
+            qp_sum[0:32, 1280:1792],
+            jnp.concatenate([qp_sum[32:48, 1280:1536], qp_sum[32:48, 1536:1792]], axis=0),
+        ],
+        axis=1,
+    )[0:24]
+    return (
+        layer_out, grad_tokens, own[0], own[1], grad_qkv, own[2:4], proj, own[4], own[5], own[6], own[7],
+        grad_expand, grad_expand_bias, grad_reduce, own[8], own[9],
+    )
 
 
 def layer_norm(values, norm_gain, norm_shift):
@@ -273,6 +798,8 @@
 
 
 def solution(mesh):
+    sizes = dict(mesh.shape)
+    chosen = packed_body if (sizes["batch"], sizes["band"]) == (8, 4) else body
     placed = (
         P("batch", "band", None),
         P("batch", "band", None),
@@ -293,7 +820,7 @@
         P(),
     )
     return jax.shard_map(
-        body,
+        chosen,
         mesh=mesh,
         in_specs=placed,
         out_specs=(

time: 618 us -> 141 us (0.23)
  waiting for transfers between devices: 368 us -> 53 us
  blocking collectives: 77.8 us -> 0 us
  matrix products: 61.1 us -> 0 us
  local copies, waits for them, and re-layouts: 60.9 us -> 13.4 us
  Pallas kernels: 0 us -> 35 us
  starting transfers between devices: 13.3 us -> 31.9 us
  other arithmetic: 20 us -> 6.3 us
  between operations: 14.4 us -> 1.16 us
    reduce_scatter x4 -> x0, waiting for transfers between devices: 346 us -> none  [the longest x1 142 us: body(): lax.psum_scatter(grad_reduce_weight, ('batch', 'band'), scatter_dimension...]
    dot_general x18 -> x0, matrix products: 61.1 us -> none  [the longest x1 6.62 us: body(): jnp.einsum('isd,isf->df', normed_two_low, grad_hidden, preferred_element_...]
    ppermute x0 -> x28, waiting for transfers between devices: none -> 53 us  [the longest x3 27.8 us: by_y(): return lax.ppermute(value, 'batch', [(i, i ^ 1) for i in range(8)])]
    unnamed x1 -> x0, blocking collectives: 41 us -> none
    all_to_all x2 -> x0, blocking collectives: 36.8 us -> none  [the longest x1 24.5 us: body(): lax.all_to_all(grad_packed, 'band', split_axis=1, concat_axis=3, tiled=True)]
    pallas_call x0 -> x5, Pallas kernels: none -> 35 us  [the longest x1 16.3 us: packed_body(): call(third_kernel, (sds((ROWS, D), F32), sds((ROWS, D), BF), sds((4, 48,...]
    ppermute x0 -> x28, starting transfers between devices: none -> 31.9 us  [the longest x9 18.3 us: by_z(): return lax.ppermute(value, 'batch', [(i, i ^ 2 * dz) for i in range(8)])]
    reshape x9, local copies, waits for them, and re-layouts: 25.1 us -> 2.01 us  [the longest x8 1.41 us: packed_body(): row = lambda v: v.reshape(1, -1)]
  transfers between devices with their start and end apart: 7 -> 28, of which waited for: 5 -> 11; matrix products, arithmetic and copies ran while one was open for 16% -> 7% of each run, Pallas kernels for 0% -> 17%
where the time goes in v1:
time: 141 us
  waiting for transfers between devices  53 us (38%)
  Pallas kernels  35 us (25%)
  starting transfers between devices  31.9 us (23%)
  local copies, waits for them, and re-layouts  13.4 us (10%)
  other arithmetic  6.3 us (4%)
    ppermute x3, waiting for transfers between devices, by_y(): return lax.ppermute(value, 'batch', [(i, i ^ 1) for i in range(8)])  27.8 us
    ppermute x9, starting transfers between devices, by_z(): return lax.ppermute(value, 'batch', [(i, i ^ 2 * dz) for i in range(8)])  18.3 us
    pallas_call x1, Pallas kernels, packed_body(): call(third_kernel, (sds((ROWS, D), F32), sds((ROWS, D), BF), sds((4, 48,...  16.3 us
    ppermute x9, waiting for transfers between devices, by_z(): return lax.ppermute(value, 'batch', [(i, i ^ 2 * dz) for i in range(8)])  14.1 us
    unnamed x61, local copies, waits for them, and re-layouts  9.79 us
    ppermute x3, waiting for transfers between devices, by_x(): return lax.ppermute(value, 'band', [(i, i ^ 2) for i in range(4)])  8.83 us
    pallas_call x1, Pallas kernels, packed_body(): call(second_kernel, (sds((ROWS, D), F32), sds((ROWS, D), F32), sds((ROWS,...  7.45 us
    ppermute x3, starting transfers between devices, by_x(): return lax.ppermute(value, 'band', [(i, i ^ 2) for i in range(4)])  5.11 us
  transfers between devices with their start and end apart: 28, of which 11 were waited for; matrix products, arithmetic and copies ran while one was open for 7% of the time, Pallas kernels for 17%

profile of v1, /device:TPU:0, one launch (start us, length us, event | category | flops | bytes accessed | tf_op | source)
XLA Modules:
  0.0 140.7 jit_solution(13478424535116237168)
XLA Ops:
  0.6 3.0 %collective-permute-start.1 = (bf16[3,64,768]{2,1,0:T(8,128)(2,1)}, bf16[3,64,768]{2,1,0:T(8,128)(2,1)S(1)}, u32[]{:S(2)}, u32[]{:S(2)}) collective-permute-start(bf16[3,64,768]{2,1,0:T(8,128)(2,1)} %t0.1), channel_id=1, source_target_pairs={{0,2},{1,3},{2,0},{3,1},{4,6},{5,7},{6,4},{7,5},{8,10},{9,11},{10,... | collective-permute-start | bytes 884744 | tf_op jit(solution)/shard_map/ppermute | solution.py:361
  3.7 7.2 %collective-permute-done.1.t2 = bf16[3,64,768]{2,1,0:T(8,128)(2,1)S(1)} collective-permute-done((bf16[3,64,768]{2,1,0:T(8,128)(2,1)}, bf16[3,64,768]{2,1,0:T(8,128)(2,1)S(1)}, u32[]{:S(2)}, u32[]{:S(2)}) %collective-permute-start.1) | collective-permute-done | bytes 294944 | tf_op jit(solution)/shard_map/ppermute | solution.py:361
  10.9 0.7 convert_element_type.84
  11.8 1.8 %collective-permute-start.3 = (f32[8,256]{1,0:T(8,128)S(1)}, f32[8,256]{1,0:T(8,128)S(1)}, u32[]{:S(2)}, u32[]{:S(2)}) collective-permute-start(f32[8,256]{1,0:T(8,128)S(1)} %dynamic_update_slice.5), channel_id=1, source_target_pairs={{0,2},{1,3},{2,0},{3,1},{4,6},{5,7},{6,4},{7,5},{8,10},{9,11},{10,... | collective-permute-start | bytes 24584 | tf_op jit(solution)/shard_map/ppermute | solution.py:361
  13.9 1.6 %collective-permute-done.3 = f32[8,256]{1,0:T(8,128)S(1)} collective-permute-done((f32[8,256]{1,0:T(8,128)S(1)}, f32[8,256]{1,0:T(8,128)S(1)}, u32[]{:S(2)}, u32[]{:S(2)}) %collective-permute-start.3) | collective-permute-done | bytes 8224 | tf_op jit(solution)/shard_map/ppermute | solution.py:361
  15.5 0.8 dynamic-slice_add_fusion
  16.6 0.7 reshape.71.gain.gain1
  17.3 0.7 reshape.72.bias
  18.0 2.0 %copy-done.1 = bf16[768,2304]{1,0:T(8,128)(2,1)S(1)} copy-done((bf16[768,2304]{1,0:T(8,128)(2,1)S(1)}, bf16[768,2304]{1,0:T(8,128)(2,1)}, u32[]{:S(2)}) %copy-start.1) | copy-done | bytes 3538968
  20.0 1.0 copy-done.6
  21.0 0.7 copy-done.9
  21.7 4.3 %shard_map.288 = (bf16[432,768]{1,0:T(8,128)(2,1)S(1)}, bf16[432,768]{1,0:T(8,128)(2,1)S(1)}, bf16[3,432,384]{2,1,0:T(8,128)(2,1)S(1)}, bf16[432,384]{1,0:T(8,128)(2,1)S(1)}, f32[8,256]{1,0:T(8,128)S(1)}) custom-call(bf16[3,64,768]{2,1,0:T(8,128)(2,1)S(1)} %copy-done.6, bf16[3,64,768]{2,1,0:T(8,128)(2,1)S(1)} %collective-permute-done.t1, ...), custom_call_target="tpu_custom_call" | custom-call | flops 1500000000 | bytes 6000000 | tf_op jit(solution)/shard_map/pallas_call | solution.py:402
  26.0 1.0 copy-done.10
  27.0 0.8 copy-done.12
  28.9 1.1 collective-permute-done.6.c1
  30.4 7.5 %shard_map.289 = (f32[432,768]{1,0:T(8,128)S(1)}, f32[432,768]{1,0:T(8,128)S(1)}, bf16[432,768]{1,0:T(8,128)(2,1)S(1)}, bf16[432,768]{1,0:T(8,128)(2,1)S(1)}, bf...) custom-call(bf16[432,384]{1,0:T(8,128)(2,1)S(1)} %get-tuple-element., ...), custom_call_target="tpu_custom_call" | custom-call | flops 5000000000 | bytes 15000000 | tf_op jit(solution)/shard_map/pallas_call | solution.py:421
  37.9 1.1 copy-done.14
  39.0 0.8 copy-done.16
  39.9 4.2 %shard_map.290 = (bf16[4,96,768]{2,1,0:T(8,128)(2,1)}, bf16[4,96,768]{2,1,0:T(8,128)(2,1)S(1)}, bf16[4,48,1536]{2,1,0:T(8,128)(2,1)}, bf16[4,48,1536]{2,1,0:T(8,128)(2,1)S(1)}, f32[8,48,128]{2,1,0:T(8,128)S(1)}) custom-call(bf16[432,768]{1,0:T(8,128)(2,1)S(1)} %get-tuple-element.54.n2, bf16[432,1536]{1,0:T(8,128)(2,1)S(1)} %get-tuple-element.55.gh, ...), custom_call_target="tpu_custom_call" | custom-call | flops 2000000000 | bytes 6000000 | tf_op jit(solution)/shard_map/pallas_call | solution.py:451
  44.1 0.9 copy-done
  45.0 1.8 %collective-permute-start.23 = (bf16[4,96,768]{2,1,0:T(8,128)(2,1)}, bf16[4,96,768]{2,1,0:T(8,128)(2,1)}, u32[]{:S(2)}, u32[]{:S(2)}) collective-permute-start(bf16[4,96,768]{2,1,0:T(8,128)(2,1)} %get-tuple-element.69), channel_id=1, source_target_pairs={{0,4},{4,0},{8,12},{12,8},{16,20},{20,16},{24,28},{28,24},{1,5},{5... | collective-permute-start | bytes 1769480 | tf_op jit(solution)/shard_map/ppermute | solution.py:365
  47.0 0.5 collective-permute-start.11
  47.5 13.9 %collective-permute-done.23 = bf16[4,96,768]{2,1,0:T(8,128)(2,1)} collective-permute-done((bf16[4,96,768]{2,1,0:T(8,128)(2,1)}, bf16[4,96,768]{2,1,0:T(8,128)(2,1)}, u32[]{:S(2)}, u32[]{:S(2)}) %collective-permute-start.23) | collective-permute-done | bytes 589856 | tf_op jit(solution)/shard_map/ppermute | solution.py:365
  61.4 1.5 %fusion.12 = (bf16[4,96,768]{2,1,0:T(8,128)(2,1)S(1)}, f32[4,96,768]{2,1,0:T(8,128)S(1)}) fusion(bf16[4,96,768]{2,1,0:T(8,128)(2,1)} %collective-permute-done.23, bf16[4,96,768]{2,1,0:T(8,128)(2,1)} %copy-done), kind=kLoop, calls=%fused_computation.56 | loop fusion | flops 1179648 | bytes 2949120 | tf_op jit(solution)/shard_map/convert.2
  63.0 1.9 %collective-permute-start.24 = (bf16[96,768]{1,0:T(8,128)(2,1)S(1)}, bf16[96,768]{1,0:T(8,128)(2,1)S(1)}, u32[]{:S(2)}, u32[]{:S(2)}) collective-permute-start(bf16[96,768]{1,0:T(8,128)(2,1)S(1)} %get-tuple-element.119), channel_id=1, source_target_pairs={{0,8},{4,12},{8,0},{12,4},{16,24},{20,28},{24,16},{28,20},{1,9},{5... | collective-permute-start | bytes 442376 | tf_op jit(solution)/shard_map/ppermute | solution.py:369
  64.9 8.6 %collective-permute-done.18 = bf16[4,48,1536]{2,1,0:T(8,128)(2,1)} collective-permute-done((bf16[4,48,1536]{2,1,0:T(8,128)(2,1)}, bf16[4,48,1536]{2,1,0:T(8,128)(2,1)}, u32[]{:S(2)}, u32[]{:S(2)}) %collective-permute-start.18) | collective-permute-done | bytes 589856 | tf_op jit(solution)/shard_map/ppermute | solution.py:365
  73.6 1.4 fusion.11
  75.0 1.9 %collective-permute-start.19 = (bf16[48,1536]{1,0:T(8,128)(2,1)S(1)}, bf16[48,1536]{1,0:T(8,128)(2,1)S(1)}, u32[]{:S(2)}, u32[]{:S(2)}) collective-permute-start(bf16[48,1536]{1,0:T(8,128)(2,1)S(1)} %get-tuple-element.122), channel_id=1, source_target_pairs={{0,8},{4,12},{8,0},{12,4},{16,24},{20,28},{24,16},{28,20},{1,9},{5... | collective-permute-start | bytes 442376 | tf_op jit(solution)/shard_map/ppermute | solution.py:369
  76.9 2.6 %collective-permute-start.20 = (bf16[48,1536]{1,0:T(8,128)(2,1)S(1)}, bf16[48,1536]{1,0:T(8,128)(2,1)S(1)}, u32[]{:S(2)}, u32[]{:S(2)}) collective-permute-start(bf16[48,1536]{1,0:T(8,128)(2,1)S(1)} %get-tuple-element.124), channel_id=1, source_target_pairs={{0,16},{4,20},{8,24},{12,28},{16,0},{20,4},{24,8},{28,12},{1,17},{... | collective-permute-start | bytes 442376 | tf_op jit(solution)/shard_map/ppermute | solution.py:369
  79.6 16.3 %shard_map.291 = (f32[432,768]{1,0:T(8,128)S(1)}, bf16[432,768]{1,0:T(8,128)(2,1)S(1)}, bf16[4,48,1792]{2,1,0:T(8,128)(2,1)S(1)}, bf16[4,48,1792]{2,1,0:T(8,128)(2,1)S(1)}) custom-call(bf16[432,768]{1,0:T(8,128)(2,1)S(1)} %copy-done.5, bf16[432,768]{1,0:T(8,128)(2,1)S(1)} %collective-permute-done.9.gn2_b, f32[432,768]{1,0:T(8,128)S(1)} %get-tuple-element.47.res, ...), custom_call_target="tpu_custom_call" | custom-call | flops 4000000000 | bytes 12000000 | tf_op jit(solution)/shard_map/pallas_call | solution.py:467
  95.9 1.9 %collective-permute-start.25 = (bf16[96,768]{1,0:T(8,128)(2,1)S(1)}, bf16[96,768]{1,0:T(8,128)(2,1)S(1)}, u32[]{:S(2)}, u32[]{:S(2)}) collective-permute-start(bf16[96,768]{1,0:T(8,128)(2,1)S(1)} %get-tuple-element.121), channel_id=1, source_target_pairs={{0,16},{4,20},{8,24},{12,28},{16,0},{20,4},{24,8},{28,12},{1,17},{... | collective-permute-start | bytes 442376 | tf_op jit(solution)/shard_map/ppermute | solution.py:369
  97.8 2.0 %collective-permute-start.26 = (bf16[96,768]{1,0:T(8,128)(2,1)S(1)}, bf16[96,768]{1,0:T(8,128)(2,1)S(1)}, u32[]{:S(2)}, u32[]{:S(2)}) collective-permute-start(bf16[96,768]{1,0:T(8,128)(2,1)S(1)} %get-tuple-element.120), channel_id=1, source_target_pairs={{0,24},{4,28},{8,16},{12,20},{16,8},{20,12},{24,0},{28,4},{1,25},{... | collective-permute-start | bytes 442376 | tf_op jit(solution)/shard_map/ppermute | solution.py:369
  99.8 1.5 %collective-permute-start.12 = (bf16[4,48,1792]{2,1,0:T(8,128)(2,1)S(1)}, bf16[4,48,1792]{2,1,0:T(8,128)(2,1)S(1)}, u32[]{:S(2)}, u32[]{:S(2)}) collective-permute-start(bf16[4,48,1792]{2,1,0:T(8,128)(2,1)S(1)} %get-tuple-element.65), channel_id=1, source_target_pairs={{0,4},{4,0},{8,12},{12,8},{16,20},{20,16},{24,28},{28,24},{1,5},{5... | collective-permute-start | bytes 2064392 | tf_op jit(solution)/shard_map/ppermute | solution.py:365
  101.5 7.4 %collective-permute-done.25 = bf16[96,768]{1,0:T(8,128)(2,1)S(1)} collective-permute-done((bf16[96,768]{1,0:T(8,128)(2,1)S(1)}, bf16[96,768]{1,0:T(8,128)(2,1)S(1)}, u32[]{:S(2)}, u32[]{:S(2)}) %collective-permute-start.25) | collective-permute-done | bytes 147488 | tf_op jit(solution)/shard_map/ppermute | solution.py:369
  109.0 0.9 collective-permute-start.27
  110.4 5.2 %collective-permute-done.12 = bf16[4,48,1792]{2,1,0:T(8,128)(2,1)S(1)} collective-permute-done((bf16[4,48,1792]{2,1,0:T(8,128)(2,1)S(1)}, bf16[4,48,1792]{2,1,0:T(8,128)(2,1)S(1)}, u32[]{:S(2)}, u32[]{:S(2)}) %collective-permute-start.12) | collective-permute-done | bytes 688160 | tf_op jit(solution)/shard_map/ppermute | solution.py:365
  115.8 0.6 collective-permute-start.13
  116.4 1.5 %collective-permute-start.14 = (bf16[48,1792]{1,0:T(8,128)(2,1)S(1)}, bf16[48,1792]{1,0:T(8,128)(2,1)S(1)}, u32[]{:S(2)}, u32[]{:S(2)}) collective-permute-start(bf16[48,1792]{1,0:T(8,128)(2,1)S(1)} %get-tuple-element.118), channel_id=1, source_target_pairs={{0,16},{4,20},{8,24},{12,28},{16,0},{20,4},{24,8},{28,12},{1,17},{... | collective-permute-start | bytes 516104 | tf_op jit(solution)/shard_map/ppermute | solution.py:369
  118.0 5.8 %collective-permute-start.15 = (bf16[48,1792]{1,0:T(8,128)(2,1)S(1)}, bf16[48,1792]{1,0:T(8,128)(2,1)S(1)}, u32[]{:S(2)}, u32[]{:S(2)}) collective-permute-start(bf16[48,1792]{1,0:T(8,128)(2,1)S(1)} %get-tuple-element.117), channel_id=1, source_target_pairs={{0,24},{4,28},{8,16},{12,20},{16,8},{20,12},{24,0},{28,4},{1,25},{... | collective-permute-start | bytes 516104 | tf_op jit(solution)/shard_map/ppermute | solution.py:369
  123.8 0.7 pad_maximum_fusion
  124.5 2.7 %shard_map.292 = (bf16[3,64,768]{2,1,0:T(8,128)(2,1)}, bf16[3,64,768]{2,1,0:T(8,128)(2,1)}) custom-call(bf16[432,768]{1,0:T(8,128)(2,1)S(1)} %get-tuple-element.59.gnp_a, bf16[432,768]{1,0:T(8,128)(2,1)S(1)} %collective-permute-done.10.gnp_b, bf16[432,768]{1,0:T(8,128)(2,1)S(1)} %get-tuple-element.44.tok, f32[432,768]{1,0:T(8,128)S(1)} %get-tuple-element.60.gres, ...), custom_call_target="tpu_custom_call" | custom-call | flops 1000000000 | bytes 8000000 | tf_op jit(solution)/shard_map/pallas_call | solution.py:492
  127.3 6.6 %collective-permute-done.13 = bf16[48,1792]{1,0:T(8,128)(2,1)S(1)} collective-permute-done((bf16[48,1792]{1,0:T(8,128)(2,1)S(1)}, bf16[48,1792]{1,0:T(8,128)(2,1)S(1)}, u32[]{:S(2)}, u32[]{:S(2)}) %collective-permute-start.13) | collective-permute-done | bytes 172064 | tf_op jit(solution)/shard_map/ppermute | solution.py:369
  134.0 2.3 %collective-permute-start.17 = (f32[24,1152]{1,0:T(8,128)S(1)}, f32[24,1152]{1,0:T(8,128)S(1)}, u32[]{:S(2)}, u32[]{:S(2)}) collective-permute-start(f32[24,1152]{1,0:T(8,128)S(1)} %slice_select_fusion.2), channel_id=1, source_target_pairs={{0,1},{1,0},{2,3},{3,2},{4,5},{5,4},{6,7},{7,6},{8,9},{9,8},{10,11... | collective-permute-start | bytes 331784 | tf_op jit(solution)/shard_map/ppermute | solution.py:357
  136.4 0.6 pad_maximum_fusion.1
  137.7 0.6 reshape.80
  138.4 0.6 copy.36
  139.0 0.8 slice_reduce_fusion
  139.9 0.8 copy.45
  (113 shorter events, 4.5 us)
Async XLA Ops:
  0.6 10.2 %collective-permute-start.1 = (bf16[3,64,768]{2,1,0:T(8,128)(2,1)}, bf16[3,64,768]{2,1,0:T(8,128)(2,1)S(1)}, u32[]{:S(2)}, u32[]{:S(2)}) collective-permute-start(bf16[3,64,768]{2,1,0:T(8,128)(2,1)} %t0.1), channel_id=1, source_target_pairs={{0,2},{1,3},{2,0},{3,1},{4,6},{5,7},{6,4},{7,5},{8,10},{9,11},{10,... | collective-permute-start | bytes 884744 | tf_op jit(solution)/shard_map/ppermute | solution.py:361
  3.6 14.4 %collective-permute-start = (bf16[3,64,768]{2,1,0:T(8,128)(2,1)}, bf16[3,64,768]{2,1,0:T(8,128)(2,1)S(1)}, u32[]{:S(2)}, u32[]{:S(2)}) collective-permute-start(bf16[3,64,768]{2,1,0:T(8,128)(2,1)} %t0.1), channel_id=1, source_target_pairs={{0,1},{1,0},{2,3},{3,2},{4,5},{5,4},{6,7},{7,6},{8,9},{9,8},{10,11... | collective-permute-start | bytes 884744 | tf_op jit(solution)/shard_map/ppermute | solution.py:357
  10.9 7.1 %collective-permute-start.2 = (bf16[3,64,768]{2,1,0:T(8,128)(2,1)S(1)}, bf16[3,64,768]{2,1,0:T(8,128)(2,1)S(1)}, u32[]{:S(2)}, u32[]{:S(2)}) collective-permute-start(bf16[3,64,768]{2,1,0:T(8,128)(2,1)S(1)} %collective-permute-done.1.t2), channel_id=1, source_target_pairs={{0,1},{1,0},{2,3},{3,2},{4,5},{5,4},{6,7},{7,6},{8,9},{9,8},{10,11... | collective-permute-start | bytes 884744 | tf_op jit(solution)/shard_map/ppermute | solution.py:357
  11.8 3.7 %collective-permute-start.3 = (f32[8,256]{1,0:T(8,128)S(1)}, f32[8,256]{1,0:T(8,128)S(1)}, u32[]{:S(2)}, u32[]{:S(2)}) collective-permute-start(f32[8,256]{1,0:T(8,128)S(1)} %dynamic_update_slice.5), channel_id=1, source_target_pairs={{0,2},{1,3},{2,0},{3,1},{4,6},{5,7},{6,4},{7,5},{8,10},{9,11},{10,... | collective-permute-start | bytes 24584 | tf_op jit(solution)/shard_map/ppermute | solution.py:361
  13.6 14.8 %collective-permute-start.7 = (bf16[3,64,768]{2,1,0:T(8,128)(2,1)}, bf16[3,64,768]{2,1,0:T(8,128)(2,1)S(1)}, u32[]{:S(2)}, u32[]{:S(2)}) collective-permute-start(bf16[3,64,768]{2,1,0:T(8,128)(2,1)} %c0.1), channel_id=1, source_target_pairs={{0,2},{1,3},{2,0},{3,1},{4,6},{5,7},{6,4},{7,5},{8,10},{9,11},{10,... | collective-permute-start | bytes 884744 | tf_op jit(solution)/shard_map/ppermute | solution.py:361
  16.5 1.5 %collective-permute-start.4 = (f32[8,256]{1,0:T(8,128)S(1)}, f32[8,256]{1,0:T(8,128)S(1)}, u32[]{:S(2)}, u32[]{:S(2)}) collective-permute-start(f32[8,256]{1,0:T(8,128)S(1)} %add.47.va), channel_id=1, source_target_pairs={{0,1},{1,0},{2,3},{3,2},{4,5},{5,4},{6,7},{7,6},{8,9},{9,8},{10,11... | collective-permute-start | bytes 24584 | tf_op jit(solution)/shard_map/ppermute | solution.py:357
  16.6 13.8 %copy-start.8 = (f32[3072]{0:T(1024)S(1)}, f32[3072]{0:T(1024)}, u32[]{:S(2)}) copy-start(f32[3072]{0:T(1024)} %param.30) | copy-start | bytes 36868
  18.0 2.0 %copy-start.1 = (bf16[768,2304]{1,0:T(8,128)(2,1)S(1)}, bf16[768,2304]{1,0:T(8,128)(2,1)}, u32[]{:S(2)}) copy-start(bf16[768,2304]{1,0:T(8,128)(2,1)} %wqkv.3) | copy-start | bytes 10616836
  21.7 6.6 %copy-start.7 = (bf16[3,64,768]{2,1,0:T(8,128)(2,1)S(1)}, bf16[3,64,768]{2,1,0:T(8,128)(2,1)}, u32[]{:S(2)}) copy-start(bf16[3,64,768]{2,1,0:T(8,128)(2,1)} %c0.1) | copy-start | bytes 884740
  21.7 7.2 %copy-start.21 = (f32[768]{0:T(1024)S(1)}, f32[768]{0:T(1024)}, u32[]{:S(2)}) copy-start(f32[768]{0:T(1024)} %param.26) | copy-start | bytes 9220
  21.7 7.2 %copy-start.22 = (f32[768]{0:T(1024)S(1)}, f32[768]{0:T(1024)}, u32[]{:S(2)}) copy-start(f32[768]{0:T(1024)} %param.27) | copy-start | bytes 9220
  21.7 7.2 %copy-start.23 = (f32[768]{0:T(1024)S(1)}, f32[768]{0:T(1024)}, u32[]{:S(2)}) copy-start(f32[768]{0:T(1024)} %param.32) | copy-start | bytes 9220
  21.7 7.2 %copy-start.24 = (f32[768]{0:T(1024)S(1)}, f32[768]{0:T(1024)}, u32[]{:S(2)}) copy-start(f32[768]{0:T(1024)} %param.33) | copy-start | bytes 9220
  21.7 7.2 %copy-start.25 = (f32[768]{0:T(1024)S(1)}, f32[768]{0:T(1024)}, u32[]{:S(2)}) copy-start(f32[768]{0:T(1024)} %param.25) | copy-start | bytes 9220
  21.7 7.2 %copy-start.26 = (f32[768]{0:T(1024)S(1)}, f32[768]{0:T(1024)}, u32[]{:S(2)}) copy-start(f32[768]{0:T(1024)} %param.28) | copy-start | bytes 9220
  21.7 8.7 %copy-start.2 = (bf16[768,768]{1,0:T(8,128)(2,1)S(1)}, bf16[768,768]{1,0:T(8,128)(2,1)}, u32[]{:S(2)}) copy-start(bf16[768,768]{1,0:T(8,128)(2,1)} %wp.3) | copy-start | bytes 3538948
  27.8 2.6 %collective-permute-start.5 = (bf16[432,384]{1,0:T(8,128)(2,1)S(1)}, bf16[432,384]{1,0:T(8,128)(2,1)S(1)}, u32[]{:S(2)}, u32[]{:S(2)}) collective-permute-start(bf16[432,384]{1,0:T(8,128)(2,1)S(1)} %get-tuple-element.43.mix_a), channel_id=1, source_target_pairs={{0,1},{1,0},{2,3},{3,2},{4,5},{5,4},{6,7},{7,6},{8,9},{9,8},{10,11... | collective-permute-start | bytes 995336 | tf_op jit(solution)/shard_map/ppermute | solution.py:357
  28.3 1.7 %collective-permute-start.6 = (bf16[3,64,768]{2,1,0:T(8,128)(2,1)S(1)}, bf16[3,64,768]{2,1,0:T(8,128)(2,1)S(1)}, u32[]{:S(2)}, u32[]{:S(2)}) collective-permute-start(bf16[3,64,768]{2,1,0:T(8,128)(2,1)S(1)} %copy-done.7), channel_id=1, source_target_pairs={{0,1},{1,0},{2,3},{3,2},{4,5},{5,4},{6,7},{7,6},{8,9},{9,8},{10,11... | collective-permute-start | bytes 884744 | tf_op jit(solution)/shard_map/ppermute | solution.py:357
  28.3 2.1 %collective-permute-start.8 = (bf16[3,64,768]{2,1,0:T(8,128)(2,1)S(1)}, bf16[3,64,768]{2,1,0:T(8,128)(2,1)S(1)}, u32[]{:S(2)}, u32[]{:S(2)}) collective-permute-start(bf16[3,64,768]{2,1,0:T(8,128)(2,1)S(1)} %collective-permute-done.7.c2), channel_id=1, source_target_pairs={{0,1},{1,0},{2,3},{3,2},{4,5},{5,4},{6,7},{7,6},{8,9},{9,8},{10,11... | collective-permute-start | bytes 884744 | tf_op jit(solution)/shard_map/ppermute | solution.py:357
  37.9 1.1 copy-start.14
  39.9 4.2 %copy-start.4 = (bf16[432,768]{1,0:T(8,128)(2,1)}, bf16[432,768]{1,0:T(8,128)(2,1)S(1)}, u32[]{:S(2)}) copy-start(bf16[432,768]{1,0:T(8,128)(2,1)S(1)} %get-tuple-element.46.gn2_a) | copy-start | bytes 1990660
  39.9 4.2 %copy-start.18 = (bf16[432,768]{1,0:T(8,128)(2,1)}, bf16[432,768]{1,0:T(8,128)(2,1)S(1)}, u32[]{:S(2)}) copy-start(bf16[432,768]{1,0:T(8,128)(2,1)S(1)} %get-tuple-element.52.mix) | copy-start | bytes 1990660
  45.0 16.5 %collective-permute-start.23 = (bf16[4,96,768]{2,1,0:T(8,128)(2,1)}, bf16[4,96,768]{2,1,0:T(8,128)(2,1)}, u32[]{:S(2)}, u32[]{:S(2)}) collective-permute-start(bf16[4,96,768]{2,1,0:T(8,128)(2,1)} %get-tuple-element.69), channel_id=1, source_target_pairs={{0,4},{4,0},{8,12},{12,8},{16,20},{20,16},{24,28},{28,24},{1,5},{5... | collective-permute-start | bytes 1769480 | tf_op jit(solution)/shard_map/ppermute | solution.py:365
  46.8 26.8 %collective-permute-start.18 = (bf16[4,48,1536]{2,1,0:T(8,128)(2,1)}, bf16[4,48,1536]{2,1,0:T(8,128)(2,1)}, u32[]{:S(2)}, u32[]{:S(2)}) collective-permute-start(bf16[4,48,1536]{2,1,0:T(8,128)(2,1)} %get-tuple-element.67), channel_id=1, source_target_pairs={{0,4},{4,0},{8,12},{12,8},{16,20},{20,16},{24,28},{28,24},{1,5},{5... | collective-permute-start | bytes 1769480 | tf_op jit(solution)/shard_map/ppermute | solution.py:365
  47.0 32.5 %collective-permute-start.9 = (bf16[432,768]{1,0:T(8,128)(2,1)}, bf16[432,768]{1,0:T(8,128)(2,1)S(1)}, u32[]{:S(2)}, u32[]{:S(2)}) collective-permute-start(bf16[432,768]{1,0:T(8,128)(2,1)} %copy-done.4), channel_id=1, source_target_pairs={{0,1},{1,0},{2,3},{3,2},{4,5},{5,4},{6,7},{7,6},{8,9},{9,8},{10,11... | collective-permute-start | bytes 1990664 | tf_op jit(solution)/shard_map/ppermute | solution.py:357
  47.0 77.5 %collective-permute-start.11 = (bf16[432,768]{1,0:T(8,128)(2,1)S(1)}, bf16[432,768]{1,0:T(8,128)(2,1)S(1)}, u32[]{:S(2)}, u32[]{:S(2)}) collective-permute-start(bf16[432,768]{1,0:T(8,128)(2,1)S(1)} %get-tuple-element.61.bt2_a), channel_id=1, source_target_pairs={{0,1},{1,0},{2,3},{3,2},{4,5},{5,4},{6,7},{7,6},{8,9},{9,8},{10,11... | collective-permute-start | bytes 1990664 | tf_op jit(solution)/shard_map/ppermute | solution.py:357
  61.4 18.1 %copy-start.15 = (f32[432,768]{1,0:T(8,128)S(1)}, f32[432,768]{1,0:T(8,128)}, u32[]{:S(2)}) copy-start(f32[432,768]{1,0:T(8,128)} %copy-done.14) | copy-start | bytes 3981316
  61.4 18.1 %copy-start.19 = (bf16[432,768]{1,0:T(8,128)(2,1)S(1)}, bf16[432,768]{1,0:T(8,128)(2,1)}, u32[]{:S(2)}) copy-start(bf16[432,768]{1,0:T(8,128)(2,1)} %copy-done.18) | copy-start | bytes 1990660
  63.0 16.5 %copy-start.17 = (bf16[432,768]{1,0:T(8,128)(2,1)S(1)}, bf16[432,768]{1,0:T(8,128)(2,1)}, u32[]{:S(2)}) copy-start(bf16[432,768]{1,0:T(8,128)(2,1)} %copy-done.16) | copy-start | bytes 1990660
  63.0 38.4 %collective-permute-start.24 = (bf16[96,768]{1,0:T(8,128)(2,1)S(1)}, bf16[96,768]{1,0:T(8,128)(2,1)S(1)}, u32[]{:S(2)}, u32[]{:S(2)}) collective-permute-start(bf16[96,768]{1,0:T(8,128)(2,1)S(1)} %get-tuple-element.119), channel_id=1, source_target_pairs={{0,8},{4,12},{8,0},{12,4},{16,24},{20,28},{24,16},{28,20},{1,9},{5... | collective-permute-start | bytes 442376 | tf_op jit(solution)/shard_map/ppermute | solution.py:369
  73.6 6.0 %copy-start.3 = (bf16[768,768]{1,0:T(8,128)(2,1)S(1)}, bf16[768,768]{1,0:T(8,128)(2,1)}, u32[]{:S(2)}) copy-start(bf16[768,768]{1,0:T(8,128)(2,1)} %wp.3) | copy-start | bytes 3538948
  73.6 6.0 %copy-start.5 = (bf16[432,768]{1,0:T(8,128)(2,1)S(1)}, bf16[432,768]{1,0:T(8,128)(2,1)}, u32[]{:S(2)}) copy-start(bf16[432,768]{1,0:T(8,128)(2,1)} %copy-done.4) | copy-start | bytes 1990660
  73.6 6.0 %copy-start.11 = (bf16[3,432,384]{2,1,0:T(8,128)(2,1)S(1)}, bf16[3,432,384]{2,1,0:T(8,128)(2,1)}, u32[]{:S(2)}) copy-start(bf16[3,432,384]{2,1,0:T(8,128)(2,1)} %copy-done.10) | copy-start | bytes 2985988
  73.6 6.0 %copy-start.13 = (bf16[432,768]{1,0:T(8,128)(2,1)S(1)}, bf16[432,768]{1,0:T(8,128)(2,1)}, u32[]{:S(2)}) copy-start(bf16[432,768]{1,0:T(8,128)(2,1)} %copy-done.12) | copy-start | bytes 1990660
  75.0 20.8 %collective-permute-start.19 = (bf16[48,1536]{1,0:T(8,128)(2,1)S(1)}, bf16[48,1536]{1,0:T(8,128)(2,1)S(1)}, u32[]{:S(2)}, u32[]{:S(2)}) collective-permute-start(bf16[48,1536]{1,0:T(8,128)(2,1)S(1)} %get-tuple-element.122), channel_id=1, source_target_pairs={{0,8},{4,12},{8,0},{12,4},{16,24},{20,28},{24,16},{28,20},{1,9},{5... | collective-permute-start | bytes 442376 | tf_op jit(solution)/shard_map/ppermute | solution.py:369
  76.9 20.9 %collective-permute-start.20 = (bf16[48,1536]{1,0:T(8,128)(2,1)S(1)}, bf16[48,1536]{1,0:T(8,128)(2,1)S(1)}, u32[]{:S(2)}, u32[]{:S(2)}) collective-permute-start(bf16[48,1536]{1,0:T(8,128)(2,1)S(1)} %get-tuple-element.124), channel_id=1, source_target_pairs={{0,16},{4,20},{8,24},{12,28},{16,0},{20,4},{24,8},{28,12},{1,17},{... | collective-permute-start | bytes 442376 | tf_op jit(solution)/shard_map/ppermute | solution.py:369
  79.5 20.3 %collective-permute-start.21 = (bf16[48,1536]{1,0:T(8,128)(2,1)S(1)}, bf16[48,1536]{1,0:T(8,128)(2,1)S(1)}, u32[]{:S(2)}, u32[]{:S(2)}) collective-permute-start(bf16[48,1536]{1,0:T(8,128)(2,1)S(1)} %get-tuple-element.123), channel_id=1, source_target_pairs={{0,24},{4,28},{8,16},{12,20},{16,8},{20,12},{24,0},{28,4},{1,25},{... | collective-permute-start | bytes 442376 | tf_op jit(solution)/shard_map/ppermute | solution.py:369
  95.9 13.1 %collective-permute-start.25 = (bf16[96,768]{1,0:T(8,128)(2,1)S(1)}, bf16[96,768]{1,0:T(8,128)(2,1)S(1)}, u32[]{:S(2)}, u32[]{:S(2)}) collective-permute-start(bf16[96,768]{1,0:T(8,128)(2,1)S(1)} %get-tuple-element.121), channel_id=1, source_target_pairs={{0,16},{4,20},{8,24},{12,28},{16,0},{20,4},{24,8},{28,12},{1,17},{... | collective-permute-start | bytes 442376 | tf_op jit(solution)/shard_map/ppermute | solution.py:369
  97.8 11.1 %collective-permute-start.26 = (bf16[96,768]{1,0:T(8,128)(2,1)S(1)}, bf16[96,768]{1,0:T(8,128)(2,1)S(1)}, u32[]{:S(2)}, u32[]{:S(2)}) collective-permute-start(bf16[96,768]{1,0:T(8,128)(2,1)S(1)} %get-tuple-element.120), channel_id=1, source_target_pairs={{0,24},{4,28},{8,16},{12,20},{16,8},{20,12},{24,0},{28,4},{1,25},{... | collective-permute-start | bytes 442376 | tf_op jit(solution)/shard_map/ppermute | solution.py:369
  99.8 15.8 %collective-permute-start.12 = (bf16[4,48,1792]{2,1,0:T(8,128)(2,1)S(1)}, bf16[4,48,1792]{2,1,0:T(8,128)(2,1)S(1)}, u32[]{:S(2)}, u32[]{:S(2)}) collective-permute-start(bf16[4,48,1792]{2,1,0:T(8,128)(2,1)S(1)} %get-tuple-element.65), channel_id=1, source_target_pairs={{0,4},{4,0},{8,12},{12,8},{16,20},{20,16},{24,28},{28,24},{1,5},{5... | collective-permute-start | bytes 2064392 | tf_op jit(solution)/shard_map/ppermute | solution.py:365
  101.4 23.1 %collective-permute-start.10 = (bf16[432,768]{1,0:T(8,128)(2,1)S(1)}, bf16[432,768]{1,0:T(8,128)(2,1)S(1)}, u32[]{:S(2)}, u32[]{:S(2)}) collective-permute-start(bf16[432,768]{1,0:T(8,128)(2,1)S(1)} %get-tuple-element.59.gnp_a), channel_id=1, source_target_pairs={{0,1},{1,0},{2,3},{3,2},{4,5},{5,4},{6,7},{7,6},{8,9},{9,8},{10,11... | collective-permute-start | bytes 1990664 | tf_op jit(solution)/shard_map/ppermute | solution.py:357
  109.0 1.4 collective-permute-start.22
  109.0 9.0 %collective-permute-start.27 = (f32[96,768]{1,0:T(8,128)S(1)}, f32[96,768]{1,0:T(8,128)S(1)}, u32[]{:S(2)}, u32[]{:S(2)}) collective-permute-start(f32[96,768]{1,0:T(8,128)S(1)} %fusion.5), channel_id=1, source_target_pairs={{0,0},{1,16},{2,8},{3,24},{4,4},{5,20},{6,12},{7,28},{8,1},{9,17},... | collective-permute-start | bytes 884744 | tf_op jit(solution)/shard_map/ppermute | solution.py:506
  115.8 18.0 %collective-permute-start.13 = (bf16[48,1792]{1,0:T(8,128)(2,1)S(1)}, bf16[48,1792]{1,0:T(8,128)(2,1)S(1)}, u32[]{:S(2)}, u32[]{:S(2)}) collective-permute-start(bf16[48,1792]{1,0:T(8,128)(2,1)S(1)} %get-tuple-element.116), channel_id=1, source_target_pairs={{0,8},{4,12},{8,0},{12,4},{16,24},{20,28},{24,16},{28,20},{1,9},{5... | collective-permute-start | bytes 516104 | tf_op jit(solution)/shard_map/ppermute | solution.py:369
  116.4 17.4 %collective-permute-start.14 = (bf16[48,1792]{1,0:T(8,128)(2,1)S(1)}, bf16[48,1792]{1,0:T(8,128)(2,1)S(1)}, u32[]{:S(2)}, u32[]{:S(2)}) collective-permute-start(bf16[48,1792]{1,0:T(8,128)(2,1)S(1)} %get-tuple-element.118), channel_id=1, source_target_pairs={{0,16},{4,20},{8,24},{12,28},{16,0},{20,4},{24,8},{28,12},{1,17},{... | collective-permute-start | bytes 516104 | tf_op jit(solution)/shard_map/ppermute | solution.py:369
  118.0 15.9 %collective-permute-start.15 = (bf16[48,1792]{1,0:T(8,128)(2,1)S(1)}, bf16[48,1792]{1,0:T(8,128)(2,1)S(1)}, u32[]{:S(2)}, u32[]{:S(2)}) collective-permute-start(bf16[48,1792]{1,0:T(8,128)(2,1)S(1)} %get-tuple-element.117), channel_id=1, source_target_pairs={{0,24},{4,28},{8,16},{12,20},{16,8},{20,12},{24,0},{28,4},{1,25},{... | collective-permute-start | bytes 516104 | tf_op jit(solution)/shard_map/ppermute | solution.py:369
  134.0 5.8 %collective-permute-start.17 = (f32[24,1152]{1,0:T(8,128)S(1)}, f32[24,1152]{1,0:T(8,128)S(1)}, u32[]{:S(2)}, u32[]{:S(2)}) collective-permute-start(f32[24,1152]{1,0:T(8,128)S(1)} %slice_select_fusion.2), channel_id=1, source_target_pairs={{0,1},{1,0},{2,3},{3,2},{4,5},{5,4},{6,7},{7,6},{8,9},{9,8},{10,11... | collective-permute-start | bytes 331784 | tf_op jit(solution)/shard_map/ppermute | solution.py:357
  136.3 1.2 collective-permute-start.16
  (7 other events, 6.0 us)

commit v2 on v0

--- a/solution.py
+++ b/solution.py
@@ -1,14 +1,669 @@
+import functools
 import math
 
 import jax
 import jax.numpy as jnp
 from jax import lax
+from jax.experimental import pallas as pl
+from jax.experimental.pallas import tpu as pltpu
 from jax.sharding import PartitionSpec as P
 
 HD = 64
-
-
 NORM_EPS = 1e-06
+PACK = 144
+SLOTS = 256
+BAND = 64
+IMGS = 3
+ROWS = IMGS * PACK
+D = 768
+HALF = D // 2
+FF = 3072
+FH = FF // 2
+SMALL = 128
+MIB = 1024 * 1024
+F32 = jnp.float32
+BF = jnp.bfloat16
+ANY = pl.BlockSpec(memory_space=pl.ANY)
+HBM = pl.BlockSpec(memory_space=pltpu.HBM)
+VM = pl.BlockSpec(memory_space=pltpu.VMEM)
+
+
+def dot(a, b):
+    return jnp.dot(a, b, preferred_element_type=F32)
+
+
+def dot_nt(a, b):
+    return lax.dot_general(a, b, (((1,), (1,)), ((), ())), preferred_element_type=F32)
+
+
+def dot_tn(a, b):
+    return lax.dot_general(a, b, (((0,), (0,)), ((), ())), preferred_element_type=F32)
+
+
+def sds(shape, dtype):
+    return jax.ShapeDtypeStruct(shape, dtype)
+
+
+def vm(shape, dtype):
+    return pltpu.VMEM(shape, dtype)
+
+
+def stay(value):
+    return pltpu.with_memory_space_constraint(value, pltpu.HBM)
+
+
+def place():
+    band = lax.axis_index("band")
+    batch = lax.axis_index("batch")
+    return band >> 1, band & 1, batch >> 1, batch & 1
+
+
+def one_hot_pack(pos, image):
+    rows = lax.broadcasted_iota(jnp.int32, (PACK, SLOTS), 0).astype(F32)
+    return jnp.where(rows == pos[image : image + 1, :], 1.0, 0.0).astype(BF)
+
+
+def feature_pick():
+    x, _, z, y = place()
+    lane = lax.broadcasted_iota(jnp.int32, (D, HALF), 1)
+    row = lax.broadcasted_iota(jnp.int32, (D, HALF), 0)
+    want = jnp.zeros((D, HALF), jnp.int32)
+    for q in range(8):
+        dy, dz = q // 4, q % 4
+        base = 96 * ((z ^ dz) * 2 + (y ^ dy)) + 48 * x - 48 * q
+        want = jnp.where((lane >= 48 * q) & (lane < 48 * q + 48), lane + base, want)
+    return jnp.where(row == want, 1.0, 0.0).astype(BF)
+
+
+def statistics(values):
+    center = values - jnp.mean(values, axis=-1, keepdims=True)
+    rstd = lax.rsqrt(jnp.mean(center * center, axis=-1, keepdims=True) + NORM_EPS)
+    return center * rstd, rstd
+
+
+def norm_back(grad, z, rstd):
+    return rstd * (
+        grad
+        - jnp.mean(grad, axis=-1, keepdims=True)
+        - z * jnp.mean(grad * z, axis=-1, keepdims=True)
+    )
+
+
+def gather_bands(blocks, dst):
+    band = lax.axis_index("band")
+    for k, block in enumerate(blocks):
+        at = pl.multiple_of((band ^ k) * BAND, BAND)
+        for i in range(IMGS):
+            dst[i, pl.ds(at, BAND), :] = block[i]
+
+
+def two_heads(v):
+    lane = lax.broadcasted_iota(jnp.int32, v.shape, 1)
+    none = jnp.zeros_like(v)
+    return jnp.concatenate([jnp.where(lane < HD, v, none), jnp.where(lane < HD, none, v)], axis=0)
+
+
+def join_heads(v):
+    lane = lax.broadcasted_iota(jnp.int32, (PACK, 128), 1)
+    return jnp.where(lane < HD, v[:PACK], v[PACK:])
+
+
+def keys_shown(pos, image):
+    shown = jnp.sum(jnp.where(pos[image : image + 1, :] >= 0, 1.0, 0.0), axis=-1, keepdims=True)
+    return lax.broadcasted_iota(jnp.int32, (1, PACK), 1).astype(F32) < shown
+
+
+TICK = vm((8, 128), F32)
+GAIN1, BIAS1, QB, VB, PB, ASC, GAIN2, BIAS2, RB, MSC = range(10)
+
+
+def prepare_kernel(
+    cot, gain1, bias1, qvb, bp, asc, gain2, bias2, br, msc, be, wqkv, wp, we, wr, vis, tok,
+    cot_o, tok_o, par_o, be_o, wqkv_o, wp_o, we_o, wr_o, vis_o, sems,
+):
+    c = lax.axis_index("band") & 1
+    units = pl.multiple_of(c * FH, 128)
+    rows = (
+        (GAIN1, gain1), (BIAS1, bias1), (QB, qvb.at[0]), (VB, qvb.at[1]), (PB, bp), (ASC, asc),
+        (GAIN2, gain2), (BIAS2, bias2), (RB, br), (MSC, msc),
+    )
+    moves = [(cot, cot_o)] + [(v, par_o.at[r]) for r, v in rows]
+    moves += [(be.at[pl.ds(units, FH)], be_o.at[0])]
+    for m in range(3):
+        moves.append((wqkv.at[:, pl.ds(pl.multiple_of(m * D + c * HALF, 128), HALF)], wqkv_o.at[m]))
+    moves += [(wp, wp_o), (we.at[:, pl.ds(units, FH)], we_o), (wr.at[pl.ds(units, FH), :], wr_o)]
+    moves += [(vis, vis_o), (tok, tok_o)]
+    copies = [pltpu.make_async_copy(a, b, sems.at[i]) for i, (a, b) in enumerate(moves)]
+    for copy in copies:
+        copy.start()
+    for copy in copies:
+        copy.wait()
+
+
+def hold_kernel(cot, tok, after_a, after_b, cot_o, tok_o):
+    cot_o[...] = cot[...]
+    tok_o[...] = tok[...]
+
+
+def first_kernel(
+    t0, t1, t2, t3, v0, v1, v2, v3, par, w,
+    tok_o, norm_o, qkv_o, mix_o, pos_o, probs_o,
+    xs, shown,
+):
+    band = lax.axis_index("band")
+    c = band & 1
+    gather_bands((t0, t1, t2, t3), xs)
+    heads = pl.multiple_of(c * HALF, 128)
+    to = lax.broadcasted_iota(jnp.int32, (BAND, SLOTS), 1) - lax.broadcasted_iota(jnp.int32, (BAND, SLOTS), 0)
+    vis = jnp.zeros((16, SLOTS), F32)
+    shown[...] = jnp.zeros_like(shown)
+    for k, v in enumerate((v0, v1, v2, v3)):
+        shown[0:IMGS, 0:BAND] = v[...].astype(F32)
+        vis = vis + dot(shown[:, 0:BAND].astype(BF), jnp.where(to == (band ^ k) * BAND, 1.0, 0.0).astype(BF))
+    upto = lax.broadcasted_iota(jnp.int32, (SLOTS, SLOTS), 0)
+    slot = lax.broadcasted_iota(jnp.int32, (SLOTS, SLOTS), 1)
+    before = jnp.where(upto < slot, 1.0, 0.0).astype(BF)
+    pos = jnp.where(vis > 0, dot(vis.astype(BF), before), -1.0)
+    pos_o[...] = pos[0:8]
+    for i in range(IMGS):
+        rows = slice(i * PACK, (i + 1) * PACK)
+        tok = dot(one_hot_pack(pos, i), xs[i])
+        tok_o[rows, :] = tok.astype(BF)
+        z, _ = statistics(tok)
+        norm_o[rows, :] = (z * par[GAIN1 : GAIN1 + 1, :] + par[BIAS1 : BIAS1 + 1, :]).astype(BF)
+    normed = norm_o[...]
+    for m in range(3):
+        part = dot(normed, w[m])
+        if m != 1:
+            r = QB if m == 0 else VB
+            part = part + par[r : r + 1, pl.ds(heads, HALF)]
+        qkv_o[m] = part.astype(BF)
+    for i in range(IMGS):
+        rows = slice(i * PACK, (i + 1) * PACK)
+        key_ok = keys_shown(pos, i)
+        for hp in range(3):
+            cols = slice(hp * 128, (hp + 1) * 128)
+            q2, k2, v2 = (qkv_o[m, rows, cols] for m in range(3))
+            scores = dot_nt(two_heads(q2), k2) * (1.0 / math.sqrt(HD))
+            scores = jnp.where(key_ok, scores, -1e30)
+            raised = jnp.exp(scores - jnp.max(scores, axis=-1, keepdims=True))
+            probs = raised / jnp.sum(raised, axis=-1, keepdims=True)
+            probs_o[i * 3 + hp] = probs
+            mix_o[rows, cols] = join_heads(dot(probs.astype(BF), v2)).astype(BF)
+
+
+def pick_kernel(normed, pick_o, pn_o):
+    pick = feature_pick()
+    pick_o[...] = pick
+    pn_o[...] = dot(normed[...], pick).astype(BF)
+
+
+def second_kernel(
+    mix_a, mix_b, tok, c0, c1, c2, c3, pos_r, par, be, wp, we, wr, after,
+    res_o, one_o, pre_o, gb2_o, n2_o, mix_o, act_o, gh_o, gn2_o, bt2_o, small_o,
+    xs, act_v,
+):
+    x, c, _, _ = place()
+    units = pl.multiple_of(c * FH, 128)
+    mine, other = pl.multiple_of(c * HALF, 128), pl.multiple_of((1 - c) * HALF, 128)
+    gather_bands((c0, c1, c2, c3), xs)
+    mix_o[:, pl.ds(mine, HALF)] = mix_a[...]
+    mix_o[:, pl.ds(other, HALF)] = mix_b[...]
+    pos = pos_r[...]
+    one = dot(mix_o[...], wp[...]) + par[PB : PB + 1, :]
+    one_o[...] = one
+    residual = tok[...].astype(F32) + par[ASC : ASC + 1, :] * one
+    res_o[...] = residual
+    z, _ = statistics(residual)
+    n2_o[...] = (z * par[GAIN2 : GAIN2 + 1, :] + par[BIAS2 : BIAS2 + 1, :]).astype(BF)
+    for i in range(IMGS):
+        rows = slice(i * PACK, (i + 1) * PACK)
+        pre = dot(one_hot_pack(pos, i), xs[i])
+        pre_o[rows, :] = pre.astype(BF)
+        gb2_o[rows, :] = (par[MSC : MSC + 1, :] * pre).astype(BF)
+    step = 256
+    for f in range(FH // step):
+        cols = slice(f * step, (f + 1) * step)
+        hidden = dot(n2_o[...], we[:, cols]) + be[0:1, cols]
+        phi = 0.5 * (1.0 + lax.erf(hidden * math.sqrt(0.5)))
+        act_v[:, cols] = (hidden * phi).astype(BF)
+        slope = phi + hidden * (jnp.exp(-0.5 * hidden * hidden) * (1.0 / math.sqrt(2.0 * math.pi)))
+        back = dot_nt(gb2_o[...], wr[cols, :])
+        gh_o[:, cols] = (back * slope).astype(BF)
+    gn2_o[...] = dot_nt(gh_o[...], we[...]).astype(BF)
+    for j in range(4):
+        lo, mid, hi = 384 * j, 384 * j + 192, 384 * j + 384
+        act_o[:, 192 * j : 192 * j + 192] = jnp.where(x == 0, act_v[:, lo:mid], act_v[:, mid:hi])
+    two = dot(act_v[...], wr[...])
+    bt2_o[...] = two.astype(BF)
+    pre = pre_o[...].astype(F32)
+    first = jnp.where(c == 0, 1.0, 0.0)
+    small_o[...] = jnp.zeros_like(small_o)
+    small_o[0:1, :] = first * jnp.sum(gb2_o[...].astype(F32), axis=0, keepdims=True)
+    small_o[1:2, :] = jnp.sum(pre * (two + first * par[RB : RB + 1, :]), axis=0, keepdims=True)
+
+
+def mlp_grads_kernel(n2, gh, act, gb2, pick, wr_send, wr_keep, we_send, we_keep, eb_o, full, wide, sums):
+    x, c, z, y = place()
+    full[...] = dot_tn(act[...], gb2[...])
+    for dy, out in ((1, wr_send), (0, wr_keep)):
+        for dz in range(2):
+            j = 2 * ((z & 1) ^ dz) + (y ^ dy)
+            for to in range(2):
+                at = pl.multiple_of(192 * j + 96 * to, 96)
+                out[2 * dz + to] = full[pl.ds(at, 96), :].astype(BF)
+    picked = dot(n2[...], pick[...]).astype(BF)
+    wide[...] = dot_tn(picked, gh[...])
+    for low, out in ((1, we_send), (0, we_keep)):
+        for i in range(4):
+            lo = 192 * (i & 1) + 48 * (low + 2 * (i >> 1))
+            out[i] = wide[lo : lo + 48, :].astype(BF)
+    sums[...] = dot_tn(gh[...], jnp.ones((ROWS, 128), BF))
+    lane = lax.broadcasted_iota(jnp.int32, (48, SMALL), 1)
+    for q in range(8):
+        b = (z ^ (q % 4)) * 2 + (y ^ (q // 4))
+        here = (b >> 2) == c
+        block = jnp.zeros((48, SMALL), F32)
+        for k in range(4):
+            at = pl.multiple_of(384 * (b & 3) + 192 * x + 48 * k, 48)
+            block = jnp.where((lane == 10 + k) & here, sums[pl.ds(at, 48), :], block)
+        eb_o[q] = block
+
+
+QC = 3 * HALF
+QW = QC + SMALL + HALF
+
+
+def third_kernel(
+    gn2_a, gn2_b, res, one, pre, tok, qkv, probs_r, mix, pn, pick, small2, eb, wp, w, par,
+    gres_o, gnp_o, send_o, keep_o, tick,
+    gp, vecs, flat,
+):
+    x, c, z, y = place()
+    tick[...] = jnp.zeros_like(tick)
+    heads = pl.multiple_of(c * HALF, 128)
+    first = jnp.where(c == 0, 1.0, 0.0)
+
+    def total(v):
+        return jnp.sum(v, axis=0, keepdims=True)
+
+    vecs[...] = jnp.zeros_like(vecs)
+    gn2 = gn2_a[...].astype(F32) + gn2_b[...].astype(F32)
+    z2, rstd2 = statistics(res[...])
+    vecs[6:7, :] = first * total(gn2 * z2)
+    vecs[7:8, :] = first * total(gn2)
+    gres = pre[...].astype(F32) + norm_back(gn2 * par[GAIN2 : GAIN2 + 1, :], z2, rstd2)
+    gres_o[...] = gres
+    vecs[5:6, :] = first * total(gres * one[...])
+    gb1 = (par[ASC : ASC + 1, :] * gres).astype(BF)
+    vecs[4:5, :] = first * total(gb1.astype(F32))
+    vecs[8:10, :] = small2[0:2, :]
+    gm = dot_nt(gb1, wp[pl.ds(heads, HALF), :]).astype(BF)
+    scale = 1.0 / math.sqrt(HD)
+    for i in range(IMGS):
+        rows = slice(i * PACK, (i + 1) * PACK)
+        for hp in range(3):
+            cols = slice(hp * 128, (hp + 1) * 128)
+            q2, k2, v2 = (qkv[m, rows, cols] for m in range(3))
+            probs = probs_r[i * 3 + hp]
+            g2 = two_heads(gm[rows, cols])
+            gprob = dot_nt(g2, v2)
+            delta = jnp.sum(probs * gprob, axis=-1, keepdims=True)
+            gscore = (probs * (gprob - delta)).astype(BF)
+            parts = (
+                join_heads(dot(gscore, k2)) * scale,
+                dot_tn(gscore, two_heads(q2)) * scale,
+                dot_tn(probs.astype(BF), g2),
+            )
+            for m in range(3):
+                gp[rows, m * HALF + hp * 128 : m * HALF + (hp + 1) * 128] = parts[m].astype(BF)
+    gnp = jnp.zeros((ROWS, D), F32)
+    for m in range(3):
+        part = w[m]
+        gnp = gnp + dot_nt(gp[:, m * HALF : (m + 1) * HALF], part)
+    gnp_o[...] = gnp.astype(BF)
+    z1, _ = statistics(tok[...].astype(F32))
+    vecs[0:1, :] = total(gnp * z1)
+    vecs[1:2, :] = total(gnp)
+    vecs[2:3, pl.ds(heads, HALF)] = total(gp[:, 0:HALF].astype(F32))
+    vecs[3:4, pl.ds(heads, HALF)] = total(gp[:, 2 * HALF : 3 * HALF].astype(F32))
+    rowl = lax.broadcasted_iota(jnp.int32, (D, 192), 0)
+    colr = lax.broadcasted_iota(jnp.int32, (D, 192), 1)
+    want = jnp.zeros((D, 192), jnp.int32)
+    for q in range(8):
+        base = 96 * ((z ^ (q % 4)) * 2 + (y ^ (q // 4))) + 48 * x + 24 * c - 24 * q
+        want = jnp.where((colr >= 24 * q) & (colr < 24 * q + 24), colr + base, want)
+    pick_p = jnp.where(rowl == want, 1.0, 0.0).astype(BF)
+    mixed = dot(mix[...], pick_p).astype(BF)
+    proj = dot_tn(mixed, gb1)
+    vec_cols = dot(vecs[...].astype(BF), pick[...]).T
+    flat[...] = dot_tn(pn[...], gp[...])
+    for dy, out in ((1, send_o), (0, keep_o)):
+        for dz in range(4):
+            q = 4 * dy + dz
+            lo = 48 * q
+            out[dz, :, 0:QC] = flat[lo : lo + 48, :].astype(BF)
+            out[dz, :, QC : QC + SMALL] = (vec_cols[lo : lo + 48] + eb[q]).astype(BF)
+            block = proj[24 * q : 24 * q + 24]
+            out[dz, :, QC + SMALL :] = jnp.concatenate([block[:, :HALF], block[:, HALF:]], axis=0).astype(BF)
+
+
+def last_kernel(gnp_a, gnp_b, tok, gres, bt2_a, bt2_b, res, pos_r, par, after, out_o, gtok_o, tick, wide):
+    tick[...] = jnp.zeros_like(tick)
+    band = lax.axis_index("band")
+    at = pl.multiple_of(band * BAND, BAND)
+    pos = pos_r[...]
+    for i in range(IMGS):
+        rows = slice(i * PACK, (i + 1) * PACK)
+        z1, rstd1 = statistics(tok[rows, :].astype(F32))
+        gnp = gnp_a[rows, :].astype(F32) + gnp_b[rows, :].astype(F32)
+        gtok = (gres[rows, :] + norm_back(gnp * par[GAIN1 : GAIN1 + 1, :], z1, rstd1)).astype(BF)
+        two = bt2_a[rows, :].astype(F32) + bt2_b[rows, :].astype(F32) + par[RB : RB + 1, :]
+        out = (res[rows, :] + par[MSC : MSC + 1, :] * two).astype(BF)
+        pack = one_hot_pack(pos, i)
+        for value, dst in ((gtok, gtok_o), (out, out_o)):
+            wide[...] = dot_tn(pack, value)
+            dst[i] = wide[pl.ds(at, BAND), :].astype(BF)
+
+
+def fold(keep, arrived, keep_o, send_o):
+    count = keep.shape[0]
+    for i in range(count):
+        total = keep[i].astype(F32) + arrived[i].astype(F32)
+        if i < count // 2:
+            keep_o[i] = total
+        else:
+            send_o[i - count // 2] = total.astype(BF)
+
+
+def fold_kernel(keep_a, arrived_a, keep_b, arrived_b, after, keep_ao, send_ao, keep_bo, send_bo, tick):
+    fold(keep_a, arrived_a, keep_ao, send_ao)
+    fold(keep_b, arrived_b, keep_bo, send_bo)
+    tick[...] = jnp.zeros_like(tick)
+
+
+def stage_kernel(
+    keep, arrived, keep_a, arrived_a, keep_b, arrived_b, after,
+    own_o, s1, s2, s3, keep_ao, send_ao, keep_bo, send_bo,
+):
+    own_o[...] = keep[0].astype(F32) + arrived[0].astype(F32)
+    for dz, out in ((1, s1), (2, s2), (3, s3)):
+        out[...] = (keep[dz].astype(F32) + arrived[dz].astype(F32)).astype(BF)
+    for i in range(2):
+        total = keep_a[i] + arrived_a[i].astype(F32)
+        keep_ao[i] = total
+        send_ao[i] = total.astype(BF)
+    fold(keep_b, arrived_b, keep_bo, send_bo)
+
+
+def finish_kernel(
+    own, r1, r2, r3, wr_k, wr_a, we_k, we_a,
+    qk_o, qs_o, vec_o, proj_o, wr_ko, wr_so, keep_o, send_o,
+    sums, both,
+):
+    tail(own, r1, r2, r3, qk_o, qs_o, vec_o, proj_o, sums)
+    c = lax.axis_index("band") & 1
+    wr_ko[...] = wr_k[c] + wr_a[c].astype(F32)
+    wr_so[...] = wr_k[1 - c] + wr_a[1 - c].astype(F32)
+    both[...] = we_k[0] + we_a[0].astype(F32)
+    keep_o[...] = both[pl.ds(pl.multiple_of(c * 24, 8), 24), :]
+    send_o[...] = both[pl.ds(pl.multiple_of(24 - c * 24, 8), 24), :]
+
+
+def tail(own, r1, r2, r3, keep_o, send_o, vec_o, proj_o, both):
+    c = lax.axis_index("band") & 1
+    both[...] = own[...] + r1[...].astype(F32) + r2[...].astype(F32) + r3[...].astype(F32)
+    keep_o[...] = both[pl.ds(pl.multiple_of(c * 24, 8), 24), 0:QC]
+    send_o[:, 0:QC] = both[pl.ds(pl.multiple_of(24 - c * 24, 8), 24), 0:QC]
+    vec = both[:, QC : QC + SMALL]
+    vec_o[...] = vec
+    send_o[:, QC : QC + SMALL] = vec[0:24]
+    send_o[:, QC + SMALL : QC + 2 * SMALL] = vec[24:48]
+    proj_o[:, 0:HALF] = both[0:24, QC + SMALL :]
+    proj_o[:, HALF:] = both[24:48, QC + SMALL :]
+
+
+def out_kernel(
+    keep, vec, arrived, we_keep, we_arrived, wr_keep, wr_arrived,
+    qkv_o, first_o, bias_o, qv_o, bp_o, asc_o, gain2_o, bias2_o, br_o, msc_o, eb_o, we_o, wr_o, both,
+):
+    _, c, z, _ = place()
+    wr_o[...] = jnp.where((z >> 1) == c, wr_keep[...], wr_arrived[...])
+    we_o[:, pl.ds(pl.multiple_of(c * FH, 128), FH)] = we_keep[...]
+    we_o[:, pl.ds(pl.multiple_of((1 - c) * FH, 128), FH)] = we_arrived[...]
+    for m in range(3):
+        mine = pl.multiple_of(m * D + c * HALF, 128)
+        other = pl.multiple_of(m * D + (1 - c) * HALF, 128)
+        qkv_o[:, pl.ds(mine, HALF)] = keep[:, m * HALF : (m + 1) * HALF]
+        qkv_o[:, pl.ds(other, HALF)] = arrived[:, m * HALF : (m + 1) * HALF]
+    both[0:24] = vec[0:24] + arrived[:, QC : QC + SMALL]
+    both[24:48] = vec[24:48] + arrived[:, QC + SMALL : QC + 2 * SMALL]
+    own = both[pl.ds(pl.multiple_of(c * 24, 8), 24), :].T
+    outs = (first_o, bias_o, None, None, bp_o, asc_o, gain2_o, bias2_o, br_o, msc_o)
+    for r, out in enumerate(outs):
+        if out is not None:
+            out[...] = own[r]
+    qv_o[...] = own[2:4]
+    units = both[...].T
+    units = jnp.where(c == 0, units[10:12], units[12:14])
+    eb_o[...] = jnp.concatenate([units[0:1], units[1:2]], axis=1).reshape(96)
+
+
+def call(kernel, outs, specs, scratch=(), flops=0, nbytes=0, vmem=24, out_specs=None):
+    return pl.pallas_call(
+        kernel,
+        out_shape=outs,
+        in_specs=specs,
+        out_specs=jax.tree.map(lambda _: VM, outs) if out_specs is None else out_specs,
+        scratch_shapes=list(scratch),
+        compiler_params=pltpu.CompilerParams(vmem_limit_bytes=vmem * MIB),
+        cost_estimate=pl.CostEstimate(flops=flops, bytes_accessed=nbytes, transcendentals=0),
+    )
+
+
+def by_core(value):
+    return lax.ppermute(value, "band", [(i, i ^ 1) for i in range(4)])
+
+
+def by_x(value):
+    return lax.ppermute(value, "band", [(i, i ^ 2) for i in range(4)])
+
+
+def by_y(value):
+    return lax.ppermute(value, "batch", [(i, i ^ 1) for i in range(8)])
+
+
+def by_z(value, dz):
+    return lax.ppermute(value, "batch", [(i, i ^ (2 * dz)) for i in range(8)])
+
+
+def fold_pair(keep_a, arrived_a, keep_b, arrived_b, after):
+    outs = []
+    for keep in (keep_a, keep_b):
+        half = (keep.shape[0] // 2,) + keep.shape[1:]
+        outs += [vm(half, F32), vm(half, BF)]
+    return call(fold_kernel, (*outs, TICK), [VM] * 4 + [ANY], nbytes=int(4e6))(
+        keep_a, arrived_a, keep_b, arrived_b, after
+    )
+
+
+def packed_body(
+    tokens, cotangent, visible, first_gain, first_bias, qkv_weight, qv_bias, proj_weight, proj_bias,
+    attn_scale, second_gain, second_bias, expand_weight, expand_bias, reduce_weight, reduce_bias, mlp_scale,
+):
+    tok_x = by_x(tokens)
+    tok_c = by_core(tokens)
+    cot, tok_own, par, be, wqkv, wp, we, wr, vis = call(
+        prepare_kernel,
+        (
+            vm(cotangent.shape, BF),
+            vm(cotangent.shape, BF),
+            vm((16, D), F32),
+            vm((8, FH), F32),
+            vm((3, D, HALF), BF),
+            vm((D, D), BF),
+            vm((D, FH), BF),
+            vm((FH, D), BF),
+            vm(visible.shape, visible.dtype),
+        ),
+        [ANY] * 17,
+        [pltpu.SemaphoreType.DMA((20,))],
+        nbytes=int(9e6),
+    )(
+        *map(
+            stay,
+            (
+                cotangent, first_gain, first_bias, qv_bias, proj_bias, attn_scale, second_gain, second_bias,
+                reduce_bias, mlp_scale, expand_bias, qkv_weight, proj_weight, expand_weight, reduce_weight, visible,
+                tokens,
+            ),
+        )
+    )
+    vis_x = by_x(vis)
+    vis_c = by_core(vis)
+    cot_c = by_core(cot)
+    block = vm(cotangent.shape, BF)
+    cot, tok_x = call(hold_kernel, (block, block), [VM] * 2 + [ANY] * 2, nbytes=int(20e6))(cot, tok_x, vis_x, par)
+    tok_d = by_core(tok_x)
+    vis_d = by_core(vis_x)
+    cot_x = by_x(cot)
+
+    tok, normed, qkv, mix_own, pos, probs = call(
+        first_kernel,
+        (
+            vm((ROWS, D), BF),
+            vm((ROWS, D), BF),
+            vm((3, ROWS, HALF), BF),
+            vm((ROWS, HALF), BF),
+            vm((8, SLOTS), F32),
+            vm((9, 2 * PACK, PACK), F32),
+        ),
+        [VM] * 10,
+        [
+            pltpu.VMEM((IMGS, SLOTS, D), BF),
+            pltpu.VMEM((16, 128), F32),
+        ],
+        flops=int(1.5e9),
+        nbytes=int(6e6),
+    )(tok_own, tok_c, tok_x, tok_d, vis, vis_c, vis_x, vis_d, par, wqkv)
+    mix_other = by_core(mix_own)
+    cot_d = by_core(cot_x)
+    pick, pn = call(
+        pick_kernel, (vm((D, HALF), BF), vm((ROWS, HALF), BF)), [VM], flops=int(5e8), nbytes=int(2e6)
+    )(normed)
+    res, one, pre, gb2, n2, mix, act, gh, gn2, bt2, small2 = call(
+        second_kernel,
+        (
+            vm((ROWS, D), F32),
+            vm((ROWS, D), F32),
+            vm((ROWS, D), BF),
+            vm((ROWS, D), BF),
+            vm((ROWS, D), BF),
+            vm((ROWS, D), BF),
+            vm((ROWS, D), BF),
+            vm((ROWS, FH), BF),
+            vm((ROWS, D), BF),
+            vm((ROWS, D), BF),
+            vm((8, D), F32),
+        ),
+        [VM] * 13 + [ANY],
+        [
+            pltpu.VMEM((IMGS, SLOTS, D), BF),
+            pltpu.VMEM((ROWS, FH), BF),
+        ],
+        flops=int(5e9),
+        nbytes=int(15e6),
+    )(mix_own, mix_other, tok, cot, cot_c, cot_x, cot_d, pos, par, be, wp, we, wr, pick)
+    gn2_other = by_core(gn2)
+    wr_send, wr_keep, we_send, we_keep, eb = call(
+        mlp_grads_kernel,
+        (
+            vm((4, 96, D), BF),
+            vm((4, 96, D), BF),
+            vm((4, 48, FH), BF),
+            vm((4, 48, FH), BF),
+            vm((8, 48, SMALL), F32),
+        ),
+        [VM] * 5,
+        [pltpu.VMEM((D, D), F32), pltpu.VMEM((HALF, FH), F32), pltpu.VMEM((FH, 128), F32)],
+        flops=int(2e9),
+        nbytes=int(6e6),
+    )(n2, gh, act, gb2, pick)
+    wr_y = by_y(wr_send)
+    we_z = by_z(we_send, 1)
+    gres, gnp, qp_send, qp_keep, tick = call(
+        third_kernel,
+        (
+            vm((ROWS, D), F32),
+            vm((ROWS, D), BF),
+            vm((4, 48, QW), BF),
+            vm((4, 48, QW), BF),
+            TICK,
+        ),
+        [VM] * 16,
+        [
+            pltpu.VMEM((ROWS, QC), BF),
+            pltpu.VMEM((SMALL, D), F32),
+            pltpu.VMEM((HALF, QC), F32),
+        ],
+        flops=int(4e9),
+        nbytes=int(12e6),
+    )(gn2, gn2_other, res, one, pre, tok, qkv, probs, mix, pn, pick, small2, eb, wp, wqkv, par)
+    qp_y = by_y(qp_send)
+    wr_keep, wr_send, we_keep, we_send, tick = fold_pair(wr_keep, wr_y, we_keep, we_z, tick)
+    wr_z = by_z(wr_send, 1)
+    we_z = by_z(we_send, 2)
+    bt2_other = by_core(bt2)
+    gnp_other = by_core(gnp)
+    layer_out, grad_tokens, tick = call(
+        last_kernel,
+        (sds((IMGS, BAND, D), BF), sds((IMGS, BAND, D), BF), TICK),
+        [VM] * 9 + [ANY],
+        [pltpu.VMEM((SLOTS, D), F32)],
+        flops=int(1e9),
+        nbytes=int(8e6),
+    )(gnp, gnp_other, tok, gres, bt2, bt2_other, res, pos, par, tick)
+    own, s1, s2, s3, wr_keep, wr_send, we_keep, we_send = call(
+        stage_kernel,
+        (vm((48, QW), F32),) + (vm((48, QW), BF),) * 3
+        + (vm((2, 96, D), F32), vm((2, 96, D), BF), vm((1, 48, FH), F32), vm((1, 48, FH), BF)),
+        [VM] * 6 + [ANY],
+        nbytes=int(2e6),
+    )(qp_keep, qp_y, wr_keep, wr_z, we_keep, we_z, tick)
+    r1, r2, r3 = by_z(s1, 1), by_z(s2, 2), by_z(s3, 3)
+    homeward = [(d, d ^ 16) for d in range(32) if (d >> 4) != (d & 1)]
+    wr_z = lax.ppermute(wr_send, ("batch", "band"), homeward)
+    we_y = by_y(we_send)
+
+    qp_keep, qp_send, vec, proj, wr_keep, wr_send, we_keep, we_send = call(
+        finish_kernel,
+        (
+            vm((24, QC), F32),
+            vm((24, QC + 2 * SMALL), F32),
+            vm((48, SMALL), F32),
+            sds((24, D), F32),
+            vm((96, D), F32),
+            vm((96, D), F32),
+            vm((24, FH), F32),
+            vm((24, FH), F32),
+        ),
+        [VM] * 8,
+        [pltpu.VMEM((48, QW), F32), pltpu.VMEM((48, FH), F32)],
+        nbytes=int(1e6),
+    )(own, r1, r2, r3, wr_keep, wr_z, we_keep, we_y)
+    vector = sds((24,), F32)
+    grad_qkv, gg1, gb1, gqv, gbp, gas, gg2, gb2, gbr, gms, geb, grad_expand, grad_reduce = call(
+        out_kernel,
+        (sds((24, 3 * D), F32), vector, vector, sds((2, 24), F32)) + (vector,) * 6
+        + (sds((96,), F32), sds((24, FF), F32), sds((96, D), F32)),
+        [VM] * 7,
+        [pltpu.VMEM((48, SMALL), F32)],
+        nbytes=int(1e6),
+    )(qp_keep, vec, by_core(qp_send), we_keep, by_core(we_send), wr_keep, by_core(wr_send))
+    return (
+        layer_out, grad_tokens, gg1, gb1, grad_qkv, gqv, proj, gbp, gas, gg2, gb2, grad_expand, geb, grad_reduce,
+        gbr, gms,
+    )
 
 
 def layer_norm(values, norm_gain, norm_shift):
@@ -273,6 +928,8 @@
 
 
 def solution(mesh):
+    sizes = dict(mesh.shape)
+    chosen = packed_body if (sizes["batch"], sizes["band"]) == (8, 4) else body
     placed = (
         P("batch", "band", None),
         P("batch", "band", None),
@@ -293,7 +950,7 @@
         P(),
     )
     return jax.shard_map(
-        body,
+        chosen,
         mesh=mesh,
         in_specs=placed,
         out_specs=(

time: 618 us -> 92.3 us (0.15)
  waiting for transfers between devices: 368 us -> 39.8 us
  blocking collectives: 77.8 us -> 0 us
  matrix products: 61.1 us -> 0 us
  local copies, waits for them, and re-layouts: 60.9 us -> 0.01 us
  Pallas kernels: 0 us -> 29.1 us
  other arithmetic: 20 us -> 0 us
  between operations: 14.4 us -> 0.86 us
  starting transfers between devices: 13.3 us -> 22.4 us
    reduce_scatter x4 -> x0, waiting for transfers between devices: 346 us -> none  [the longest x1 142 us: body(): lax.psum_scatter(grad_reduce_weight, ('batch', 'band'), scatter_dimension...]
    dot_general x18 -> x0, matrix products: 61.1 us -> none  [the longest x1 6.62 us: body(): jnp.einsum('isd,isf->df', normed_two_low, grad_hidden, preferred_element_...]
    unnamed x1 -> x0, blocking collectives: 41 us -> none
    ppermute x0 -> x26, waiting for transfers between devices: none -> 39.8 us  [the longest x6 21.5 us: by_z(): return lax.ppermute(value, 'batch', [(i, i ^ 2 * dz) for i in range(8)])]
    all_to_all x2 -> x0, blocking collectives: 36.8 us -> none  [the longest x1 24.5 us: body(): lax.all_to_all(grad_packed, 'band', split_axis=1, concat_axis=3, tiled=True)]
    pallas_call x0 -> x12, Pallas kernels: none -> 29.1 us  [the longest x1 7.88 us: packed_body(): call(third_kernel, (vm((ROWS, D), F32), vm((ROWS, D), BF), vm((4, 48, QW)...]
    reshape x9 -> x0, local copies, waits for them, and re-layouts: 25.1 us -> none  [the longest x2 7.57 us: split_rows(): unpacked = packed_rows.reshape(item_count, slot_count, 3, heads_here, HD)]
    ppermute x0 -> x26, starting transfers between devices: none -> 22.4 us  [the longest x6 11 us: by_z(): return lax.ppermute(value, 'batch', [(i, i ^ 2 * dz) for i in range(8)])]
  transfers between devices with their start and end apart: 7 -> 26, of which waited for: 5 -> 12; matrix products, arithmetic and copies ran while one was open for 16% -> 0% of each run, Pallas kernels for 0% -> 23%
where the time goes in v2:
time: 92.3 us; the launch traced here: 92.1 us
  waiting for transfers between devices  39.8 us (43%)
  Pallas kernels  29.1 us (32%)
  starting transfers between devices  22.4 us (24%)
    ppermute x6, waiting for transfers between devices, by_z(): return lax.ppermute(value, 'batch', [(i, i ^ 2 * dz) for i in range(8)])  21.5 us
    ppermute x6, starting transfers between devices, by_z(): return lax.ppermute(value, 'batch', [(i, i ^ 2 * dz) for i in range(8)])  11 us
    ppermute x3, waiting for transfers between devices, by_y(): return lax.ppermute(value, 'batch', [(i, i ^ 1) for i in range(8)])  8.9 us
    pallas_call x1, Pallas kernels, packed_body(): call(third_kernel, (vm((ROWS, D), F32), vm((ROWS, D), BF), vm((4, 48, QW)...  7.88 us
    pallas_call x1, Pallas kernels, packed_body(): call(second_kernel, (vm((ROWS, D), F32), vm((ROWS, D), F32), vm((ROWS, D)...  6.05 us
    ppermute x3, waiting for transfers between devices, by_x(): return lax.ppermute(value, 'band', [(i, i ^ 2) for i in range(4)])  5.99 us
    ppermute x3, starting transfers between devices, by_x(): return lax.ppermute(value, 'band', [(i, i ^ 2) for i in range(4)])  4.83 us
    pallas_call x1, Pallas kernels, packed_body(): call(prepare_kernel, (vm(cotangent.shape, BF), vm(cotangent.shape, BF), v...  3.68 us
  transfers between devices with their start and end apart: 26, of which 12 were waited for; matrix products, arithmetic and copies ran while one was open for 0% of the time, Pallas kernels for 23%

profile of v2, /device:TPU:0, one launch (start us, length us, event | category | flops | bytes accessed | tf_op | source)
XLA Modules:
  0.0 92.1 jit_solution(2125807283174664432)
XLA Ops:
  0.7 3.0 %collective-permute-start.1 = (bf16[3,64,768]{2,1,0:T(8,128)(2,1)}, bf16[3,64,768]{2,1,0:T(8,128)(2,1)S(1)}, u32[]{:S(2)}, u32[]{:S(2)}) collective-permute-start(bf16[3,64,768]{2,1,0:T(8,128)(2,1)} %tok.1), channel_id=1, source_target_pairs={{0,2},{1,3},{2,0},{3,1},{4,6},{5,7},{6,4},{7,5},{8,10},{9,11},{10,... | collective-permute-start | bytes 884744 | tf_op jit(solution)/shard_map/ppermute | solution.py:469
  3.7 3.7 %shard_map.288 = (bf16[3,64,768]{2,1,0:T(8,128)(2,1)S(1)}, bf16[3,64,768]{2,1,0:T(8,128)(2,1)S(1)}, f32[16,768]{1,0:T(8,128)S(1)}, f32[8,1536]{1,0:T(8,128)S(1)}...) custom-call(bf16[3,64,768]{2,1,0:T(8,128)(2,1)} %cot.1, ...), custom_call_target="tpu_custom_call" | custom-call | bytes 9000000 | tf_op jit(solution)/shard_map/pallas_call | solution.py:496
  7.4 0.1 collective-permute-start.2
  7.5 0.1 collective-permute-start
  7.5 3.5 %collective-permute-done.2.after_a.v2 = s32[3,64]{1,0:T(4,128)S(1)} collective-permute-done((s32[3,64]{1,0:T(4,128)S(1)}, s32[3,64]{1,0:T(4,128)S(1)}, u32[]{:S(2)}, u32[]{:S(2)}) %collective-permute-start.2) | collective-permute-done | bytes 800 | tf_op jit(solution)/shard_map/ppermute | solution.py:469
  11.1 0.1 collective-permute-start.3
  11.1 1.7 %collective-permute-start.8 = (bf16[3,64,768]{2,1,0:T(8,128)(2,1)S(1)}, bf16[3,64,768]{2,1,0:T(8,128)(2,1)S(1)}, u32[]{:S(2)}, u32[]{:S(2)}) collective-permute-start(bf16[3,64,768]{2,1,0:T(8,128)(2,1)S(1)} %get-tuple-element.101.c0), channel_id=1, source_target_pairs={{0,2},{1,3},{2,0},{3,1},{4,6},{5,7},{6,4},{7,5},{8,10},{9,11},{10,... | collective-permute-start | bytes 884744 | tf_op jit(solution)/shard_map/ppermute | solution.py:469
  12.9 0.2 collective-permute-start.4
  13.0 0.3 collective-permute-start.5
  13.4 0.6 collective-permute-done.4.v1
  14.0 0.2 collective-permute-done.5.v3
  14.2 0.0 collective-permute-done.t1
  14.2 0.0 collective-permute-done.3.t3
  14.2 3.3 %shard_map.290 = (bf16[432,768]{1,0:T(8,128)(2,1)S(1)}, bf16[432,768]{1,0:T(8,128)(2,1)S(1)}, bf16[3,432,384]{2,1,0:T(8,128)(2,1)S(1)}, bf16[432,384]{1,0:T(8,12...) custom-call(bf16[3,64,768]{2,1,0:T(8,128)(2,1)S(1)} %get-tuple-element.93.t0, ...), custom_call_target="tpu_custom_call" | custom-call | flops 1500000000 | bytes 6000000 | tf_op jit(solution)/shard_map/pallas_call | solution.py:531
  17.5 0.4 collective-permute-start.6
  17.9 0.2 collective-permute-start.7
  18.1 2.5 %collective-permute-done.8.c2 = bf16[3,64,768]{2,1,0:T(8,128)(2,1)S(1)} collective-permute-done((bf16[3,64,768]{2,1,0:T(8,128)(2,1)S(1)}, bf16[3,64,768]{2,1,0:T(8,128)(2,1)S(1)}, u32[]{:S(2)}, u32[]{:S(2)}) %collective-permute-start.8) | collective-permute-done | bytes 294944 | tf_op jit(solution)/shard_map/ppermute | solution.py:469
  20.6 0.5 shard_map.291
  21.1 1.0 %collective-permute-done.9.c3 = bf16[3,64,768]{2,1,0:T(8,128)(2,1)S(1)} collective-permute-done((bf16[3,64,768]{2,1,0:T(8,128)(2,1)S(1)}, bf16[3,64,768]{2,1,0:T(8,128)(2,1)S(1)}, u32[]{:S(2)}, u32[]{:S(2)}) %collective-permute-start.9) | collective-permute-done | bytes 294944 | tf_op jit(solution)/shard_map/ppermute | solution.py:465
  22.1 6.0 %shard_map.292 = (f32[432,768]{1,0:T(8,128)S(1)}, f32[432,768]{1,0:T(8,128)S(1)}, bf16[432,768]{1,0:T(8,128)(2,1)S(1)}, bf16[432,768]{1,0:T(8,128)(2,1)S(1)}, bf...) custom-call(bf16[432,384]{1,0:T(8,128)(2,1)S(1)} %get-tuple-element., ...), custom_call_target="tpu_custom_call" | custom-call | flops 5000000000 | bytes 15000000 | tf_op jit(solution)/shard_map/pallas_call | solution.py:554
  28.2 0.2 collective-permute-start.10
  28.4 0.4 collective-permute-start.12
  28.8 2.7 %shard_map.293 = (bf16[4,96,768]{2,1,0:T(8,128)(2,1)S(1)}, bf16[4,96,768]{2,1,0:T(8,128)(2,1)S(1)}, bf16[4,48,1536]{2,1,0:T(8,128)(2,1)S(1)}, bf16[4,48,1536]{2,1,0:T(8,128)(2,1)S(1)}, f32[8,48,128]{2,1,0:T(8,128)S(1)}) custom-call(bf16[432,768]{1,0:T(8,128)(2,1)S(1)} %get-tuple-element.118.n2, bf16[432,1536]{1,0:T(8,128)(2,1)S(1)} %get-tuple-element.119.gh, ...), custom_call_target="tpu_custom_call" | custom-call | flops 2000000000 | bytes 6000000 | tf_op jit(solution)/shard_map/pallas_call | solution.py:578
  31.5 1.8 %collective-permute-start.13 = (bf16[4,96,768]{2,1,0:T(8,128)(2,1)S(1)}, bf16[4,96,768]{2,1,0:T(8,128)(2,1)S(1)}, u32[]{:S(2)}, u32[]{:S(2)}) collective-permute-start(bf16[4,96,768]{2,1,0:T(8,128)(2,1)S(1)} %get-tuple-element.127), channel_id=1, source_target_pairs={{0,4},{4,0},{8,12},{12,8},{16,20},{20,16},{24,28},{28,24},{1,5},{5... | collective-permute-start | bytes 1769480 | tf_op jit(solution)/shard_map/ppermute | solution.py:473
  33.2 1.6 %collective-permute-start.14 = (bf16[4,48,1536]{2,1,0:T(8,128)(2,1)S(1)}, bf16[4,48,1536]{2,1,0:T(8,128)(2,1)S(1)}, u32[]{:S(2)}, u32[]{:S(2)}) collective-permute-start(bf16[4,48,1536]{2,1,0:T(8,128)(2,1)S(1)} %get-tuple-element.129), channel_id=1, source_target_pairs={{0,8},{4,12},{8,0},{12,4},{16,24},{20,28},{24,16},{28,20},{1,9},{5... | collective-permute-start | bytes 1769480 | tf_op jit(solution)/shard_map/ppermute | solution.py:477
  34.9 7.9 %shard_map.294 = (f32[432,768]{1,0:T(8,128)S(1)}, bf16[432,768]{1,0:T(8,128)(2,1)S(1)}, bf16[4,48,1664]{2,1,0:T(8,128)(2,1)S(1)}, bf16[4,48,1664]{2,1,0:T(8,128)(2,1)S(1)}, f32[8,128]{1,0:T(8,128)S(1)}) custom-call(bf16[432,768]{1,0:T(8,128)(2,1)S(1)} %get-tuple-element.109.gn2_a, bf16[432,768]{1,0:T(8,128)(2,1)S(1)} %collective-permute-done.10.gn2_b, ...), custom_call_target="tpu_custom_call" | custom-call | flops 4000000000 | bytes 12000000 | tf_op jit(solution)/shard_map/pallas_call | solution.py:594
  42.7 0.1 collective-permute-start.11
  42.8 0.5 collective-permute-start.15
  43.3 4.4 %collective-permute-done.13.arrived_a = bf16[4,96,768]{2,1,0:T(8,128)(2,1)S(1)} collective-permute-done((bf16[4,96,768]{2,1,0:T(8,128)(2,1)S(1)}, bf16[4,96,768]{2,1,0:T(8,128)(2,1)S(1)}, u32[]{:S(2)}, u32[]{:S(2)}) %collective-permute-start.13) | collective-permute-done | bytes 589856 | tf_op jit(solution)/shard_map/ppermute | solution.py:473
  47.7 0.6 collective-permute-done.14.arrived_b
  48.3 0.2 shard_map.295
  48.6 1.7 %collective-permute-start.16 = (bf16[2,96,768]{2,1,0:T(8,128)(2,1)S(1)}, bf16[2,96,768]{2,1,0:T(8,128)(2,1)S(1)}, u32[]{:S(2)}, u32[]{:S(2)}) collective-permute-start(bf16[2,96,768]{2,1,0:T(8,128)(2,1)S(1)} %get-tuple-element.137), channel_id=1, source_target_pairs={{0,8},{4,12},{8,0},{12,4},{16,24},{20,28},{24,16},{28,20},{1,9},{5... | collective-permute-start | bytes 884744 | tf_op jit(solution)/shard_map/ppermute | solution.py:477
  50.3 2.6 %collective-permute-start.17 = (bf16[2,48,1536]{2,1,0:T(8,128)(2,1)S(1)}, bf16[2,48,1536]{2,1,0:T(8,128)(2,1)S(1)}, u32[]{:S(2)}, u32[]{:S(2)}) collective-permute-start(bf16[2,48,1536]{2,1,0:T(8,128)(2,1)S(1)} %get-tuple-element.139), channel_id=1, source_target_pairs={{0,16},{4,20},{8,24},{12,28},{16,0},{20,4},{24,8},{28,12},{1,17},{... | collective-permute-start | bytes 884744 | tf_op jit(solution)/shard_map/ppermute | solution.py:477
  52.9 2.7 %shard_map.296 = (bf16[3,64,768]{2,1,0:T(8,128)(2,1)}, bf16[3,64,768]{2,1,0:T(8,128)(2,1)}, f32[8,128]{1,0:T(8,128)S(1)}) custom-call(bf16[432,768]{1,0:T(8,128)(2,1)S(1)} %get-tuple-element.123.gnp_a, bf16[432,768]{1,0:T(8,128)(2,1)S(1)} %collective-permute-done.11.gnp_b, bf16[432,768]{1,0:T(8,128)(2,1)S(1)} %get-tuple-element.100.tok, ...), custom_call_target="tpu_custom_call" | custom-call | flops 1000000000 | bytes 8000000 | tf_op jit(solution)/shard_map/pallas_call | solution.py:618
  55.6 7.2 %collective-permute-done.16.arrived_a = bf16[2,96,768]{2,1,0:T(8,128)(2,1)S(1)} collective-permute-done((bf16[2,96,768]{2,1,0:T(8,128)(2,1)S(1)}, bf16[2,96,768]{2,1,0:T(8,128)(2,1)S(1)}, u32[]{:S(2)}, u32[]{:S(2)}) %collective-permute-start.16) | collective-permute-done | bytes 294944 | tf_op jit(solution)/shard_map/ppermute | solution.py:477
  62.7 2.4 %collective-permute-done.17.arrived_b = bf16[2,48,1536]{2,1,0:T(8,128)(2,1)S(1)} collective-permute-done((bf16[2,48,1536]{2,1,0:T(8,128)(2,1)S(1)}, bf16[2,48,1536]{2,1,0:T(8,128)(2,1)S(1)}, u32[]{:S(2)}, u32[]{:S(2)}) %collective-permute-start.17) | collective-permute-done | bytes 294944 | tf_op jit(solution)/shard_map/ppermute | solution.py:477
  65.1 0.3 shard_map.297
  65.4 1.3 %collective-permute-start.21 = (bf16[2,96,768]{2,1,0:T(8,128)(2,1)S(1)}, bf16[2,96,768]{2,1,0:T(8,128)(2,1)S(1)}, u32[]{:S(2)}, u32[]{:S(2)}) collective-permute-start(bf16[2,96,768]{2,1,0:T(8,128)(2,1)S(1)} %get-tuple-element.146), channel_id=1, source_target_pairs={{1,17},{3,19},{5,21},{7,23},{9,25},{11,27},{13,29},{15,31},{16,0},... | collective-permute-start | bytes 884744 | tf_op jit(solution)/shard_map/ppermute | solution.py:635
  66.7 0.5 collective-permute-start.18
  67.2 3.6 %collective-permute-start.19 = (bf16[48,1664]{1,0:T(8,128)(2,1)S(1)}, bf16[48,1664]{1,0:T(8,128)(2,1)S(1)}, u32[]{:S(2)}, u32[]{:S(2)}) collective-permute-start(bf16[48,1664]{1,0:T(8,128)(2,1)S(1)} %get-tuple-element.143), channel_id=1, source_target_pairs={{0,16},{4,20},{8,24},{12,28},{16,0},{20,4},{24,8},{28,12},{1,17},{... | collective-permute-start | bytes 479240 | tf_op jit(solution)/shard_map/ppermute | solution.py:477
  70.8 1.0 %collective-permute-start.20 = (bf16[48,1664]{1,0:T(8,128)(2,1)S(1)}, bf16[48,1664]{1,0:T(8,128)(2,1)S(1)}, u32[]{:S(2)}, u32[]{:S(2)}) collective-permute-start(bf16[48,1664]{1,0:T(8,128)(2,1)S(1)} %get-tuple-element.144), channel_id=1, source_target_pairs={{0,24},{4,28},{8,16},{12,20},{16,8},{20,12},{24,0},{28,4},{1,25},{... | collective-permute-start | bytes 479240 | tf_op jit(solution)/shard_map/ppermute | solution.py:477
  71.8 0.6 collective-permute-start.22
  72.4 4.5 %collective-permute-done.22.we_a = bf16[1,48,1536]{2,1,0:T(8,128)(2,1)S(1)} collective-permute-done((bf16[1,48,1536]{2,1,0:T(8,128)(2,1)S(1)}, bf16[1,48,1536]{2,1,0:T(8,128)(2,1)S(1)}, u32[]{:S(2)}, u32[]{:S(2)}) %collective-permute-start.22) | collective-permute-done | bytes 147488 | tf_op jit(solution)/shard_map/ppermute | solution.py:473
  77.0 11.4 %collective-permute-done.19.r2 = bf16[48,1664]{1,0:T(8,128)(2,1)S(1)} collective-permute-done((bf16[48,1664]{1,0:T(8,128)(2,1)S(1)}, bf16[48,1664]{1,0:T(8,128)(2,1)S(1)}, u32[]{:S(2)}, u32[]{:S(2)}) %collective-permute-start.19) | collective-permute-done | bytes 159776 | tf_op jit(solution)/shard_map/ppermute | solution.py:477
  88.3 0.8 shard_map.298
  89.1 0.5 collective-permute-start.24
  89.6 1.5 %collective-permute-done.23.arrived = f32[24,1408]{1,0:T(8,128)S(1)} collective-permute-done((f32[24,1408]{1,0:T(8,128)S(1)}, f32[24,1408]{1,0:T(8,128)S(1)}, u32[]{:S(2)}, u32[]{:S(2)}) %collective-permute-start.23) | collective-permute-done | bytes 135200 | tf_op jit(solution)/shard_map/ppermute | solution.py:465
  91.1 0.9 %shard_map.299 = (f32[24,2304]{1,0:T(8,128)}, f32[24]{0:T(128)}, f32[24]{0:T(128)}, f32[2,24]{1,0:T(2,128)}, f32[24]{0:T(128)}, /*index=5*/f32[24]{0:T(128)}, f3...) custom-call(f32[24,1152]{1,0:T(8,128)S(1)} %get-tuple-element.149.ke, ...), custom_call_target="tpu_custom_call" | custom-call | bytes 1000000 | tf_op jit(solution)/shard_map/pallas_call | solution.py:655
  (18 shorter events, 0.1 us)
Async XLA Ops:
  0.6 6.8 %copy-start = (bf16[3,64,768]{2,1,0:T(8,128)(2,1)S(1)}, bf16[3,64,768]{2,1,0:T(8,128)(2,1)}, u32[]{:S(2)}) copy-start(bf16[3,64,768]{2,1,0:T(8,128)(2,1)} %tok.1) | copy-start | bytes 884740
  0.7 10.3 %collective-permute-start.1 = (bf16[3,64,768]{2,1,0:T(8,128)(2,1)}, bf16[3,64,768]{2,1,0:T(8,128)(2,1)S(1)}, u32[]{:S(2)}, u32[]{:S(2)}) collective-permute-start(bf16[3,64,768]{2,1,0:T(8,128)(2,1)} %tok.1), channel_id=1, source_target_pairs={{0,2},{1,3},{2,0},{3,1},{4,6},{5,7},{6,4},{7,5},{8,10},{9,11},{10,... | collective-permute-start | bytes 884744 | tf_op jit(solution)/shard_map/ppermute | solution.py:469
  7.4 3.7 %collective-permute-start.2 = (s32[3,64]{1,0:T(4,128)S(1)}, s32[3,64]{1,0:T(4,128)S(1)}, u32[]{:S(2)}, u32[]{:S(2)}) collective-permute-start(s32[3,64]{1,0:T(4,128)S(1)} %get-tuple-element.95.v0), channel_id=1, source_target_pairs={{0,2},{1,3},{2,0},{3,1},{4,6},{5,7},{6,4},{7,5},{8,10},{9,11},{10,... | collective-permute-start | bytes 2312 | tf_op jit(solution)/shard_map/ppermute | solution.py:469
  7.5 6.7 %collective-permute-start = (bf16[3,64,768]{2,1,0:T(8,128)(2,1)S(1)}, bf16[3,64,768]{2,1,0:T(8,128)(2,1)S(1)}, u32[]{:S(2)}, u32[]{:S(2)}) collective-permute-start(bf16[3,64,768]{2,1,0:T(8,128)(2,1)S(1)} %copy-done), channel_id=1, source_target_pairs={{0,1},{1,0},{2,3},{3,2},{4,5},{5,4},{6,7},{7,6},{8,9},{9,8},{10,11... | collective-permute-start | bytes 884744 | tf_op jit(solution)/shard_map/ppermute | solution.py:465
  11.1 3.1 %collective-permute-start.3 = (bf16[3,64,768]{2,1,0:T(8,128)(2,1)S(1)}, bf16[3,64,768]{2,1,0:T(8,128)(2,1)S(1)}, u32[]{:S(2)}, u32[]{:S(2)}) collective-permute-start(bf16[3,64,768]{2,1,0:T(8,128)(2,1)S(1)} %get-tuple-element.97.t2), channel_id=1, source_target_pairs={{0,1},{1,0},{2,3},{3,2},{4,5},{5,4},{6,7},{7,6},{8,9},{9,8},{10,11... | collective-permute-start | bytes 884744 | tf_op jit(solution)/shard_map/ppermute | solution.py:465
  11.1 9.4 %collective-permute-start.8 = (bf16[3,64,768]{2,1,0:T(8,128)(2,1)S(1)}, bf16[3,64,768]{2,1,0:T(8,128)(2,1)S(1)}, u32[]{:S(2)}, u32[]{:S(2)}) collective-permute-start(bf16[3,64,768]{2,1,0:T(8,128)(2,1)S(1)} %get-tuple-element.101.c0), channel_id=1, source_target_pairs={{0,2},{1,3},{2,0},{3,1},{4,6},{5,7},{6,4},{7,5},{8,10},{9,11},{10,... | collective-permute-start | bytes 884744 | tf_op jit(solution)/shard_map/ppermute | solution.py:469
  12.9 1.2 %collective-permute-start.4 = (s32[3,64]{1,0:T(4,128)S(1)}, s32[3,64]{1,0:T(4,128)S(1)}, u32[]{:S(2)}, u32[]{:S(2)}) collective-permute-start(s32[3,64]{1,0:T(4,128)S(1)} %get-tuple-element.95.v0), channel_id=1, source_target_pairs={{0,1},{1,0},{2,3},{3,2},{4,5},{5,4},{6,7},{7,6},{8,9},{9,8},{10,11... | collective-permute-start | bytes 2312 | tf_op jit(solution)/shard_map/ppermute | solution.py:465
  13.0 1.2 %collective-permute-start.5 = (s32[3,64]{1,0:T(4,128)S(1)}, s32[3,64]{1,0:T(4,128)S(1)}, u32[]{:S(2)}, u32[]{:S(2)}) collective-permute-start(s32[3,64]{1,0:T(4,128)S(1)} %collective-permute-done.2.after_a.v2), channel_id=1, source_target_pairs={{0,1},{1,0},{2,3},{3,2},{4,5},{5,4},{6,7},{7,6},{8,9},{9,8},{10,11... | collective-permute-start | bytes 2312 | tf_op jit(solution)/shard_map/ppermute | solution.py:465
  17.5 4.7 %collective-permute-start.6 = (bf16[432,384]{1,0:T(8,128)(2,1)S(1)}, bf16[432,384]{1,0:T(8,128)(2,1)S(1)}, u32[]{:S(2)}, u32[]{:S(2)}) collective-permute-start(bf16[432,384]{1,0:T(8,128)(2,1)S(1)} %get-tuple-element.99.mix_a), channel_id=1, source_target_pairs={{0,1},{1,0},{2,3},{3,2},{4,5},{5,4},{6,7},{7,6},{8,9},{9,8},{10,11... | collective-permute-start | bytes 995336 | tf_op jit(solution)/shard_map/ppermute | solution.py:465
  17.9 3.2 %collective-permute-start.7 = (bf16[3,64,768]{2,1,0:T(8,128)(2,1)S(1)}, bf16[3,64,768]{2,1,0:T(8,128)(2,1)S(1)}, u32[]{:S(2)}, u32[]{:S(2)}) collective-permute-start(bf16[3,64,768]{2,1,0:T(8,128)(2,1)S(1)} %get-tuple-element.94.cot), channel_id=1, source_target_pairs={{0,1},{1,0},{2,3},{3,2},{4,5},{5,4},{6,7},{7,6},{8,9},{9,8},{10,11... | collective-permute-start | bytes 884744 | tf_op jit(solution)/shard_map/ppermute | solution.py:465
  20.6 1.6 %collective-permute-start.9 = (bf16[3,64,768]{2,1,0:T(8,128)(2,1)S(1)}, bf16[3,64,768]{2,1,0:T(8,128)(2,1)S(1)}, u32[]{:S(2)}, u32[]{:S(2)}) collective-permute-start(bf16[3,64,768]{2,1,0:T(8,128)(2,1)S(1)} %collective-permute-done.8.c2), channel_id=1, source_target_pairs={{0,1},{1,0},{2,3},{3,2},{4,5},{5,4},{6,7},{7,6},{8,9},{9,8},{10,11... | collective-permute-start | bytes 884744 | tf_op jit(solution)/shard_map/ppermute | solution.py:465
  28.2 6.7 %collective-permute-start.10 = (bf16[432,768]{1,0:T(8,128)(2,1)S(1)}, bf16[432,768]{1,0:T(8,128)(2,1)S(1)}, u32[]{:S(2)}, u32[]{:S(2)}) collective-permute-start(bf16[432,768]{1,0:T(8,128)(2,1)S(1)} %get-tuple-element.109.gn2_a), channel_id=1, source_target_pairs={{0,1},{1,0},{2,3},{3,2},{4,5},{5,4},{6,7},{7,6},{8,9},{9,8},{10,11... | collective-permute-start | bytes 1990664 | tf_op jit(solution)/shard_map/ppermute | solution.py:465
  28.4 24.5 %collective-permute-start.12 = (bf16[432,768]{1,0:T(8,128)(2,1)S(1)}, bf16[432,768]{1,0:T(8,128)(2,1)S(1)}, u32[]{:S(2)}, u32[]{:S(2)}) collective-permute-start(bf16[432,768]{1,0:T(8,128)(2,1)S(1)} %get-tuple-element.125.bt2_a), channel_id=1, source_target_pairs={{0,1},{1,0},{2,3},{3,2},{4,5},{5,4},{6,7},{7,6},{8,9},{9,8},{10,11... | collective-permute-start | bytes 1990664 | tf_op jit(solution)/shard_map/ppermute | solution.py:465
  31.5 16.2 %collective-permute-start.13 = (bf16[4,96,768]{2,1,0:T(8,128)(2,1)S(1)}, bf16[4,96,768]{2,1,0:T(8,128)(2,1)S(1)}, u32[]{:S(2)}, u32[]{:S(2)}) collective-permute-start(bf16[4,96,768]{2,1,0:T(8,128)(2,1)S(1)} %get-tuple-element.127), channel_id=1, source_target_pairs={{0,4},{4,0},{8,12},{12,8},{16,20},{20,16},{24,28},{28,24},{1,5},{5... | collective-permute-start | bytes 1769480 | tf_op jit(solution)/shard_map/ppermute | solution.py:473
  33.2 15.1 %collective-permute-start.14 = (bf16[4,48,1536]{2,1,0:T(8,128)(2,1)S(1)}, bf16[4,48,1536]{2,1,0:T(8,128)(2,1)S(1)}, u32[]{:S(2)}, u32[]{:S(2)}) collective-permute-start(bf16[4,48,1536]{2,1,0:T(8,128)(2,1)S(1)} %get-tuple-element.129), channel_id=1, source_target_pairs={{0,8},{4,12},{8,0},{12,4},{16,24},{20,28},{24,16},{28,20},{1,9},{5... | collective-permute-start | bytes 1769480 | tf_op jit(solution)/shard_map/ppermute | solution.py:477
  42.7 10.1 %collective-permute-start.11 = (bf16[432,768]{1,0:T(8,128)(2,1)S(1)}, bf16[432,768]{1,0:T(8,128)(2,1)S(1)}, u32[]{:S(2)}, u32[]{:S(2)}) collective-permute-start(bf16[432,768]{1,0:T(8,128)(2,1)S(1)} %get-tuple-element.123.gnp_a), channel_id=1, source_target_pairs={{0,1},{1,0},{2,3},{3,2},{4,5},{5,4},{6,7},{7,6},{8,9},{9,8},{10,11... | collective-permute-start | bytes 1990664 | tf_op jit(solution)/shard_map/ppermute | solution.py:465
  42.8 22.3 %collective-permute-start.15 = (bf16[4,48,1664]{2,1,0:T(8,128)(2,1)S(1)}, bf16[4,48,1664]{2,1,0:T(8,128)(2,1)S(1)}, u32[]{:S(2)}, u32[]{:S(2)}) collective-permute-start(bf16[4,48,1664]{2,1,0:T(8,128)(2,1)S(1)} %get-tuple-element.135), channel_id=1, source_target_pairs={{0,4},{4,0},{8,12},{12,8},{16,20},{20,16},{24,28},{28,24},{1,5},{5... | collective-permute-start | bytes 1916936 | tf_op jit(solution)/shard_map/ppermute | solution.py:473
  48.6 14.1 %collective-permute-start.16 = (bf16[2,96,768]{2,1,0:T(8,128)(2,1)S(1)}, bf16[2,96,768]{2,1,0:T(8,128)(2,1)S(1)}, u32[]{:S(2)}, u32[]{:S(2)}) collective-permute-start(bf16[2,96,768]{2,1,0:T(8,128)(2,1)S(1)} %get-tuple-element.137), channel_id=1, source_target_pairs={{0,8},{4,12},{8,0},{12,4},{16,24},{20,28},{24,16},{28,20},{1,9},{5... | collective-permute-start | bytes 884744 | tf_op jit(solution)/shard_map/ppermute | solution.py:477
  50.3 14.9 %collective-permute-start.17 = (bf16[2,48,1536]{2,1,0:T(8,128)(2,1)S(1)}, bf16[2,48,1536]{2,1,0:T(8,128)(2,1)S(1)}, u32[]{:S(2)}, u32[]{:S(2)}) collective-permute-start(bf16[2,48,1536]{2,1,0:T(8,128)(2,1)S(1)} %get-tuple-element.139), channel_id=1, source_target_pairs={{0,16},{4,20},{8,24},{12,28},{16,0},{20,4},{24,8},{28,12},{1,17},{... | collective-permute-start | bytes 884744 | tf_op jit(solution)/shard_map/ppermute | solution.py:477
  65.4 22.9 %collective-permute-start.21 = (bf16[2,96,768]{2,1,0:T(8,128)(2,1)S(1)}, bf16[2,96,768]{2,1,0:T(8,128)(2,1)S(1)}, u32[]{:S(2)}, u32[]{:S(2)}) collective-permute-start(bf16[2,96,768]{2,1,0:T(8,128)(2,1)S(1)} %get-tuple-element.146), channel_id=1, source_target_pairs={{1,17},{3,19},{5,21},{7,23},{9,25},{11,27},{13,29},{15,31},{16,0},... | collective-permute-start | bytes 884744 | tf_op jit(solution)/shard_map/ppermute | solution.py:635
  66.7 10.2 %collective-permute-start.18 = (bf16[48,1664]{1,0:T(8,128)(2,1)S(1)}, bf16[48,1664]{1,0:T(8,128)(2,1)S(1)}, u32[]{:S(2)}, u32[]{:S(2)}) collective-permute-start(bf16[48,1664]{1,0:T(8,128)(2,1)S(1)} %get-tuple-element.142), channel_id=1, source_target_pairs={{0,8},{4,12},{8,0},{12,4},{16,24},{20,28},{24,16},{28,20},{1,9},{5... | collective-permute-start | bytes 479240 | tf_op jit(solution)/shard_map/ppermute | solution.py:477
  67.2 21.1 %collective-permute-start.19 = (bf16[48,1664]{1,0:T(8,128)(2,1)S(1)}, bf16[48,1664]{1,0:T(8,128)(2,1)S(1)}, u32[]{:S(2)}, u32[]{:S(2)}) collective-permute-start(bf16[48,1664]{1,0:T(8,128)(2,1)S(1)} %get-tuple-element.143), channel_id=1, source_target_pairs={{0,16},{4,20},{8,24},{12,28},{16,0},{20,4},{24,8},{28,12},{1,17},{... | collective-permute-start | bytes 479240 | tf_op jit(solution)/shard_map/ppermute | solution.py:477
  70.8 17.6 %collective-permute-start.20 = (bf16[48,1664]{1,0:T(8,128)(2,1)S(1)}, bf16[48,1664]{1,0:T(8,128)(2,1)S(1)}, u32[]{:S(2)}, u32[]{:S(2)}) collective-permute-start(bf16[48,1664]{1,0:T(8,128)(2,1)S(1)} %get-tuple-element.144), channel_id=1, source_target_pairs={{0,24},{4,28},{8,16},{12,20},{16,8},{20,12},{24,0},{28,4},{1,25},{... | collective-permute-start | bytes 479240 | tf_op jit(solution)/shard_map/ppermute | solution.py:477
  71.8 5.1 %collective-permute-start.22 = (bf16[1,48,1536]{2,1,0:T(8,128)(2,1)S(1)}, bf16[1,48,1536]{2,1,0:T(8,128)(2,1)S(1)}, u32[]{:S(2)}, u32[]{:S(2)}) collective-permute-start(bf16[1,48,1536]{2,1,0:T(8,128)(2,1)S(1)} %get-tuple-element.148), channel_id=1, source_target_pairs={{0,4},{4,0},{8,12},{12,8},{16,20},{20,16},{24,28},{28,24},{1,5},{5... | collective-permute-start | bytes 442376 | tf_op jit(solution)/shard_map/ppermute | solution.py:473
  89.1 2.0 %collective-permute-start.25 = (f32[96,768]{1,0:T(8,128)S(1)}, f32[96,768]{1,0:T(8,128)S(1)}, u32[]{:S(2)}, u32[]{:S(2)}) collective-permute-start(f32[96,768]{1,0:T(8,128)S(1)} %get-tuple-element.155), channel_id=1, source_target_pairs={{0,1},{1,0},{2,3},{3,2},{4,5},{5,4},{6,7},{7,6},{8,9},{9,8},{10,11... | collective-permute-start | bytes 884744 | tf_op jit(solution)/shard_map/ppermute | solution.py:465
  89.1 2.0 %collective-permute-start.24 = (f32[24,1536]{1,0:T(8,128)S(1)}, f32[24,1536]{1,0:T(8,128)S(1)}, u32[]{:S(2)}, u32[]{:S(2)}) collective-permute-start(f32[24,1536]{1,0:T(8,128)S(1)} %get-tuple-element.153), channel_id=1, source_target_pairs={{0,1},{1,0},{2,3},{3,2},{4,5},{5,4},{6,7},{7,6},{8,9},{9,8},{10,11... | collective-permute-start | bytes 442376 | tf_op jit(solution)/shard_map/ppermute | solution.py:465
  89.6 1.5 %collective-permute-start.23 = (f32[24,1408]{1,0:T(8,128)S(1)}, f32[24,1408]{1,0:T(8,128)S(1)}, u32[]{:S(2)}, u32[]{:S(2)}) collective-permute-start(f32[24,1408]{1,0:T(8,128)S(1)} %get-tuple-element.151), channel_id=1, source_target_pairs={{0,1},{1,0},{2,3},{3,2},{4,5},{5,4},{6,7},{7,6},{8,9},{9,8},{10,11... | collective-permute-start | bytes 405512 | tf_op jit(solution)/shard_map/ppermute | solution.py:465

commit v3 on v2

--- a/solution.py
+++ b/solution.py
@@ -1,4 +1,3 @@
-import functools
 import math
 
 import jax
@@ -59,20 +58,23 @@
 
 
 def one_hot_pack(pos, image):
-    rows = lax.broadcasted_iota(jnp.int32, (PACK, SLOTS), 0).astype(F32)
+    rows = lax.broadcasted_iota(jnp.int32, (PACK, pos.shape[1]), 0).astype(F32)
     return jnp.where(rows == pos[image : image + 1, :], 1.0, 0.0).astype(BF)
 
 
-def feature_pick():
-    x, _, z, y = place()
-    lane = lax.broadcasted_iota(jnp.int32, (D, HALF), 1)
-    row = lax.broadcasted_iota(jnp.int32, (D, HALF), 0)
-    want = jnp.zeros((D, HALF), jnp.int32)
-    for q in range(8):
-        dy, dz = q // 4, q % 4
-        base = 96 * ((z ^ dz) * 2 + (y ^ dy)) + 48 * x - 48 * q
-        want = jnp.where((lane >= 48 * q) & (lane < 48 * q + 48), lane + base, want)
-    return jnp.where(row == want, 1.0, 0.0).astype(BF)
+def shard_picks():
+    x, c, z, y = place()
+
+    def pick(width, base):
+        lane = lax.broadcasted_iota(jnp.int32, (1, 8 * width), 1)
+        want = jnp.zeros((1, 8 * width), jnp.int32)
+        for q in range(8):
+            first = 96 * ((z ^ (q % 4)) * 2 + (y ^ (q // 4))) + base - width * q
+            want = jnp.where((lane >= width * q) & (lane < width * (q + 1)), lane + first, want)
+        row = lax.broadcasted_iota(jnp.int32, (D, 8 * width), 0)
+        return jnp.where(row == want, 1.0, 0.0).astype(BF)
+
+    return pick(48, 48 * x), pick(24, 48 * x + 24 * c)
 
 
 def statistics(values):
@@ -147,7 +149,7 @@
 
 def first_kernel(
     t0, t1, t2, t3, v0, v1, v2, v3, par, w,
-    tok_o, norm_o, qkv_o, mix_o, pos_o, probs_o,
+    tok_o, norm_o, qkv_o, mix_o, pos_o, probs_o, mine_o, theirs_o,
     xs, shown,
 ):
     band = lax.axis_index("band")
@@ -165,6 +167,9 @@
     before = jnp.where(upto < slot, 1.0, 0.0).astype(BF)
     pos = jnp.where(vis > 0, dot(vis.astype(BF), before), -1.0)
     pos_o[...] = pos[0:8]
+    slot = lax.broadcasted_iota(jnp.int32, (SLOTS, BAND), 0) - lax.broadcasted_iota(jnp.int32, (SLOTS, BAND), 1)
+    for out, b in ((mine_o, band), (theirs_o, band ^ 1)):
+        out[...] = dot(pos.astype(BF), jnp.where(slot == b * BAND, 1.0, 0.0).astype(BF))
     for i in range(IMGS):
         rows = slice(i * PACK, (i + 1) * PACK)
         tok = dot(one_hot_pack(pos, i), xs[i])
@@ -192,112 +197,99 @@
             mix_o[rows, cols] = join_heads(dot(probs.astype(BF), v2)).astype(BF)
 
 
-def pick_kernel(normed, pick_o, pn_o):
-    pick = feature_pick()
+def pick_kernel(normed, pick_o, pick_p_o, pn_o):
+    pick, pick_p = shard_picks()
     pick_o[...] = pick
+    pick_p_o[...] = pick_p
     pn_o[...] = dot(normed[...], pick).astype(BF)
 
 
-def second_kernel(
-    mix_a, mix_b, tok, c0, c1, c2, c3, pos_r, par, be, wp, we, wr, after,
-    res_o, one_o, pre_o, gb2_o, n2_o, mix_o, act_o, gh_o, gn2_o, bt2_o, small_o,
-    xs, act_v,
-):
-    x, c, _, _ = place()
-    units = pl.multiple_of(c * FH, 128)
+def hidden_kernel(mix_a, mix_b, tok, par, be, wp, we, after, res_o, one_o, n2_o, mix_o, act_o, slope_o):
+    c = lax.axis_index("band") & 1
     mine, other = pl.multiple_of(c * HALF, 128), pl.multiple_of((1 - c) * HALF, 128)
-    gather_bands((c0, c1, c2, c3), xs)
     mix_o[:, pl.ds(mine, HALF)] = mix_a[...]
     mix_o[:, pl.ds(other, HALF)] = mix_b[...]
-    pos = pos_r[...]
     one = dot(mix_o[...], wp[...]) + par[PB : PB + 1, :]
     one_o[...] = one
     residual = tok[...].astype(F32) + par[ASC : ASC + 1, :] * one
     res_o[...] = residual
     z, _ = statistics(residual)
     n2_o[...] = (z * par[GAIN2 : GAIN2 + 1, :] + par[BIAS2 : BIAS2 + 1, :]).astype(BF)
+    step = 256
+    for f in range(FH // step):
+        cols = slice(f * step, (f + 1) * step)
+        hidden = dot(n2_o[...], we[:, cols]) + be[0:1, cols]
+        phi = 0.5 * (1.0 + lax.erf(hidden * math.sqrt(0.5)))
+        act_o[:, cols] = (hidden * phi).astype(BF)
+        slope_o[:, cols] = phi + hidden * (jnp.exp(-0.5 * hidden * hidden) * (1.0 / math.sqrt(2.0 * math.pi)))
+
+
+def reduce_grad_kernel(c0, c1, c2, c3, pos_r, par, act, pre_o, gb2_o, send_o, keep_o, xs, act_x, full):
+    x, c, z, y = place()
+    gather_bands((c0, c1, c2, c3), xs)
+    pos = pos_r[...]
     for i in range(IMGS):
         rows = slice(i * PACK, (i + 1) * PACK)
         pre = dot(one_hot_pack(pos, i), xs[i])
         pre_o[rows, :] = pre.astype(BF)
         gb2_o[rows, :] = (par[MSC : MSC + 1, :] * pre).astype(BF)
-    step = 256
-    for f in range(FH // step):
-        cols = slice(f * step, (f + 1) * step)
-        hidden = dot(n2_o[...], we[:, cols]) + be[0:1, cols]
-        phi = 0.5 * (1.0 + lax.erf(hidden * math.sqrt(0.5)))
-        act_v[:, cols] = (hidden * phi).astype(BF)
-        slope = phi + hidden * (jnp.exp(-0.5 * hidden * hidden) * (1.0 / math.sqrt(2.0 * math.pi)))
-        back = dot_nt(gb2_o[...], wr[cols, :])
-        gh_o[:, cols] = (back * slope).astype(BF)
-    gn2_o[...] = dot_nt(gh_o[...], we[...]).astype(BF)
     for j in range(4):
         lo, mid, hi = 384 * j, 384 * j + 192, 384 * j + 384
-        act_o[:, 192 * j : 192 * j + 192] = jnp.where(x == 0, act_v[:, lo:mid], act_v[:, mid:hi])
-    two = dot(act_v[...], wr[...])
-    bt2_o[...] = two.astype(BF)
-    pre = pre_o[...].astype(F32)
-    first = jnp.where(c == 0, 1.0, 0.0)
-    small_o[...] = jnp.zeros_like(small_o)
-    small_o[0:1, :] = first * jnp.sum(gb2_o[...].astype(F32), axis=0, keepdims=True)
-    small_o[1:2, :] = jnp.sum(pre * (two + first * par[RB : RB + 1, :]), axis=0, keepdims=True)
-
-
-def mlp_grads_kernel(n2, gh, act, gb2, pick, wr_send, wr_keep, we_send, we_keep, eb_o, full, wide, sums):
-    x, c, z, y = place()
-    full[...] = dot_tn(act[...], gb2[...])
-    for dy, out in ((1, wr_send), (0, wr_keep)):
+        act_x[:, 192 * j : 192 * j + 192] = jnp.where(x == 0, act[:, lo:mid], act[:, mid:hi])
+    full[...] = dot_tn(act_x[...], gb2_o[...])
+    for dy, out in ((1, send_o), (0, keep_o)):
         for dz in range(2):
             j = 2 * ((z & 1) ^ dz) + (y ^ dy)
             for to in range(2):
                 at = pl.multiple_of(192 * j + 96 * to, 96)
                 out[2 * dz + to] = full[pl.ds(at, 96), :].astype(BF)
+
+
+def back_kernel(gb2, wr, slope, we, gh_o, left_o, right_o):
+    step = 256
+    for f in range(FH // step):
+        cols = slice(f * step, (f + 1) * step)
+        back = dot_nt(gb2[...], wr[cols, :])
+        gh_o[:, cols] = (back * slope[:, cols]).astype(BF)
+    gn2 = dot_nt(gh_o[...], we[...]).astype(BF)
+    left_o[...] = gn2[:, :HALF]
+    right_o[...] = gn2[:, HALF:]
+
+
+def expand_grad_kernel(n2, gh, pick, send_o, keep_o, tick, wide):
+    tick[...] = jnp.zeros_like(tick)
     picked = dot(n2[...], pick[...]).astype(BF)
     wide[...] = dot_tn(picked, gh[...])
-    for low, out in ((1, we_send), (0, we_keep)):
+    for low, out in ((1, send_o), (0, keep_o)):
         for i in range(4):
             lo = 192 * (i & 1) + 48 * (low + 2 * (i >> 1))
             out[i] = wide[lo : lo + 48, :].astype(BF)
-    sums[...] = dot_tn(gh[...], jnp.ones((ROWS, 128), BF))
-    lane = lax.broadcasted_iota(jnp.int32, (48, SMALL), 1)
-    for q in range(8):
-        b = (z ^ (q % 4)) * 2 + (y ^ (q // 4))
-        here = (b >> 2) == c
-        block = jnp.zeros((48, SMALL), F32)
-        for k in range(4):
-            at = pl.multiple_of(384 * (b & 3) + 192 * x + 48 * k, 48)
-            block = jnp.where((lane == 10 + k) & here, sums[pl.ds(at, 48), :], block)
-        eb_o[q] = block
 
 
 QC = 3 * HALF
-QW = QC + SMALL + HALF
-
-
-def third_kernel(
-    gn2_a, gn2_b, res, one, pre, tok, qkv, probs_r, mix, pn, pick, small2, eb, wp, w, par,
-    gres_o, gnp_o, send_o, keep_o, tick,
-    gp, vecs, flat,
+QW = QC + HALF
+QS = QW + SMALL
+
+
+def both_halves(l_a, l_b, r_a, r_b):
+    left = l_a[...].astype(F32) + l_b[...].astype(F32)
+    right = r_a[...].astype(F32) + r_b[...].astype(F32)
+    return jnp.concatenate([left, right], axis=1)
+
+
+def attention_back_kernel(
+    l_a, l_b, r_a, r_b, res, pre, qkv, probs_r, mix, pn, pick_p, wp, par, after,
+    gres_o, gp, send_o, keep_o, tick,
+    flat,
 ):
-    x, c, z, y = place()
     tick[...] = jnp.zeros_like(tick)
+    c = lax.axis_index("band") & 1
     heads = pl.multiple_of(c * HALF, 128)
-    first = jnp.where(c == 0, 1.0, 0.0)
-
-    def total(v):
-        return jnp.sum(v, axis=0, keepdims=True)
-
-    vecs[...] = jnp.zeros_like(vecs)
-    gn2 = gn2_a[...].astype(F32) + gn2_b[...].astype(F32)
+    gn2 = both_halves(l_a, l_b, r_a, r_b)
     z2, rstd2 = statistics(res[...])
-    vecs[6:7, :] = first * total(gn2 * z2)
-    vecs[7:8, :] = first * total(gn2)
     gres = pre[...].astype(F32) + norm_back(gn2 * par[GAIN2 : GAIN2 + 1, :], z2, rstd2)
     gres_o[...] = gres
-    vecs[5:6, :] = first * total(gres * one[...])
     gb1 = (par[ASC : ASC + 1, :] * gres).astype(BF)
-    vecs[4:5, :] = first * total(gb1.astype(F32))
-    vecs[8:10, :] = small2[0:2, :]
     gm = dot_nt(gb1, wp[pl.ds(heads, HALF), :]).astype(BF)
     scale = 1.0 / math.sqrt(HD)
     for i in range(IMGS):
@@ -317,110 +309,142 @@
             )
             for m in range(3):
                 gp[rows, m * HALF + hp * 128 : m * HALF + (hp + 1) * 128] = parts[m].astype(BF)
+    mixed = dot(mix[...], pick_p[...]).astype(BF)
+    proj = dot_tn(mixed, gb1)
+    flat[...] = dot_tn(pn[...], gp[...])
+    for dy, out in ((1, send_o), (0, keep_o)):
+        for i, dz in enumerate((0, 2, 1, 3)):
+            q = 4 * dy + dz
+            out[i, :, 0:QC] = flat[48 * q : 48 * q + 48, :].astype(BF)
+            block = proj[24 * q : 24 * q + 24]
+            out[i, :, QC:QW] = jnp.concatenate([block[:, :HALF], block[:, HALF:]], axis=0).astype(BF)
+
+
+def vectors_kernel(
+    l_a, l_b, r_a, r_b, res, one, gres, gp, w, act, wr, gb2, gh, pre, tok, pick, par, mine, theirs, after,
+    gb_keep, gb_send, send_o, keep_o, tick,
+    vecs, sums,
+):
+    tick[...] = jnp.zeros_like(tick)
+    x, c, z, y = place()
+    heads = pl.multiple_of(c * HALF, 128)
+    first = jnp.where(c == 0, 1.0, 0.0)
+
+    def total(v):
+        return jnp.sum(v, axis=0, keepdims=True)
+
+    vecs[...] = jnp.zeros_like(vecs)
     gnp = jnp.zeros((ROWS, D), F32)
     for m in range(3):
-        part = w[m]
-        gnp = gnp + dot_nt(gp[:, m * HALF : (m + 1) * HALF], part)
-    gnp_o[...] = gnp.astype(BF)
+        gnp = gnp + dot_nt(gp[:, m * HALF : (m + 1) * HALF], w[m])
     z1, _ = statistics(tok[...].astype(F32))
-    vecs[0:1, :] = total(gnp * z1)
-    vecs[1:2, :] = total(gnp)
-    vecs[2:3, pl.ds(heads, HALF)] = total(gp[:, 0:HALF].astype(F32))
-    vecs[3:4, pl.ds(heads, HALF)] = total(gp[:, 2 * HALF : 3 * HALF].astype(F32))
-    rowl = lax.broadcasted_iota(jnp.int32, (D, 192), 0)
-    colr = lax.broadcasted_iota(jnp.int32, (D, 192), 1)
-    want = jnp.zeros((D, 192), jnp.int32)
-    for q in range(8):
-        base = 96 * ((z ^ (q % 4)) * 2 + (y ^ (q // 4))) + 48 * x + 24 * c - 24 * q
-        want = jnp.where((colr >= 24 * q) & (colr < 24 * q + 24), colr + base, want)
-    pick_p = jnp.where(rowl == want, 1.0, 0.0).astype(BF)
-    mixed = dot(mix[...], pick_p).astype(BF)
-    proj = dot_tn(mixed, gb1)
-    vec_cols = dot(vecs[...].astype(BF), pick[...]).T
-    flat[...] = dot_tn(pn[...], gp[...])
+    vecs[GAIN1 : GAIN1 + 1, :] = total(gnp * z1)
+    vecs[BIAS1 : BIAS1 + 1, :] = total(gnp)
+    vecs[QB : QB + 1, pl.ds(heads, HALF)] = total(gp[:, 0:HALF].astype(F32))
+    vecs[VB : VB + 1, pl.ds(heads, HALF)] = total(gp[:, 2 * HALF : 3 * HALF].astype(F32))
+    gb1 = (par[ASC : ASC + 1, :] * gres[...]).astype(BF)
+    vecs[PB : PB + 1, :] = first * total(gb1.astype(F32))
+    vecs[ASC : ASC + 1, :] = first * total(gres[...] * one[...])
+    gn2 = both_halves(l_a, l_b, r_a, r_b)
+    z2, _ = statistics(res[...])
+    vecs[GAIN2 : GAIN2 + 1, :] = first * total(gn2 * z2)
+    vecs[BIAS2 : BIAS2 + 1, :] = first * total(gn2)
+    vecs[RB : RB + 1, :] = first * total(gb2[...].astype(F32))
+    two = dot(act[...], wr[...])
+    for m, value in enumerate((gnp.astype(BF), two.astype(BF))):
+        for i in range(IMGS):
+            rows = slice(i * PACK, (i + 1) * PACK)
+            for at, out in ((mine, gb_keep), (theirs, gb_send)):
+                out[m, i] = dot_tn(one_hot_pack(at[...], i), value[rows]).astype(BF)
+    vecs[MSC : MSC + 1, :] = total(pre[...].astype(F32) * (two + first * par[RB : RB + 1, :]))
+    cols = dot(vecs[...].astype(BF), pick[...]).T
+    sums[...] = dot_tn(gh[...], jnp.ones((ROWS, SMALL), BF))
+    lane = lax.broadcasted_iota(jnp.int32, (48, SMALL), 1)
     for dy, out in ((1, send_o), (0, keep_o)):
-        for dz in range(4):
+        for i, dz in enumerate((0, 2, 1, 3)):
+            b = (z ^ dz) * 2 + (y ^ dy)
             q = 4 * dy + dz
-            lo = 48 * q
-            out[dz, :, 0:QC] = flat[lo : lo + 48, :].astype(BF)
-            out[dz, :, QC : QC + SMALL] = (vec_cols[lo : lo + 48] + eb[q]).astype(BF)
-            block = proj[24 * q : 24 * q + 24]
-            out[dz, :, QC + SMALL :] = jnp.concatenate([block[:, :HALF], block[:, HALF:]], axis=0).astype(BF)
-
-
-def last_kernel(gnp_a, gnp_b, tok, gres, bt2_a, bt2_b, res, pos_r, par, after, out_o, gtok_o, tick, wide):
+            block = cols[48 * q : 48 * q + 48]
+            for k in range(4):
+                at = pl.multiple_of(384 * (b & 3) + 192 * x + 48 * k, 48)
+                block = jnp.where((lane == 10 + k) & ((b >> 2) == c), sums[pl.ds(at, 48), :], block)
+            out[i] = block.astype(BF)
+
+
+def last_kernel(gb_a, gb_b, tok, gres, res, mine, par, after, out_o, gtok_o, tick):
     tick[...] = jnp.zeros_like(tick)
-    band = lax.axis_index("band")
-    at = pl.multiple_of(band * BAND, BAND)
-    pos = pos_r[...]
+
+    def own_rows(pack, value):
+        high = value.astype(BF)
+        return dot_tn(pack, high) + dot_tn(pack, (value - high.astype(F32)).astype(BF))
+
     for i in range(IMGS):
         rows = slice(i * PACK, (i + 1) * PACK)
-        z1, rstd1 = statistics(tok[rows, :].astype(F32))
-        gnp = gnp_a[rows, :].astype(F32) + gnp_b[rows, :].astype(F32)
-        gtok = (gres[rows, :] + norm_back(gnp * par[GAIN1 : GAIN1 + 1, :], z1, rstd1)).astype(BF)
-        two = bt2_a[rows, :].astype(F32) + bt2_b[rows, :].astype(F32) + par[RB : RB + 1, :]
-        out = (res[rows, :] + par[MSC : MSC + 1, :] * two).astype(BF)
-        pack = one_hot_pack(pos, i)
-        for value, dst in ((gtok, gtok_o), (out, out_o)):
-            wide[...] = dot_tn(pack, value)
-            dst[i] = wide[pl.ds(at, BAND), :].astype(BF)
+        pack = one_hot_pack(mine[...], i)
+        z1, rstd1 = statistics(tok[i].astype(F32))
+        gnp = gb_a[0, i].astype(F32) + gb_b[0, i].astype(F32)
+        gtok = own_rows(pack, gres[rows, :]) + norm_back(gnp * par[GAIN1 : GAIN1 + 1, :], z1, rstd1)
+        gtok_o[i] = gtok.astype(BF)
+        ones = dot_tn(pack, jnp.ones((PACK, D), BF))
+        two = gb_a[1, i].astype(F32) + gb_b[1, i].astype(F32) + ones * par[RB : RB + 1, :]
+        out_o[i] = (own_rows(pack, res[rows, :]) + par[MSC : MSC + 1, :] * two).astype(BF)
+
+
+def fold_kernel(keep, arrived, we_keep, we_arrived, after, keep_ao, send_ao, keep_bo, send_bo, tick):
+    tick[...] = jnp.zeros_like(tick)
+    fold(keep, arrived, keep_ao, send_ao)
+    fold(we_keep, we_arrived, keep_bo, send_bo)
 
 
 def fold(keep, arrived, keep_o, send_o):
-    count = keep.shape[0]
-    for i in range(count):
-        total = keep[i].astype(F32) + arrived[i].astype(F32)
-        if i < count // 2:
-            keep_o[i] = total
-        else:
-            send_o[i - count // 2] = total.astype(BF)
-
-
-def fold_kernel(keep_a, arrived_a, keep_b, arrived_b, after, keep_ao, send_ao, keep_bo, send_bo, tick):
-    fold(keep_a, arrived_a, keep_ao, send_ao)
-    fold(keep_b, arrived_b, keep_bo, send_bo)
+    half = keep.shape[0] // 2
+    for i in range(half):
+        keep_o[i] = keep[i].astype(F32) + arrived[i].astype(F32)
+        send_o[i] = (keep[half + i].astype(F32) + arrived[half + i].astype(F32)).astype(BF)
+
+
+def second_fold_kernel(keep, arrived, we_keep, we_arrived, after, keep_o, send_o, we_keep_o, we_send_o, tick):
     tick[...] = jnp.zeros_like(tick)
-
-
-def stage_kernel(
-    keep, arrived, keep_a, arrived_a, keep_b, arrived_b, after,
-    own_o, s1, s2, s3, keep_ao, send_ao, keep_bo, send_bo,
-):
-    own_o[...] = keep[0].astype(F32) + arrived[0].astype(F32)
-    for dz, out in ((1, s1), (2, s2), (3, s3)):
-        out[...] = (keep[dz].astype(F32) + arrived[dz].astype(F32)).astype(BF)
     for i in range(2):
-        total = keep_a[i] + arrived_a[i].astype(F32)
-        keep_ao[i] = total
-        send_ao[i] = total.astype(BF)
-    fold(keep_b, arrived_b, keep_bo, send_bo)
+        total = keep[i] + arrived[i].astype(F32)
+        keep_o[i] = total
+        send_o[i] = total.astype(BF)
+    fold(we_keep, we_arrived, we_keep_o, we_send_o)
+
+
+def join_kernel(keep, arrived, vec_keep, vec_arrived, after, keep_o, send_o, tick):
+    tick[...] = jnp.zeros_like(tick)
+    fold(keep, arrived, keep_o.at[:, :, 0:QW], send_o.at[:, :, 0:QW])
+    fold(vec_keep, vec_arrived, keep_o.at[:, :, QW:QS], send_o.at[:, :, QW:QS])
+
+
+def third_fold_kernel(keep, arrived, after, keep_o, send_o, tick):
+    tick[...] = jnp.zeros_like(tick)
+    fold(keep, arrived, keep_o, send_o)
 
 
 def finish_kernel(
-    own, r1, r2, r3, wr_k, wr_a, we_k, we_a,
+    qp_k, qp_a, wr_k, wr_a, we_k, we_a, after,
     qk_o, qs_o, vec_o, proj_o, wr_ko, wr_so, keep_o, send_o,
     sums, both,
 ):
-    tail(own, r1, r2, r3, qk_o, qs_o, vec_o, proj_o, sums)
     c = lax.axis_index("band") & 1
-    wr_ko[...] = wr_k[c] + wr_a[c].astype(F32)
-    wr_so[...] = wr_k[1 - c] + wr_a[1 - c].astype(F32)
+    mine = pl.multiple_of(c * 24, 8)
+    other = pl.multiple_of(24 - c * 24, 8)
+    sums[...] = qp_k[0] + qp_a[0].astype(F32)
+    qk_o[...] = sums[pl.ds(mine, 24), 0:QC]
+    qs_o[:, 0:QC] = sums[pl.ds(other, 24), 0:QC]
+    vec = sums[:, QW:QS]
+    vec_o[...] = vec
+    qs_o[:, QC : QC + SMALL] = vec[0:24]
+    qs_o[:, QC + SMALL : QC + 2 * SMALL] = vec[24:48]
+    proj_o[:, 0:HALF] = sums[0:24, QC:QW]
+    proj_o[:, HALF:] = sums[24:48, QC:QW]
+    for at, out in ((c, wr_ko), (1 - c, wr_so)):
+        out[...] = wr_k[at] + wr_a[at].astype(F32)
     both[...] = we_k[0] + we_a[0].astype(F32)
-    keep_o[...] = both[pl.ds(pl.multiple_of(c * 24, 8), 24), :]
-    send_o[...] = both[pl.ds(pl.multiple_of(24 - c * 24, 8), 24), :]
-
-
-def tail(own, r1, r2, r3, keep_o, send_o, vec_o, proj_o, both):
-    c = lax.axis_index("band") & 1
-    both[...] = own[...] + r1[...].astype(F32) + r2[...].astype(F32) + r3[...].astype(F32)
-    keep_o[...] = both[pl.ds(pl.multiple_of(c * 24, 8), 24), 0:QC]
-    send_o[:, 0:QC] = both[pl.ds(pl.multiple_of(24 - c * 24, 8), 24), 0:QC]
-    vec = both[:, QC : QC + SMALL]
-    vec_o[...] = vec
-    send_o[:, QC : QC + SMALL] = vec[0:24]
-    send_o[:, QC + SMALL : QC + 2 * SMALL] = vec[24:48]
-    proj_o[:, 0:HALF] = both[0:24, QC + SMALL :]
-    proj_o[:, HALF:] = both[24:48, QC + SMALL :]
+    keep_o[...] = both[pl.ds(mine, 24), :]
+    send_o[...] = both[pl.ds(other, 24), :]
 
 
 def out_kernel(
@@ -449,15 +473,35 @@
     eb_o[...] = jnp.concatenate([units[0:1], units[1:2]], axis=1).reshape(96)
 
 
-def call(kernel, outs, specs, scratch=(), flops=0, nbytes=0, vmem=24, out_specs=None):
+COSTS = {
+    "first_kernel": (1500000000, 6000000),
+    "pick_kernel": (500000000, 2000000),
+    "hidden_kernel": (3000000000, 9000000),
+    "reduce_grad_kernel": (1000000000, 4000000),
+    "back_kernel": (2000000000, 6000000),
+    "expand_grad_kernel": (1000000000, 4000000),
+    "attention_back_kernel": (4000000000, 12000000),
+    "vectors_kernel": (2000000000, 8000000),
+    "fold_kernel": (0, 4000000),
+    "second_fold_kernel": (0, 2000000),
+    "last_kernel": (1000000000, 8000000),
+    "spread_kernel": (0, 2000000),
+    "finish_kernel": (0, 1000000),
+    "out_kernel": (0, 1000000),
+    "prepare_kernel": (0, 9000000),
+    "hold_kernel": (0, 20000000),
+}
+
+
+def call(kernel, outs, specs, scratch=(), vmem=24):
     return pl.pallas_call(
         kernel,
         out_shape=outs,
         in_specs=specs,
-        out_specs=jax.tree.map(lambda _: VM, outs) if out_specs is None else out_specs,
+        out_specs=jax.tree.map(lambda _: VM, outs),
         scratch_shapes=list(scratch),
         compiler_params=pltpu.CompilerParams(vmem_limit_bytes=vmem * MIB),
-        cost_estimate=pl.CostEstimate(flops=flops, bytes_accessed=nbytes, transcendentals=0),
+        cost_estimate=pl.CostEstimate(flops=COSTS.get(kernel.__name__, (0, 0))[0], bytes_accessed=COSTS.get(kernel.__name__, (0, 0))[1], transcendentals=0),
     )
 
 
@@ -477,27 +521,24 @@
     return lax.ppermute(value, "batch", [(i, i ^ (2 * dz)) for i in range(8)])
 
 
-def fold_pair(keep_a, arrived_a, keep_b, arrived_b, after):
-    outs = []
-    for keep in (keep_a, keep_b):
-        half = (keep.shape[0] // 2,) + keep.shape[1:]
-        outs += [vm(half, F32), vm(half, BF)]
-    return call(fold_kernel, (*outs, TICK), [VM] * 4 + [ANY], nbytes=int(4e6))(
-        keep_a, arrived_a, keep_b, arrived_b, after
-    )
+def homeward(value, dz):
+    pairs = [(d, d ^ (8 * dz)) for d in range(32) if ((d ^ (8 * dz)) >> 4) == (d & 1)]
+    return lax.ppermute(value, ("batch", "band"), pairs)
 
 
 def packed_body(
     tokens, cotangent, visible, first_gain, first_bias, qkv_weight, qv_bias, proj_weight, proj_bias,
     attn_scale, second_gain, second_bias, expand_weight, expand_bias, reduce_weight, reduce_bias, mlp_scale,
 ):
+    block = vm(cotangent.shape, BF)
+    rows_f, rows_b = vm((ROWS, D), F32), vm((ROWS, D), BF)
     tok_x = by_x(tokens)
     tok_c = by_core(tokens)
     cot, tok_own, par, be, wqkv, wp, we, wr, vis = call(
         prepare_kernel,
         (
-            vm(cotangent.shape, BF),
-            vm(cotangent.shape, BF),
+            block,
+            block,
             vm((16, D), F32),
             vm((8, FH), F32),
             vm((3, D, HALF), BF),
@@ -507,8 +548,7 @@
             vm(visible.shape, visible.dtype),
         ),
         [ANY] * 17,
-        [pltpu.SemaphoreType.DMA((20,))],
-        nbytes=int(9e6),
+        [pltpu.SemaphoreType.DMA((20,))]
     )(
         *map(
             stay,
@@ -522,119 +562,94 @@
     vis_x = by_x(vis)
     vis_c = by_core(vis)
     cot_c = by_core(cot)
-    block = vm(cotangent.shape, BF)
-    cot, tok_x = call(hold_kernel, (block, block), [VM] * 2 + [ANY] * 2, nbytes=int(20e6))(cot, tok_x, vis_x, par)
+    cot, tok_x = call(hold_kernel, (block, block), [VM] * 2 + [ANY] * 2)(cot, tok_x, vis_x, par)
     tok_d = by_core(tok_x)
     vis_d = by_core(vis_x)
     cot_x = by_x(cot)
-
-    tok, normed, qkv, mix_own, pos, probs = call(
+    tok, normed, qkv, mix_own, pos, probs, pos_mine, pos_theirs = call(
         first_kernel,
         (
-            vm((ROWS, D), BF),
-            vm((ROWS, D), BF),
+            rows_b,
+            rows_b,
             vm((3, ROWS, HALF), BF),
             vm((ROWS, HALF), BF),
             vm((8, SLOTS), F32),
             vm((9, 2 * PACK, PACK), F32),
+            vm((16, BAND), F32),
+            vm((16, BAND), F32),
         ),
         [VM] * 10,
-        [
-            pltpu.VMEM((IMGS, SLOTS, D), BF),
-            pltpu.VMEM((16, 128), F32),
-        ],
-        flops=int(1.5e9),
-        nbytes=int(6e6),
+        [pltpu.VMEM((IMGS, SLOTS, D), BF), pltpu.VMEM((16, 128), F32)],
     )(tok_own, tok_c, tok_x, tok_d, vis, vis_c, vis_x, vis_d, par, wqkv)
     mix_other = by_core(mix_own)
     cot_d = by_core(cot_x)
-    pick, pn = call(
-        pick_kernel, (vm((D, HALF), BF), vm((ROWS, HALF), BF)), [VM], flops=int(5e8), nbytes=int(2e6)
-    )(normed)
-    res, one, pre, gb2, n2, mix, act, gh, gn2, bt2, small2 = call(
-        second_kernel,
-        (
-            vm((ROWS, D), F32),
-            vm((ROWS, D), F32),
-            vm((ROWS, D), BF),
-            vm((ROWS, D), BF),
-            vm((ROWS, D), BF),
-            vm((ROWS, D), BF),
-            vm((ROWS, D), BF),
-            vm((ROWS, FH), BF),
-            vm((ROWS, D), BF),
-            vm((ROWS, D), BF),
-            vm((8, D), F32),
-        ),
+    pick, pick_p, pn = call(pick_kernel, (vm((D, HALF), BF), vm((D, 192), BF), vm((ROWS, HALF), BF)), [VM])(normed)
+    res, one, n2, mix, act, slope = call(
+        hidden_kernel,
+        (rows_f, rows_f, rows_b, rows_b, vm((ROWS, FH), BF), vm((ROWS, FH), F32)),
+        [VM] * 7 + [ANY],
+    )(mix_own, mix_other, tok, par, be, wp, we, pick)
+    pre, gb2, wr_send, wr_keep = call(
+        reduce_grad_kernel,
+        (rows_b, rows_b, vm((4, 96, D), BF), vm((4, 96, D), BF)),
+        [VM] * 7,
+        [pltpu.VMEM((IMGS, SLOTS, D), BF), pltpu.VMEM((ROWS, D), BF), pltpu.VMEM((D, D), F32)],
+    )(cot, cot_c, cot_x, cot_d, pos, par, act)
+    wr_y = by_y(wr_send)
+    half_b = vm((ROWS, HALF), BF)
+    gh, left, right = call(back_kernel, (vm((ROWS, FH), BF), half_b, half_b), [VM] * 4)(gb2, wr, slope, we)
+    gn2 = (left, by_core(left), right, by_core(right))
+    we_send, we_keep, tick = call(
+        expand_grad_kernel,
+        (vm((4, 48, FH), BF), vm((4, 48, FH), BF), TICK),
+        [VM] * 3,
+        [pltpu.VMEM((HALF, FH), F32)],
+    )(n2, gh, pick)
+    we_z = by_z(we_send, 1)
+    gres, gp, qp_send, qp_keep, tick = call(
+        attention_back_kernel,
+        (rows_f, vm((ROWS, QC), BF), vm((4, 48, QW), BF), vm((4, 48, QW), BF), TICK),
         [VM] * 13 + [ANY],
-        [
-            pltpu.VMEM((IMGS, SLOTS, D), BF),
-            pltpu.VMEM((ROWS, FH), BF),
-        ],
-        flops=int(5e9),
-        nbytes=int(15e6),
-    )(mix_own, mix_other, tok, cot, cot_c, cot_x, cot_d, pos, par, be, wp, we, wr, pick)
-    gn2_other = by_core(gn2)
-    wr_send, wr_keep, we_send, we_keep, eb = call(
-        mlp_grads_kernel,
-        (
-            vm((4, 96, D), BF),
-            vm((4, 96, D), BF),
-            vm((4, 48, FH), BF),
-            vm((4, 48, FH), BF),
-            vm((8, 48, SMALL), F32),
-        ),
-        [VM] * 5,
-        [pltpu.VMEM((D, D), F32), pltpu.VMEM((HALF, FH), F32), pltpu.VMEM((FH, 128), F32)],
-        flops=int(2e9),
-        nbytes=int(6e6),
-    )(n2, gh, act, gb2, pick)
-    wr_y = by_y(wr_send)
-    we_z = by_z(we_send, 1)
-    gres, gnp, qp_send, qp_keep, tick = call(
-        third_kernel,
-        (
-            vm((ROWS, D), F32),
-            vm((ROWS, D), BF),
-            vm((4, 48, QW), BF),
-            vm((4, 48, QW), BF),
-            TICK,
-        ),
-        [VM] * 16,
-        [
-            pltpu.VMEM((ROWS, QC), BF),
-            pltpu.VMEM((SMALL, D), F32),
-            pltpu.VMEM((HALF, QC), F32),
-        ],
-        flops=int(4e9),
-        nbytes=int(12e6),
-    )(gn2, gn2_other, res, one, pre, tok, qkv, probs, mix, pn, pick, small2, eb, wp, wqkv, par)
+        [pltpu.VMEM((HALF, QC), F32)],
+    )(*gn2, res, pre, qkv, probs, mix, pn, pick_p, wp, par, tick)
     qp_y = by_y(qp_send)
-    wr_keep, wr_send, we_keep, we_send, tick = fold_pair(wr_keep, wr_y, we_keep, we_z, tick)
+    gb_keep, gb_send, vec_send, vec_keep, tick = call(
+        vectors_kernel,
+        (vm((2, *tokens.shape), BF), vm((2, *tokens.shape), BF), vm((4, 48, SMALL), BF), vm((4, 48, SMALL), BF), TICK),
+        [VM] * 19 + [ANY],
+        [pltpu.VMEM((SMALL, D), F32), pltpu.VMEM((FH, SMALL), F32)],
+    )(*gn2, res, one, gres, gp, wqkv, act, wr, gb2, gh, pre, tok, pick, par, pos_mine, pos_theirs, tick)
+    vec_y = by_y(vec_send)
+    gb_other = by_core(gb_send)
+    we_half = (2, 48, FH)
+    wr_keep, wr_send, we_keep, we_send, tick = call(
+        fold_kernel,
+        (vm((2, 96, D), F32), vm((2, 96, D), BF), vm(we_half, F32), vm(we_half, BF), TICK),
+        [VM] * 4 + [ANY],
+    )(wr_keep, wr_y, we_keep, we_z, tick)
     wr_z = by_z(wr_send, 1)
     we_z = by_z(we_send, 2)
-    bt2_other = by_core(bt2)
-    gnp_other = by_core(gnp)
+    qp_half = (2, 48, QS)
+    qp_keep, qp_send, tick = call(
+        join_kernel, (vm(qp_half, F32), vm(qp_half, BF), TICK), [VM] * 4 + [ANY]
+    )(qp_keep, qp_y, vec_keep, vec_y, tick)
+    qp_z = by_z(qp_send, 1)
+    wr_keep, wr_send, we_keep, we_send, tick = call(
+        second_fold_kernel,
+        (vm((2, 96, D), F32), vm((2, 96, D), BF), vm((1, 48, FH), F32), vm((1, 48, FH), BF), TICK),
+        [VM] * 4 + [ANY],
+    )(wr_keep, wr_z, we_keep, we_z, tick)
+    wr_z = homeward(wr_send, 2)
+    we_y = by_y(we_send)
     layer_out, grad_tokens, tick = call(
         last_kernel,
-        (sds((IMGS, BAND, D), BF), sds((IMGS, BAND, D), BF), TICK),
-        [VM] * 9 + [ANY],
-        [pltpu.VMEM((SLOTS, D), F32)],
-        flops=int(1e9),
-        nbytes=int(8e6),
-    )(gnp, gnp_other, tok, gres, bt2, bt2_other, res, pos, par, tick)
-    own, s1, s2, s3, wr_keep, wr_send, we_keep, we_send = call(
-        stage_kernel,
-        (vm((48, QW), F32),) + (vm((48, QW), BF),) * 3
-        + (vm((2, 96, D), F32), vm((2, 96, D), BF), vm((1, 48, FH), F32), vm((1, 48, FH), BF)),
-        [VM] * 6 + [ANY],
-        nbytes=int(2e6),
-    )(qp_keep, qp_y, wr_keep, wr_z, we_keep, we_z, tick)
-    r1, r2, r3 = by_z(s1, 1), by_z(s2, 2), by_z(s3, 3)
-    homeward = [(d, d ^ 16) for d in range(32) if (d >> 4) != (d & 1)]
-    wr_z = lax.ppermute(wr_send, ("batch", "band"), homeward)
-    we_y = by_y(we_send)
-
+        (sds(tokens.shape, BF), sds(tokens.shape, BF), TICK),
+        [VM] * 7 + [ANY],
+    )(gb_keep, gb_other, tok_own, gres, res, pos_mine, par, tick)
+    qp_keep, qp_send, tick = call(
+        third_fold_kernel, (vm((1, 48, QS), F32), vm((1, 48, QS), BF), TICK), [VM] * 2 + [ANY]
+    )(qp_keep, qp_z, tick)
+    qp_z = by_z(qp_send, 2)
     qp_keep, qp_send, vec, proj, wr_keep, wr_send, we_keep, we_send = call(
         finish_kernel,
         (
@@ -647,18 +662,18 @@
             vm((24, FH), F32),
             vm((24, FH), F32),
         ),
-        [VM] * 8,
-        [pltpu.VMEM((48, QW), F32), pltpu.VMEM((48, FH), F32)],
-        nbytes=int(1e6),
-    )(own, r1, r2, r3, wr_keep, wr_z, we_keep, we_y)
+        [VM] * 6 + [ANY],
+        [pltpu.VMEM((48, QS), F32), pltpu.VMEM((48, FH), F32)],
+    )(qp_keep, qp_z, wr_keep, wr_z, we_keep, we_y, tick)
     vector = sds((24,), F32)
     grad_qkv, gg1, gb1, gqv, gbp, gas, gg2, gb2, gbr, gms, geb, grad_expand, grad_reduce = call(
         out_kernel,
-        (sds((24, 3 * D), F32), vector, vector, sds((2, 24), F32)) + (vector,) * 6
-        + (sds((96,), F32), sds((24, FF), F32), sds((96, D), F32)),
+        (
+            sds((24, 3 * D), F32), vector, vector, sds((2, 24), F32), vector, vector, vector, vector, vector, vector,
+            sds((96,), F32), sds((24, FF), F32), sds((96, D), F32),
+        ),
         [VM] * 7,
         [pltpu.VMEM((48, SMALL), F32)],
-        nbytes=int(1e6),
     )(qp_keep, vec, by_core(qp_send), we_keep, by_core(we_send), wr_keep, by_core(wr_send))
     return (
         layer_out, grad_tokens, gg1, gb1, grad_qkv, gqv, proj, gbp, gas, gg2, gb2, grad_expand, geb, grad_reduce,

time: 92.3 us -> 87.2 us (0.945)
  waiting for transfers between devices: 39.8 us -> 34.1 us
  Pallas kernels: 29.1 us -> 31 us
  starting transfers between devices: 22.4 us -> 21 us
    ppermute x6 -> x5, waiting for transfers between devices: 21.5 us -> 11.7 us  [by_z(): return lax.ppermute(value, 'batch', [(i, i ^ 2 * dz) for i in range(8)])]
    ppermute x3 -> x4, waiting for transfers between devices: 8.9 us -> 13.9 us  [by_y(): return lax.ppermute(value, 'batch', [(i, i ^ 1) for i in range(8)])]
    ppermute x6 -> x5, starting transfers between devices: 11 us -> 7.26 us  [by_z(): return lax.ppermute(value, 'batch', [(i, i ^ 2 * dz) for i in range(8)])]
    ppermute x3 -> x4, starting transfers between devices: 2.89 us -> 5.16 us  [by_y(): return lax.ppermute(value, 'batch', [(i, i ^ 1) for i in range(8)])]
    pallas_call x10 -> x15, Pallas kernels: 27.4 us -> 29.3 us  [the longest x1 6.39 us: packed_body(): call(attention_back_kernel, (rows_f, vm((ROWS, QC), BF), vm((4, 48, QW),...]
    ppermute x13, waiting for transfers between devices: 3.34 us -> 1.5 us  [by_core(): return lax.ppermute(value, 'band', [(i, i ^ 1) for i in range(4)])]
    ppermute x3, waiting for transfers between devices: 5.99 us -> 7.07 us  [by_x(): return lax.ppermute(value, 'band', [(i, i ^ 2) for i in range(4)])]
  transfers between devices with their start and end apart: 26 -> 26, of which waited for: 12 -> 10; matrix products, arithmetic and copies ran while one was open for 0% -> 0% of each run, Pallas kernels for 23% -> 29%
where the time goes in v3:
time: 87.2 us; the launch traced here: 87 us
  waiting for transfers between devices  34.1 us (39%)
  Pallas kernels  31 us (36%)
  starting transfers between devices  21 us (24%)
  between operations  0.92 us (1%)
    ppermute x4, waiting for transfers between devices, by_y(): return lax.ppermute(value, 'batch', [(i, i ^ 1) for i in range(8)])  13.9 us
    ppermute x5, waiting for transfers between devices, by_z(): return lax.ppermute(value, 'batch', [(i, i ^ 2 * dz) for i in range(8)])  11.7 us
    ppermute x5, starting transfers between devices, by_z(): return lax.ppermute(value, 'batch', [(i, i ^ 2 * dz) for i in range(8)])  7.26 us
    ppermute x3, waiting for transfers between devices, by_x(): return lax.ppermute(value, 'band', [(i, i ^ 2) for i in range(4)])  7.07 us
    pallas_call x1, Pallas kernels, packed_body(): call(attention_back_kernel, (rows_f, vm((ROWS, QC), BF), vm((4, 48, QW),...  6.39 us
    ppermute x4, starting transfers between devices, by_y(): return lax.ppermute(value, 'batch', [(i, i ^ 1) for i in range(8)])  5.16 us
    ppermute x3, starting transfers between devices, by_x(): return lax.ppermute(value, 'band', [(i, i ^ 2) for i in range(4)])  4.76 us
    pallas_call x1, Pallas kernels, packed_body(): call(vectors_kernel, (vm((2, *tokens.shape), BF), vm((2, *tokens.shape),...  4.35 us
  transfers between devices with their start and end apart: 26, of which 10 were waited for; matrix products, arithmetic and copies ran while one was open for 0% of the time, Pallas kernels for 29%

profile of v3, /device:TPU:0, one launch (start us, length us, event | category | flops | bytes accessed | tf_op | source)
XLA Modules:
  0.0 87.0 jit_solution(2652225767580274984)
XLA Ops:
  0.7 3.0 %collective-permute-start = (bf16[3,64,768]{2,1,0:T(8,128)(2,1)}, bf16[3,64,768]{2,1,0:T(8,128)(2,1)S(1)}, u32[]{:S(2)}, u32[]{:S(2)}) collective-permute-start(bf16[3,64,768]{2,1,0:T(8,128)(2,1)} %tok.1), channel_id=1, source_target_pairs={{0,2},{1,3},{2,0},{3,1},{4,6},{5,7},{6,4},{7,5},{8,10},{9,11},{10,... | collective-permute-start | bytes 884744 | tf_op jit(solution)/shard_map/ppermute | solution.py:513
  3.7 3.7 %shard_map.288 = (bf16[3,64,768]{2,1,0:T(8,128)(2,1)S(1)}, bf16[3,64,768]{2,1,0:T(8,128)(2,1)S(1)}, f32[16,768]{1,0:T(8,128)S(1)}, f32[8,1536]{1,0:T(8,128)S(1)}...) custom-call(bf16[3,64,768]{2,1,0:T(8,128)(2,1)} %cot.1, ...), custom_call_target="tpu_custom_call" | custom-call | bytes 9000000 | tf_op jit(solution)/shard_map/pallas_call | solution.py:537
  7.4 0.1 collective-permute-start.1
  7.5 0.1 collective-permute-start.5
  7.5 3.5 %collective-permute-done.1.after_a.v2 = s32[3,64]{1,0:T(4,128)S(1)} collective-permute-done((s32[3,64]{1,0:T(4,128)S(1)}, s32[3,64]{1,0:T(4,128)S(1)}, u32[]{:S(2)}, u32[]{:S(2)}) %collective-permute-start.1) | collective-permute-done | bytes 800 | tf_op jit(solution)/shard_map/ppermute | solution.py:513
  11.1 0.1 collective-permute-start.6
  11.1 0.5 collective-permute-start.7
  11.6 0.1 collective-permute-start.8
  11.7 1.7 %collective-permute-start.3 = (bf16[3,64,768]{2,1,0:T(8,128)(2,1)S(1)}, bf16[3,64,768]{2,1,0:T(8,128)(2,1)S(1)}, u32[]{:S(2)}, u32[]{:S(2)}) collective-permute-start(bf16[3,64,768]{2,1,0:T(8,128)(2,1)S(1)} %get-tuple-element.107.c0), channel_id=1, source_target_pairs={{0,2},{1,3},{2,0},{3,1},{4,6},{5,7},{6,4},{7,5},{8,10},{9,11},{10,... | collective-permute-start | bytes 884744 | tf_op jit(solution)/shard_map/ppermute | solution.py:513
  13.4 3.5 %shard_map.290 = (bf16[432,768]{1,0:T(8,128)(2,1)S(1)}, bf16[432,768]{1,0:T(8,128)(2,1)S(1)}, bf16[3,432,384]{2,1,0:T(8,128)(2,1)S(1)}, bf16[432,384]{1,0:T(8,12...) custom-call(bf16[3,64,768]{2,1,0:T(8,128)(2,1)S(1)} %get-tuple-eleme, ...), custom_call_target="tpu_custom_call" | custom-call | flops 1500000000 | bytes 6000000 | tf_op jit(solution)/shard_map/pallas_call | solution.py:569
  16.9 0.2 collective-permute-start.9
  17.1 0.3 collective-permute-start.2
  17.5 3.6 %collective-permute-done.3.c2 = bf16[3,64,768]{2,1,0:T(8,128)(2,1)S(1)} collective-permute-done((bf16[3,64,768]{2,1,0:T(8,128)(2,1)S(1)}, bf16[3,64,768]{2,1,0:T(8,128)(2,1)S(1)}, u32[]{:S(2)}, u32[]{:S(2)}) %collective-permute-start.3) | collective-permute-done | bytes 294944 | tf_op jit(solution)/shard_map/ppermute | solution.py:513
  21.1 0.6 shard_map.291
  21.7 2.9 %shard_map.292 = (f32[432,768]{1,0:T(8,128)S(1)}, f32[432,768]{1,0:T(8,128)S(1)}, bf16[432,768]{1,0:T(8,128)(2,1)S(1)}, bf16[432,768]{1,0:T(8,128)(2,1)S(1)}, bf...) custom-call(bf16[432,384]{1,0:T(8,128)(2,1)S(1)} %get-tuple-element.112.mix_a, ...), custom_call_target="tpu_custom_call" | custom-call | flops 3000000000 | bytes 9000000 | tf_op jit(solution)/shard_map/pallas_call | solution.py:587
  24.6 1.7 %shard_map.293 = (bf16[432,768]{1,0:T(8,128)(2,1)S(1)}, bf16[432,768]{1,0:T(8,128)(2,1)S(1)}, bf16[4,96,768]{2,1,0:T(8,128)(2,1)S(1)}, bf16[4,96,768]{2,1,0:T(8,128)(2,1)S(1)}) custom-call(bf16[3,64,768]{2,1,0:T(8,128)(2,1)S(1)} %get-tuple-element.107.c0, bf16[3,64,768]{2,1,0:T(8,128)(2,1)S(1)} %collective-permute-done.2.c1, ...), custom_call_target="tpu_custom_call" | custom-call | flops 1000000000 | bytes 4000000 | tf_op jit(solution)/shard_map/pallas_call | solution.py:592
  26.3 2.4 %shard_map.294 = (bf16[432,1536]{1,0:T(8,128)(2,1)S(1)}, bf16[432,384]{1,0:T(8,128)(2,1)S(1)}, bf16[432,384]{1,0:T(8,128)(2,1)S(1)}) custom-call(bf16[432,768]{1,0:T(8,128)(2,1)S(1)} %get-tuple-element.120.gb2, bf16[1536,768]{1,0:T(8,128)(2,1)S(1)} %get-tuple-element.121.wr, f32[432,1536]{1,0:T(8,128)S(1)} %get-tuple-element.122.slope, ...), custom_call_target="tpu_custom_call" | custom-call | flops 2000000000 | bytes 6000000 | tf_op jit(solution)/shard_map/pallas_call | solution.py:600
  28.8 0.6 collective-permute-start.10
  29.3 0.1 collective-permute-start.11
  29.4 1.3 %shard_map.295 = (bf16[4,48,1536]{2,1,0:T(8,128)(2,1)S(1)}, bf16[4,48,1536]{2,1,0:T(8,128)(2,1)S(1)}, f32[8,128]{1,0:T(8,128)S(1)}) custom-call(bf16[432,768]{1,0:T(8,128)(2,1)S(1)} %get-tuple-element.133.n2, bf16[432,1536]{1,0:T(8,128)(2,1)S(1)} %get-tuple-element.134.gh, bf16[768,384]{1,0:T(8,128)(2,1)S(1)} %get-tuple-element.118.after.pick), custom_call_target="tpu_custom_call" | custom-call | flops 1000000000 | bytes 4000000 | tf_op jit(solution)/shard_map/pallas_call | solution.py:602
  30.6 1.8 %collective-permute-start.14 = (bf16[4,48,1536]{2,1,0:T(8,128)(2,1)S(1)}, bf16[4,48,1536]{2,1,0:T(8,128)(2,1)S(1)}, u32[]{:S(2)}, u32[]{:S(2)}) collective-permute-start(bf16[4,48,1536]{2,1,0:T(8,128)(2,1)S(1)} %get-tuple-element.146), channel_id=1, source_target_pairs={{0,8},{4,12},{8,0},{12,4},{16,24},{20,28},{24,16},{28,20},{1,9},{5... | collective-permute-start | bytes 1769480 | tf_op jit(solution)/shard_map/ppermute | solution.py:521
  32.5 1.6 %collective-permute-start.13 = (bf16[4,96,768]{2,1,0:T(8,128)(2,1)S(1)}, bf16[4,96,768]{2,1,0:T(8,128)(2,1)S(1)}, u32[]{:S(2)}, u32[]{:S(2)}) collective-permute-start(bf16[4,96,768]{2,1,0:T(8,128)(2,1)S(1)} %get-tuple-element.144), channel_id=1, source_target_pairs={{0,4},{4,0},{8,12},{12,8},{16,20},{20,16},{24,28},{28,24},{1,5},{5... | collective-permute-start | bytes 1769480 | tf_op jit(solution)/shard_map/ppermute | solution.py:517
  34.0 6.4 %shard_map.296 = (f32[432,768]{1,0:T(8,128)S(1)}, bf16[432,1152]{1,0:T(8,128)(2,1)S(1)}, bf16[4,48,1536]{2,1,0:T(8,128)(2,1)S(1)}, bf16[4,48,1536]{2,1,0:T(8,128)(2,1)S(1)}, f32[8,128]{1,0:T(8,128)S(1)}) custom-call(bf16[432,384]{1,0:T(8,128)(2,1)S(1)} %get-tuple-element.123.l_a, bf16[432,384]{1,0:T(8,128)(2,1)S(1)} %collective-permute-done.10.l_b, ...), custom_call_target="tpu_custom_call" | custom-call | flops 4000000000 | bytes 12000000 | tf_op jit(solution)/shard_map/pallas_call | solution.py:609
  40.4 0.5 collective-permute-start.17
  40.9 4.3 %shard_map.297 = (bf16[2,3,64,768]{3,2,1,0:T(8,128)(2,1)S(1)}, bf16[2,3,64,768]{3,2,1,0:T(8,128)(2,1)S(1)}, bf16[4,48,128]{2,1,0:T(8,128)(2,1)S(1)}, bf16[4,48,128]{2,1,0:T(8,128)(2,1)S(1)}, f32[8,128]{1,0:T(8,128)S(1)}) custom-call(bf16[432,384]{1,0:T(8,128)(2,1)S(1)} %get-tuple-element.123.l_a, bf16[432,384]{1,0:T(8,128)(2,1)S(1)} %collective-permute-done.10.l_b, ...), custom_call_target="tpu_custom_call" | custom-call | flops 2000000000 | bytes 8000000 | tf_op jit(solution)/shard_map/pallas_call | solution.py:616
  45.3 0.1 collective-permute-start.12
  45.4 1.0 %collective-permute-done.14.we_arrived = bf16[4,48,1536]{2,1,0:T(8,128)(2,1)S(1)} collective-permute-done((bf16[4,48,1536]{2,1,0:T(8,128)(2,1)S(1)}, bf16[4,48,1536]{2,1,0:T(8,128)(2,1)S(1)}, u32[]{:S(2)}, u32[]{:S(2)}) %collective-permute-start.14) | collective-permute-done | bytes 589856 | tf_op jit(solution)/shard_map/ppermute | solution.py:521
  46.4 2.2 %collective-permute-done.13.arrived = bf16[4,96,768]{2,1,0:T(8,128)(2,1)S(1)} collective-permute-done((bf16[4,96,768]{2,1,0:T(8,128)(2,1)S(1)}, bf16[4,96,768]{2,1,0:T(8,128)(2,1)S(1)}, u32[]{:S(2)}, u32[]{:S(2)}) %collective-permute-start.13) | collective-permute-done | bytes 589856 | tf_op jit(solution)/shard_map/ppermute | solution.py:517
  48.6 0.3 shard_map.298
  48.9 0.3 collective-permute-start.15
  49.2 2.8 %collective-permute-start.16 = (bf16[2,48,1536]{2,1,0:T(8,128)(2,1)S(1)}, bf16[2,48,1536]{2,1,0:T(8,128)(2,1)S(1)}, u32[]{:S(2)}, u32[]{:S(2)}) collective-permute-start(bf16[2,48,1536]{2,1,0:T(8,128)(2,1)S(1)} %get-tuple-element.151), channel_id=1, source_target_pairs={{0,16},{4,20},{8,24},{12,28},{16,0},{20,4},{24,8},{28,12},{1,17},{... | collective-permute-start | bytes 884744 | tf_op jit(solution)/shard_map/ppermute | solution.py:521
  52.0 1.5 %collective-permute-start.18 = (bf16[4,48,128]{2,1,0:T(8,128)(2,1)S(1)}, bf16[4,48,128]{2,1,0:T(8,128)(2,1)S(1)}, u32[]{:S(2)}, u32[]{:S(2)}) collective-permute-start(bf16[4,48,128]{2,1,0:T(8,128)(2,1)S(1)} %get-tuple-element.155), channel_id=1, source_target_pairs={{0,4},{4,0},{8,12},{12,8},{16,20},{20,16},{24,28},{28,24},{1,5},{5... | collective-permute-start | bytes 147464 | tf_op jit(solution)/shard_map/ppermute | solution.py:517
  53.5 8.0 %collective-permute-done.18.vec_arrived = bf16[4,48,128]{2,1,0:T(8,128)(2,1)S(1)} collective-permute-done((bf16[4,48,128]{2,1,0:T(8,128)(2,1)S(1)}, bf16[4,48,128]{2,1,0:T(8,128)(2,1)S(1)}, u32[]{:S(2)}, u32[]{:S(2)}) %collective-permute-start.18) | collective-permute-done | bytes 49184 | tf_op jit(solution)/shard_map/ppermute | solution.py:517
  61.5 0.1 shard_map.299
  61.7 0.4 collective-permute-start.19
  62.1 0.6 collective-permute-done.15.arrived
  62.7 0.2 shard_map.300
  62.9 1.3 %collective-permute-start.21 = (bf16[2,96,768]{2,1,0:T(8,128)(2,1)S(1)}, bf16[2,96,768]{2,1,0:T(8,128)(2,1)S(1)}, u32[]{:S(2)}, u32[]{:S(2)}) collective-permute-start(bf16[2,96,768]{2,1,0:T(8,128)(2,1)S(1)} %get-tuple-element.167), channel_id=1, source_target_pairs={{1,17},{3,19},{5,21},{7,23},{9,25},{11,27},{13,29},{15,31},{16,0},... | collective-permute-start | bytes 884744 | tf_op jit(solution)/shard_map/ppermute | solution.py:526
  64.2 1.8 %shard_map.301 = (bf16[3,64,768]{2,1,0:T(8,128)(2,1)}, bf16[3,64,768]{2,1,0:T(8,128)(2,1)}, f32[8,128]{1,0:T(8,128)S(1)}) custom-call(bf16[2,3,64,768]{3,2,1,0:T(8,128)(2,1)S(1)} %get-tuple-element.141.gb_a, bf16[2,3,64,768]{3,2,1,0:T(8,128)(2,1)S(1)} %collective-permute-done.12.gb_b, bf16[3,64,768]{2,1,0:T(8,128)(2,1)S(1)} %get-tuple-element.108.t0.tok, ...), custom_call_target="tpu_custom_call" | custom-call | flops 1000000000 | bytes 8000000 | tf_op jit(solution)/shard_map/pallas_call | solution.py:644
  66.0 7.6 %collective-permute-done.19.arrived = bf16[2,48,1664]{2,1,0:T(8,128)(2,1)S(1)} collective-permute-done((bf16[2,48,1664]{2,1,0:T(8,128)(2,1)S(1)}, bf16[2,48,1664]{2,1,0:T(8,128)(2,1)S(1)}, u32[]{:S(2)}, u32[]{:S(2)}) %collective-permute-start.19) | collective-permute-done | bytes 319520 | tf_op jit(solution)/shard_map/ppermute | solution.py:521
  73.7 1.9 %collective-permute-start.20 = (bf16[1,48,1664]{2,1,0:T(8,128)(2,1)S(1)}, bf16[1,48,1664]{2,1,0:T(8,128)(2,1)S(1)}, u32[]{:S(2)}, u32[]{:S(2)}) collective-permute-start(bf16[1,48,1664]{2,1,0:T(8,128)(2,1)S(1)} %get-tuple-element.165), channel_id=1, source_target_pairs={{0,16},{4,20},{8,24},{12,28},{16,0},{20,4},{24,8},{28,12},{1,17},{... | collective-permute-start | bytes 479240 | tf_op jit(solution)/shard_map/ppermute | solution.py:521
  75.7 1.6 %collective-permute-start.22 = (bf16[1,48,1536]{2,1,0:T(8,128)(2,1)S(1)}, bf16[1,48,1536]{2,1,0:T(8,128)(2,1)S(1)}, u32[]{:S(2)}, u32[]{:S(2)}) collective-permute-start(bf16[1,48,1536]{2,1,0:T(8,128)(2,1)S(1)} %get-tuple-element.169), channel_id=1, source_target_pairs={{0,4},{4,0},{8,12},{12,8},{16,20},{20,16},{24,28},{28,24},{1,5},{5... | collective-permute-start | bytes 442376 | tf_op jit(solution)/shard_map/ppermute | solution.py:517
  77.2 3.6 %collective-permute-done.22.we_a = bf16[1,48,1536]{2,1,0:T(8,128)(2,1)S(1)} collective-permute-done((bf16[1,48,1536]{2,1,0:T(8,128)(2,1)S(1)}, bf16[1,48,1536]{2,1,0:T(8,128)(2,1)S(1)}, u32[]{:S(2)}, u32[]{:S(2)}) %collective-permute-start.22) | collective-permute-done | bytes 147488 | tf_op jit(solution)/shard_map/ppermute | solution.py:517
  80.8 2.4 %collective-permute-done.20.qp_a = bf16[1,48,1664]{2,1,0:T(8,128)(2,1)S(1)} collective-permute-done((bf16[1,48,1664]{2,1,0:T(8,128)(2,1)S(1)}, bf16[1,48,1664]{2,1,0:T(8,128)(2,1)S(1)}, u32[]{:S(2)}, u32[]{:S(2)}) %collective-permute-start.20) | collective-permute-done | bytes 159776 | tf_op jit(solution)/shard_map/ppermute | solution.py:521
  83.2 0.8 shard_map.303
  84.0 0.5 collective-permute-start.24
  84.5 1.5 %collective-permute-done.23.arrived = f32[24,1408]{1,0:T(8,128)S(1)} collective-permute-done((f32[24,1408]{1,0:T(8,128)S(1)}, f32[24,1408]{1,0:T(8,128)S(1)}, u32[]{:S(2)}, u32[]{:S(2)}) %collective-permute-start.23) | collective-permute-done | bytes 135200 | tf_op jit(solution)/shard_map/ppermute | solution.py:509
  86.0 0.9 %shard_map.304 = (f32[24,2304]{1,0:T(8,128)}, f32[24]{0:T(128)}, f32[24]{0:T(128)}, f32[2,24]{1,0:T(2,128)}, f32[24]{0:T(128)}, /*index=5*/f32[24]{0:T(128)}, f3...) custom-call(f32[24,1152]{1,0:T(8,128)S(1)} %get-tuple-element.171.ke, ...), custom_call_target="tpu_custom_call" | custom-call | bytes 1000000 | tf_op jit(solution)/shard_map/pallas_call | solution.py:669
  (23 shorter events, 0.1 us)
Async XLA Ops:
  0.6 6.8 %copy-start = (bf16[3,64,768]{2,1,0:T(8,128)(2,1)S(1)}, bf16[3,64,768]{2,1,0:T(8,128)(2,1)}, u32[]{:S(2)}) copy-start(bf16[3,64,768]{2,1,0:T(8,128)(2,1)} %tok.1) | copy-start | bytes 884740
  0.7 10.3 %collective-permute-start = (bf16[3,64,768]{2,1,0:T(8,128)(2,1)}, bf16[3,64,768]{2,1,0:T(8,128)(2,1)S(1)}, u32[]{:S(2)}, u32[]{:S(2)}) collective-permute-start(bf16[3,64,768]{2,1,0:T(8,128)(2,1)} %tok.1), channel_id=1, source_target_pairs={{0,2},{1,3},{2,0},{3,1},{4,6},{5,7},{6,4},{7,5},{8,10},{9,11},{10,... | collective-permute-start | bytes 884744 | tf_op jit(solution)/shard_map/ppermute | solution.py:513
  7.4 3.7 %collective-permute-start.1 = (s32[3,64]{1,0:T(4,128)S(1)}, s32[3,64]{1,0:T(4,128)S(1)}, u32[]{:S(2)}, u32[]{:S(2)}) collective-permute-start(s32[3,64]{1,0:T(4,128)S(1)} %get-tuple-element.105.v0), channel_id=1, source_target_pairs={{0,2},{1,3},{2,0},{3,1},{4,6},{5,7},{6,4},{7,5},{8,10},{9,11},{10,... | collective-permute-start | bytes 2312 | tf_op jit(solution)/shard_map/ppermute | solution.py:513
  7.5 5.9 %collective-permute-start.5 = (bf16[3,64,768]{2,1,0:T(8,128)(2,1)S(1)}, bf16[3,64,768]{2,1,0:T(8,128)(2,1)S(1)}, u32[]{:S(2)}, u32[]{:S(2)}) collective-permute-start(bf16[3,64,768]{2,1,0:T(8,128)(2,1)S(1)} %copy-done), channel_id=1, source_target_pairs={{0,1},{1,0},{2,3},{3,2},{4,5},{5,4},{6,7},{7,6},{8,9},{9,8},{10,11... | collective-permute-start | bytes 884744 | tf_op jit(solution)/shard_map/ppermute | solution.py:509
  11.1 2.3 %collective-permute-start.6 = (bf16[3,64,768]{2,1,0:T(8,128)(2,1)S(1)}, bf16[3,64,768]{2,1,0:T(8,128)(2,1)S(1)}, u32[]{:S(2)}, u32[]{:S(2)}) collective-permute-start(bf16[3,64,768]{2,1,0:T(8,128)(2,1)S(1)} %get-tuple-element.109.t2), channel_id=1, source_target_pairs={{0,1},{1,0},{2,3},{3,2},{4,5},{5,4},{6,7},{7,6},{8,9},{9,8},{10,11... | collective-permute-start | bytes 884744 | tf_op jit(solution)/shard_map/ppermute | solution.py:509
  11.1 2.2 %collective-permute-start.7 = (s32[3,64]{1,0:T(4,128)S(1)}, s32[3,64]{1,0:T(4,128)S(1)}, u32[]{:S(2)}, u32[]{:S(2)}) collective-permute-start(s32[3,64]{1,0:T(4,128)S(1)} %get-tuple-element.105.v0), channel_id=1, source_target_pairs={{0,1},{1,0},{2,3},{3,2},{4,5},{5,4},{6,7},{7,6},{8,9},{9,8},{10,11... | collective-permute-start | bytes 2312 | tf_op jit(solution)/shard_map/ppermute | solution.py:509
  11.6 1.7 %collective-permute-start.8 = (s32[3,64]{1,0:T(4,128)S(1)}, s32[3,64]{1,0:T(4,128)S(1)}, u32[]{:S(2)}, u32[]{:S(2)}) collective-permute-start(s32[3,64]{1,0:T(4,128)S(1)} %collective-permute-done.1.after_a.v2), channel_id=1, source_target_pairs={{0,1},{1,0},{2,3},{3,2},{4,5},{5,4},{6,7},{7,6},{8,9},{9,8},{10,11... | collective-permute-start | bytes 2312 | tf_op jit(solution)/shard_map/ppermute | solution.py:509
  11.7 9.4 %collective-permute-start.3 = (bf16[3,64,768]{2,1,0:T(8,128)(2,1)S(1)}, bf16[3,64,768]{2,1,0:T(8,128)(2,1)S(1)}, u32[]{:S(2)}, u32[]{:S(2)}) collective-permute-start(bf16[3,64,768]{2,1,0:T(8,128)(2,1)S(1)} %get-tuple-element.107.c0), channel_id=1, source_target_pairs={{0,2},{1,3},{2,0},{3,1},{4,6},{5,7},{6,4},{7,5},{8,10},{9,11},{10,... | collective-permute-start | bytes 884744 | tf_op jit(solution)/shard_map/ppermute | solution.py:513
  16.9 4.7 %collective-permute-start.9 = (bf16[432,384]{1,0:T(8,128)(2,1)S(1)}, bf16[432,384]{1,0:T(8,128)(2,1)S(1)}, u32[]{:S(2)}, u32[]{:S(2)}) collective-permute-start(bf16[432,384]{1,0:T(8,128)(2,1)S(1)} %get-tuple-element.112.mix_a), channel_id=1, source_target_pairs={{0,1},{1,0},{2,3},{3,2},{4,5},{5,4},{6,7},{7,6},{8,9},{9,8},{10,11... | collective-permute-start | bytes 995336 | tf_op jit(solution)/shard_map/ppermute | solution.py:509
  17.1 7.4 %collective-permute-start.2 = (bf16[3,64,768]{2,1,0:T(8,128)(2,1)S(1)}, bf16[3,64,768]{2,1,0:T(8,128)(2,1)S(1)}, u32[]{:S(2)}, u32[]{:S(2)}) collective-permute-start(bf16[3,64,768]{2,1,0:T(8,128)(2,1)S(1)} %get-tuple-element.104.cot), channel_id=1, source_target_pairs={{0,1},{1,0},{2,3},{3,2},{4,5},{5,4},{6,7},{7,6},{8,9},{9,8},{10,11... | collective-permute-start | bytes 884744 | tf_op jit(solution)/shard_map/ppermute | solution.py:509
  21.1 3.5 %collective-permute-start.4 = (bf16[3,64,768]{2,1,0:T(8,128)(2,1)S(1)}, bf16[3,64,768]{2,1,0:T(8,128)(2,1)S(1)}, u32[]{:S(2)}, u32[]{:S(2)}) collective-permute-start(bf16[3,64,768]{2,1,0:T(8,128)(2,1)S(1)} %collective-permute-done.3.c2), channel_id=1, source_target_pairs={{0,1},{1,0},{2,3},{3,2},{4,5},{5,4},{6,7},{7,6},{8,9},{9,8},{10,11... | collective-permute-start | bytes 884744 | tf_op jit(solution)/shard_map/ppermute | solution.py:509
  28.8 5.3 %collective-permute-start.10 = (bf16[432,384]{1,0:T(8,128)(2,1)S(1)}, bf16[432,384]{1,0:T(8,128)(2,1)S(1)}, u32[]{:S(2)}, u32[]{:S(2)}) collective-permute-start(bf16[432,384]{1,0:T(8,128)(2,1)S(1)} %get-tuple-element.123.l_a), channel_id=1, source_target_pairs={{0,1},{1,0},{2,3},{3,2},{4,5},{5,4},{6,7},{7,6},{8,9},{9,8},{10,11... | collective-permute-start | bytes 995336 | tf_op jit(solution)/shard_map/ppermute | solution.py:509
  29.3 4.7 %collective-permute-start.11 = (bf16[432,384]{1,0:T(8,128)(2,1)S(1)}, bf16[432,384]{1,0:T(8,128)(2,1)S(1)}, u32[]{:S(2)}, u32[]{:S(2)}) collective-permute-start(bf16[432,384]{1,0:T(8,128)(2,1)S(1)} %get-tuple-element.124.r_a), channel_id=1, source_target_pairs={{0,1},{1,0},{2,3},{3,2},{4,5},{5,4},{6,7},{7,6},{8,9},{9,8},{10,11... | collective-permute-start | bytes 995336 | tf_op jit(solution)/shard_map/ppermute | solution.py:509
  30.6 15.7 %collective-permute-start.14 = (bf16[4,48,1536]{2,1,0:T(8,128)(2,1)S(1)}, bf16[4,48,1536]{2,1,0:T(8,128)(2,1)S(1)}, u32[]{:S(2)}, u32[]{:S(2)}) collective-permute-start(bf16[4,48,1536]{2,1,0:T(8,128)(2,1)S(1)} %get-tuple-element.146), channel_id=1, source_target_pairs={{0,8},{4,12},{8,0},{12,4},{16,24},{20,28},{24,16},{28,20},{1,9},{5... | collective-permute-start | bytes 1769480 | tf_op jit(solution)/shard_map/ppermute | solution.py:521
  32.5 16.2 %collective-permute-start.13 = (bf16[4,96,768]{2,1,0:T(8,128)(2,1)S(1)}, bf16[4,96,768]{2,1,0:T(8,128)(2,1)S(1)}, u32[]{:S(2)}, u32[]{:S(2)}) collective-permute-start(bf16[4,96,768]{2,1,0:T(8,128)(2,1)S(1)} %get-tuple-element.144), channel_id=1, source_target_pairs={{0,4},{4,0},{8,12},{12,8},{16,20},{20,16},{24,28},{28,24},{1,5},{5... | collective-permute-start | bytes 1769480 | tf_op jit(solution)/shard_map/ppermute | solution.py:517
  40.4 21.1 %collective-permute-start.17 = (bf16[4,48,1536]{2,1,0:T(8,128)(2,1)S(1)}, bf16[4,48,1536]{2,1,0:T(8,128)(2,1)S(1)}, u32[]{:S(2)}, u32[]{:S(2)}) collective-permute-start(bf16[4,48,1536]{2,1,0:T(8,128)(2,1)S(1)} %get-tuple-element.153), channel_id=1, source_target_pairs={{0,4},{4,0},{8,12},{12,8},{16,20},{20,16},{24,28},{28,24},{1,5},{5... | collective-permute-start | bytes 1769480 | tf_op jit(solution)/shard_map/ppermute | solution.py:517
  45.3 18.9 %collective-permute-start.12 = (bf16[2,3,64,768]{3,2,1,0:T(8,128)(2,1)S(1)}, bf16[2,3,64,768]{3,2,1,0:T(8,128)(2,1)S(1)}, u32[]{:S(2)}, u32[]{:S(2)}) collective-permute-start(bf16[2,3,64,768]{3,2,1,0:T(8,128)(2,1)S(1)} %get-tuple-element.142), channel_id=1, source_target_pairs={{0,1},{1,0},{2,3},{3,2},{4,5},{5,4},{6,7},{7,6},{8,9},{9,8},{10,11... | collective-permute-start | bytes 1769480 | tf_op jit(solution)/shard_map/ppermute | solution.py:509
  48.9 13.8 %collective-permute-start.15 = (bf16[2,96,768]{2,1,0:T(8,128)(2,1)S(1)}, bf16[2,96,768]{2,1,0:T(8,128)(2,1)S(1)}, u32[]{:S(2)}, u32[]{:S(2)}) collective-permute-start(bf16[2,96,768]{2,1,0:T(8,128)(2,1)S(1)} %get-tuple-element.149), channel_id=1, source_target_pairs={{0,8},{4,12},{8,0},{12,4},{16,24},{20,28},{24,16},{28,20},{1,9},{5... | collective-permute-start | bytes 884744 | tf_op jit(solution)/shard_map/ppermute | solution.py:521
  49.2 13.5 %collective-permute-start.16 = (bf16[2,48,1536]{2,1,0:T(8,128)(2,1)S(1)}, bf16[2,48,1536]{2,1,0:T(8,128)(2,1)S(1)}, u32[]{:S(2)}, u32[]{:S(2)}) collective-permute-start(bf16[2,48,1536]{2,1,0:T(8,128)(2,1)S(1)} %get-tuple-element.151), channel_id=1, source_target_pairs={{0,16},{4,20},{8,24},{12,28},{16,0},{20,4},{24,8},{28,12},{1,17},{... | collective-permute-start | bytes 884744 | tf_op jit(solution)/shard_map/ppermute | solution.py:521
  52.0 9.5 %collective-permute-start.18 = (bf16[4,48,128]{2,1,0:T(8,128)(2,1)S(1)}, bf16[4,48,128]{2,1,0:T(8,128)(2,1)S(1)}, u32[]{:S(2)}, u32[]{:S(2)}) collective-permute-start(bf16[4,48,128]{2,1,0:T(8,128)(2,1)S(1)} %get-tuple-element.155), channel_id=1, source_target_pairs={{0,4},{4,0},{8,12},{12,8},{16,20},{20,16},{24,28},{28,24},{1,5},{5... | collective-permute-start | bytes 147464 | tf_op jit(solution)/shard_map/ppermute | solution.py:517
  61.7 12.0 %collective-permute-start.19 = (bf16[2,48,1664]{2,1,0:T(8,128)(2,1)S(1)}, bf16[2,48,1664]{2,1,0:T(8,128)(2,1)S(1)}, u32[]{:S(2)}, u32[]{:S(2)}) collective-permute-start(bf16[2,48,1664]{2,1,0:T(8,128)(2,1)S(1)} %get-tuple-element.162), channel_id=1, source_target_pairs={{0,8},{4,12},{8,0},{12,4},{16,24},{20,28},{24,16},{28,20},{1,9},{5... | collective-permute-start | bytes 958472 | tf_op jit(solution)/shard_map/ppermute | solution.py:521
  62.9 17.9 %collective-permute-start.21 = (bf16[2,96,768]{2,1,0:T(8,128)(2,1)S(1)}, bf16[2,96,768]{2,1,0:T(8,128)(2,1)S(1)}, u32[]{:S(2)}, u32[]{:S(2)}) collective-permute-start(bf16[2,96,768]{2,1,0:T(8,128)(2,1)S(1)} %get-tuple-element.167), channel_id=1, source_target_pairs={{1,17},{3,19},{5,21},{7,23},{9,25},{11,27},{13,29},{15,31},{16,0},... | collective-permute-start | bytes 884744 | tf_op jit(solution)/shard_map/ppermute | solution.py:526
  73.7 9.5 %collective-permute-start.20 = (bf16[1,48,1664]{2,1,0:T(8,128)(2,1)S(1)}, bf16[1,48,1664]{2,1,0:T(8,128)(2,1)S(1)}, u32[]{:S(2)}, u32[]{:S(2)}) collective-permute-start(bf16[1,48,1664]{2,1,0:T(8,128)(2,1)S(1)} %get-tuple-element.165), channel_id=1, source_target_pairs={{0,16},{4,20},{8,24},{12,28},{16,0},{20,4},{24,8},{28,12},{1,17},{... | collective-permute-start | bytes 479240 | tf_op jit(solution)/shard_map/ppermute | solution.py:521
  75.7 5.1 %collective-permute-start.22 = (bf16[1,48,1536]{2,1,0:T(8,128)(2,1)S(1)}, bf16[1,48,1536]{2,1,0:T(8,128)(2,1)S(1)}, u32[]{:S(2)}, u32[]{:S(2)}) collective-permute-start(bf16[1,48,1536]{2,1,0:T(8,128)(2,1)S(1)} %get-tuple-element.169), channel_id=1, source_target_pairs={{0,4},{4,0},{8,12},{12,8},{16,20},{20,16},{24,28},{28,24},{1,5},{5... | collective-permute-start | bytes 442376 | tf_op jit(solution)/shard_map/ppermute | solution.py:517
  84.0 2.0 %collective-permute-start.25 = (f32[96,768]{1,0:T(8,128)S(1)}, f32[96,768]{1,0:T(8,128)S(1)}, u32[]{:S(2)}, u32[]{:S(2)}) collective-permute-start(f32[96,768]{1,0:T(8,128)S(1)} %get-tuple-element.177), channel_id=1, source_target_pairs={{0,1},{1,0},{2,3},{3,2},{4,5},{5,4},{6,7},{7,6},{8,9},{9,8},{10,11... | collective-permute-start | bytes 884744 | tf_op jit(solution)/shard_map/ppermute | solution.py:509
  84.0 2.0 %collective-permute-start.24 = (f32[24,1536]{1,0:T(8,128)S(1)}, f32[24,1536]{1,0:T(8,128)S(1)}, u32[]{:S(2)}, u32[]{:S(2)}) collective-permute-start(f32[24,1536]{1,0:T(8,128)S(1)} %get-tuple-element.175), channel_id=1, source_target_pairs={{0,1},{1,0},{2,3},{3,2},{4,5},{5,4},{6,7},{7,6},{8,9},{9,8},{10,11... | collective-permute-start | bytes 442376 | tf_op jit(solution)/shard_map/ppermute | solution.py:509
  84.5 1.5 %collective-permute-start.23 = (f32[24,1408]{1,0:T(8,128)S(1)}, f32[24,1408]{1,0:T(8,128)S(1)}, u32[]{:S(2)}, u32[]{:S(2)}) collective-permute-start(f32[24,1408]{1,0:T(8,128)S(1)} %get-tuple-element.173), channel_id=1, source_target_pairs={{0,1},{1,0},{2,3},{3,2},{4,5},{5,4},{6,7},{7,6},{8,9},{9,8},{10,11... | collective-permute-start | bytes 405512 | tf_op jit(solution)/shard_map/ppermute | solution.py:509

commit v4 on v3

--- a/solution.py
+++ b/solution.py
@@ -149,7 +149,7 @@
 
 def first_kernel(
     t0, t1, t2, t3, v0, v1, v2, v3, par, w,
-    tok_o, norm_o, qkv_o, mix_o, pos_o, probs_o, mine_o, theirs_o,
+    tok_o, norm_o, qkv_o, mix_o, mix2_o, pos_o, probs_o, mine_o, theirs_o,
     xs, shown,
 ):
     band = lax.axis_index("band")
@@ -194,7 +194,11 @@
             raised = jnp.exp(scores - jnp.max(scores, axis=-1, keepdims=True))
             probs = raised / jnp.sum(raised, axis=-1, keepdims=True)
             probs_o[i * 3 + hp] = probs
-            mix_o[rows, cols] = join_heads(dot(probs.astype(BF), v2)).astype(BF)
+            mixed = join_heads(dot(probs.astype(BF), v2)).astype(BF)
+            if hp < 2:
+                mix_o[rows, cols] = mixed
+            else:
+                mix2_o[rows, :] = mixed
 
 
 def pick_kernel(normed, pick_o, pick_p_o, pn_o):
@@ -204,27 +208,43 @@
     pn_o[...] = dot(normed[...], pick).astype(BF)
 
 
-def hidden_kernel(mix_a, mix_b, tok, par, be, wp, we, after, res_o, one_o, n2_o, mix_o, act_o, slope_o):
+def hidden_units(n2, be, we, cols, act_o, slope_o):
+    step = 256
+    for f in range(cols // step):
+        at = slice(f * step, (f + 1) * step)
+        hidden = dot(n2[...], we[:, at]) + be[0:1, at]
+        phi = 0.5 * (1.0 + lax.erf(hidden * math.sqrt(0.5)))
+        act_o[:, at] = (hidden * phi).astype(BF)
+        slope_o[:, at] = phi + hidden * (jnp.exp(-0.5 * hidden * hidden) * (1.0 / math.sqrt(2.0 * math.pi)))
+
+
+def hidden_kernel(
+    mix_a, mix_b, mix2_a, mix2_b, tok, par, be, wp, we, after, res_o, one_o, n2_o, mix_o, act_o, slope_o, tick
+):
+    tick[...] = jnp.zeros_like(tick)
     c = lax.axis_index("band") & 1
     mine, other = pl.multiple_of(c * HALF, 128), pl.multiple_of((1 - c) * HALF, 128)
-    mix_o[:, pl.ds(mine, HALF)] = mix_a[...]
-    mix_o[:, pl.ds(other, HALF)] = mix_b[...]
+    for at, first, second in ((mine, mix_a, mix2_a), (other, mix_b, mix2_b)):
+        mix_o[:, pl.ds(at, 256)] = first[...]
+        mix_o[:, pl.ds(pl.multiple_of(at + 256, 128), 128)] = second[...]
     one = dot(mix_o[...], wp[...]) + par[PB : PB + 1, :]
     one_o[...] = one
     residual = tok[...].astype(F32) + par[ASC : ASC + 1, :] * one
     res_o[...] = residual
     z, _ = statistics(residual)
     n2_o[...] = (z * par[GAIN2 : GAIN2 + 1, :] + par[BIAS2 : BIAS2 + 1, :]).astype(BF)
-    step = 256
-    for f in range(FH // step):
-        cols = slice(f * step, (f + 1) * step)
-        hidden = dot(n2_o[...], we[:, cols]) + be[0:1, cols]
-        phi = 0.5 * (1.0 + lax.erf(hidden * math.sqrt(0.5)))
-        act_o[:, cols] = (hidden * phi).astype(BF)
-        slope_o[:, cols] = phi + hidden * (jnp.exp(-0.5 * hidden * hidden) * (1.0 / math.sqrt(2.0 * math.pi)))
-
-
-def reduce_grad_kernel(c0, c1, c2, c3, pos_r, par, act, pre_o, gb2_o, send_o, keep_o, xs, act_x, full):
+    hidden_units(n2_o, be, we, D, act_o, slope_o)
+
+
+def more_hidden_kernel(n2, be, we, act_o, slope_o):
+    hidden_units(n2, be.at[:, D:FH], we.at[:, D:FH], FH - D, act_o, slope_o)
+
+
+def pass_kernel(v, after, out):
+    out[...] = v[...]
+
+
+def reduce_grad_kernel(c0, c1, c2, c3, pos_r, par, act_a, act_b, pre_o, gb2_o, send_o, keep_o, xs, act_x, full):
     x, c, z, y = place()
     gather_bands((c0, c1, c2, c3), xs)
     pos = pos_r[...]
@@ -234,7 +254,9 @@
         pre_o[rows, :] = pre.astype(BF)
         gb2_o[rows, :] = (par[MSC : MSC + 1, :] * pre).astype(BF)
     for j in range(4):
-        lo, mid, hi = 384 * j, 384 * j + 192, 384 * j + 384
+        act = act_a if j < 2 else act_b
+        lo = 384 * (j & 1)
+        mid, hi = lo + 192, lo + 384
         act_x[:, 192 * j : 192 * j + 192] = jnp.where(x == 0, act[:, lo:mid], act[:, mid:hi])
     full[...] = dot_tn(act_x[...], gb2_o[...])
     for dy, out in ((1, send_o), (0, keep_o)):
@@ -245,12 +267,14 @@
                 out[2 * dz + to] = full[pl.ds(at, 96), :].astype(BF)
 
 
-def back_kernel(gb2, wr, slope, we, gh_o, left_o, right_o):
+def back_kernel(gb2, wr, slope_a, slope_b, we, gh_o, left_o, right_o):
     step = 256
     for f in range(FH // step):
         cols = slice(f * step, (f + 1) * step)
         back = dot_nt(gb2[...], wr[cols, :])
-        gh_o[:, cols] = (back * slope[:, cols]).astype(BF)
+        slope = slope_a if f < 3 else slope_b
+        at = slice((f % 3) * step, (f % 3 + 1) * step)
+        gh_o[:, cols] = (back * slope[:, at]).astype(BF)
     gn2 = dot_nt(gh_o[...], we[...]).astype(BF)
     left_o[...] = gn2[:, :HALF]
     right_o[...] = gn2[:, HALF:]
@@ -262,13 +286,14 @@
     wide[...] = dot_tn(picked, gh[...])
     for low, out in ((1, send_o), (0, keep_o)):
         for i in range(4):
-            lo = 192 * (i & 1) + 48 * (low + 2 * (i >> 1))
+            lo = 192 * (i >> 1) + 48 * (low + 2 * (i & 1))
             out[i] = wide[lo : lo + 48, :].astype(BF)
 
 
 QC = 3 * HALF
 QW = QC + HALF
 QS = QW + SMALL
+FS = FH + 2 * SMALL
 
 
 def both_halves(l_a, l_b, r_a, r_b):
@@ -321,7 +346,7 @@
 
 
 def vectors_kernel(
-    l_a, l_b, r_a, r_b, res, one, gres, gp, w, act, wr, gb2, gh, pre, tok, pick, par, mine, theirs, after,
+    l_a, l_b, r_a, r_b, res, one, gres, gp, w, act_a, act_b, wr, gb2, gh, pre, tok, pick, par, mine, theirs, after,
     gb_keep, gb_send, send_o, keep_o, tick,
     vecs, sums,
 ):
@@ -350,7 +375,7 @@
     vecs[GAIN2 : GAIN2 + 1, :] = first * total(gn2 * z2)
     vecs[BIAS2 : BIAS2 + 1, :] = first * total(gn2)
     vecs[RB : RB + 1, :] = first * total(gb2[...].astype(F32))
-    two = dot(act[...], wr[...])
+    two = dot(act_a[...], wr[0:D, :]) + dot(act_b[...], wr[D:FH, :])
     for m, value in enumerate((gnp.astype(BF), two.astype(BF))):
         for i in range(IMGS):
             rows = slice(i * PACK, (i + 1) * PACK)
@@ -361,14 +386,14 @@
     sums[...] = dot_tn(gh[...], jnp.ones((ROWS, SMALL), BF))
     lane = lax.broadcasted_iota(jnp.int32, (48, SMALL), 1)
     for dy, out in ((1, send_o), (0, keep_o)):
-        for i, dz in enumerate((0, 2, 1, 3)):
+        for dz in range(4):
             b = (z ^ dz) * 2 + (y ^ dy)
             q = 4 * dy + dz
             block = cols[48 * q : 48 * q + 48]
             for k in range(4):
                 at = pl.multiple_of(384 * (b & 3) + 192 * x + 48 * k, 48)
                 block = jnp.where((lane == 10 + k) & ((b >> 2) == c), sums[pl.ds(at, 48), :], block)
-            out[i] = block.astype(BF)
+            out[dz >> 1, :, SMALL * (dz & 1) : SMALL * (dz & 1) + SMALL] = block.astype(BF)
 
 
 def last_kernel(gb_a, gb_b, tok, gres, res, mine, par, after, out_o, gtok_o, tick):
@@ -390,12 +415,6 @@
         out_o[i] = (own_rows(pack, res[rows, :]) + par[MSC : MSC + 1, :] * two).astype(BF)
 
 
-def fold_kernel(keep, arrived, we_keep, we_arrived, after, keep_ao, send_ao, keep_bo, send_bo, tick):
-    tick[...] = jnp.zeros_like(tick)
-    fold(keep, arrived, keep_ao, send_ao)
-    fold(we_keep, we_arrived, keep_bo, send_bo)
-
-
 def fold(keep, arrived, keep_o, send_o):
     half = keep.shape[0] // 2
     for i in range(half):
@@ -403,6 +422,31 @@
         send_o[i] = (keep[half + i].astype(F32) + arrived[half + i].astype(F32)).astype(BF)
 
 
+def fold_kernel(keep, arrived, after, keep_o, send_o, tick):
+    tick[...] = jnp.zeros_like(tick)
+    fold(keep, arrived, keep_o, send_o)
+
+
+def home_kernel(keep, arrived, after, keep_o, send_o, tick):
+    tick[...] = jnp.zeros_like(tick)
+    for i in range(4):
+        total = keep[i].astype(F32) + arrived[i].astype(F32)
+        keep_o[i] = total
+        send_o[i] = total.astype(BF)
+
+
+def fold(keep, arrived, keep_o, send_o):
+    half = keep.shape[0] // 2
+    for i in range(half):
+        keep_o[i] = keep[i].astype(F32) + arrived[i].astype(F32)
+        send_o[i] = (keep[half + i].astype(F32) + arrived[half + i].astype(F32)).astype(BF)
+
+
+def fold_kernel(keep, arrived, after, keep_o, send_o, tick):
+    tick[...] = jnp.zeros_like(tick)
+    fold(keep, arrived, keep_o, send_o)
+
+
 def second_fold_kernel(keep, arrived, we_keep, we_arrived, after, keep_o, send_o, we_keep_o, we_send_o, tick):
     tick[...] = jnp.zeros_like(tick)
     for i in range(2):
@@ -412,39 +456,49 @@
     fold(we_keep, we_arrived, we_keep_o, we_send_o)
 
 
-def join_kernel(keep, arrived, vec_keep, vec_arrived, after, keep_o, send_o, tick):
+def join_kernel(keep, arrived, vec_keep, vec_send, after, keep_o, send_o, tick):
+    tick[...] = jnp.zeros_like(tick)
+    fold(keep, arrived, keep_o.at[:, :, 0:FH], send_o.at[:, :, 0:FH])
+    keep_o[:, :, FH:FS] = vec_keep[...].astype(F32)
+    send_o[:, :, FH:FS] = vec_send[...]
+
+
+def part_kernel(keep, arrived, after, keep_o, send_o, vec_ko, vec_so, tick):
+    tick[...] = jnp.zeros_like(tick)
+    fold(keep.at[:, :, 0:FH], arrived.at[:, :, 0:FH], keep_o, send_o)
+    for hi in range(2):
+        total = keep[hi, :, FH:FS] + arrived[hi, :, FH:FS].astype(F32)
+        vec_ko[hi] = total[:, 0:SMALL]
+        vec_so[hi] = total[:, SMALL:].astype(BF)
+
+
+def rejoin_kernel(keep, arrived, vec_k, vec_a, after, keep_o, send_o, tick):
     tick[...] = jnp.zeros_like(tick)
     fold(keep, arrived, keep_o.at[:, :, 0:QW], send_o.at[:, :, 0:QW])
-    fold(vec_keep, vec_arrived, keep_o.at[:, :, QW:QS], send_o.at[:, :, QW:QS])
-
-
-def third_fold_kernel(keep, arrived, after, keep_o, send_o, tick):
-    tick[...] = jnp.zeros_like(tick)
-    fold(keep, arrived, keep_o, send_o)
-
-
-def finish_kernel(
-    qp_k, qp_a, wr_k, wr_a, we_k, we_a, after,
-    qk_o, qs_o, vec_o, proj_o, wr_ko, wr_so, keep_o, send_o,
-    sums, both,
-):
+    fold(vec_k, vec_a, keep_o.at[:, :, QW:QS], send_o.at[:, :, QW:QS])
+
+
+def settle_kernel(wr_k, wr_a, we_k, we_a, after, wr_ko, wr_so, we_ko, we_so, tick, both):
+    tick[...] = jnp.zeros_like(tick)
     c = lax.axis_index("band") & 1
-    mine = pl.multiple_of(c * 24, 8)
-    other = pl.multiple_of(24 - c * 24, 8)
-    sums[...] = qp_k[0] + qp_a[0].astype(F32)
-    qk_o[...] = sums[pl.ds(mine, 24), 0:QC]
-    qs_o[:, 0:QC] = sums[pl.ds(other, 24), 0:QC]
-    vec = sums[:, QW:QS]
-    vec_o[...] = vec
-    qs_o[:, QC : QC + SMALL] = vec[0:24]
-    qs_o[:, QC + SMALL : QC + 2 * SMALL] = vec[24:48]
-    proj_o[:, 0:HALF] = sums[0:24, QC:QW]
-    proj_o[:, HALF:] = sums[24:48, QC:QW]
     for at, out in ((c, wr_ko), (1 - c, wr_so)):
         out[...] = wr_k[at] + wr_a[at].astype(F32)
     both[...] = we_k[0] + we_a[0].astype(F32)
-    keep_o[...] = both[pl.ds(mine, 24), :]
-    send_o[...] = both[pl.ds(other, 24), :]
+    we_ko[...] = both[pl.ds(pl.multiple_of(c * 24, 8), 24), :]
+    we_so[...] = both[pl.ds(pl.multiple_of(24 - c * 24, 8), 24), :]
+
+
+def finish_kernel(qp_k, qp_a, after, keep_o, send_o, vec_o, proj_o, sums):
+    c = lax.axis_index("band") & 1
+    sums[...] = qp_k[0] + qp_a[0].astype(F32)
+    keep_o[...] = sums[pl.ds(pl.multiple_of(c * 24, 8), 24), 0:QC]
+    send_o[:, 0:QC] = sums[pl.ds(pl.multiple_of(24 - c * 24, 8), 24), 0:QC]
+    vec = sums[:, QW:QS]
+    vec_o[...] = vec
+    send_o[:, QC : QC + SMALL] = vec[0:24]
+    send_o[:, QC + SMALL :] = vec[24:48]
+    proj_o[:, 0:HALF] = sums[0:24, QC:QW]
+    proj_o[:, HALF:] = sums[24:48, QC:QW]
 
 
 def out_kernel(
@@ -461,7 +515,7 @@
         qkv_o[:, pl.ds(mine, HALF)] = keep[:, m * HALF : (m + 1) * HALF]
         qkv_o[:, pl.ds(other, HALF)] = arrived[:, m * HALF : (m + 1) * HALF]
     both[0:24] = vec[0:24] + arrived[:, QC : QC + SMALL]
-    both[24:48] = vec[24:48] + arrived[:, QC + SMALL : QC + 2 * SMALL]
+    both[24:48] = vec[24:48] + arrived[:, QC + SMALL :]
     own = both[pl.ds(pl.multiple_of(c * 24, 8), 24), :].T
     outs = (first_o, bias_o, None, None, bp_o, asc_o, gain2_o, bias2_o, br_o, msc_o)
     for r, out in enumerate(outs):
@@ -474,22 +528,23 @@
 
 
 COSTS = {
-    "first_kernel": (1500000000, 6000000),
-    "pick_kernel": (500000000, 2000000),
-    "hidden_kernel": (3000000000, 9000000),
+    "first_kernel": (0, 0),
+    "pick_kernel": (0, 0),
+    "hidden_kernel": (0, 0),
     "reduce_grad_kernel": (1000000000, 4000000),
-    "back_kernel": (2000000000, 6000000),
-    "expand_grad_kernel": (1000000000, 4000000),
-    "attention_back_kernel": (4000000000, 12000000),
-    "vectors_kernel": (2000000000, 8000000),
-    "fold_kernel": (0, 4000000),
+    "back_kernel": (0, 0),
+    "expand_grad_kernel": (0, 0),
+    "attention_back_kernel": (0, 0),
+    "vectors_kernel": (8000000000, 20000000),
+    "fold_kernel": (0, 0),
     "second_fold_kernel": (0, 2000000),
-    "last_kernel": (1000000000, 8000000),
+    "last_kernel": (0, 4000000),
     "spread_kernel": (0, 2000000),
     "finish_kernel": (0, 1000000),
     "out_kernel": (0, 1000000),
     "prepare_kernel": (0, 9000000),
     "hold_kernel": (0, 20000000),
+    "home_kernel": (0, 0),
 }
 
 
@@ -503,6 +558,11 @@
         compiler_params=pltpu.CompilerParams(vmem_limit_bytes=vmem * MIB),
         cost_estimate=pl.CostEstimate(flops=COSTS.get(kernel.__name__, (0, 0))[0], bytes_accessed=COSTS.get(kernel.__name__, (0, 0))[1], transcendentals=0),
     )
+
+
+def fold_call(keep, arrived, after):
+    half = (keep.shape[0] // 2, *keep.shape[1:])
+    return call(fold_kernel, (vm(half, F32), vm(half, BF), TICK), [VM] * 2 + [ANY])(keep, arrived, after)
 
 
 def by_core(value):
@@ -566,13 +626,14 @@
     tok_d = by_core(tok_x)
     vis_d = by_core(vis_x)
     cot_x = by_x(cot)
-    tok, normed, qkv, mix_own, pos, probs, pos_mine, pos_theirs = call(
+    tok, normed, qkv, mix_own, mix2_own, pos, probs, pos_mine, pos_theirs = call(
         first_kernel,
         (
             rows_b,
             rows_b,
             vm((3, ROWS, HALF), BF),
-            vm((ROWS, HALF), BF),
+            vm((ROWS, 256), BF),
+            vm((ROWS, 128), BF),
             vm((8, SLOTS), F32),
             vm((9, 2 * PACK, PACK), F32),
             vm((16, BAND), F32),
@@ -581,23 +642,25 @@
         [VM] * 10,
         [pltpu.VMEM((IMGS, SLOTS, D), BF), pltpu.VMEM((16, 128), F32)],
     )(tok_own, tok_c, tok_x, tok_d, vis, vis_c, vis_x, vis_d, par, wqkv)
-    mix_other = by_core(mix_own)
+    mix_other, mix2_other = by_core(mix_own), by_core(mix2_own)
+    pick, pick_p, pn = call(pick_kernel, (vm((D, HALF), BF), vm((D, 192), BF), vm((ROWS, HALF), BF)), [VM])(normed)
+    res, one, n2, mix, act, slope, tick = call(
+        hidden_kernel,
+        (rows_f, rows_f, rows_b, rows_b, rows_b, rows_f, TICK),
+        [VM] * 9 + [ANY],
+    )(mix_own, mix_other, mix2_own, mix2_other, tok, par, be, wp, we, pick)
+    cot_x = call(pass_kernel, block, [VM, ANY])(cot_x, tick)
     cot_d = by_core(cot_x)
-    pick, pick_p, pn = call(pick_kernel, (vm((D, HALF), BF), vm((D, 192), BF), vm((ROWS, HALF), BF)), [VM])(normed)
-    res, one, n2, mix, act, slope = call(
-        hidden_kernel,
-        (rows_f, rows_f, rows_b, rows_b, vm((ROWS, FH), BF), vm((ROWS, FH), F32)),
-        [VM] * 7 + [ANY],
-    )(mix_own, mix_other, tok, par, be, wp, we, pick)
+    act_b, slope_b = call(more_hidden_kernel, (rows_b, rows_f), [VM] * 3)(n2, be, we)
     pre, gb2, wr_send, wr_keep = call(
         reduce_grad_kernel,
         (rows_b, rows_b, vm((4, 96, D), BF), vm((4, 96, D), BF)),
-        [VM] * 7,
+        [VM] * 8,
         [pltpu.VMEM((IMGS, SLOTS, D), BF), pltpu.VMEM((ROWS, D), BF), pltpu.VMEM((D, D), F32)],
-    )(cot, cot_c, cot_x, cot_d, pos, par, act)
+    )(cot, cot_c, cot_x, cot_d, pos, par, act, act_b)
     wr_y = by_y(wr_send)
     half_b = vm((ROWS, HALF), BF)
-    gh, left, right = call(back_kernel, (vm((ROWS, FH), BF), half_b, half_b), [VM] * 4)(gb2, wr, slope, we)
+    gh, left, right = call(back_kernel, (vm((ROWS, FH), BF), half_b, half_b), [VM] * 5)(gb2, wr, slope, slope_b, we)
     gn2 = (left, by_core(left), right, by_core(right))
     we_send, we_keep, tick = call(
         expand_grad_kernel,
@@ -613,58 +676,54 @@
         [pltpu.VMEM((HALF, QC), F32)],
     )(*gn2, res, pre, qkv, probs, mix, pn, pick_p, wp, par, tick)
     qp_y = by_y(qp_send)
+    wr_keep, wr_send, tick = call(
+        home_kernel, (vm((4, 96, D), F32), vm((4, 96, D), BF), TICK), [VM] * 2 + [ANY]
+    )(wr_keep, wr_y, tick)
+    wr_z = homeward(wr_send, 2)
     gb_keep, gb_send, vec_send, vec_keep, tick = call(
         vectors_kernel,
-        (vm((2, *tokens.shape), BF), vm((2, *tokens.shape), BF), vm((4, 48, SMALL), BF), vm((4, 48, SMALL), BF), TICK),
-        [VM] * 19 + [ANY],
+        (vm((2, *tokens.shape), BF), vm((2, *tokens.shape), BF), vm((2, 48, 2 * SMALL), BF), vm((2, 48, 2 * SMALL), BF), TICK),
+        [VM] * 20 + [ANY],
         [pltpu.VMEM((SMALL, D), F32), pltpu.VMEM((FH, SMALL), F32)],
-    )(*gn2, res, one, gres, gp, wqkv, act, wr, gb2, gh, pre, tok, pick, par, pos_mine, pos_theirs, tick)
-    vec_y = by_y(vec_send)
+    )(*gn2, res, one, gres, gp, wqkv, act, act_b, wr, gb2, gh, pre, tok, pick, par, pos_mine, pos_theirs, tick)
     gb_other = by_core(gb_send)
-    we_half = (2, 48, FH)
+    we_keep, we_send, tick = call(
+        join_kernel, (vm((2, 48, FS), F32), vm((2, 48, FS), BF), TICK), [VM] * 4 + [ANY]
+    )(we_keep, we_z, vec_keep, vec_send, tick)
+    we_y = by_y(we_send)
+    qp_keep, qp_send, tick = fold_call(qp_keep, qp_y, tick)
+    qp_z = by_z(qp_send, 1)
+    wr_keep, wr_send, tick = fold_call(wr_keep, wr_z, tick)
+    wr_z = homeward(wr_send, 1)
+    we_keep, we_send, vec_keep, vec_send, tick = call(
+        part_kernel,
+        (vm((1, 48, FH), F32), vm((1, 48, FH), BF), vm((2, 48, SMALL), F32), vm((2, 48, SMALL), BF), TICK),
+        [VM] * 2 + [ANY],
+    )(we_keep, we_y, tick)
+    vec_z = by_z(vec_send, 1)
+    we_z = by_z(we_send, 2)
+    qp_keep, qp_send, tick = call(
+        rejoin_kernel, (vm((1, 48, QS), F32), vm((1, 48, QS), BF), TICK), [VM] * 4 + [ANY]
+    )(qp_keep, qp_z, vec_keep, vec_z, tick)
+    qp_z = by_z(qp_send, 2)
     wr_keep, wr_send, we_keep, we_send, tick = call(
-        fold_kernel,
-        (vm((2, 96, D), F32), vm((2, 96, D), BF), vm(we_half, F32), vm(we_half, BF), TICK),
+        settle_kernel,
+        (vm((96, D), F32), vm((96, D), F32), vm((24, FH), F32), vm((24, FH), F32), TICK),
         [VM] * 4 + [ANY],
-    )(wr_keep, wr_y, we_keep, we_z, tick)
-    wr_z = by_z(wr_send, 1)
-    we_z = by_z(we_send, 2)
-    qp_half = (2, 48, QS)
-    qp_keep, qp_send, tick = call(
-        join_kernel, (vm(qp_half, F32), vm(qp_half, BF), TICK), [VM] * 4 + [ANY]
-    )(qp_keep, qp_y, vec_keep, vec_y, tick)
-    qp_z = by_z(qp_send, 1)
-    wr_keep, wr_send, we_keep, we_send, tick = call(
-        second_fold_kernel,
-        (vm((2, 96, D), F32), vm((2, 96, D), BF), vm((1, 48, FH), F32), vm((1, 48, FH), BF), TICK),
-        [VM] * 4 + [ANY],
+        [pltpu.VMEM((48, FH), F32)],
     )(wr_keep, wr_z, we_keep, we_z, tick)
-    wr_z = homeward(wr_send, 2)
-    we_y = by_y(we_send)
+    we_other, wr_other = by_core(we_send), by_core(wr_send)
     layer_out, grad_tokens, tick = call(
         last_kernel,
         (sds(tokens.shape, BF), sds(tokens.shape, BF), TICK),
         [VM] * 7 + [ANY],
     )(gb_keep, gb_other, tok_own, gres, res, pos_mine, par, tick)
-    qp_keep, qp_send, tick = call(
-        third_fold_kernel, (vm((1, 48, QS), F32), vm((1, 48, QS), BF), TICK), [VM] * 2 + [ANY]
+    qp_keep, qp_send, vec, proj = call(
+        finish_kernel,
+        (vm((24, QC), F32), vm((24, QC + 2 * SMALL), F32), vm((48, SMALL), F32), sds((24, D), F32)),
+        [VM] * 2 + [ANY],
+        [pltpu.VMEM((48, QS), F32)],
     )(qp_keep, qp_z, tick)
-    qp_z = by_z(qp_send, 2)
-    qp_keep, qp_send, vec, proj, wr_keep, wr_send, we_keep, we_send = call(
-        finish_kernel,
-        (
-            vm((24, QC), F32),
-            vm((24, QC + 2 * SMALL), F32),
-            vm((48, SMALL), F32),
-            sds((24, D), F32),
-            vm((96, D), F32),
-            vm((96, D), F32),
-            vm((24, FH), F32),
-            vm((24, FH), F32),
-        ),
-        [VM] * 6 + [ANY],
-        [pltpu.VMEM((48, QS), F32), pltpu.VMEM((48, FH), F32)],
-    )(qp_keep, qp_z, wr_keep, wr_z, we_keep, we_y, tick)
     vector = sds((24,), F32)
     grad_qkv, gg1, gb1, gqv, gbp, gas, gg2, gb2, gbr, gms, geb, grad_expand, grad_reduce = call(
         out_kernel,
@@ -674,7 +733,7 @@
         ),
         [VM] * 7,
         [pltpu.VMEM((48, SMALL), F32)],
-    )(qp_keep, vec, by_core(qp_send), we_keep, by_core(we_send), wr_keep, by_core(wr_send))
+    )(qp_keep, vec, by_core(qp_send), we_keep, we_other, wr_keep, wr_other)
     return (
         layer_out, grad_tokens, gg1, gb1, grad_qkv, gqv, proj, gbp, gas, gg2, gb2, grad_expand, geb, grad_reduce,
         gbr, gms,

time: 87.2 us -> 84.5 us (0.969)
  waiting for transfers between devices: 34.1 us -> 29.7 us
  starting transfers between devices: 21 us -> 22.2 us
    ppermute x4 -> x3, waiting for transfers between devices: 13.9 us -> 5.98 us  [by_y(): return lax.ppermute(value, 'batch', [(i, i ^ 1) for i in range(8)])]
    ppermute x1 -> x2, waiting for transfers between devices: 0.01 us -> 4.1 us  [homeward(): return lax.ppermute(value, ('batch', 'band'), pairs)]
    ppermute x3, waiting for transfers between devices: 7.07 us -> 3.49 us  [by_x(): return lax.ppermute(value, 'band', [(i, i ^ 2) for i in range(4)])]
    ppermute x13 -> x14, starting transfers between devices: 2.51 us -> 5.03 us  [by_core(): return lax.ppermute(value, 'band', [(i, i ^ 1) for i in range(4)])]
    ppermute x5, starting transfers between devices: 7.26 us -> 5.13 us  [by_z(): return lax.ppermute(value, 'batch', [(i, i ^ 2 * dz) for i in range(8)])]
    ppermute x1 -> x2, starting transfers between devices: 1.29 us -> 3.21 us  [homeward(): return lax.ppermute(value, ('batch', 'band'), pairs)]
    ppermute x5, waiting for transfers between devices: 11.7 us -> 13.5 us  [by_z(): return lax.ppermute(value, 'batch', [(i, i ^ 2 * dz) for i in range(8)])]
    ppermute x4 -> x3, starting transfers between devices: 5.16 us -> 3.95 us  [by_y(): return lax.ppermute(value, 'batch', [(i, i ^ 1) for i in range(8)])]
  transfers between devices with their start and end apart: 26 -> 27, of which waited for: 10 -> 11; matrix products, arithmetic and copies ran while one was open for 0% -> 0% of each run, Pallas kernels for 29% -> 34%
where the time goes in v4:
time: 84.5 us; the launch traced here: 84.3 us
  Pallas kernels  31.4 us (37%)
  waiting for transfers between devices  29.7 us (35%)
  starting transfers between devices  22.2 us (26%)
  between operations  0.97 us (1%)
    ppermute x5, waiting for transfers between devices, by_z(): return lax.ppermute(value, 'batch', [(i, i ^ 2 * dz) for i in range(8)])  13.5 us
    pallas_call x1, Pallas kernels, packed_body(): call(attention_back_kernel, (rows_f, vm((ROWS, QC), BF), vm((4, 48, QW),...  6.37 us
    ppermute x3, waiting for transfers between devices, by_y(): return lax.ppermute(value, 'batch', [(i, i ^ 1) for i in range(8)])  5.98 us
    ppermute x5, starting transfers between devices, by_z(): return lax.ppermute(value, 'batch', [(i, i ^ 2 * dz) for i in range(8)])  5.13 us
    ppermute x14, starting transfers between devices, by_core(): return lax.ppermute(value, 'band', [(i, i ^ 1) for i in range(4)])  5.03 us
    ppermute x3, starting transfers between devices, by_x(): return lax.ppermute(value, 'band', [(i, i ^ 2) for i in range(4)])  4.83 us
    pallas_call x1, Pallas kernels, packed_body(): call(vectors_kernel, (vm((2, *tokens.shape), BF), vm((2, *tokens.shape),...  4.37 us
    ppermute x2, waiting for transfers between devices, homeward(): return lax.ppermute(value, ('batch', 'band'), pairs)  4.1 us
  transfers between devices with their start and end apart: 27, of which 11 were waited for; matrix products, arithmetic and copies ran while one was open for 0% of the time, Pallas kernels for 34%

profile of v4, /device:TPU:0, one launch (start us, length us, event | category | flops | bytes accessed | tf_op | source)
XLA Modules:
  0.0 84.3 jit_solution(7507373187331331358)
XLA Ops:
  0.7 3.0 %collective-permute-start = (bf16[3,64,768]{2,1,0:T(8,128)(2,1)}, bf16[3,64,768]{2,1,0:T(8,128)(2,1)S(1)}, u32[]{:S(2)}, u32[]{:S(2)}) collective-permute-start(bf16[3,64,768]{2,1,0:T(8,128)(2,1)} %tok.1), channel_id=1, source_target_pairs={{0,2},{1,3},{2,0},{3,1},{4,6},{5,7},{6,4},{7,5},{8,10},{9,11},{10,... | collective-permute-start | bytes 884744 | tf_op jit(solution)/shard_map/ppermute | solution.py:573
  3.7 3.7 %shard_map.288 = (bf16[3,64,768]{2,1,0:T(8,128)(2,1)S(1)}, bf16[3,64,768]{2,1,0:T(8,128)(2,1)S(1)}, f32[16,768]{1,0:T(8,128)S(1)}, f32[8,1536]{1,0:T(8,128)S(1)}...) custom-call(bf16[3,64,768]{2,1,0:T(8,128)(2,1)} %cot.1, ...), custom_call_target="tpu_custom_call" | custom-call | bytes 9000000 | tf_op jit(solution)/shard_map/pallas_call | solution.py:597
  7.5 3.5 %collective-permute-done.1.after_a.v2 = s32[3,64]{1,0:T(4,128)S(1)} collective-permute-done((s32[3,64]{1,0:T(4,128)S(1)}, s32[3,64]{1,0:T(4,128)S(1)}, u32[]{:S(2)}, u32[]{:S(2)}) %collective-permute-start.1) | collective-permute-done | bytes 800 | tf_op jit(solution)/shard_map/ppermute | solution.py:573
  11.1 1.7 %collective-permute-start.3 = (bf16[3,64,768]{2,1,0:T(8,128)(2,1)S(1)}, bf16[3,64,768]{2,1,0:T(8,128)(2,1)S(1)}, u32[]{:S(2)}, u32[]{:S(2)}) collective-permute-start(bf16[3,64,768]{2,1,0:T(8,128)(2,1)S(1)} %get-tuple-element.116.c0), channel_id=1, source_target_pairs={{0,2},{1,3},{2,0},{3,1},{4,6},{5,7},{6,4},{7,5},{8,10},{9,11},{10,... | collective-permute-start | bytes 884744 | tf_op jit(solution)/shard_map/ppermute | solution.py:573
  12.9 0.2 collective-permute-start.6
  13.0 0.3 collective-permute-start.7
  13.4 0.6 collective-permute-done.6.v1
  14.0 0.2 collective-permute-done.7.v3
  14.2 3.5 %shard_map.290 = (bf16[432,768]{1,0:T(8,128)(2,1)S(1)}, bf16[432,768]{1,0:T(8,128)(2,1)S(1)}, bf16[3,432,384]{2,1,0:T(8,128)(2,1)S(1)}, bf16[432,256]{1,0:T(8,12...) custom-call(bf16[3,64,768]{2,1,0:T(8,128)(2,1)S(1)} %get-tuple-eleme, ...), custom_call_target="tpu_custom_call" | custom-call | tf_op jit(solution)/shard_map/pallas_call | solution.py:629
  17.7 0.4 collective-permute-start.8
  18.1 0.2 collective-permute-start.9
  18.3 0.3 collective-permute-start.2
  18.6 0.6 shard_map.291
  19.2 0.2 collective-permute-done.9.mix2_b
  19.4 2.2 %shard_map.292 = (f32[432,768]{1,0:T(8,128)S(1)}, f32[432,768]{1,0:T(8,128)S(1)}, bf16[432,768]{1,0:T(8,128)(2,1)S(1)}, bf16[432,768]{1,0:T(8,128)(2,1)S(1)}, bf...) custom-call(bf16[432,256]{1,0:T(8,128)(2,1)S(1)} %get-tuple-element.120.mix_a, ...), custom_call_target="tpu_custom_call" | custom-call | tf_op jit(solution)/shard_map/pallas_call | solution.py:647
  21.7 0.4 collective-permute-start.10
  22.1 1.0 %shard_map.294 = (bf16[432,768]{1,0:T(8,128)(2,1)S(1)}, f32[432,768]{1,0:T(8,128)S(1)}) custom-call(bf16[432,768]{1,0:T(8,128)(2,1)S(1)} %get-tuple-element.131.n2, f32[8,1536]{1,0:T(8,128)S(1)} %get-tuple-element.123.be, bf16[768,1536]{1,0:T(8,128)(2,1)S(1)} %get-tuple-element.125.we), custom_call_target="tpu_custom_call" | custom-call | tf_op jit(solution)/shard_map/pallas_call | solution.py:654
  23.1 0.3 collective-permute-done.10.c3
  23.4 1.7 %shard_map.295 = (bf16[432,768]{1,0:T(8,128)(2,1)S(1)}, bf16[432,768]{1,0:T(8,128)(2,1)S(1)}, bf16[4,96,768]{2,1,0:T(8,128)(2,1)S(1)}, bf16[4,96,768]{2,1,0:T(8,128)(2,1)S(1)}) custom-call(bf16[3,64,768]{2,1,0:T(8,128)(2,1)S(1)} %get-tuple-element.116.c0, bf16[3,64,768]{2,1,0:T(8,128)(2,1)S(1)} %collective-permute-done.2.c1, ...), custom_call_target="tpu_custom_call" | custom-call | flops 1000000000 | bytes 4000000 | tf_op jit(solution)/shard_map/pallas_call | solution.py:655
  25.1 1.6 %collective-permute-start.13 = (bf16[4,96,768]{2,1,0:T(8,128)(2,1)S(1)}, bf16[4,96,768]{2,1,0:T(8,128)(2,1)S(1)}, u32[]{:S(2)}, u32[]{:S(2)}) collective-permute-start(bf16[4,96,768]{2,1,0:T(8,128)(2,1)S(1)} %get-tuple-element.154), channel_id=1, source_target_pairs={{0,4},{4,0},{8,12},{12,8},{16,20},{20,16},{24,28},{28,24},{1,5},{5... | collective-permute-start | bytes 1769480 | tf_op jit(solution)/shard_map/ppermute | solution.py:577
  26.7 2.4 %shard_map.296 = (bf16[432,1536]{1,0:T(8,128)(2,1)S(1)}, bf16[432,384]{1,0:T(8,128)(2,1)S(1)}, bf16[432,384]{1,0:T(8,128)(2,1)S(1)}) custom-call(bf16[432,768]{1,0:T(8,128)(2,1)S(1)} %get-tuple-element.133.gb2, bf16[1536,768]{1,0:T(8,128)(2,1)S(1)} %get-tuple-element.134.wr, f32[432,768]{1,0:T(8,128)S(1)} %get-tuple-element.135.slope_a, ...), custom_call_target="tpu_custom_call" | custom-call | tf_op jit(solution)/shard_map/pallas_call | solution.py:663
  29.2 0.5 collective-permute-start.12
  29.7 1.2 %shard_map.297 = (bf16[4,48,1536]{2,1,0:T(8,128)(2,1)S(1)}, bf16[4,48,1536]{2,1,0:T(8,128)(2,1)S(1)}, f32[8,128]{1,0:T(8,128)S(1)}) custom-call(bf16[432,768]{1,0:T(8,128)(2,1)S(1)} %get-tuple-element.131.n2, bf16[432,1536]{1,0:T(8,128)(2,1)S(1)} %get-tuple-element.147.gh, bf16[768,384]{1,0:T(8,128)(2,1)S(1)} %get-tuple-element.127.after.pick), custom_call_target="tpu_custom_call" | custom-call | tf_op jit(solution)/shard_map/pallas_call | solution.py:665
  30.9 1.7 %collective-permute-start.17 = (bf16[4,48,1536]{2,1,0:T(8,128)(2,1)S(1)}, bf16[4,48,1536]{2,1,0:T(8,128)(2,1)S(1)}, u32[]{:S(2)}, u32[]{:S(2)}) collective-permute-start(bf16[4,48,1536]{2,1,0:T(8,128)(2,1)S(1)} %get-tuple-element.164), channel_id=1, source_target_pairs={{0,8},{4,12},{8,0},{12,4},{16,24},{20,28},{24,16},{28,20},{1,9},{5... | collective-permute-start | bytes 1769480 | tf_op jit(solution)/shard_map/ppermute | solution.py:581
  32.6 6.4 %shard_map.298 = (f32[432,768]{1,0:T(8,128)S(1)}, bf16[432,1152]{1,0:T(8,128)(2,1)S(1)}, bf16[4,48,1536]{2,1,0:T(8,128)(2,1)S(1)}, bf16[4,48,1536]{2,1,0:T(8,128)(2,1)S(1)}, f32[8,128]{1,0:T(8,128)S(1)}) custom-call(bf16[432,384]{1,0:T(8,128)(2,1)S(1)} %get-tuple-element.137.l_a, bf16[432,384]{1,0:T(8,128)(2,1)S(1)} %collective-permute-done.11.l_b, ...), custom_call_target="tpu_custom_call" | custom-call | tf_op jit(solution)/shard_map/pallas_call | solution.py:672
  39.0 0.5 collective-permute-start.16
  39.5 1.2 %collective-permute-done.13.arrived = bf16[4,96,768]{2,1,0:T(8,128)(2,1)S(1)} collective-permute-done((bf16[4,96,768]{2,1,0:T(8,128)(2,1)S(1)}, bf16[4,96,768]{2,1,0:T(8,128)(2,1)S(1)}, u32[]{:S(2)}, u32[]{:S(2)}) %collective-permute-start.13) | collective-permute-done | bytes 589856 | tf_op jit(solution)/shard_map/ppermute | solution.py:577
  40.7 0.2 shard_map.299
  40.9 1.3 %collective-permute-start.15 = (bf16[4,96,768]{2,1,0:T(8,128)(2,1)S(1)}, bf16[4,96,768]{2,1,0:T(8,128)(2,1)S(1)}, u32[]{:S(2)}, u32[]{:S(2)}) collective-permute-start(bf16[4,96,768]{2,1,0:T(8,128)(2,1)S(1)} %get-tuple-element.160), channel_id=1, source_target_pairs={{1,17},{3,19},{5,21},{7,23},{9,25},{11,27},{13,29},{15,31},{16,0},... | collective-permute-start | bytes 1769480 | tf_op jit(solution)/shard_map/ppermute | solution.py:586
  42.2 4.4 %shard_map.300 = (bf16[2,3,64,768]{3,2,1,0:T(8,128)(2,1)S(1)}, bf16[2,3,64,768]{3,2,1,0:T(8,128)(2,1)S(1)}, bf16[2,48,256]{2,1,0:T(8,128)(2,1)S(1)}, bf16[2,48,256]{2,1,0:T(8,128)(2,1)S(1)}, f32[8,128]{1,0:T(8,128)S(1)}) custom-call(bf16[432,384]{1,0:T(8,128)(2,1)S(1)} %get-tuple-element.137.l_a, bf16[432,384]{1,0:T(8,128)(2,1)S(1)} %collective-permute-done.11.l_b, ...), custom_call_target="tpu_custom_call" | custom-call | flops 8000000000 | bytes 20000000 | tf_op jit(solution)/shard_map/pallas_call | solution.py:683
  46.6 0.1 shard_map.301
  46.7 1.8 %collective-permute-start.19 = (bf16[2,48,1792]{2,1,0:T(8,128)(2,1)S(1)}, bf16[2,48,1792]{2,1,0:T(8,128)(2,1)S(1)}, u32[]{:S(2)}, u32[]{:S(2)}) collective-permute-start(bf16[2,48,1792]{2,1,0:T(8,128)(2,1)S(1)} %get-tuple-element.173), channel_id=1, source_target_pairs={{0,4},{4,0},{8,12},{12,8},{16,20},{20,16},{24,28},{28,24},{1,5},{5... | collective-permute-start | bytes 1032200 | tf_op jit(solution)/shard_map/ppermute | solution.py:577
  48.5 1.9 %collective-permute-start.14 = (bf16[2,3,64,768]{3,2,1,0:T(8,128)(2,1)S(1)}, bf16[2,3,64,768]{3,2,1,0:T(8,128)(2,1)S(1)}, u32[]{:S(2)}, u32[]{:S(2)}) collective-permute-start(bf16[2,3,64,768]{3,2,1,0:T(8,128)(2,1)S(1)} %get-tuple-element.158), channel_id=1, source_target_pairs={{0,1},{1,0},{2,3},{3,2},{4,5},{5,4},{6,7},{7,6},{8,9},{9,8},{10,11... | collective-permute-start | bytes 1769480 | tf_op jit(solution)/shard_map/ppermute | solution.py:569
  50.5 4.8 %collective-permute-done.16.arrived = bf16[4,48,1536]{2,1,0:T(8,128)(2,1)S(1)} collective-permute-done((bf16[4,48,1536]{2,1,0:T(8,128)(2,1)S(1)}, bf16[4,48,1536]{2,1,0:T(8,128)(2,1)S(1)}, u32[]{:S(2)}, u32[]{:S(2)}) %collective-permute-start.16) | collective-permute-done | bytes 589856 | tf_op jit(solution)/shard_map/ppermute | solution.py:577
  55.3 0.2 shard_map.302
  55.4 0.4 collective-permute-start.21
  55.9 4.1 %collective-permute-done.15.arrived = bf16[4,96,768]{2,1,0:T(8,128)(2,1)S(1)} collective-permute-done((bf16[4,96,768]{2,1,0:T(8,128)(2,1)S(1)}, bf16[4,96,768]{2,1,0:T(8,128)(2,1)S(1)}, u32[]{:S(2)}, u32[]{:S(2)}) %collective-permute-start.15) | collective-permute-done | bytes 589856 | tf_op jit(solution)/shard_map/ppermute | solution.py:586
  60.1 1.9 %collective-permute-start.18 = (bf16[2,96,768]{2,1,0:T(8,128)(2,1)S(1)}, bf16[2,96,768]{2,1,0:T(8,128)(2,1)S(1)}, u32[]{:S(2)}, u32[]{:S(2)}) collective-permute-start(bf16[2,96,768]{2,1,0:T(8,128)(2,1)S(1)} %get-tuple-element.171), channel_id=1, source_target_pairs={{0,8},{2,10},{4,12},{6,14},{8,0},{10,2},{12,4},{14,6},{17,25},{19,... | collective-permute-start | bytes 884744 | tf_op jit(solution)/shard_map/ppermute | solution.py:586
  62.1 2.1 %collective-permute-start.20 = (bf16[1,48,1536]{2,1,0:T(8,128)(2,1)S(1)}, bf16[1,48,1536]{2,1,0:T(8,128)(2,1)S(1)}, u32[]{:S(2)}, u32[]{:S(2)}) collective-permute-start(bf16[1,48,1536]{2,1,0:T(8,128)(2,1)S(1)} %get-tuple-element.176), channel_id=1, source_target_pairs={{0,16},{4,20},{8,24},{12,28},{16,0},{20,4},{24,8},{28,12},{1,17},{... | collective-permute-start | bytes 442376 | tf_op jit(solution)/shard_map/ppermute | solution.py:581
  64.2 0.8 %collective-permute-start.22 = (bf16[2,48,128]{2,1,0:T(8,128)(2,1)S(1)}, bf16[2,48,128]{2,1,0:T(8,128)(2,1)S(1)}, u32[]{:S(2)}, u32[]{:S(2)}) collective-permute-start(bf16[2,48,128]{2,1,0:T(8,128)(2,1)S(1)} %get-tuple-element.180), channel_id=1, source_target_pairs={{0,8},{4,12},{8,0},{12,4},{16,24},{20,28},{24,16},{28,20},{1,9},{5... | collective-permute-start | bytes 73736 | tf_op jit(solution)/shard_map/ppermute | solution.py:581
  65.0 8.0 %collective-permute-done.22.vec_a = bf16[2,48,128]{2,1,0:T(8,128)(2,1)S(1)} collective-permute-done((bf16[2,48,128]{2,1,0:T(8,128)(2,1)S(1)}, bf16[2,48,128]{2,1,0:T(8,128)(2,1)S(1)}, u32[]{:S(2)}, u32[]{:S(2)}) %collective-permute-start.22) | collective-permute-done | bytes 24608 | tf_op jit(solution)/shard_map/ppermute | solution.py:581
  73.2 0.1 shard_map.306
  73.4 0.5 collective-permute-start.25
  73.9 1.8 %shard_map.307 = (bf16[3,64,768]{2,1,0:T(8,128)(2,1)}, bf16[3,64,768]{2,1,0:T(8,128)(2,1)}, f32[8,128]{1,0:T(8,128)S(1)}) custom-call(bf16[2,3,64,768]{3,2,1,0:T(8,128)(2,1)S(1)} %get-tuple-element.157.gb_a, bf16[2,3,64,768]{3,2,1,0:T(8,128)(2,1)S(1)} %collective-permute-done.14.gb_b, bf16[3,64,768]{2,1,0:T(8,128)(2,1)S(1)} %get-tuple-element.117.t0.tok, ...), custom_call_target="tpu_custom_call" | custom-call | bytes 4000000 | tf_op jit(solution)/shard_map/pallas_call | solution.py:716
  75.8 5.4 %collective-permute-done.23.qp_a = bf16[1,48,1664]{2,1,0:T(8,128)(2,1)S(1)} collective-permute-done((bf16[1,48,1664]{2,1,0:T(8,128)(2,1)S(1)}, bf16[1,48,1664]{2,1,0:T(8,128)(2,1)S(1)}, u32[]{:S(2)}, u32[]{:S(2)}) %collective-permute-start.23) | collective-permute-done | bytes 159776 | tf_op jit(solution)/shard_map/ppermute | solution.py:581
  81.2 0.7 shard_map.308
  81.9 1.4 %collective-permute-done.24.arrived = f32[24,1408]{1,0:T(8,128)S(1)} collective-permute-done((f32[24,1408]{1,0:T(8,128)S(1)}, f32[24,1408]{1,0:T(8,128)S(1)}, u32[]{:S(2)}, u32[]{:S(2)}) %collective-permute-start.24) | collective-permute-done | bytes 135200 | tf_op jit(solution)/shard_map/ppermute | solution.py:569
  83.2 0.9 %shard_map.309 = (f32[24,2304]{1,0:T(8,128)}, f32[24]{0:T(128)}, f32[24]{0:T(128)}, f32[2,24]{1,0:T(2,128)}, f32[24]{0:T(128)}, /*index=5*/f32[24]{0:T(128)}, f3...) custom-call(f32[24,1152]{1,0:T(8,128)S(1)} %get-tuple-element.189.ke, ...), custom_call_target="tpu_custom_call" | custom-call | bytes 1000000 | tf_op jit(solution)/shard_map/pallas_call | solution.py:728
  (30 shorter events, 0.8 us)
Async XLA Ops:
  0.6 6.8 %copy-start = (bf16[3,64,768]{2,1,0:T(8,128)(2,1)S(1)}, bf16[3,64,768]{2,1,0:T(8,128)(2,1)}, u32[]{:S(2)}) copy-start(bf16[3,64,768]{2,1,0:T(8,128)(2,1)} %tok.1) | copy-start | bytes 884740
  0.7 10.3 %collective-permute-start = (bf16[3,64,768]{2,1,0:T(8,128)(2,1)}, bf16[3,64,768]{2,1,0:T(8,128)(2,1)S(1)}, u32[]{:S(2)}, u32[]{:S(2)}) collective-permute-start(bf16[3,64,768]{2,1,0:T(8,128)(2,1)} %tok.1), channel_id=1, source_target_pairs={{0,2},{1,3},{2,0},{3,1},{4,6},{5,7},{6,4},{7,5},{8,10},{9,11},{10,... | collective-permute-start | bytes 884744 | tf_op jit(solution)/shard_map/ppermute | solution.py:573
  7.4 3.7 %collective-permute-start.1 = (s32[3,64]{1,0:T(4,128)S(1)}, s32[3,64]{1,0:T(4,128)S(1)}, u32[]{:S(2)}, u32[]{:S(2)}) collective-permute-start(s32[3,64]{1,0:T(4,128)S(1)} %get-tuple-element.114.v0), channel_id=1, source_target_pairs={{0,2},{1,3},{2,0},{3,1},{4,6},{5,7},{6,4},{7,5},{8,10},{9,11},{10,... | collective-permute-start | bytes 2312 | tf_op jit(solution)/shard_map/ppermute | solution.py:573
  7.5 6.7 %collective-permute-start.4 = (bf16[3,64,768]{2,1,0:T(8,128)(2,1)S(1)}, bf16[3,64,768]{2,1,0:T(8,128)(2,1)S(1)}, u32[]{:S(2)}, u32[]{:S(2)}) collective-permute-start(bf16[3,64,768]{2,1,0:T(8,128)(2,1)S(1)} %copy-done), channel_id=1, source_target_pairs={{0,1},{1,0},{2,3},{3,2},{4,5},{5,4},{6,7},{7,6},{8,9},{9,8},{10,11... | collective-permute-start | bytes 884744 | tf_op jit(solution)/shard_map/ppermute | solution.py:569
  11.1 3.1 %collective-permute-start.5 = (bf16[3,64,768]{2,1,0:T(8,128)(2,1)S(1)}, bf16[3,64,768]{2,1,0:T(8,128)(2,1)S(1)}, u32[]{:S(2)}, u32[]{:S(2)}) collective-permute-start(bf16[3,64,768]{2,1,0:T(8,128)(2,1)S(1)} %get-tuple-element.118.t2), channel_id=1, source_target_pairs={{0,1},{1,0},{2,3},{3,2},{4,5},{5,4},{6,7},{7,6},{8,9},{9,8},{10,11... | collective-permute-start | bytes 884744 | tf_op jit(solution)/shard_map/ppermute | solution.py:569
  11.1 10.5 %collective-permute-start.3 = (bf16[3,64,768]{2,1,0:T(8,128)(2,1)S(1)}, bf16[3,64,768]{2,1,0:T(8,128)(2,1)S(1)}, u32[]{:S(2)}, u32[]{:S(2)}) collective-permute-start(bf16[3,64,768]{2,1,0:T(8,128)(2,1)S(1)} %get-tuple-element.116.c0), channel_id=1, source_target_pairs={{0,2},{1,3},{2,0},{3,1},{4,6},{5,7},{6,4},{7,5},{8,10},{9,11},{10,... | collective-permute-start | bytes 884744 | tf_op jit(solution)/shard_map/ppermute | solution.py:573
  12.9 1.2 %collective-permute-start.6 = (s32[3,64]{1,0:T(4,128)S(1)}, s32[3,64]{1,0:T(4,128)S(1)}, u32[]{:S(2)}, u32[]{:S(2)}) collective-permute-start(s32[3,64]{1,0:T(4,128)S(1)} %get-tuple-element.114.v0), channel_id=1, source_target_pairs={{0,1},{1,0},{2,3},{3,2},{4,5},{5,4},{6,7},{7,6},{8,9},{9,8},{10,11... | collective-permute-start | bytes 2312 | tf_op jit(solution)/shard_map/ppermute | solution.py:569
  13.0 1.2 %collective-permute-start.7 = (s32[3,64]{1,0:T(4,128)S(1)}, s32[3,64]{1,0:T(4,128)S(1)}, u32[]{:S(2)}, u32[]{:S(2)}) collective-permute-start(s32[3,64]{1,0:T(4,128)S(1)} %collective-permute-done.1.after_a.v2), channel_id=1, source_target_pairs={{0,1},{1,0},{2,3},{3,2},{4,5},{5,4},{6,7},{7,6},{8,9},{9,8},{10,11... | collective-permute-start | bytes 2312 | tf_op jit(solution)/shard_map/ppermute | solution.py:569
  17.7 1.7 %collective-permute-start.8 = (bf16[432,256]{1,0:T(8,128)(2,1)S(1)}, bf16[432,256]{1,0:T(8,128)(2,1)S(1)}, u32[]{:S(2)}, u32[]{:S(2)}) collective-permute-start(bf16[432,256]{1,0:T(8,128)(2,1)S(1)} %get-tuple-element.120.mix_a), channel_id=1, source_target_pairs={{0,1},{1,0},{2,3},{3,2},{4,5},{5,4},{6,7},{7,6},{8,9},{9,8},{10,11... | collective-permute-start | bytes 663560 | tf_op jit(solution)/shard_map/ppermute | solution.py:569
  18.1 1.3 %collective-permute-start.9 = (bf16[432,128]{1,0:T(8,128)(2,1)S(1)}, bf16[432,128]{1,0:T(8,128)(2,1)S(1)}, u32[]{:S(2)}, u32[]{:S(2)}) collective-permute-start(bf16[432,128]{1,0:T(8,128)(2,1)S(1)} %get-tuple-element.121.mix2_a), channel_id=1, source_target_pairs={{0,1},{1,0},{2,3},{3,2},{4,5},{5,4},{6,7},{7,6},{8,9},{9,8},{10,11... | collective-permute-start | bytes 331784 | tf_op jit(solution)/shard_map/ppermute | solution.py:569
  18.3 4.8 %collective-permute-start.2 = (bf16[3,64,768]{2,1,0:T(8,128)(2,1)S(1)}, bf16[3,64,768]{2,1,0:T(8,128)(2,1)S(1)}, u32[]{:S(2)}, u32[]{:S(2)}) collective-permute-start(bf16[3,64,768]{2,1,0:T(8,128)(2,1)S(1)} %get-tuple-element.113.cot), channel_id=1, source_target_pairs={{0,1},{1,0},{2,3},{3,2},{4,5},{5,4},{6,7},{7,6},{8,9},{9,8},{10,11... | collective-permute-start | bytes 884744 | tf_op jit(solution)/shard_map/ppermute | solution.py:569
  21.7 1.6 %collective-permute-start.10 = (bf16[3,64,768]{2,1,0:T(8,128)(2,1)S(1)}, bf16[3,64,768]{2,1,0:T(8,128)(2,1)S(1)}, u32[]{:S(2)}, u32[]{:S(2)}) collective-permute-start(bf16[3,64,768]{2,1,0:T(8,128)(2,1)S(1)} %shard_map.293.c2), channel_id=1, source_target_pairs={{0,1},{1,0},{2,3},{3,2},{4,5},{5,4},{6,7},{7,6},{8,9},{9,8},{10,11... | collective-permute-start | bytes 884744 | tf_op jit(solution)/shard_map/ppermute | solution.py:569
  25.1 15.6 %collective-permute-start.13 = (bf16[4,96,768]{2,1,0:T(8,128)(2,1)S(1)}, bf16[4,96,768]{2,1,0:T(8,128)(2,1)S(1)}, u32[]{:S(2)}, u32[]{:S(2)}) collective-permute-start(bf16[4,96,768]{2,1,0:T(8,128)(2,1)S(1)} %get-tuple-element.154), channel_id=1, source_target_pairs={{0,4},{4,0},{8,12},{12,8},{16,20},{20,16},{24,28},{28,24},{1,5},{5... | collective-permute-start | bytes 1769480 | tf_op jit(solution)/shard_map/ppermute | solution.py:577
  29.1 3.5 %collective-permute-start.11 = (bf16[432,384]{1,0:T(8,128)(2,1)S(1)}, bf16[432,384]{1,0:T(8,128)(2,1)S(1)}, u32[]{:S(2)}, u32[]{:S(2)}) collective-permute-start(bf16[432,384]{1,0:T(8,128)(2,1)S(1)} %get-tuple-element.137.l_a), channel_id=1, source_target_pairs={{0,1},{1,0},{2,3},{3,2},{4,5},{5,4},{6,7},{7,6},{8,9},{9,8},{10,11... | collective-permute-start | bytes 995336 | tf_op jit(solution)/shard_map/ppermute | solution.py:569
  29.2 3.4 %collective-permute-start.12 = (bf16[432,384]{1,0:T(8,128)(2,1)S(1)}, bf16[432,384]{1,0:T(8,128)(2,1)S(1)}, u32[]{:S(2)}, u32[]{:S(2)}) collective-permute-start(bf16[432,384]{1,0:T(8,128)(2,1)S(1)} %get-tuple-element.138.r_a), channel_id=1, source_target_pairs={{0,1},{1,0},{2,3},{3,2},{4,5},{5,4},{6,7},{7,6},{8,9},{9,8},{10,11... | collective-permute-start | bytes 995336 | tf_op jit(solution)/shard_map/ppermute | solution.py:569
  30.9 15.6 %collective-permute-start.17 = (bf16[4,48,1536]{2,1,0:T(8,128)(2,1)S(1)}, bf16[4,48,1536]{2,1,0:T(8,128)(2,1)S(1)}, u32[]{:S(2)}, u32[]{:S(2)}) collective-permute-start(bf16[4,48,1536]{2,1,0:T(8,128)(2,1)S(1)} %get-tuple-element.164), channel_id=1, source_target_pairs={{0,8},{4,12},{8,0},{12,4},{16,24},{20,28},{24,16},{28,20},{1,9},{5... | collective-permute-start | bytes 1769480 | tf_op jit(solution)/shard_map/ppermute | solution.py:581
  39.0 16.3 %collective-permute-start.16 = (bf16[4,48,1536]{2,1,0:T(8,128)(2,1)S(1)}, bf16[4,48,1536]{2,1,0:T(8,128)(2,1)S(1)}, u32[]{:S(2)}, u32[]{:S(2)}) collective-permute-start(bf16[4,48,1536]{2,1,0:T(8,128)(2,1)S(1)} %get-tuple-element.162), channel_id=1, source_target_pairs={{0,4},{4,0},{8,12},{12,8},{16,20},{20,16},{24,28},{28,24},{1,5},{5... | collective-permute-start | bytes 1769480 | tf_op jit(solution)/shard_map/ppermute | solution.py:577
  40.9 19.1 %collective-permute-start.15 = (bf16[4,96,768]{2,1,0:T(8,128)(2,1)S(1)}, bf16[4,96,768]{2,1,0:T(8,128)(2,1)S(1)}, u32[]{:S(2)}, u32[]{:S(2)}) collective-permute-start(bf16[4,96,768]{2,1,0:T(8,128)(2,1)S(1)} %get-tuple-element.160), channel_id=1, source_target_pairs={{1,17},{3,19},{5,21},{7,23},{9,25},{11,27},{13,29},{15,31},{16,0},... | collective-permute-start | bytes 1769480 | tf_op jit(solution)/shard_map/ppermute | solution.py:586
  46.7 15.3 %collective-permute-start.19 = (bf16[2,48,1792]{2,1,0:T(8,128)(2,1)S(1)}, bf16[2,48,1792]{2,1,0:T(8,128)(2,1)S(1)}, u32[]{:S(2)}, u32[]{:S(2)}) collective-permute-start(bf16[2,48,1792]{2,1,0:T(8,128)(2,1)S(1)} %get-tuple-element.173), channel_id=1, source_target_pairs={{0,4},{4,0},{8,12},{12,8},{16,20},{20,16},{24,28},{28,24},{1,5},{5... | collective-permute-start | bytes 1032200 | tf_op jit(solution)/shard_map/ppermute | solution.py:577
  48.5 25.4 %collective-permute-start.14 = (bf16[2,3,64,768]{3,2,1,0:T(8,128)(2,1)S(1)}, bf16[2,3,64,768]{3,2,1,0:T(8,128)(2,1)S(1)}, u32[]{:S(2)}, u32[]{:S(2)}) collective-permute-start(bf16[2,3,64,768]{3,2,1,0:T(8,128)(2,1)S(1)} %get-tuple-element.158), channel_id=1, source_target_pairs={{0,1},{1,0},{2,3},{3,2},{4,5},{5,4},{6,7},{7,6},{8,9},{9,8},{10,11... | collective-permute-start | bytes 1769480 | tf_op jit(solution)/shard_map/ppermute | solution.py:569
  55.4 17.6 %collective-permute-start.21 = (bf16[2,48,1536]{2,1,0:T(8,128)(2,1)S(1)}, bf16[2,48,1536]{2,1,0:T(8,128)(2,1)S(1)}, u32[]{:S(2)}, u32[]{:S(2)}) collective-permute-start(bf16[2,48,1536]{2,1,0:T(8,128)(2,1)S(1)} %get-tuple-element.178), channel_id=1, source_target_pairs={{0,8},{4,12},{8,0},{12,4},{16,24},{20,28},{24,16},{28,20},{1,9},{5... | collective-permute-start | bytes 884744 | tf_op jit(solution)/shard_map/ppermute | solution.py:581
  60.1 13.1 %collective-permute-start.18 = (bf16[2,96,768]{2,1,0:T(8,128)(2,1)S(1)}, bf16[2,96,768]{2,1,0:T(8,128)(2,1)S(1)}, u32[]{:S(2)}, u32[]{:S(2)}) collective-permute-start(bf16[2,96,768]{2,1,0:T(8,128)(2,1)S(1)} %get-tuple-element.171), channel_id=1, source_target_pairs={{0,8},{2,10},{4,12},{6,14},{8,0},{10,2},{12,4},{14,6},{17,25},{19,... | collective-permute-start | bytes 884744 | tf_op jit(solution)/shard_map/ppermute | solution.py:586
  62.1 11.1 %collective-permute-start.20 = (bf16[1,48,1536]{2,1,0:T(8,128)(2,1)S(1)}, bf16[1,48,1536]{2,1,0:T(8,128)(2,1)S(1)}, u32[]{:S(2)}, u32[]{:S(2)}) collective-permute-start(bf16[1,48,1536]{2,1,0:T(8,128)(2,1)S(1)} %get-tuple-element.176), channel_id=1, source_target_pairs={{0,16},{4,20},{8,24},{12,28},{16,0},{20,4},{24,8},{28,12},{1,17},{... | collective-permute-start | bytes 442376 | tf_op jit(solution)/shard_map/ppermute | solution.py:581
  64.2 8.9 %collective-permute-start.22 = (bf16[2,48,128]{2,1,0:T(8,128)(2,1)S(1)}, bf16[2,48,128]{2,1,0:T(8,128)(2,1)S(1)}, u32[]{:S(2)}, u32[]{:S(2)}) collective-permute-start(bf16[2,48,128]{2,1,0:T(8,128)(2,1)S(1)} %get-tuple-element.180), channel_id=1, source_target_pairs={{0,8},{4,12},{8,0},{12,4},{16,24},{20,28},{24,16},{28,20},{1,9},{5... | collective-permute-start | bytes 73736 | tf_op jit(solution)/shard_map/ppermute | solution.py:581
  73.1 8.1 %collective-permute-start.23 = (bf16[1,48,1664]{2,1,0:T(8,128)(2,1)S(1)}, bf16[1,48,1664]{2,1,0:T(8,128)(2,1)S(1)}, u32[]{:S(2)}, u32[]{:S(2)}) collective-permute-start(bf16[1,48,1664]{2,1,0:T(8,128)(2,1)S(1)} %get-tuple-element.187), channel_id=1, source_target_pairs={{0,16},{4,20},{8,24},{12,28},{16,0},{20,4},{24,8},{28,12},{1,17},{... | collective-permute-start | bytes 479240 | tf_op jit(solution)/shard_map/ppermute | solution.py:581
  73.4 9.9 %collective-permute-start.26 = (f32[96,768]{1,0:T(8,128)S(1)}, f32[96,768]{1,0:T(8,128)S(1)}, u32[]{:S(2)}, u32[]{:S(2)}) collective-permute-start(f32[96,768]{1,0:T(8,128)S(1)} %get-tuple-element.195), channel_id=1, source_target_pairs={{0,1},{1,0},{2,3},{3,2},{4,5},{5,4},{6,7},{7,6},{8,9},{9,8},{10,11... | collective-permute-start | bytes 884744 | tf_op jit(solution)/shard_map/ppermute | solution.py:569
  73.4 9.8 %collective-permute-start.25 = (f32[24,1536]{1,0:T(8,128)S(1)}, f32[24,1536]{1,0:T(8,128)S(1)}, u32[]{:S(2)}, u32[]{:S(2)}) collective-permute-start(f32[24,1536]{1,0:T(8,128)S(1)} %get-tuple-element.193), channel_id=1, source_target_pairs={{0,1},{1,0},{2,3},{3,2},{4,5},{5,4},{6,7},{7,6},{8,9},{9,8},{10,11... | collective-permute-start | bytes 442376 | tf_op jit(solution)/shard_map/ppermute | solution.py:569
  81.9 1.4 %collective-permute-start.24 = (f32[24,1408]{1,0:T(8,128)S(1)}, f32[24,1408]{1,0:T(8,128)S(1)}, u32[]{:S(2)}, u32[]{:S(2)}) collective-permute-start(f32[24,1408]{1,0:T(8,128)S(1)} %get-tuple-element.191), channel_id=1, source_target_pairs={{0,1},{1,0},{2,3},{3,2},{4,5},{5,4},{6,7},{7,6},{8,9},{9,8},{10,11... | collective-permute-start | bytes 405512 | tf_op jit(solution)/shard_map/ppermute | solution.py:569

commit v5 on v4

--- a/solution.py
+++ b/solution.py
@@ -96,7 +96,8 @@
     for k, block in enumerate(blocks):
         at = pl.multiple_of((band ^ k) * BAND, BAND)
         for i in range(IMGS):
-            dst[i, pl.ds(at, BAND), :] = block[i]
+            rows = block[i] if len(block.shape) == 3 else block[i * BAND : (i + 1) * BAND, :]
+            dst[i, pl.ds(at, BAND), :] = rows
 
 
 def two_heads(v):
@@ -119,9 +120,13 @@
 GAIN1, BIAS1, QB, VB, PB, ASC, GAIN2, BIAS2, RB, MSC = range(10)
 
 
+OWN = IMGS * BAND
+
+
 def prepare_kernel(
-    cot, gain1, bias1, qvb, bp, asc, gain2, bias2, br, msc, be, wqkv, wp, we, wr, vis, tok,
-    cot_o, tok_o, par_o, be_o, wqkv_o, wp_o, we_o, wr_o, vis_o, sems,
+    cot, gain1, bias1, qvb, bp, asc, gain2, bias2, br, msc, be, wqkv, wp, we, wr, visible, tok,
+    cot_o, own_o, par_o, be_o, wqkv_o, wp_o, we_o, wr_o, vis_o,
+    vis, sems,
 ):
     c = lax.axis_index("band") & 1
     units = pl.multiple_of(c * FH, 128)
@@ -134,23 +139,32 @@
     for m in range(3):
         moves.append((wqkv.at[:, pl.ds(pl.multiple_of(m * D + c * HALF, 128), HALF)], wqkv_o.at[m]))
     moves += [(wp, wp_o), (we.at[:, pl.ds(units, FH)], we_o), (wr.at[pl.ds(units, FH), :], wr_o)]
-    moves += [(vis, vis_o), (tok, tok_o)]
+    moves += [(tok.at[i], own_o.at[pl.ds(i * BAND, BAND), :]) for i in range(IMGS)]
+    moves += [(visible, vis)]
     copies = [pltpu.make_async_copy(a, b, sems.at[i]) for i, (a, b) in enumerate(moves)]
     for copy in copies:
         copy.start()
-    for copy in copies:
+    copies[-1].wait()
+    seen = jnp.concatenate([vis[...].astype(F32), jnp.zeros((IMGS, 128 - BAND), F32)], axis=1)
+    seen = jnp.concatenate([seen, jnp.zeros((16 - IMGS, 128), F32)], axis=0).astype(BF)
+    vis_o[...] = seen
+    own_o[OWN:, :] = jnp.zeros((16, D), BF)
+    own_o[OWN:, 0:128] = seen
+    for copy in copies[:-1]:
         copy.wait()
 
 
-def hold_kernel(cot, tok, after_a, after_b, cot_o, tok_o):
-    cot_o[...] = cot[...]
-    tok_o[...] = tok[...]
+def hold_kernel(tok, vis, after, out):
+    for i in range(IMGS):
+        out[i * BAND : (i + 1) * BAND, :] = tok[i]
+    out[OWN:, :] = jnp.zeros((16, D), BF)
+    out[OWN:, 0:128] = vis[...]
 
 
 def first_kernel(
-    t0, t1, t2, t3, v0, v1, v2, v3, par, w,
+    t0, t1, t2, t3, par, w,
     tok_o, norm_o, qkv_o, mix_o, mix2_o, pos_o, probs_o, mine_o, theirs_o,
-    xs, shown,
+    xs,
 ):
     band = lax.axis_index("band")
     c = band & 1
@@ -158,10 +172,8 @@
     heads = pl.multiple_of(c * HALF, 128)
     to = lax.broadcasted_iota(jnp.int32, (BAND, SLOTS), 1) - lax.broadcasted_iota(jnp.int32, (BAND, SLOTS), 0)
     vis = jnp.zeros((16, SLOTS), F32)
-    shown[...] = jnp.zeros_like(shown)
-    for k, v in enumerate((v0, v1, v2, v3)):
-        shown[0:IMGS, 0:BAND] = v[...].astype(F32)
-        vis = vis + dot(shown[:, 0:BAND].astype(BF), jnp.where(to == (band ^ k) * BAND, 1.0, 0.0).astype(BF))
+    for k, t in enumerate((t0, t1, t2, t3)):
+        vis = vis + dot(t[OWN:, 0:BAND], jnp.where(to == (band ^ k) * BAND, 1.0, 0.0).astype(BF))
     upto = lax.broadcasted_iota(jnp.int32, (SLOTS, SLOTS), 0)
     slot = lax.broadcasted_iota(jnp.int32, (SLOTS, SLOTS), 1)
     before = jnp.where(upto < slot, 1.0, 0.0).astype(BF)
@@ -292,7 +304,6 @@
 
 QC = 3 * HALF
 QW = QC + HALF
-QS = QW + SMALL
 FS = FH + 2 * SMALL
 
 
@@ -406,7 +417,7 @@
     for i in range(IMGS):
         rows = slice(i * PACK, (i + 1) * PACK)
         pack = one_hot_pack(mine[...], i)
-        z1, rstd1 = statistics(tok[i].astype(F32))
+        z1, rstd1 = statistics(tok[i * BAND : (i + 1) * BAND, :].astype(F32))
         gnp = gb_a[0, i].astype(F32) + gb_b[0, i].astype(F32)
         gtok = own_rows(pack, gres[rows, :]) + norm_back(gnp * par[GAIN1 : GAIN1 + 1, :], z1, rstd1)
         gtok_o[i] = gtok.astype(BF)
@@ -472,28 +483,22 @@
         vec_so[hi] = total[:, SMALL:].astype(BF)
 
 
-def rejoin_kernel(keep, arrived, vec_k, vec_a, after, keep_o, send_o, tick):
-    tick[...] = jnp.zeros_like(tick)
-    fold(keep, arrived, keep_o.at[:, :, 0:QW], send_o.at[:, :, 0:QW])
-    fold(vec_k, vec_a, keep_o.at[:, :, QW:QS], send_o.at[:, :, QW:QS])
-
-
 def settle_kernel(wr_k, wr_a, we_k, we_a, after, wr_ko, wr_so, we_ko, we_so, tick, both):
     tick[...] = jnp.zeros_like(tick)
     c = lax.axis_index("band") & 1
     for at, out in ((c, wr_ko), (1 - c, wr_so)):
-        out[...] = wr_k[at] + wr_a[at].astype(F32)
+        out[...] = (wr_k[at] + wr_a[at].astype(F32)).astype(out.dtype)
     both[...] = we_k[0] + we_a[0].astype(F32)
     we_ko[...] = both[pl.ds(pl.multiple_of(c * 24, 8), 24), :]
     we_so[...] = both[pl.ds(pl.multiple_of(24 - c * 24, 8), 24), :]
 
 
-def finish_kernel(qp_k, qp_a, after, keep_o, send_o, vec_o, proj_o, sums):
+def finish_kernel(qp_k, qp_a, vec_k, vec_a, after, keep_o, send_o, vec_o, proj_o, sums):
     c = lax.axis_index("band") & 1
     sums[...] = qp_k[0] + qp_a[0].astype(F32)
     keep_o[...] = sums[pl.ds(pl.multiple_of(c * 24, 8), 24), 0:QC]
     send_o[:, 0:QC] = sums[pl.ds(pl.multiple_of(24 - c * 24, 8), 24), 0:QC]
-    vec = sums[:, QW:QS]
+    vec = vec_k[0] + vec_a[0].astype(F32)
     vec_o[...] = vec
     send_o[:, QC : QC + SMALL] = vec[0:24]
     send_o[:, QC + SMALL :] = vec[24:48]
@@ -506,7 +511,7 @@
     qkv_o, first_o, bias_o, qv_o, bp_o, asc_o, gain2_o, bias2_o, br_o, msc_o, eb_o, we_o, wr_o, both,
 ):
     _, c, z, _ = place()
-    wr_o[...] = jnp.where((z >> 1) == c, wr_keep[...], wr_arrived[...])
+    wr_o[...] = jnp.where((z >> 1) == c, wr_keep[...], wr_arrived[...].astype(F32))
     we_o[:, pl.ds(pl.multiple_of(c * FH, 128), FH)] = we_keep[...]
     we_o[:, pl.ds(pl.multiple_of((1 - c) * FH, 128), FH)] = we_arrived[...]
     for m in range(3):
@@ -538,7 +543,7 @@
     "vectors_kernel": (8000000000, 20000000),
     "fold_kernel": (0, 0),
     "second_fold_kernel": (0, 2000000),
-    "last_kernel": (0, 4000000),
+    "last_kernel": (0, 1000000),
     "spread_kernel": (0, 2000000),
     "finish_kernel": (0, 1000000),
     "out_kernel": (0, 1000000),
@@ -593,22 +598,22 @@
     block = vm(cotangent.shape, BF)
     rows_f, rows_b = vm((ROWS, D), F32), vm((ROWS, D), BF)
     tok_x = by_x(tokens)
-    tok_c = by_core(tokens)
+    tok_block = vm((OWN + 16, D), BF)
     cot, tok_own, par, be, wqkv, wp, we, wr, vis = call(
         prepare_kernel,
         (
             block,
-            block,
+            tok_block,
             vm((16, D), F32),
             vm((8, FH), F32),
             vm((3, D, HALF), BF),
             vm((D, D), BF),
             vm((D, FH), BF),
             vm((FH, D), BF),
-            vm(visible.shape, visible.dtype),
+            vm((16, 128), BF),
         ),
         [ANY] * 17,
-        [pltpu.SemaphoreType.DMA((20,))]
+        [pltpu.VMEM(visible.shape, jnp.int32), pltpu.SemaphoreType.DMA((22,))],
     )(
         *map(
             stay,
@@ -620,11 +625,10 @@
         )
     )
     vis_x = by_x(vis)
-    vis_c = by_core(vis)
+    tok_c = by_core(tok_own)
     cot_c = by_core(cot)
-    cot, tok_x = call(hold_kernel, (block, block), [VM] * 2 + [ANY] * 2)(cot, tok_x, vis_x, par)
+    tok_x = call(hold_kernel, tok_block, [VM] * 2 + [ANY])(tok_x, vis_x, par)
     tok_d = by_core(tok_x)
-    vis_d = by_core(vis_x)
     cot_x = by_x(cot)
     tok, normed, qkv, mix_own, mix2_own, pos, probs, pos_mine, pos_theirs = call(
         first_kernel,
@@ -639,9 +643,9 @@
             vm((16, BAND), F32),
             vm((16, BAND), F32),
         ),
-        [VM] * 10,
-        [pltpu.VMEM((IMGS, SLOTS, D), BF), pltpu.VMEM((16, 128), F32)],
-    )(tok_own, tok_c, tok_x, tok_d, vis, vis_c, vis_x, vis_d, par, wqkv)
+        [VM] * 6,
+        [pltpu.VMEM((IMGS, SLOTS, D), BF)],
+    )(tok_own, tok_c, tok_x, tok_d, par, wqkv)
     mix_other, mix2_other = by_core(mix_own), by_core(mix2_own)
     pick, pick_p, pn = call(pick_kernel, (vm((D, HALF), BF), vm((D, 192), BF), vm((ROWS, HALF), BF)), [VM])(normed)
     res, one, n2, mix, act, slope, tick = call(
@@ -702,28 +706,28 @@
     )(we_keep, we_y, tick)
     vec_z = by_z(vec_send, 1)
     we_z = by_z(we_send, 2)
-    qp_keep, qp_send, tick = call(
-        rejoin_kernel, (vm((1, 48, QS), F32), vm((1, 48, QS), BF), TICK), [VM] * 4 + [ANY]
-    )(qp_keep, qp_z, vec_keep, vec_z, tick)
-    qp_z = by_z(qp_send, 2)
-    wr_keep, wr_send, we_keep, we_send, tick = call(
-        settle_kernel,
-        (vm((96, D), F32), vm((96, D), F32), vm((24, FH), F32), vm((24, FH), F32), TICK),
-        [VM] * 4 + [ANY],
-        [pltpu.VMEM((48, FH), F32)],
-    )(wr_keep, wr_z, we_keep, we_z, tick)
-    we_other, wr_other = by_core(we_send), by_core(wr_send)
     layer_out, grad_tokens, tick = call(
         last_kernel,
         (sds(tokens.shape, BF), sds(tokens.shape, BF), TICK),
         [VM] * 7 + [ANY],
     )(gb_keep, gb_other, tok_own, gres, res, pos_mine, par, tick)
+    qp_keep, qp_send, tick = fold_call(qp_keep, qp_z, tick)
+    qp_z = by_z(qp_send, 2)
+    vec_keep, vec_send, tick = fold_call(vec_keep, vec_z, tick)
+    vec_z = by_z(vec_send, 2)
+    wr_keep, wr_send, we_keep, we_send, tick = call(
+        settle_kernel,
+        (vm((96, D), F32), vm((96, D), BF), vm((24, FH), F32), vm((24, FH), F32), TICK),
+        [VM] * 4 + [ANY],
+        [pltpu.VMEM((48, FH), F32)],
+    )(wr_keep, wr_z, we_keep, we_z, tick)
+    we_other, wr_other = by_core(we_send), by_core(wr_send)
     qp_keep, qp_send, vec, proj = call(
         finish_kernel,
         (vm((24, QC), F32), vm((24, QC + 2 * SMALL), F32), vm((48, SMALL), F32), sds((24, D), F32)),
-        [VM] * 2 + [ANY],
-        [pltpu.VMEM((48, QS), F32)],
-    )(qp_keep, qp_z, tick)
+        [VM] * 4 + [ANY],
+        [pltpu.VMEM((48, QW), F32)],
+    )(qp_keep, qp_z, vec_keep, vec_z, tick)
     vector = sds((24,), F32)
     grad_qkv, gg1, gb1, gqv, gbp, gas, gg2, gb2, gbr, gms, geb, grad_expand, grad_reduce = call(
         out_kernel,

time: 84.5 us -> 80.2 us (0.949)
  waiting for transfers between devices: 29.7 us -> 21.7 us
  starting transfers between devices: 22.2 us -> 25.9 us
    ppermute x5 -> x6, waiting for transfers between devices: 13.5 us -> 6.32 us  [by_z(): return lax.ppermute(value, 'batch', [(i, i ^ 2 * dz) for i in range(8)])]
    ppermute x5 -> x6, starting transfers between devices: 5.13 us -> 9.26 us  [by_z(): return lax.ppermute(value, 'batch', [(i, i ^ 2 * dz) for i in range(8)])]
    ppermute x14 -> x12, waiting for transfers between devices: 2.69 us -> 2.21 us  [by_core(): return lax.ppermute(value, 'band', [(i, i ^ 1) for i in range(4)])]
    ppermute x14 -> x12, starting transfers between devices: 5.03 us -> 4.7 us  [by_core(): return lax.ppermute(value, 'band', [(i, i ^ 1) for i in range(4)])]
    pallas_call x4 -> x3, Pallas kernels: 3.92 us -> 3.84 us  [the longest x1 3.7 us: packed_body(): call(prepare_kernel, (block, tok_block, vm((16, D), F32), vm((8, FH), F32...]
  transfers between devices with their start and end apart: 27 -> 26, of which waited for: 11 -> 11; matrix products, arithmetic and copies ran while one was open for 0% -> 0% of each run, Pallas kernels for 34% -> 36%
where the time goes in v5:
time: 80.2 us; the launch traced here: 79.9 us
  Pallas kernels  31.4 us (39%)
  starting transfers between devices  25.9 us (32%)
  waiting for transfers between devices  21.7 us (27%)
  between operations  0.95 us (1%)
    ppermute x6, starting transfers between devices, by_z(): return lax.ppermute(value, 'batch', [(i, i ^ 2 * dz) for i in range(8)])  9.26 us
    pallas_call x1, Pallas kernels, packed_body(): call(attention_back_kernel, (rows_f, vm((ROWS, QC), BF), vm((4, 48, QW),...  6.36 us
    ppermute x6, waiting for transfers between devices, by_z(): return lax.ppermute(value, 'batch', [(i, i ^ 2 * dz) for i in range(8)])  6.32 us
    ppermute x3, waiting for transfers between devices, by_y(): return lax.ppermute(value, 'batch', [(i, i ^ 1) for i in range(8)])  5.67 us
    ppermute x3, starting transfers between devices, by_x(): return lax.ppermute(value, 'band', [(i, i ^ 2) for i in range(4)])  4.83 us
    ppermute x12, starting transfers between devices, by_core(): return lax.ppermute(value, 'band', [(i, i ^ 1) for i in range(4)])  4.7 us
    pallas_call x1, Pallas kernels, packed_body(): call(vectors_kernel, (vm((2, *tokens.shape), BF), vm((2, *tokens.shape),...  4.37 us
    ppermute x3, starting transfers between devices, by_y(): return lax.ppermute(value, 'batch', [(i, i ^ 1) for i in range(8)])  3.87 us
  transfers between devices with their start and end apart: 26, of which 11 were waited for; matrix products, arithmetic and copies ran while one was open for 0% of the time, Pallas kernels for 36%

profile of v5, /device:TPU:0, one launch (start us, length us, event | category | flops | bytes accessed | tf_op | source)
XLA Modules:
  0.0 79.9 jit_solution(4863114182446747620)
XLA Ops:
  0.6 3.0 %collective-permute-start.3 = (bf16[3,64,768]{2,1,0:T(8,128)(2,1)}, bf16[3,64,768]{2,1,0:T(8,128)(2,1)S(1)}, u32[]{:S(2)}, u32[]{:S(2)}) collective-permute-start(bf16[3,64,768]{2,1,0:T(8,128)(2,1)} %tok.1), channel_id=1, source_target_pairs={{0,2},{1,3},{2,0},{3,1},{4,6},{5,7},{6,4},{7,5},{8,10},{9,11},{10,... | collective-permute-start | bytes 884744 | tf_op jit(solution)/shard_map/ppermute | solution.py:578
  3.7 3.7 %shard_map.288 = (bf16[3,64,768]{2,1,0:T(8,128)(2,1)S(1)}, bf16[208,768]{1,0:T(8,128)(2,1)S(1)}, f32[16,768]{1,0:T(8,128)S(1)}, f32[8,1536]{1,0:T(8,128)S(1)}, b...) custom-call(bf16[3,64,768]{2,1,0:T(8,128)(2,1)} %cot.1, ...), custom_call_target="tpu_custom_call" | custom-call | bytes 9000000 | tf_op jit(solution)/shard_map/pallas_call | solution.py:602
  7.5 3.5 %collective-permute-done.4.vis = bf16[16,128]{1,0:T(8,128)(2,1)S(1)} collective-permute-done((bf16[16,128]{1,0:T(8,128)(2,1)S(1)}, bf16[16,128]{1,0:T(8,128)(2,1)S(1)}, u32[]{:S(2)}, u32[]{:S(2)}) %collective-permute-start.4) | collective-permute-done | bytes 4128 | tf_op jit(solution)/shard_map/ppermute | solution.py:578
  11.1 1.7 %collective-permute-start.1 = (bf16[3,64,768]{2,1,0:T(8,128)(2,1)S(1)}, bf16[3,64,768]{2,1,0:T(8,128)(2,1)S(1)}, u32[]{:S(2)}, u32[]{:S(2)}) collective-permute-start(bf16[3,64,768]{2,1,0:T(8,128)(2,1)S(1)} %get-tuple-element.114.c0), channel_id=1, source_target_pairs={{0,2},{1,3},{2,0},{3,1},{4,6},{5,7},{6,4},{7,5},{8,10},{9,11},{10,... | collective-permute-start | bytes 884744 | tf_op jit(solution)/shard_map/ppermute | solution.py:578
  12.9 3.5 %shard_map.290 = (bf16[432,768]{1,0:T(8,128)(2,1)S(1)}, bf16[432,768]{1,0:T(8,128)(2,1)S(1)}, bf16[3,432,384]{2,1,0:T(8,128)(2,1)S(1)}, bf16[432,256]{1,0:T(8,12...) custom-call(bf16[208,768]{1,0:T(8,128)(2,1)S(1)} %get-tuple-element., ...), custom_call_target="tpu_custom_call" | custom-call | tf_op jit(solution)/shard_map/pallas_call | solution.py:633
  16.4 0.2 collective-permute-start.6
  16.6 0.3 collective-permute-start.7
  17.0 0.2 collective-permute-start
  17.1 0.6 shard_map.291
  17.7 0.4 collective-permute-done.7.mix2_b
  18.1 2.2 %shard_map.292 = (f32[432,768]{1,0:T(8,128)S(1)}, f32[432,768]{1,0:T(8,128)S(1)}, bf16[432,768]{1,0:T(8,128)(2,1)S(1)}, bf16[432,768]{1,0:T(8,128)(2,1)S(1)}, bf...) custom-call(bf16[432,256]{1,0:T(8,128)(2,1)S(1)} %get-tuple-element.119.mix_a, ...), custom_call_target="tpu_custom_call" | custom-call | tf_op jit(solution)/shard_map/pallas_call | solution.py:651
  20.3 0.2 collective-permute-done.1.v
  20.7 1.0 %shard_map.294 = (bf16[432,768]{1,0:T(8,128)(2,1)S(1)}, f32[432,768]{1,0:T(8,128)S(1)}) custom-call(bf16[432,768]{1,0:T(8,128)(2,1)S(1)} %get-tuple-element.130.n2, f32[8,1536]{1,0:T(8,128)S(1)} %get-tuple-element.122.be, bf16[768,1536]{1,0:T(8,128)(2,1)S(1)} %get-tuple-element.124.we), custom_call_target="tpu_custom_call" | custom-call | tf_op jit(solution)/shard_map/pallas_call | solution.py:658
  21.7 0.6 collective-permute-done.8.c3
  22.2 1.7 %shard_map.295 = (bf16[432,768]{1,0:T(8,128)(2,1)S(1)}, bf16[432,768]{1,0:T(8,128)(2,1)S(1)}, bf16[4,96,768]{2,1,0:T(8,128)(2,1)S(1)}, bf16[4,96,768]{2,1,0:T(8,128)(2,1)S(1)}) custom-call(bf16[3,64,768]{2,1,0:T(8,128)(2,1)S(1)} %get-tuple-element.114.c0, bf16[3,64,768]{2,1,0:T(8,128)(2,1)S(1)} %collective-permute-done.c1, ...), custom_call_target="tpu_custom_call" | custom-call | flops 1000000000 | bytes 4000000 | tf_op jit(solution)/shard_map/pallas_call | solution.py:659
  24.0 1.8 %collective-permute-start.11 = (bf16[4,96,768]{2,1,0:T(8,128)(2,1)S(1)}, bf16[4,96,768]{2,1,0:T(8,128)(2,1)S(1)}, u32[]{:S(2)}, u32[]{:S(2)}) collective-permute-start(bf16[4,96,768]{2,1,0:T(8,128)(2,1)S(1)} %get-tuple-element.153), channel_id=1, source_target_pairs={{0,4},{4,0},{8,12},{12,8},{16,20},{20,16},{24,28},{28,24},{1,5},{5... | collective-permute-start | bytes 1769480 | tf_op jit(solution)/shard_map/ppermute | solution.py:582
  25.7 2.4 %shard_map.296 = (bf16[432,1536]{1,0:T(8,128)(2,1)S(1)}, bf16[432,384]{1,0:T(8,128)(2,1)S(1)}, bf16[432,384]{1,0:T(8,128)(2,1)S(1)}) custom-call(bf16[432,768]{1,0:T(8,128)(2,1)S(1)} %get-tuple-element.132.gb2, bf16[1536,768]{1,0:T(8,128)(2,1)S(1)} %get-tuple-element.133.wr, f32[432,768]{1,0:T(8,128)S(1)} %get-tuple-element.134.slope_a, ...), custom_call_target="tpu_custom_call" | custom-call | tf_op jit(solution)/shard_map/pallas_call | solution.py:667
  28.3 0.5 collective-permute-start.10
  28.8 1.2 %shard_map.297 = (bf16[4,48,1536]{2,1,0:T(8,128)(2,1)S(1)}, bf16[4,48,1536]{2,1,0:T(8,128)(2,1)S(1)}, f32[8,128]{1,0:T(8,128)S(1)}) custom-call(bf16[432,768]{1,0:T(8,128)(2,1)S(1)} %get-tuple-element.130.n2, bf16[432,1536]{1,0:T(8,128)(2,1)S(1)} %get-tuple-element.146.gh, bf16[768,384]{1,0:T(8,128)(2,1)S(1)} %get-tuple-element.126.after.pick), custom_call_target="tpu_custom_call" | custom-call | tf_op jit(solution)/shard_map/pallas_call | solution.py:669
  30.0 1.7 %collective-permute-start.13 = (bf16[4,48,1536]{2,1,0:T(8,128)(2,1)S(1)}, bf16[4,48,1536]{2,1,0:T(8,128)(2,1)S(1)}, u32[]{:S(2)}, u32[]{:S(2)}) collective-permute-start(bf16[4,48,1536]{2,1,0:T(8,128)(2,1)S(1)} %get-tuple-element.159), channel_id=1, source_target_pairs={{0,8},{4,12},{8,0},{12,4},{16,24},{20,28},{24,16},{28,20},{1,9},{5... | collective-permute-start | bytes 1769480 | tf_op jit(solution)/shard_map/ppermute | solution.py:586
  31.7 6.4 %shard_map.298 = (f32[432,768]{1,0:T(8,128)S(1)}, bf16[432,1152]{1,0:T(8,128)(2,1)S(1)}, bf16[4,48,1536]{2,1,0:T(8,128)(2,1)S(1)}, bf16[4,48,1536]{2,1,0:T(8,128)(2,1)S(1)}, f32[8,128]{1,0:T(8,128)S(1)}) custom-call(bf16[432,384]{1,0:T(8,128)(2,1)S(1)} %get-tuple-element.136.l_a, bf16[432,384]{1,0:T(8,128)(2,1)S(1)} %collective-permute-done.9.l_b, ...), custom_call_target="tpu_custom_call" | custom-call | tf_op jit(solution)/shard_map/pallas_call | solution.py:676
  38.0 0.5 collective-permute-start.16
  38.6 0.8 %collective-permute-done.11.arrived = bf16[4,96,768]{2,1,0:T(8,128)(2,1)S(1)} collective-permute-done((bf16[4,96,768]{2,1,0:T(8,128)(2,1)S(1)}, bf16[4,96,768]{2,1,0:T(8,128)(2,1)S(1)}, u32[]{:S(2)}, u32[]{:S(2)}) %collective-permute-start.11) | collective-permute-done | bytes 589856 | tf_op jit(solution)/shard_map/ppermute | solution.py:582
  39.4 0.2 shard_map.299
  39.6 1.3 %collective-permute-start.15 = (bf16[4,96,768]{2,1,0:T(8,128)(2,1)S(1)}, bf16[4,96,768]{2,1,0:T(8,128)(2,1)S(1)}, u32[]{:S(2)}, u32[]{:S(2)}) collective-permute-start(bf16[4,96,768]{2,1,0:T(8,128)(2,1)S(1)} %get-tuple-element.166), channel_id=1, source_target_pairs={{1,17},{3,19},{5,21},{7,23},{9,25},{11,27},{13,29},{15,31},{16,0},... | collective-permute-start | bytes 1769480 | tf_op jit(solution)/shard_map/ppermute | solution.py:591
  40.9 4.4 %shard_map.300 = (bf16[2,3,64,768]{3,2,1,0:T(8,128)(2,1)S(1)}, bf16[2,3,64,768]{3,2,1,0:T(8,128)(2,1)S(1)}, bf16[2,48,256]{2,1,0:T(8,128)(2,1)S(1)}, bf16[2,48,256]{2,1,0:T(8,128)(2,1)S(1)}, f32[8,128]{1,0:T(8,128)S(1)}) custom-call(bf16[432,384]{1,0:T(8,128)(2,1)S(1)} %get-tuple-element.136.l_a, bf16[432,384]{1,0:T(8,128)(2,1)S(1)} %collective-permute-done.9.l_b, ...), custom_call_target="tpu_custom_call" | custom-call | flops 8000000000 | bytes 20000000 | tf_op jit(solution)/shard_map/pallas_call | solution.py:687
  45.3 2.5 %collective-permute-start.12 = (bf16[2,3,64,768]{3,2,1,0:T(8,128)(2,1)S(1)}, bf16[2,3,64,768]{3,2,1,0:T(8,128)(2,1)S(1)}, u32[]{:S(2)}, u32[]{:S(2)}) collective-permute-start(bf16[2,3,64,768]{3,2,1,0:T(8,128)(2,1)S(1)} %get-tuple-element.157), channel_id=1, source_target_pairs={{0,1},{1,0},{2,3},{3,2},{4,5},{5,4},{6,7},{7,6},{8,9},{9,8},{10,11... | collective-permute-start | bytes 1769480 | tf_op jit(solution)/shard_map/ppermute | solution.py:574
  47.8 0.1 shard_map.301
  47.9 1.6 %collective-permute-start.14 = (bf16[2,48,1792]{2,1,0:T(8,128)(2,1)S(1)}, bf16[2,48,1792]{2,1,0:T(8,128)(2,1)S(1)}, u32[]{:S(2)}, u32[]{:S(2)}) collective-permute-start(bf16[2,48,1792]{2,1,0:T(8,128)(2,1)S(1)} %get-tuple-element.164), channel_id=1, source_target_pairs={{0,4},{4,0},{8,12},{12,8},{16,20},{20,16},{24,28},{28,24},{1,5},{5... | collective-permute-start | bytes 1032200 | tf_op jit(solution)/shard_map/ppermute | solution.py:582
  49.5 4.8 %collective-permute-done.16.arrived = bf16[4,48,1536]{2,1,0:T(8,128)(2,1)S(1)} collective-permute-done((bf16[4,48,1536]{2,1,0:T(8,128)(2,1)S(1)}, bf16[4,48,1536]{2,1,0:T(8,128)(2,1)S(1)}, u32[]{:S(2)}, u32[]{:S(2)}) %collective-permute-start.16) | collective-permute-done | bytes 589856 | tf_op jit(solution)/shard_map/ppermute | solution.py:582
  54.3 0.2 shard_map.302
  54.5 0.4 collective-permute-start.17
  54.9 3.7 %collective-permute-done.15.arrived = bf16[4,96,768]{2,1,0:T(8,128)(2,1)S(1)} collective-permute-done((bf16[4,96,768]{2,1,0:T(8,128)(2,1)S(1)}, bf16[4,96,768]{2,1,0:T(8,128)(2,1)S(1)}, u32[]{:S(2)}, u32[]{:S(2)}) %collective-permute-start.15) | collective-permute-done | bytes 589856 | tf_op jit(solution)/shard_map/ppermute | solution.py:591
  58.7 0.1 shard_map.303
  58.8 1.9 %collective-permute-start.21 = (bf16[2,96,768]{2,1,0:T(8,128)(2,1)S(1)}, bf16[2,96,768]{2,1,0:T(8,128)(2,1)S(1)}, u32[]{:S(2)}, u32[]{:S(2)}) collective-permute-start(bf16[2,96,768]{2,1,0:T(8,128)(2,1)S(1)} %get-tuple-element.186), channel_id=1, source_target_pairs={{0,8},{2,10},{4,12},{6,14},{8,0},{10,2},{12,4},{14,6},{17,25},{19,... | collective-permute-start | bytes 884744 | tf_op jit(solution)/shard_map/ppermute | solution.py:591
  60.8 2.4 %collective-permute-start.22 = (bf16[1,48,1536]{2,1,0:T(8,128)(2,1)S(1)}, bf16[1,48,1536]{2,1,0:T(8,128)(2,1)S(1)}, u32[]{:S(2)}, u32[]{:S(2)}) collective-permute-start(bf16[1,48,1536]{2,1,0:T(8,128)(2,1)S(1)} %get-tuple-element.188), channel_id=1, source_target_pairs={{0,16},{4,20},{8,24},{12,28},{16,0},{20,4},{24,8},{28,12},{1,17},{... | collective-permute-start | bytes 442376 | tf_op jit(solution)/shard_map/ppermute | solution.py:586
  63.2 1.8 %shard_map.305 = (bf16[3,64,768]{2,1,0:T(8,128)(2,1)}, bf16[3,64,768]{2,1,0:T(8,128)(2,1)}, f32[8,128]{1,0:T(8,128)S(1)}) custom-call(bf16[2,3,64,768]{3,2,1,0:T(8,128)(2,1)S(1)} %get-tuple-element.156.gb_a, bf16[2,3,64,768]{3,2,1,0:T(8,128)(2,1)S(1)} %collective-permute-done.12.gb_b, bf16[208,768]{1,0:T(8,128)(2,1)S(1)} %get-tuple-element.115.t0.tok, ...), custom_call_target="tpu_custom_call" | custom-call | bytes 1000000 | tf_op jit(solution)/shard_map/pallas_call | solution.py:709
  65.1 2.6 %collective-permute-done.17.arrived = bf16[2,48,1536]{2,1,0:T(8,128)(2,1)S(1)} collective-permute-done((bf16[2,48,1536]{2,1,0:T(8,128)(2,1)S(1)}, bf16[2,48,1536]{2,1,0:T(8,128)(2,1)S(1)}, u32[]{:S(2)}, u32[]{:S(2)}) %collective-permute-start.17) | collective-permute-done | bytes 294944 | tf_op jit(solution)/shard_map/ppermute | solution.py:586
  67.8 1.9 %collective-permute-start.19 = (bf16[2,48,128]{2,1,0:T(8,128)(2,1)S(1)}, bf16[2,48,128]{2,1,0:T(8,128)(2,1)S(1)}, u32[]{:S(2)}, u32[]{:S(2)}) collective-permute-start(bf16[2,48,128]{2,1,0:T(8,128)(2,1)S(1)} %get-tuple-element.181), channel_id=1, source_target_pairs={{0,8},{4,12},{8,0},{12,4},{16,24},{20,28},{24,16},{28,20},{1,9},{5... | collective-permute-start | bytes 73736 | tf_op jit(solution)/shard_map/ppermute | solution.py:586
  69.7 2.2 %collective-permute-done.19.arrived = bf16[2,48,128]{2,1,0:T(8,128)(2,1)S(1)} collective-permute-done((bf16[2,48,128]{2,1,0:T(8,128)(2,1)S(1)}, bf16[2,48,128]{2,1,0:T(8,128)(2,1)S(1)}, u32[]{:S(2)}, u32[]{:S(2)}) %collective-permute-start.19) | collective-permute-done | bytes 24608 | tf_op jit(solution)/shard_map/ppermute | solution.py:586
  71.9 2.7 %collective-permute-start.20 = (bf16[1,48,128]{2,1,0:T(8,128)(2,1)S(1)}, bf16[1,48,128]{2,1,0:T(8,128)(2,1)S(1)}, u32[]{:S(2)}, u32[]{:S(2)}) collective-permute-start(bf16[1,48,128]{2,1,0:T(8,128)(2,1)S(1)} %get-tuple-element.184), channel_id=1, source_target_pairs={{0,16},{4,20},{8,24},{12,28},{16,0},{20,4},{24,8},{28,12},{1,17},{... | collective-permute-start | bytes 36872 | tf_op jit(solution)/shard_map/ppermute | solution.py:586
  74.6 0.1 shard_map.308
  74.8 0.5 collective-permute-start.25
  75.3 1.5 %collective-permute-done.20.vec_a = bf16[1,48,128]{2,1,0:T(8,128)(2,1)S(1)} collective-permute-done((bf16[1,48,128]{2,1,0:T(8,128)(2,1)S(1)}, bf16[1,48,128]{2,1,0:T(8,128)(2,1)S(1)}, u32[]{:S(2)}, u32[]{:S(2)}) %collective-permute-start.20) | collective-permute-done | bytes 12320 | tf_op jit(solution)/shard_map/ppermute | solution.py:586
  76.9 0.7 shard_map.309
  77.6 0.1 collective-permute-start.23
  77.7 1.2 %collective-permute-done.23.arrived = f32[24,1408]{1,0:T(8,128)S(1)} collective-permute-done((f32[24,1408]{1,0:T(8,128)S(1)}, f32[24,1408]{1,0:T(8,128)S(1)}, u32[]{:S(2)}, u32[]{:S(2)}) %collective-permute-start.23) | collective-permute-done | bytes 135200 | tf_op jit(solution)/shard_map/ppermute | solution.py:574
  78.9 0.9 %shard_map.310 = (f32[24,2304]{1,0:T(8,128)}, f32[24]{0:T(128)}, f32[24]{0:T(128)}, f32[2,24]{1,0:T(2,128)}, f32[24]{0:T(128)}, /*index=5*/f32[24]{0:T(128)}, f3...) custom-call(f32[24,1152]{1,0:T(8,128)S(1)} %get-tuple-element.191.ke, ...), custom_call_target="tpu_custom_call" | custom-call | bytes 1000000 | tf_op jit(solution)/shard_map/pallas_call | solution.py:732
  (27 shorter events, 0.7 us)
Async XLA Ops:
  0.6 10.4 %collective-permute-start.3 = (bf16[3,64,768]{2,1,0:T(8,128)(2,1)}, bf16[3,64,768]{2,1,0:T(8,128)(2,1)S(1)}, u32[]{:S(2)}, u32[]{:S(2)}) collective-permute-start(bf16[3,64,768]{2,1,0:T(8,128)(2,1)} %tok.1), channel_id=1, source_target_pairs={{0,2},{1,3},{2,0},{3,1},{4,6},{5,7},{6,4},{7,5},{8,10},{9,11},{10,... | collective-permute-start | bytes 884744 | tf_op jit(solution)/shard_map/ppermute | solution.py:578
  7.4 3.7 %collective-permute-start.4 = (bf16[16,128]{1,0:T(8,128)(2,1)S(1)}, bf16[16,128]{1,0:T(8,128)(2,1)S(1)}, u32[]{:S(2)}, u32[]{:S(2)}) collective-permute-start(bf16[16,128]{1,0:T(8,128)(2,1)S(1)} %get-tuple-element.116), channel_id=1, source_target_pairs={{0,2},{1,3},{2,0},{3,1},{4,6},{5,7},{6,4},{7,5},{8,10},{9,11},{10,... | collective-permute-start | bytes 12296 | tf_op jit(solution)/shard_map/ppermute | solution.py:578
  7.5 5.4 %collective-permute-start.2 = (bf16[208,768]{1,0:T(8,128)(2,1)S(1)}, bf16[208,768]{1,0:T(8,128)(2,1)S(1)}, u32[]{:S(2)}, u32[]{:S(2)}) collective-permute-start(bf16[208,768]{1,0:T(8,128)(2,1)S(1)} %get-tuple-element.115.t0.tok), channel_id=1, source_target_pairs={{0,1},{1,0},{2,3},{3,2},{4,5},{5,4},{6,7},{7,6},{8,9},{9,8},{10,11... | collective-permute-start | bytes 958472 | tf_op jit(solution)/shard_map/ppermute | solution.py:574
  11.1 1.8 %collective-permute-start.5 = (bf16[208,768]{1,0:T(8,128)(2,1)S(1)}, bf16[208,768]{1,0:T(8,128)(2,1)S(1)}, u32[]{:S(2)}, u32[]{:S(2)}) collective-permute-start(bf16[208,768]{1,0:T(8,128)(2,1)S(1)} %shard_map.289.t2), channel_id=1, source_target_pairs={{0,1},{1,0},{2,3},{3,2},{4,5},{5,4},{6,7},{7,6},{8,9},{9,8},{10,11... | collective-permute-start | bytes 958472 | tf_op jit(solution)/shard_map/ppermute | solution.py:574
  11.1 9.4 %collective-permute-start.1 = (bf16[3,64,768]{2,1,0:T(8,128)(2,1)S(1)}, bf16[3,64,768]{2,1,0:T(8,128)(2,1)S(1)}, u32[]{:S(2)}, u32[]{:S(2)}) collective-permute-start(bf16[3,64,768]{2,1,0:T(8,128)(2,1)S(1)} %get-tuple-element.114.c0), channel_id=1, source_target_pairs={{0,2},{1,3},{2,0},{3,1},{4,6},{5,7},{6,4},{7,5},{8,10},{9,11},{10,... | collective-permute-start | bytes 884744 | tf_op jit(solution)/shard_map/ppermute | solution.py:578
  16.4 1.7 %collective-permute-start.6 = (bf16[432,256]{1,0:T(8,128)(2,1)S(1)}, bf16[432,256]{1,0:T(8,128)(2,1)S(1)}, u32[]{:S(2)}, u32[]{:S(2)}) collective-permute-start(bf16[432,256]{1,0:T(8,128)(2,1)S(1)} %get-tuple-element.119.mix_a), channel_id=1, source_target_pairs={{0,1},{1,0},{2,3},{3,2},{4,5},{5,4},{6,7},{7,6},{8,9},{9,8},{10,11... | collective-permute-start | bytes 663560 | tf_op jit(solution)/shard_map/ppermute | solution.py:574
  16.6 1.5 %collective-permute-start.7 = (bf16[432,128]{1,0:T(8,128)(2,1)S(1)}, bf16[432,128]{1,0:T(8,128)(2,1)S(1)}, u32[]{:S(2)}, u32[]{:S(2)}) collective-permute-start(bf16[432,128]{1,0:T(8,128)(2,1)S(1)} %get-tuple-element.120.mix2_a), channel_id=1, source_target_pairs={{0,1},{1,0},{2,3},{3,2},{4,5},{5,4},{6,7},{7,6},{8,9},{9,8},{10,11... | collective-permute-start | bytes 331784 | tf_op jit(solution)/shard_map/ppermute | solution.py:574
  17.0 4.7 %collective-permute-start = (bf16[3,64,768]{2,1,0:T(8,128)(2,1)S(1)}, bf16[3,64,768]{2,1,0:T(8,128)(2,1)S(1)}, u32[]{:S(2)}, u32[]{:S(2)}) collective-permute-start(bf16[3,64,768]{2,1,0:T(8,128)(2,1)S(1)} %get-tuple-element.114.c0), channel_id=1, source_target_pairs={{0,1},{1,0},{2,3},{3,2},{4,5},{5,4},{6,7},{7,6},{8,9},{9,8},{10,11... | collective-permute-start | bytes 884744 | tf_op jit(solution)/shard_map/ppermute | solution.py:574
  20.6 1.6 %collective-permute-start.8 = (bf16[3,64,768]{2,1,0:T(8,128)(2,1)S(1)}, bf16[3,64,768]{2,1,0:T(8,128)(2,1)S(1)}, u32[]{:S(2)}, u32[]{:S(2)}) collective-permute-start(bf16[3,64,768]{2,1,0:T(8,128)(2,1)S(1)} %shard_map.293.c2), channel_id=1, source_target_pairs={{0,1},{1,0},{2,3},{3,2},{4,5},{5,4},{6,7},{7,6},{8,9},{9,8},{10,11... | collective-permute-start | bytes 884744 | tf_op jit(solution)/shard_map/ppermute | solution.py:574
  24.0 15.4 %collective-permute-start.11 = (bf16[4,96,768]{2,1,0:T(8,128)(2,1)S(1)}, bf16[4,96,768]{2,1,0:T(8,128)(2,1)S(1)}, u32[]{:S(2)}, u32[]{:S(2)}) collective-permute-start(bf16[4,96,768]{2,1,0:T(8,128)(2,1)S(1)} %get-tuple-element.153), channel_id=1, source_target_pairs={{0,4},{4,0},{8,12},{12,8},{16,20},{20,16},{24,28},{28,24},{1,5},{5... | collective-permute-start | bytes 1769480 | tf_op jit(solution)/shard_map/ppermute | solution.py:582
  28.2 3.5 %collective-permute-start.9 = (bf16[432,384]{1,0:T(8,128)(2,1)S(1)}, bf16[432,384]{1,0:T(8,128)(2,1)S(1)}, u32[]{:S(2)}, u32[]{:S(2)}) collective-permute-start(bf16[432,384]{1,0:T(8,128)(2,1)S(1)} %get-tuple-element.136.l_a), channel_id=1, source_target_pairs={{0,1},{1,0},{2,3},{3,2},{4,5},{5,4},{6,7},{7,6},{8,9},{9,8},{10,11... | collective-permute-start | bytes 995336 | tf_op jit(solution)/shard_map/ppermute | solution.py:574
  28.3 3.4 %collective-permute-start.10 = (bf16[432,384]{1,0:T(8,128)(2,1)S(1)}, bf16[432,384]{1,0:T(8,128)(2,1)S(1)}, u32[]{:S(2)}, u32[]{:S(2)}) collective-permute-start(bf16[432,384]{1,0:T(8,128)(2,1)S(1)} %get-tuple-element.137.r_a), channel_id=1, source_target_pairs={{0,1},{1,0},{2,3},{3,2},{4,5},{5,4},{6,7},{7,6},{8,9},{9,8},{10,11... | collective-permute-start | bytes 995336 | tf_op jit(solution)/shard_map/ppermute | solution.py:574
  30.0 17.8 %collective-permute-start.13 = (bf16[4,48,1536]{2,1,0:T(8,128)(2,1)S(1)}, bf16[4,48,1536]{2,1,0:T(8,128)(2,1)S(1)}, u32[]{:S(2)}, u32[]{:S(2)}) collective-permute-start(bf16[4,48,1536]{2,1,0:T(8,128)(2,1)S(1)} %get-tuple-element.159), channel_id=1, source_target_pairs={{0,8},{4,12},{8,0},{12,4},{16,24},{20,28},{24,16},{28,20},{1,9},{5... | collective-permute-start | bytes 1769480 | tf_op jit(solution)/shard_map/ppermute | solution.py:586
  38.0 16.3 %collective-permute-start.16 = (bf16[4,48,1536]{2,1,0:T(8,128)(2,1)S(1)}, bf16[4,48,1536]{2,1,0:T(8,128)(2,1)S(1)}, u32[]{:S(2)}, u32[]{:S(2)}) collective-permute-start(bf16[4,48,1536]{2,1,0:T(8,128)(2,1)S(1)} %get-tuple-element.168), channel_id=1, source_target_pairs={{0,4},{4,0},{8,12},{12,8},{16,20},{20,16},{24,28},{28,24},{1,5},{5... | collective-permute-start | bytes 1769480 | tf_op jit(solution)/shard_map/ppermute | solution.py:582
  39.6 19.1 %collective-permute-start.15 = (bf16[4,96,768]{2,1,0:T(8,128)(2,1)S(1)}, bf16[4,96,768]{2,1,0:T(8,128)(2,1)S(1)}, u32[]{:S(2)}, u32[]{:S(2)}) collective-permute-start(bf16[4,96,768]{2,1,0:T(8,128)(2,1)S(1)} %get-tuple-element.166), channel_id=1, source_target_pairs={{1,17},{3,19},{5,21},{7,23},{9,25},{11,27},{13,29},{15,31},{16,0},... | collective-permute-start | bytes 1769480 | tf_op jit(solution)/shard_map/ppermute | solution.py:591
  45.3 18.0 %collective-permute-start.12 = (bf16[2,3,64,768]{3,2,1,0:T(8,128)(2,1)S(1)}, bf16[2,3,64,768]{3,2,1,0:T(8,128)(2,1)S(1)}, u32[]{:S(2)}, u32[]{:S(2)}) collective-permute-start(bf16[2,3,64,768]{3,2,1,0:T(8,128)(2,1)S(1)} %get-tuple-element.157), channel_id=1, source_target_pairs={{0,1},{1,0},{2,3},{3,2},{4,5},{5,4},{6,7},{7,6},{8,9},{9,8},{10,11... | collective-permute-start | bytes 1769480 | tf_op jit(solution)/shard_map/ppermute | solution.py:574
  47.9 12.8 %collective-permute-start.14 = (bf16[2,48,1792]{2,1,0:T(8,128)(2,1)S(1)}, bf16[2,48,1792]{2,1,0:T(8,128)(2,1)S(1)}, u32[]{:S(2)}, u32[]{:S(2)}) collective-permute-start(bf16[2,48,1792]{2,1,0:T(8,128)(2,1)S(1)} %get-tuple-element.164), channel_id=1, source_target_pairs={{0,4},{4,0},{8,12},{12,8},{16,20},{20,16},{24,28},{28,24},{1,5},{5... | collective-permute-start | bytes 1032200 | tf_op jit(solution)/shard_map/ppermute | solution.py:582
  54.5 13.2 %collective-permute-start.17 = (bf16[2,48,1536]{2,1,0:T(8,128)(2,1)S(1)}, bf16[2,48,1536]{2,1,0:T(8,128)(2,1)S(1)}, u32[]{:S(2)}, u32[]{:S(2)}) collective-permute-start(bf16[2,48,1536]{2,1,0:T(8,128)(2,1)S(1)} %get-tuple-element.176), channel_id=1, source_target_pairs={{0,8},{4,12},{8,0},{12,4},{16,24},{20,28},{24,16},{28,20},{1,9},{5... | collective-permute-start | bytes 884744 | tf_op jit(solution)/shard_map/ppermute | solution.py:586
  58.8 15.8 %collective-permute-start.21 = (bf16[2,96,768]{2,1,0:T(8,128)(2,1)S(1)}, bf16[2,96,768]{2,1,0:T(8,128)(2,1)S(1)}, u32[]{:S(2)}, u32[]{:S(2)}) collective-permute-start(bf16[2,96,768]{2,1,0:T(8,128)(2,1)S(1)} %get-tuple-element.186), channel_id=1, source_target_pairs={{0,8},{2,10},{4,12},{6,14},{8,0},{10,2},{12,4},{14,6},{17,25},{19,... | collective-permute-start | bytes 884744 | tf_op jit(solution)/shard_map/ppermute | solution.py:591
  60.8 13.8 %collective-permute-start.22 = (bf16[1,48,1536]{2,1,0:T(8,128)(2,1)S(1)}, bf16[1,48,1536]{2,1,0:T(8,128)(2,1)S(1)}, u32[]{:S(2)}, u32[]{:S(2)}) collective-permute-start(bf16[1,48,1536]{2,1,0:T(8,128)(2,1)S(1)} %get-tuple-element.188), channel_id=1, source_target_pairs={{0,16},{4,20},{8,24},{12,28},{16,0},{20,4},{24,8},{28,12},{1,17},{... | collective-permute-start | bytes 442376 | tf_op jit(solution)/shard_map/ppermute | solution.py:586
  67.7 9.1 %collective-permute-start.18 = (bf16[1,48,1536]{2,1,0:T(8,128)(2,1)S(1)}, bf16[1,48,1536]{2,1,0:T(8,128)(2,1)S(1)}, u32[]{:S(2)}, u32[]{:S(2)}) collective-permute-start(bf16[1,48,1536]{2,1,0:T(8,128)(2,1)S(1)} %get-tuple-element.179), channel_id=1, source_target_pairs={{0,16},{4,20},{8,24},{12,28},{16,0},{20,4},{24,8},{28,12},{1,17},{... | collective-permute-start | bytes 442376 | tf_op jit(solution)/shard_map/ppermute | solution.py:586
  67.8 4.1 %collective-permute-start.19 = (bf16[2,48,128]{2,1,0:T(8,128)(2,1)S(1)}, bf16[2,48,128]{2,1,0:T(8,128)(2,1)S(1)}, u32[]{:S(2)}, u32[]{:S(2)}) collective-permute-start(bf16[2,48,128]{2,1,0:T(8,128)(2,1)S(1)} %get-tuple-element.181), channel_id=1, source_target_pairs={{0,8},{4,12},{8,0},{12,4},{16,24},{20,28},{24,16},{28,20},{1,9},{5... | collective-permute-start | bytes 73736 | tf_op jit(solution)/shard_map/ppermute | solution.py:586
  71.9 5.0 %collective-permute-start.20 = (bf16[1,48,128]{2,1,0:T(8,128)(2,1)S(1)}, bf16[1,48,128]{2,1,0:T(8,128)(2,1)S(1)}, u32[]{:S(2)}, u32[]{:S(2)}) collective-permute-start(bf16[1,48,128]{2,1,0:T(8,128)(2,1)S(1)} %get-tuple-element.184), channel_id=1, source_target_pairs={{0,16},{4,20},{8,24},{12,28},{16,0},{20,4},{24,8},{28,12},{1,17},{... | collective-permute-start | bytes 36872 | tf_op jit(solution)/shard_map/ppermute | solution.py:586
  74.7 4.2 %collective-permute-start.24 = (f32[24,1536]{1,0:T(8,128)S(1)}, f32[24,1536]{1,0:T(8,128)S(1)}, u32[]{:S(2)}, u32[]{:S(2)}) collective-permute-start(f32[24,1536]{1,0:T(8,128)S(1)} %get-tuple-element.195), channel_id=1, source_target_pairs={{0,1},{1,0},{2,3},{3,2},{4,5},{5,4},{6,7},{7,6},{8,9},{9,8},{10,11... | collective-permute-start | bytes 442376 | tf_op jit(solution)/shard_map/ppermute | solution.py:574
  74.8 4.1 %collective-permute-start.25 = (bf16[96,768]{1,0:T(8,128)(2,1)S(1)}, bf16[96,768]{1,0:T(8,128)(2,1)S(1)}, u32[]{:S(2)}, u32[]{:S(2)}) collective-permute-start(bf16[96,768]{1,0:T(8,128)(2,1)S(1)} %get-tuple-element.197), channel_id=1, source_target_pairs={{0,1},{1,0},{2,3},{3,2},{4,5},{5,4},{6,7},{7,6},{8,9},{9,8},{10,11... | collective-permute-start | bytes 442376 | tf_op jit(solution)/shard_map/ppermute | solution.py:574
  77.6 1.4 %collective-permute-start.23 = (f32[24,1408]{1,0:T(8,128)S(1)}, f32[24,1408]{1,0:T(8,128)S(1)}, u32[]{:S(2)}, u32[]{:S(2)}) collective-permute-start(f32[24,1408]{1,0:T(8,128)S(1)} %get-tuple-element.193), channel_id=1, source_target_pairs={{0,1},{1,0},{2,3},{3,2},{4,5},{5,4},{6,7},{7,6},{8,9},{9,8},{10,11... | collective-permute-start | bytes 405512 | tf_op jit(solution)/shard_map/ppermute | solution.py:574

commit v6 on v5

--- a/solution.py
+++ b/solution.py
@@ -66,13 +66,13 @@
     x, c, z, y = place()
 
     def pick(width, base):
-        lane = lax.broadcasted_iota(jnp.int32, (1, 8 * width), 1)
-        want = jnp.zeros((1, 8 * width), jnp.int32)
+        row = lax.broadcasted_iota(jnp.int32, (8 * width, 1), 0)
+        want = jnp.zeros((8 * width, 1), jnp.int32)
         for q in range(8):
             first = 96 * ((z ^ (q % 4)) * 2 + (y ^ (q // 4))) + base - width * q
-            want = jnp.where((lane >= width * q) & (lane < width * (q + 1)), lane + first, want)
-        row = lax.broadcasted_iota(jnp.int32, (D, 8 * width), 0)
-        return jnp.where(row == want, 1.0, 0.0).astype(BF)
+            want = jnp.where((row >= width * q) & (row < width * (q + 1)), row + first, want)
+        lane = lax.broadcasted_iota(jnp.int32, (8 * width, D), 1)
+        return jnp.where(lane == want, 1.0, 0.0).astype(BF)
 
     return pick(48, 48 * x), pick(24, 48 * x + 24 * c)
 
@@ -96,8 +96,23 @@
     for k, block in enumerate(blocks):
         at = pl.multiple_of((band ^ k) * BAND, BAND)
         for i in range(IMGS):
-            rows = block[i] if len(block.shape) == 3 else block[i * BAND : (i + 1) * BAND, :]
-            dst[i, pl.ds(at, BAND), :] = rows
+            dst[i, pl.ds(at, BAND), :] = block(i)
+
+
+def images(ref):
+    return lambda i: ref[i] if len(ref.shape) == 3 else ref[i * BAND : (i + 1) * BAND, :]
+
+
+def images_of_two(a, b):
+    count = a.shape[0]
+
+    def block(i):
+        lo, hi = i * BAND, (i + 1) * BAND
+        parts = [a[lo : min(hi, count), :]] if lo < count else []
+        parts += [b[max(lo, count) - count : hi - count, :]] if hi > count else []
+        return parts[0] if len(parts) == 1 else jnp.concatenate(parts, axis=0)
+
+    return block
 
 
 def two_heads(v):
@@ -111,9 +126,15 @@
     return jnp.where(lane < HD, v[:PACK], v[PACK:])
 
 
+def head_pairs():
+    for i in range(IMGS):
+        for hp in range(3):
+            yield i, slice(i * PACK, (i + 1) * PACK), hp, slice(hp * 128, (hp + 1) * 128)
+
+
 def keys_shown(pos, image):
     shown = jnp.sum(jnp.where(pos[image : image + 1, :] >= 0, 1.0, 0.0), axis=-1, keepdims=True)
-    return lax.broadcasted_iota(jnp.int32, (1, PACK), 1).astype(F32) < shown
+    return lax.broadcasted_iota(jnp.int32, (PACK, 1), 0).astype(F32) < shown
 
 
 TICK = vm((8, 128), F32)
@@ -125,7 +146,7 @@
 
 def prepare_kernel(
     cot, gain1, bias1, qvb, bp, asc, gain2, bias2, br, msc, be, wqkv, wp, we, wr, visible, tok,
-    cot_o, own_o, par_o, be_o, wqkv_o, wp_o, we_o, wr_o, vis_o,
+    cot_o, own_o, par_o, be_o, wqkv_o, wp_o, we_o, wr_o, vis_o, pick_o, pick_p_o,
     vis, sems,
 ):
     c = lax.axis_index("band") & 1
@@ -137,7 +158,8 @@
     moves = [(cot, cot_o)] + [(v, par_o.at[r]) for r, v in rows]
     moves += [(be.at[pl.ds(units, FH)], be_o.at[0])]
     for m in range(3):
-        moves.append((wqkv.at[:, pl.ds(pl.multiple_of(m * D + c * HALF, 128), HALF)], wqkv_o.at[m]))
+        src = wqkv.at[:, pl.ds(pl.multiple_of(m * D + c * HALF, 128), HALF)]
+        moves.append((src, wqkv_o.at[:, pl.ds(m * HALF, HALF)]))
     moves += [(wp, wp_o), (we.at[:, pl.ds(units, FH)], we_o), (wr.at[pl.ds(units, FH), :], wr_o)]
     moves += [(tok.at[i], own_o.at[pl.ds(i * BAND, BAND), :]) for i in range(IMGS)]
     moves += [(visible, vis)]
@@ -147,40 +169,50 @@
     copies[-1].wait()
     seen = jnp.concatenate([vis[...].astype(F32), jnp.zeros((IMGS, 128 - BAND), F32)], axis=1)
     seen = jnp.concatenate([seen, jnp.zeros((16 - IMGS, 128), F32)], axis=0).astype(BF)
-    vis_o[...] = seen
+    vis_o[...] = jnp.zeros((16, D), BF)
+    vis_o[:, 0:128] = seen
     own_o[OWN:, :] = jnp.zeros((16, D), BF)
     own_o[OWN:, 0:128] = seen
+    pick_o[...], pick_p_o[...] = shard_picks()
     for copy in copies[:-1]:
         copy.wait()
 
 
-def hold_kernel(tok, vis, after, out):
+SPLIT = 224
+EARLY = 160
+
+
+def hold_kernel(tok, vis, after, out, rest):
+    count = out.shape[0]
     for i in range(IMGS):
-        out[i * BAND : (i + 1) * BAND, :] = tok[i]
-    out[OWN:, :] = jnp.zeros((16, D), BF)
-    out[OWN:, 0:128] = vis[...]
+        lo, hi = i * BAND, (i + 1) * BAND
+        if lo < count:
+            out[lo : min(hi, count), :] = tok[i, 0 : min(hi, count) - lo, :]
+        if hi > count:
+            rest[max(lo, count) - count : hi - count, :] = tok[i, max(lo, count) - lo :, :]
+    rest[OWN - count :, :] = vis[...]
 
 
 def first_kernel(
-    t0, t1, t2, t3, par, w,
-    tok_o, norm_o, qkv_o, mix_o, mix2_o, pos_o, probs_o, mine_o, theirs_o,
-    xs,
+    t0, t1, x_a, x_b, d_a, d_b, par, w,
+    tok_o, norm_o, qkv_o, mix_o, mix2_o, pos_o, probs_o, mine_o, theirs_o, far_o,
+    xs, mix,
 ):
     band = lax.axis_index("band")
     c = band & 1
-    gather_bands((t0, t1, t2, t3), xs)
+    gather_bands((images(t0), images(t1), images_of_two(x_a, x_b), images_of_two(d_a, d_b)), xs)
     heads = pl.multiple_of(c * HALF, 128)
     to = lax.broadcasted_iota(jnp.int32, (BAND, SLOTS), 1) - lax.broadcasted_iota(jnp.int32, (BAND, SLOTS), 0)
     vis = jnp.zeros((16, SLOTS), F32)
-    for k, t in enumerate((t0, t1, t2, t3)):
-        vis = vis + dot(t[OWN:, 0:BAND], jnp.where(to == (band ^ k) * BAND, 1.0, 0.0).astype(BF))
+    for k, t in enumerate((t0, t1, x_b, d_b)):
+        vis = vis + dot(t[t.shape[0] - 16 :, 0:BAND], jnp.where(to == (band ^ k) * BAND, 1.0, 0.0).astype(BF))
     upto = lax.broadcasted_iota(jnp.int32, (SLOTS, SLOTS), 0)
     slot = lax.broadcasted_iota(jnp.int32, (SLOTS, SLOTS), 1)
     before = jnp.where(upto < slot, 1.0, 0.0).astype(BF)
     pos = jnp.where(vis > 0, dot(vis.astype(BF), before), -1.0)
     pos_o[...] = pos[0:8]
     slot = lax.broadcasted_iota(jnp.int32, (SLOTS, BAND), 0) - lax.broadcasted_iota(jnp.int32, (SLOTS, BAND), 1)
-    for out, b in ((mine_o, band), (theirs_o, band ^ 1)):
+    for out, b in ((mine_o, band), (theirs_o, band ^ 1), (far_o, band ^ 3)):
         out[...] = dot(pos.astype(BF), jnp.where(slot == b * BAND, 1.0, 0.0).astype(BF))
     for i in range(IMGS):
         rows = slice(i * PACK, (i + 1) * PACK)
@@ -189,87 +221,88 @@
         z, _ = statistics(tok)
         norm_o[rows, :] = (z * par[GAIN1 : GAIN1 + 1, :] + par[BIAS1 : BIAS1 + 1, :]).astype(BF)
     normed = norm_o[...]
+    packed = dot(normed, w[...])
     for m in range(3):
-        part = dot(normed, w[m])
+        part = packed[:, m * HALF : (m + 1) * HALF]
         if m != 1:
             r = QB if m == 0 else VB
             part = part + par[r : r + 1, pl.ds(heads, HALF)]
         qkv_o[m] = part.astype(BF)
+    scores = []
+    for i, rows, hp, cols in head_pairs():
+        scores.append(dot_nt(qkv_o[1, rows, cols], two_heads(qkv_o[0, rows, cols] * BF(HD**-0.5))))
+    probs = []
+    for n, (i, rows, hp, cols) in enumerate(head_pairs()):
+        shown = jnp.where(keys_shown(pos, i), scores[n], -1e30)
+        raised = jnp.exp(shown - jnp.max(shown, axis=0, keepdims=True))
+        probs.append(raised / jnp.sum(raised, axis=0, keepdims=True))
+    for n, (i, rows, hp, cols) in enumerate(head_pairs()):
+        probs_o[n] = probs[n]
+        mixed = join_heads(dot_tn(probs[n].astype(BF), qkv_o[2, rows, cols])).astype(BF)
+        mix[rows, cols] = mixed
+    mix_o[...] = mix[0:SPLIT, :]
+    mix2_o[...] = mix[SPLIT:ROWS, :]
+
+
+def half_kernel(mix_a, mix2_a, wp, c0, c1, x_a, x_b, pos_r, one_o, pre_o, xs):
+    c = lax.axis_index("band") & 1
+    mine = pl.multiple_of(c * HALF, 128)
+    weights = wp[pl.ds(mine, HALF), :]
+    one_o[0:SPLIT, :] = dot(mix_a[...], weights)
+    one_o[SPLIT:ROWS, :] = dot(mix2_a[...], weights)
+    gather_bands((images(c0), images(c1), images_of_two(x_a, x_b), lambda i: jnp.zeros((BAND, D), BF)), xs)
+    pos = pos_r[...]
+    for i in range(IMGS):
+        pre_o[i * PACK : (i + 1) * PACK, :] = dot(one_hot_pack(pos, i), xs[i])
+
+
+def hidden_kernel(half, mix_b, mix2_b, tok, par, be, wp, we, after, res_o, one_o, n2_o, act_o, slope_o):
+    c = lax.axis_index("band") & 1
+    weights = wp[pl.ds(pl.multiple_of((1 - c) * HALF, 128), HALF), :]
+    one_o[0:SPLIT, :] = half[0:SPLIT, :] + dot(mix_b[...], weights) + par[PB : PB + 1, :]
+    one_o[SPLIT:ROWS, :] = half[SPLIT:ROWS, :] + dot(mix2_b[...], weights) + par[PB : PB + 1, :]
     for i in range(IMGS):
         rows = slice(i * PACK, (i + 1) * PACK)
-        key_ok = keys_shown(pos, i)
-        for hp in range(3):
-            cols = slice(hp * 128, (hp + 1) * 128)
-            q2, k2, v2 = (qkv_o[m, rows, cols] for m in range(3))
-            scores = dot_nt(two_heads(q2), k2) * (1.0 / math.sqrt(HD))
-            scores = jnp.where(key_ok, scores, -1e30)
-            raised = jnp.exp(scores - jnp.max(scores, axis=-1, keepdims=True))
-            probs = raised / jnp.sum(raised, axis=-1, keepdims=True)
-            probs_o[i * 3 + hp] = probs
-            mixed = join_heads(dot(probs.astype(BF), v2)).astype(BF)
-            if hp < 2:
-                mix_o[rows, cols] = mixed
-            else:
-                mix2_o[rows, :] = mixed
-
-
-def pick_kernel(normed, pick_o, pick_p_o, pn_o):
-    pick, pick_p = shard_picks()
-    pick_o[...] = pick
-    pick_p_o[...] = pick_p
-    pn_o[...] = dot(normed[...], pick).astype(BF)
-
-
-def hidden_units(n2, be, we, cols, act_o, slope_o):
-    step = 256
-    for f in range(cols // step):
-        at = slice(f * step, (f + 1) * step)
-        hidden = dot(n2[...], we[:, at]) + be[0:1, at]
-        phi = 0.5 * (1.0 + lax.erf(hidden * math.sqrt(0.5)))
-        act_o[:, at] = (hidden * phi).astype(BF)
-        slope_o[:, at] = phi + hidden * (jnp.exp(-0.5 * hidden * hidden) * (1.0 / math.sqrt(2.0 * math.pi)))
-
-
-def hidden_kernel(
-    mix_a, mix_b, mix2_a, mix2_b, tok, par, be, wp, we, after, res_o, one_o, n2_o, mix_o, act_o, slope_o, tick
-):
-    tick[...] = jnp.zeros_like(tick)
-    c = lax.axis_index("band") & 1
-    mine, other = pl.multiple_of(c * HALF, 128), pl.multiple_of((1 - c) * HALF, 128)
-    for at, first, second in ((mine, mix_a, mix2_a), (other, mix_b, mix2_b)):
-        mix_o[:, pl.ds(at, 256)] = first[...]
-        mix_o[:, pl.ds(pl.multiple_of(at + 256, 128), 128)] = second[...]
-    one = dot(mix_o[...], wp[...]) + par[PB : PB + 1, :]
-    one_o[...] = one
-    residual = tok[...].astype(F32) + par[ASC : ASC + 1, :] * one
-    res_o[...] = residual
-    z, _ = statistics(residual)
-    n2_o[...] = (z * par[GAIN2 : GAIN2 + 1, :] + par[BIAS2 : BIAS2 + 1, :]).astype(BF)
-    hidden_units(n2_o, be, we, D, act_o, slope_o)
-
-
-def more_hidden_kernel(n2, be, we, act_o, slope_o):
-    hidden_units(n2, be.at[:, D:FH], we.at[:, D:FH], FH - D, act_o, slope_o)
-
-
-def pass_kernel(v, after, out):
-    out[...] = v[...]
-
-
-def reduce_grad_kernel(c0, c1, c2, c3, pos_r, par, act_a, act_b, pre_o, gb2_o, send_o, keep_o, xs, act_x, full):
+        residual = tok[rows, :].astype(F32) + par[ASC : ASC + 1, :] * one_o[rows, :]
+        res_o[rows, :] = residual
+        z, _ = statistics(residual)
+        n2_o[rows, :] = (z * par[GAIN2 : GAIN2 + 1, :] + par[BIAS2 : BIAS2 + 1, :]).astype(BF)
+    for f in range(FH // 256):
+        cols = slice(f * 256, (f + 1) * 256)
+        for i in range(IMGS):
+            rows = slice(i * PACK, (i + 1) * PACK)
+            hidden = dot(n2_o[rows, :], we[:, cols]) + be[0:1, cols]
+            phi = 0.5 * (1.0 + lax.erf(hidden * math.sqrt(0.5)))
+            act_o[rows, cols] = (hidden * phi).astype(BF)
+            density = jnp.exp(-0.5 * hidden * hidden) * (1.0 / math.sqrt(2.0 * math.pi))
+            slope_o[rows, cols] = phi + hidden * density
+
+
+def split_kernel(v, out_a, out_b):
+    for i in range(IMGS):
+        lo = i * BAND
+        for first, out in ((0, out_a), (OWN // 2, out_b)):
+            start, stop = max(lo, first), min(lo + BAND, first + OWN // 2)
+            if start < stop:
+                out[start - first : stop - first, :] = v[i, start - lo : stop - lo, :]
+
+
+def reduce_grad_kernel(part, d_a, d_b, far_r, par, act, pre_o, gb2_o, send_o, keep_o, act_x, full):
     x, c, z, y = place()
-    gather_bands((c0, c1, c2, c3), xs)
-    pos = pos_r[...]
+    block = images_of_two(d_a, d_b)
     for i in range(IMGS):
         rows = slice(i * PACK, (i + 1) * PACK)
-        pre = dot(one_hot_pack(pos, i), xs[i])
+        pre = part[rows, :] + dot(one_hot_pack(far_r[...], i), block(i))
         pre_o[rows, :] = pre.astype(BF)
         gb2_o[rows, :] = (par[MSC : MSC + 1, :] * pre).astype(BF)
-    for j in range(4):
-        act = act_a if j < 2 else act_b
-        lo = 384 * (j & 1)
-        mid, hi = lo + 192, lo + 384
-        act_x[:, 192 * j : 192 * j + 192] = jnp.where(x == 0, act[:, lo:mid], act[:, mid:hi])
+    for chip in range(2):
+
+        @pl.when(x == chip)
+        def _():
+            for j in range(4):
+                lo = 384 * j + 192 * chip
+                act_x[:, 192 * j : 192 * j + 192] = act[:, lo : lo + 192]
+
     full[...] = dot_tn(act_x[...], gb2_o[...])
     for dy, out in ((1, send_o), (0, keep_o)):
         for dz in range(2):
@@ -279,14 +312,12 @@
                 out[2 * dz + to] = full[pl.ds(at, 96), :].astype(BF)
 
 
-def back_kernel(gb2, wr, slope_a, slope_b, we, gh_o, left_o, right_o):
+def back_kernel(gb2, wr, slope, we, gh_o, left_o, right_o):
     step = 256
     for f in range(FH // step):
         cols = slice(f * step, (f + 1) * step)
         back = dot_nt(gb2[...], wr[cols, :])
-        slope = slope_a if f < 3 else slope_b
-        at = slice((f % 3) * step, (f % 3 + 1) * step)
-        gh_o[:, cols] = (back * slope[:, at]).astype(BF)
+        gh_o[:, cols] = (back * slope[:, cols]).astype(BF)
     gn2 = dot_nt(gh_o[...], we[...]).astype(BF)
     left_o[...] = gn2[:, :HALF]
     right_o[...] = gn2[:, HALF:]
@@ -294,8 +325,8 @@
 
 def expand_grad_kernel(n2, gh, pick, send_o, keep_o, tick, wide):
     tick[...] = jnp.zeros_like(tick)
-    picked = dot(n2[...], pick[...]).astype(BF)
-    wide[...] = dot_tn(picked, gh[...])
+    picked = dot_nt(pick[...], n2[...]).astype(BF)
+    wide[...] = dot(picked, gh[...])
     for low, out in ((1, send_o), (0, keep_o)):
         for i in range(4):
             lo = 192 * (i >> 1) + 48 * (low + 2 * (i & 1))
@@ -314,7 +345,7 @@
 
 
 def attention_back_kernel(
-    l_a, l_b, r_a, r_b, res, pre, qkv, probs_r, mix, pn, pick_p, wp, par, after,
+    l_a, l_b, r_a, r_b, res, pre, qkv, probs_r, mix_a, mix2_a, mix_b, mix2_b, normed, pick, pick_p, wp, par, after,
     gres_o, gp, send_o, keep_o, tick,
     flat,
 ):
@@ -327,27 +358,29 @@
     gres_o[...] = gres
     gb1 = (par[ASC : ASC + 1, :] * gres).astype(BF)
     gm = dot_nt(gb1, wp[pl.ds(heads, HALF), :]).astype(BF)
-    scale = 1.0 / math.sqrt(HD)
-    for i in range(IMGS):
-        rows = slice(i * PACK, (i + 1) * PACK)
-        for hp in range(3):
-            cols = slice(hp * 128, (hp + 1) * 128)
-            q2, k2, v2 = (qkv[m, rows, cols] for m in range(3))
-            probs = probs_r[i * 3 + hp]
-            g2 = two_heads(gm[rows, cols])
-            gprob = dot_nt(g2, v2)
-            delta = jnp.sum(probs * gprob, axis=-1, keepdims=True)
-            gscore = (probs * (gprob - delta)).astype(BF)
-            parts = (
-                join_heads(dot(gscore, k2)) * scale,
-                dot_tn(gscore, two_heads(q2)) * scale,
-                dot_tn(probs.astype(BF), g2),
-            )
-            for m in range(3):
-                gp[rows, m * HALF + hp * 128 : m * HALF + (hp + 1) * 128] = parts[m].astype(BF)
-    mixed = dot(mix[...], pick_p[...]).astype(BF)
-    proj = dot_tn(mixed, gb1)
-    flat[...] = dot_tn(pn[...], gp[...])
+    grads = [two_heads(gm[rows, cols]) for i, rows, hp, cols in head_pairs()]
+    gprobs = [dot_nt(qkv[2, rows, cols], grads[n]) for n, (i, rows, hp, cols) in enumerate(head_pairs())]
+    gscores = []
+    for n in range(9):
+        product = probs_r[n] * gprobs[n]
+        gscores.append((product - probs_r[n] * jnp.sum(product, axis=0, keepdims=True)).astype(BF))
+    for n, (i, rows, hp, cols) in enumerate(head_pairs()):
+        parts = (
+            join_heads(dot_tn(gscores[n], qkv[1, rows, cols] * BF(HD**-0.5))),
+            dot(gscores[n], two_heads(qkv[0, rows, cols] * BF(HD**-0.5))),
+            dot(probs_r[n].astype(BF), grads[n]),
+        )
+        for m in range(3):
+            gp[rows, m * HALF + hp * 128 : m * HALF + (hp + 1) * 128] = parts[m].astype(BF)
+    others = pl.multiple_of((1 - c) * HALF, 128)
+    mixed = []
+    for first, second in ((mix_a, mix_b), (mix2_a, mix2_b)):
+        part = dot_nt(pick_p[:, pl.ds(heads, HALF)], first[...])
+        mixed.append(part + dot_nt(pick_p[:, pl.ds(others, HALF)], second[...]))
+    mixed = jnp.concatenate(mixed, axis=1).astype(BF)
+    pn = dot_nt(pick[...], normed[...]).astype(BF)
+    proj = dot(mixed, gb1)
+    flat[...] = dot(pn, gp[...])
     for dy, out in ((1, send_o), (0, keep_o)):
         for i, dz in enumerate((0, 2, 1, 3)):
             q = 4 * dy + dz
@@ -357,7 +390,7 @@
 
 
 def vectors_kernel(
-    l_a, l_b, r_a, r_b, res, one, gres, gp, w, act_a, act_b, wr, gb2, gh, pre, tok, pick, par, mine, theirs, after,
+    l_a, l_b, r_a, r_b, res, one, gres, gp, w, act, wr, gb2, gh, pre, tok, pick, par, mine, theirs, after,
     gb_keep, gb_send, send_o, keep_o, tick,
     vecs, sums,
 ):
@@ -370,9 +403,7 @@
         return jnp.sum(v, axis=0, keepdims=True)
 
     vecs[...] = jnp.zeros_like(vecs)
-    gnp = jnp.zeros((ROWS, D), F32)
-    for m in range(3):
-        gnp = gnp + dot_nt(gp[:, m * HALF : (m + 1) * HALF], w[m])
+    gnp = dot_nt(gp[...], w[...])
     z1, _ = statistics(tok[...].astype(F32))
     vecs[GAIN1 : GAIN1 + 1, :] = total(gnp * z1)
     vecs[BIAS1 : BIAS1 + 1, :] = total(gnp)
@@ -386,14 +417,14 @@
     vecs[GAIN2 : GAIN2 + 1, :] = first * total(gn2 * z2)
     vecs[BIAS2 : BIAS2 + 1, :] = first * total(gn2)
     vecs[RB : RB + 1, :] = first * total(gb2[...].astype(F32))
-    two = dot(act_a[...], wr[0:D, :]) + dot(act_b[...], wr[D:FH, :])
+    two = dot(act[...], wr[...])
     for m, value in enumerate((gnp.astype(BF), two.astype(BF))):
         for i in range(IMGS):
             rows = slice(i * PACK, (i + 1) * PACK)
             for at, out in ((mine, gb_keep), (theirs, gb_send)):
                 out[m, i] = dot_tn(one_hot_pack(at[...], i), value[rows]).astype(BF)
     vecs[MSC : MSC + 1, :] = total(pre[...].astype(F32) * (two + first * par[RB : RB + 1, :]))
-    cols = dot(vecs[...].astype(BF), pick[...]).T
+    cols = dot_nt(pick[...], vecs[...].astype(BF))
     sums[...] = dot_tn(gh[...], jnp.ones((ROWS, SMALL), BF))
     lane = lax.broadcasted_iota(jnp.int32, (48, SMALL), 1)
     for dy, out in ((1, send_o), (0, keep_o)):
@@ -493,7 +524,16 @@
     we_so[...] = both[pl.ds(pl.multiple_of(24 - c * 24, 8), 24), :]
 
 
-def finish_kernel(qp_k, qp_a, vec_k, vec_a, after, keep_o, send_o, vec_o, proj_o, sums):
+def early_out_kernel(we_keep, we_arrived, wr_keep, wr_arrived, after, we_o, wr_o, tick):
+    tick[...] = jnp.zeros_like(tick)
+    _, c, z, _ = place()
+    wr_o[...] = jnp.where((z >> 1) == c, wr_keep[...], wr_arrived[...].astype(F32))
+    we_o[:, pl.ds(pl.multiple_of(c * FH, 128), FH)] = we_keep[...]
+    we_o[:, pl.ds(pl.multiple_of((1 - c) * FH, 128), FH)] = we_arrived[...]
+
+
+def finish_kernel(qp_k, qp_a, vec_k, vec_a, after, keep_o, send_o, vec_o, proj_o, tick, sums):
+    tick[...] = jnp.zeros_like(tick)
     c = lax.axis_index("band") & 1
     sums[...] = qp_k[0] + qp_a[0].astype(F32)
     keep_o[...] = sums[pl.ds(pl.multiple_of(c * 24, 8), 24), 0:QC]
@@ -507,13 +547,11 @@
 
 
 def out_kernel(
-    keep, vec, arrived, we_keep, we_arrived, wr_keep, wr_arrived,
-    qkv_o, first_o, bias_o, qv_o, bp_o, asc_o, gain2_o, bias2_o, br_o, msc_o, eb_o, we_o, wr_o, both,
+    keep, vec, proj, arrived, after,
+    qkv_o, first_o, bias_o, qv_o, bp_o, asc_o, gain2_o, bias2_o, br_o, msc_o, eb_o, proj_o, both,
 ):
-    _, c, z, _ = place()
-    wr_o[...] = jnp.where((z >> 1) == c, wr_keep[...], wr_arrived[...].astype(F32))
-    we_o[:, pl.ds(pl.multiple_of(c * FH, 128), FH)] = we_keep[...]
-    we_o[:, pl.ds(pl.multiple_of((1 - c) * FH, 128), FH)] = we_arrived[...]
+    c = lax.axis_index("band") & 1
+    proj_o[...] = proj[...]
     for m in range(3):
         mine = pl.multiple_of(m * D + c * HALF, 128)
         other = pl.multiple_of(m * D + (1 - c) * HALF, 128)
@@ -536,7 +574,7 @@
     "first_kernel": (0, 0),
     "pick_kernel": (0, 0),
     "hidden_kernel": (0, 0),
-    "reduce_grad_kernel": (1000000000, 4000000),
+    "reduce_grad_kernel": (0, 0),
     "back_kernel": (0, 0),
     "expand_grad_kernel": (0, 0),
     "attention_back_kernel": (0, 0),
@@ -548,12 +586,13 @@
     "finish_kernel": (0, 1000000),
     "out_kernel": (0, 1000000),
     "prepare_kernel": (0, 9000000),
-    "hold_kernel": (0, 20000000),
+    "hold_kernel": (0, 0),
     "home_kernel": (0, 0),
+    "half_kernel": (0, 0),
 }
 
 
-def call(kernel, outs, specs, scratch=(), vmem=24):
+def call(kernel, outs, specs, scratch=(), vmem=24, cost=0):
     return pl.pallas_call(
         kernel,
         out_shape=outs,
@@ -561,13 +600,13 @@
         out_specs=jax.tree.map(lambda _: VM, outs),
         scratch_shapes=list(scratch),
         compiler_params=pltpu.CompilerParams(vmem_limit_bytes=vmem * MIB),
-        cost_estimate=pl.CostEstimate(flops=COSTS.get(kernel.__name__, (0, 0))[0], bytes_accessed=COSTS.get(kernel.__name__, (0, 0))[1], transcendentals=0),
-    )
-
-
-def fold_call(keep, arrived, after):
+        cost_estimate=pl.CostEstimate(flops=COSTS.get(kernel.__name__, (0, 0))[0] + cost, bytes_accessed=COSTS.get(kernel.__name__, (0, 0))[1], transcendentals=0),
+    )
+
+
+def fold_call(keep, arrived, after, cost=0):
     half = (keep.shape[0] // 2, *keep.shape[1:])
-    return call(fold_kernel, (vm(half, F32), vm(half, BF), TICK), [VM] * 2 + [ANY])(keep, arrived, after)
+    return call(fold_kernel, (vm(half, F32), vm(half, BF), TICK), [VM] * 2 + [ANY], cost=cost)(keep, arrived, after)
 
 
 def by_core(value):
@@ -599,18 +638,20 @@
     rows_f, rows_b = vm((ROWS, D), F32), vm((ROWS, D), BF)
     tok_x = by_x(tokens)
     tok_block = vm((OWN + 16, D), BF)
-    cot, tok_own, par, be, wqkv, wp, we, wr, vis = call(
+    cot, tok_own, par, be, wqkv, wp, we, wr, vis, pick, pick_p = call(
         prepare_kernel,
         (
             block,
             tok_block,
             vm((16, D), F32),
             vm((8, FH), F32),
-            vm((3, D, HALF), BF),
+            vm((D, QC), BF),
             vm((D, D), BF),
             vm((D, FH), BF),
             vm((FH, D), BF),
-            vm((16, 128), BF),
+            vm((16, D), BF),
+            vm((HALF, D), BF),
+            vm((192, D), BF),
         ),
         [ANY] * 17,
         [pltpu.VMEM(visible.shape, jnp.int32), pltpu.SemaphoreType.DMA((22,))],
@@ -627,44 +668,46 @@
     vis_x = by_x(vis)
     tok_c = by_core(tok_own)
     cot_c = by_core(cot)
-    tok_x = call(hold_kernel, tok_block, [VM] * 2 + [ANY])(tok_x, vis_x, par)
-    tok_d = by_core(tok_x)
-    cot_x = by_x(cot)
-    tok, normed, qkv, mix_own, mix2_own, pos, probs, pos_mine, pos_theirs = call(
+    parts = (vm((EARLY, D), BF), vm((OWN + 16 - EARLY, D), BF))
+    tok_x = call(hold_kernel, parts, [VM] * 2 + [ANY])(tok_x, vis_x, par)
+    tok_d = [by_core(v) for v in tok_x]
+    cot_x = call(split_kernel, (vm((OWN // 2, D), BF),) * 2, [VM])(by_x(cot))
+    cot_d = [by_core(v) for v in cot_x]
+    tok, normed, qkv, mix_own, mix2_own, pos, probs, pos_mine, pos_theirs, pos_far = call(
         first_kernel,
         (
             rows_b,
             rows_b,
             vm((3, ROWS, HALF), BF),
-            vm((ROWS, 256), BF),
-            vm((ROWS, 128), BF),
+            vm((SPLIT, HALF), BF),
+            vm((ROWS - SPLIT, HALF), BF),
             vm((8, SLOTS), F32),
-            vm((9, 2 * PACK, PACK), F32),
+            vm((9, PACK, 2 * PACK), F32),
+            vm((16, BAND), F32),
             vm((16, BAND), F32),
             vm((16, BAND), F32),
         ),
-        [VM] * 6,
-        [pltpu.VMEM((IMGS, SLOTS, D), BF)],
-    )(tok_own, tok_c, tok_x, tok_d, par, wqkv)
+        [VM] * 8,
+        [pltpu.VMEM((IMGS, SLOTS, D), BF), pltpu.VMEM((ROWS, HALF), BF)],
+    )(tok_own, tok_c, *tok_x, *tok_d, par, wqkv)
     mix_other, mix2_other = by_core(mix_own), by_core(mix2_own)
-    pick, pick_p, pn = call(pick_kernel, (vm((D, HALF), BF), vm((D, 192), BF), vm((ROWS, HALF), BF)), [VM])(normed)
-    res, one, n2, mix, act, slope, tick = call(
+    half_one, half_pre = call(
+        half_kernel, (rows_f, rows_f), [VM] * 8, [pltpu.VMEM((IMGS, SLOTS, D), BF)]
+    )(mix_own, mix2_own, wp, cot, cot_c, *cot_x, pos)
+    res, one, n2, act, slope = call(
         hidden_kernel,
-        (rows_f, rows_f, rows_b, rows_b, rows_b, rows_f, TICK),
-        [VM] * 9 + [ANY],
-    )(mix_own, mix_other, mix2_own, mix2_other, tok, par, be, wp, we, pick)
-    cot_x = call(pass_kernel, block, [VM, ANY])(cot_x, tick)
-    cot_d = by_core(cot_x)
-    act_b, slope_b = call(more_hidden_kernel, (rows_b, rows_f), [VM] * 3)(n2, be, we)
+        (rows_f, rows_f, rows_b, vm((ROWS, FH), BF), vm((ROWS, FH), F32)),
+        [VM] * 8 + [ANY],
+    )(half_one, mix_other, mix2_other, tok, par, be, wp, we, pick)
     pre, gb2, wr_send, wr_keep = call(
         reduce_grad_kernel,
         (rows_b, rows_b, vm((4, 96, D), BF), vm((4, 96, D), BF)),
-        [VM] * 8,
-        [pltpu.VMEM((IMGS, SLOTS, D), BF), pltpu.VMEM((ROWS, D), BF), pltpu.VMEM((D, D), F32)],
-    )(cot, cot_c, cot_x, cot_d, pos, par, act, act_b)
+        [VM] * 6,
+        [pltpu.VMEM((ROWS, D), BF), pltpu.VMEM((D, D), F32)],
+    )(half_pre, *cot_d, pos_far, par, act)
     wr_y = by_y(wr_send)
     half_b = vm((ROWS, HALF), BF)
-    gh, left, right = call(back_kernel, (vm((ROWS, FH), BF), half_b, half_b), [VM] * 5)(gb2, wr, slope, slope_b, we)
+    gh, left, right = call(back_kernel, (vm((ROWS, FH), BF), half_b, half_b), [VM] * 4)(gb2, wr, slope, we)
     gn2 = (left, by_core(left), right, by_core(right))
     we_send, we_keep, tick = call(
         expand_grad_kernel,
@@ -676,9 +719,9 @@
     gres, gp, qp_send, qp_keep, tick = call(
         attention_back_kernel,
         (rows_f, vm((ROWS, QC), BF), vm((4, 48, QW), BF), vm((4, 48, QW), BF), TICK),
-        [VM] * 13 + [ANY],
+        [VM] * 17 + [ANY],
         [pltpu.VMEM((HALF, QC), F32)],
-    )(*gn2, res, pre, qkv, probs, mix, pn, pick_p, wp, par, tick)
+    )(*gn2, res, pre, qkv, probs, mix_own, mix2_own, mix_other, mix2_other, normed, pick, pick_p, wp, par, tick)
     qp_y = by_y(qp_send)
     wr_keep, wr_send, tick = call(
         home_kernel, (vm((4, 96, D), F32), vm((4, 96, D), BF), TICK), [VM] * 2 + [ANY]
@@ -687,9 +730,9 @@
     gb_keep, gb_send, vec_send, vec_keep, tick = call(
         vectors_kernel,
         (vm((2, *tokens.shape), BF), vm((2, *tokens.shape), BF), vm((2, 48, 2 * SMALL), BF), vm((2, 48, 2 * SMALL), BF), TICK),
-        [VM] * 20 + [ANY],
+        [VM] * 19 + [ANY],
         [pltpu.VMEM((SMALL, D), F32), pltpu.VMEM((FH, SMALL), F32)],
-    )(*gn2, res, one, gres, gp, wqkv, act, act_b, wr, gb2, gh, pre, tok, pick, par, pos_mine, pos_theirs, tick)
+    )(*gn2, res, one, gres, gp, wqkv, act, wr, gb2, gh, pre, tok, pick, par, pos_mine, pos_theirs, tick)
     gb_other = by_core(gb_send)
     we_keep, we_send, tick = call(
         join_kernel, (vm((2, 48, FS), F32), vm((2, 48, FS), BF), TICK), [VM] * 4 + [ANY]
@@ -713,7 +756,7 @@
     )(gb_keep, gb_other, tok_own, gres, res, pos_mine, par, tick)
     qp_keep, qp_send, tick = fold_call(qp_keep, qp_z, tick)
     qp_z = by_z(qp_send, 2)
-    vec_keep, vec_send, tick = fold_call(vec_keep, vec_z, tick)
+    vec_keep, vec_send, tick = fold_call(vec_keep, vec_z, tick, cost=4000000000)
     vec_z = by_z(vec_send, 2)
     wr_keep, wr_send, we_keep, we_send, tick = call(
         settle_kernel,
@@ -722,24 +765,28 @@
         [pltpu.VMEM((48, FH), F32)],
     )(wr_keep, wr_z, we_keep, we_z, tick)
     we_other, wr_other = by_core(we_send), by_core(wr_send)
-    qp_keep, qp_send, vec, proj = call(
+    qp_keep, qp_send, vec, proj, tick = call(
         finish_kernel,
-        (vm((24, QC), F32), vm((24, QC + 2 * SMALL), F32), vm((48, SMALL), F32), sds((24, D), F32)),
+        (vm((24, QC), F32), vm((24, QC + 2 * SMALL), F32), vm((48, SMALL), F32), vm((24, D), F32), TICK),
         [VM] * 4 + [ANY],
         [pltpu.VMEM((48, QW), F32)],
     )(qp_keep, qp_z, vec_keep, vec_z, tick)
+    qp_other = by_core(qp_send)
+    grad_expand, grad_reduce, tick = call(
+        early_out_kernel, (sds((24, FF), F32), sds((96, D), F32), TICK), [VM] * 4 + [ANY]
+    )(we_keep, we_other, wr_keep, wr_other, tick)
     vector = sds((24,), F32)
-    grad_qkv, gg1, gb1, gqv, gbp, gas, gg2, gb2, gbr, gms, geb, grad_expand, grad_reduce = call(
+    grad_qkv, gg1, gb1, gqv, gbp, gas, gg2, gb2, gbr, gms, geb, grad_proj = call(
         out_kernel,
         (
             sds((24, 3 * D), F32), vector, vector, sds((2, 24), F32), vector, vector, vector, vector, vector, vector,
-            sds((96,), F32), sds((24, FF), F32), sds((96, D), F32),
+            sds((96,), F32), sds((24, D), F32),
         ),
-        [VM] * 7,
+        [VM] * 4 + [ANY],
         [pltpu.VMEM((48, SMALL), F32)],
-    )(qp_keep, vec, by_core(qp_send), we_keep, we_other, wr_keep, wr_other)
+    )(qp_keep, vec, proj, qp_other, tick)
     return (
-        layer_out, grad_tokens, gg1, gb1, grad_qkv, gqv, proj, gbp, gas, gg2, gb2, grad_expand, geb, grad_reduce,
+        layer_out, grad_tokens, gg1, gb1, grad_qkv, gqv, grad_proj, gbp, gas, gg2, gb2, grad_expand, geb, grad_reduce,
         gbr, gms,
     )
 

time: 80.2 us -> 78.8 us (0.983)
  Pallas kernels: 31.4 us -> 27.8 us
  starting transfers between devices: 25.9 us -> 28.7 us
    ppermute x6, waiting for transfers between devices: 6.32 us -> 1.13 us  [by_z(): return lax.ppermute(value, 'batch', [(i, i ^ 2 * dz) for i in range(8)])]
    ppermute x2, waiting for transfers between devices: 3.75 us -> 8.57 us  [homeward(): return lax.ppermute(value, ('batch', 'band'), pairs)]
    pallas_call x1, Pallas kernels: 6.36 us -> 4.21 us  [packed_body(): call(attention_back_kernel, (rows_f, vm((ROWS, QC), BF), vm((4, 48, QW),...]
    ppermute x6, starting transfers between devices: 9.26 us -> 10.9 us  [by_z(): return lax.ppermute(value, 'batch', [(i, i ^ 2 * dz) for i in range(8)])]
    ppermute x3, waiting for transfers between devices: 5.67 us -> 7.05 us  [by_y(): return lax.ppermute(value, 'batch', [(i, i ^ 1) for i in range(8)])]
    ppermute x3, waiting for transfers between devices: 3.77 us -> 2.41 us  [by_x(): return lax.ppermute(value, 'band', [(i, i ^ 2) for i in range(4)])]
    ppermute x12 -> x14, waiting for transfers between devices: 2.21 us -> 1.93 us  [by_core(): return lax.ppermute(value, 'band', [(i, i ^ 1) for i in range(4)])]
    ppermute x12 -> x14, starting transfers between devices: 4.7 us -> 4.8 us  [by_core(): return lax.ppermute(value, 'band', [(i, i ^ 1) for i in range(4)])]
  transfers between devices with their start and end apart: 26 -> 28, of which waited for: 11 -> 9; matrix products, arithmetic and copies ran while one was open for 0% -> 0% of each run, Pallas kernels for 36% -> 32%
where the time goes in v6:
time: 78.8 us; the launch traced here: 78.6 us
  starting transfers between devices  28.7 us (36%)
  Pallas kernels  27.8 us (35%)
  waiting for transfers between devices  21.1 us (27%)
  between operations  1.08 us (1%)
    ppermute x6, starting transfers between devices, by_z(): return lax.ppermute(value, 'batch', [(i, i ^ 2 * dz) for i in range(8)])  10.9 us
    ppermute x2, waiting for transfers between devices, homeward(): return lax.ppermute(value, ('batch', 'band'), pairs)  8.57 us
    ppermute x3, waiting for transfers between devices, by_y(): return lax.ppermute(value, 'batch', [(i, i ^ 1) for i in range(8)])  7.05 us
    ppermute x3, starting transfers between devices, by_x(): return lax.ppermute(value, 'band', [(i, i ^ 2) for i in range(4)])  5.09 us
    ppermute x14, starting transfers between devices, by_core(): return lax.ppermute(value, 'band', [(i, i ^ 1) for i in range(4)])  4.8 us
    pallas_call x1, Pallas kernels, packed_body(): call(vectors_kernel, (vm((2, *tokens.shape), BF), vm((2, *tokens.shape),...  4.25 us
    pallas_call x1, Pallas kernels, packed_body(): call(attention_back_kernel, (rows_f, vm((ROWS, QC), BF), vm((4, 48, QW),...  4.21 us
    ppermute x3, starting transfers between devices, by_y(): return lax.ppermute(value, 'batch', [(i, i ^ 1) for i in range(8)])  3.98 us
  transfers between devices with their start and end apart: 28, of which 9 were waited for; matrix products, arithmetic and copies ran while one was open for 0% of the time, Pallas kernels for 32%

profile of v6, /device:TPU:0, one launch (start us, length us, event | category | flops | bytes accessed | tf_op | source)
XLA Modules:
  0.0 78.6 jit_solution(11693582553571205161)
XLA Ops:
  0.6 3.0 %collective-permute-start.1 = (bf16[3,64,768]{2,1,0:T(8,128)(2,1)}, bf16[3,64,768]{2,1,0:T(8,128)(2,1)S(1)}, u32[]{:S(2)}, u32[]{:S(2)}) collective-permute-start(bf16[3,64,768]{2,1,0:T(8,128)(2,1)} %tok.1), channel_id=1, source_target_pairs={{0,2},{1,3},{2,0},{3,1},{4,6},{5,7},{6,4},{7,5},{8,10},{9,11},{10,... | collective-permute-start | bytes 884744 | tf_op jit(solution)/shard_map/ppermute | solution.py:617
  3.7 3.7 %shard_map.288 = (bf16[3,64,768]{2,1,0:T(8,128)(2,1)S(1)}, bf16[208,768]{1,0:T(8,128)(2,1)S(1)}, f32[16,768]{1,0:T(8,128)S(1)}, f32[8,1536]{1,0:T(8,128)S(1)}, b...) custom-call(bf16[3,64,768]{2,1,0:T(8,128)(2,1)} %cot.1, ...), custom_call_target="tpu_custom_call" | custom-call | bytes 9000000 | tf_op jit(solution)/shard_map/pallas_call | solution.py:641
  7.4 0.1 collective-permute-start.2
  7.5 2.0 %collective-permute-start.6 = (bf16[3,64,768]{2,1,0:T(8,128)(2,1)S(1)}, bf16[3,64,768]{2,1,0:T(8,128)(2,1)S(1)}, u32[]{:S(2)}, u32[]{:S(2)}) collective-permute-start(bf16[3,64,768]{2,1,0:T(8,128)(2,1)S(1)} %get-tuple-element.128.c0), channel_id=1, source_target_pairs={{0,2},{1,3},{2,0},{3,1},{4,6},{5,7},{6,4},{7,5},{8,10},{9,11},{10,... | collective-permute-start | bytes 884744 | tf_op jit(solution)/shard_map/ppermute | solution.py:617
  9.5 2.1 %collective-permute-done.2.vis = bf16[16,768]{1,0:T(8,128)(2,1)S(1)} collective-permute-done((bf16[16,768]{1,0:T(8,128)(2,1)S(1)}, bf16[16,768]{1,0:T(8,128)(2,1)S(1)}, u32[]{:S(2)}, u32[]{:S(2)}) %collective-permute-start.2) | collective-permute-done | bytes 24608 | tf_op jit(solution)/shard_map/ppermute | solution.py:617
  11.8 0.5 collective-permute-start.5
  12.3 0.1 collective-permute-start.4
  12.3 1.4 %collective-permute-done.4.d_b = bf16[48,768]{1,0:T(8,128)(2,1)S(1)} collective-permute-done((bf16[48,768]{1,0:T(8,128)(2,1)S(1)}, bf16[48,768]{1,0:T(8,128)(2,1)S(1)}, u32[]{:S(2)}, u32[]{:S(2)}) %collective-permute-start.4) | collective-permute-done | bytes 73760 | tf_op jit(solution)/shard_map/ppermute | solution.py:613
  13.8 3.1 %shard_map.290 = (bf16[432,768]{1,0:T(8,128)(2,1)S(1)}, bf16[432,768]{1,0:T(8,128)(2,1)S(1)}, bf16[3,432,384]{2,1,0:T(8,128)(2,1)S(1)}, bf16[224,384]{1,0:T(8,12...) custom-call(bf16[208,768]{1,0:T(8,128)(2,1)S(1)} %get-tuple-element., ...), custom_call_target="tpu_custom_call" | custom-call | tf_op jit(solution)/shard_map/pallas_call | solution.py:676
  16.9 0.2 collective-permute-start.9
  17.1 0.4 collective-permute-start.10
  17.4 0.3 collective-permute-done.6.v
  17.8 0.5 collective-permute-start.8
  18.3 0.7 shard_map.292
  19.1 2.3 %shard_map.293 = (f32[432,768]{1,0:T(8,128)S(1)}, f32[432,768]{1,0:T(8,128)S(1)}, bf16[432,768]{1,0:T(8,128)(2,1)S(1)}, bf16[432,1536]{1,0:T(8,128)(2,1)S(1)}, f32[432,1536]{1,0:T(8,128)S(1)}) custom-call(f32[432,768]{1,0:T(8,128)S(1)} %get-tuple-element.134.half, bf16[224,384]{1,0:T(8,128)(2,1)S(1)} %collective-permute-done.9.mix_b, ...), custom_call_target="tpu_custom_call" | custom-call | tf_op jit(solution)/shard_map/pallas_call | solution.py:697
  21.4 1.7 %shard_map.294 = (bf16[432,768]{1,0:T(8,128)(2,1)S(1)}, bf16[432,768]{1,0:T(8,128)(2,1)S(1)}, bf16[4,96,768]{2,1,0:T(8,128)(2,1)S(1)}, bf16[4,96,768]{2,1,0:T(8,128)(2,1)S(1)}) custom-call(f32[432,768]{1,0:T(8,128)S(1)} %get-tuple-element.132.part, bf16[96,768]{1,0:T(8,128)(2,1)S(1)} %collective-permute-done.7.d_a, ...), custom_call_target="tpu_custom_call" | custom-call | tf_op jit(solution)/shard_map/pallas_call | solution.py:702
  23.1 1.8 %collective-permute-start.13 = (bf16[4,96,768]{2,1,0:T(8,128)(2,1)S(1)}, bf16[4,96,768]{2,1,0:T(8,128)(2,1)S(1)}, u32[]{:S(2)}, u32[]{:S(2)}) collective-permute-start(bf16[4,96,768]{2,1,0:T(8,128)(2,1)S(1)} %get-tuple-element.160), channel_id=1, source_target_pairs={{0,4},{4,0},{8,12},{12,8},{16,20},{20,16},{24,28},{28,24},{1,5},{5... | collective-permute-start | bytes 1769480 | tf_op jit(solution)/shard_map/ppermute | solution.py:621
  24.9 2.4 %shard_map.295 = (bf16[432,1536]{1,0:T(8,128)(2,1)S(1)}, bf16[432,384]{1,0:T(8,128)(2,1)S(1)}, bf16[432,384]{1,0:T(8,128)(2,1)S(1)}) custom-call(bf16[432,768]{1,0:T(8,128)(2,1)S(1)} %get-tuple-element.140.gb2, bf16[1536,768]{1,0:T(8,128)(2,1)S(1)} %get-tuple-element.141.wr, f32[432,1536]{1,0:T(8,128)S(1)} %get-tuple-element.142.slope, ...), custom_call_target="tpu_custom_call" | custom-call | tf_op jit(solution)/shard_map/pallas_call | solution.py:710
  27.4 0.5 collective-permute-start.12
  27.9 1.2 %shard_map.296 = (bf16[4,48,1536]{2,1,0:T(8,128)(2,1)S(1)}, bf16[4,48,1536]{2,1,0:T(8,128)(2,1)S(1)}, f32[8,128]{1,0:T(8,128)S(1)}) custom-call(bf16[432,768]{1,0:T(8,128)(2,1)S(1)} %get-tuple-element.152.n2, bf16[432,1536]{1,0:T(8,128)(2,1)S(1)} %get-tuple-element.153.gh, bf16[384,768]{1,0:T(8,128)(2,1)S(1)} %get-tuple-element.138.after.pick), custom_call_target="tpu_custom_call" | custom-call | tf_op jit(solution)/shard_map/pallas_call | solution.py:712
  29.1 1.7 %collective-permute-start.15 = (bf16[4,48,1536]{2,1,0:T(8,128)(2,1)S(1)}, bf16[4,48,1536]{2,1,0:T(8,128)(2,1)S(1)}, u32[]{:S(2)}, u32[]{:S(2)}) collective-permute-start(bf16[4,48,1536]{2,1,0:T(8,128)(2,1)S(1)} %get-tuple-element.166), channel_id=1, source_target_pairs={{0,8},{4,12},{8,0},{12,4},{16,24},{20,28},{24,16},{28,20},{1,9},{5... | collective-permute-start | bytes 1769480 | tf_op jit(solution)/shard_map/ppermute | solution.py:625
  30.7 4.2 %shard_map.297 = (f32[432,768]{1,0:T(8,128)S(1)}, bf16[432,1152]{1,0:T(8,128)(2,1)S(1)}, bf16[4,48,1536]{2,1,0:T(8,128)(2,1)S(1)}, bf16[4,48,1536]{2,1,0:T(8,128)(2,1)S(1)}, f32[8,128]{1,0:T(8,128)S(1)}) custom-call(bf16[432,384]{1,0:T(8,128)(2,1)S(1)} %get-tuple-element.143.l_a, bf16[432,384]{1,0:T(8,128)(2,1)S(1)} %collective-permute-done.11.l_b, ...), custom_call_target="tpu_custom_call" | custom-call | tf_op jit(solution)/shard_map/pallas_call | solution.py:719
  35.0 0.5 collective-permute-start.18
  35.5 3.8 %collective-permute-done.13.arrived = bf16[4,96,768]{2,1,0:T(8,128)(2,1)S(1)} collective-permute-done((bf16[4,96,768]{2,1,0:T(8,128)(2,1)S(1)}, bf16[4,96,768]{2,1,0:T(8,128)(2,1)S(1)}, u32[]{:S(2)}, u32[]{:S(2)}) %collective-permute-start.13) | collective-permute-done | bytes 589856 | tf_op jit(solution)/shard_map/ppermute | solution.py:621
  39.3 0.2 shard_map.298
  39.5 1.5 %collective-permute-start.17 = (bf16[4,96,768]{2,1,0:T(8,128)(2,1)S(1)}, bf16[4,96,768]{2,1,0:T(8,128)(2,1)S(1)}, u32[]{:S(2)}, u32[]{:S(2)}) collective-permute-start(bf16[4,96,768]{2,1,0:T(8,128)(2,1)S(1)} %get-tuple-element.173), channel_id=1, source_target_pairs={{1,17},{3,19},{5,21},{7,23},{9,25},{11,27},{13,29},{15,31},{16,0},... | collective-permute-start | bytes 1769480 | tf_op jit(solution)/shard_map/ppermute | solution.py:630
  41.0 4.3 %shard_map.299 = (bf16[2,3,64,768]{3,2,1,0:T(8,128)(2,1)S(1)}, bf16[2,3,64,768]{3,2,1,0:T(8,128)(2,1)S(1)}, bf16[2,48,256]{2,1,0:T(8,128)(2,1)S(1)}, bf16[2,48,256]{2,1,0:T(8,128)(2,1)S(1)}, f32[8,128]{1,0:T(8,128)S(1)}) custom-call(bf16[432,384]{1,0:T(8,128)(2,1)S(1)} %get-tuple-element.143.l_a, bf16[432,384]{1,0:T(8,128)(2,1)S(1)} %collective-permute-done.11.l_b, ...), custom_call_target="tpu_custom_call" | custom-call | flops 8000000000 | bytes 20000000 | tf_op jit(solution)/shard_map/pallas_call | solution.py:730
  45.3 1.7 %collective-permute-start.14 = (bf16[2,3,64,768]{3,2,1,0:T(8,128)(2,1)S(1)}, bf16[2,3,64,768]{3,2,1,0:T(8,128)(2,1)S(1)}, u32[]{:S(2)}, u32[]{:S(2)}) collective-permute-start(bf16[2,3,64,768]{3,2,1,0:T(8,128)(2,1)S(1)} %get-tuple-element.164), channel_id=1, source_target_pairs={{0,1},{1,0},{2,3},{3,2},{4,5},{5,4},{6,7},{7,6},{8,9},{9,8},{10,11... | collective-permute-start | bytes 1769480 | tf_op jit(solution)/shard_map/ppermute | solution.py:613
  47.0 0.1 shard_map.300
  47.1 1.6 %collective-permute-start.16 = (bf16[2,48,1792]{2,1,0:T(8,128)(2,1)S(1)}, bf16[2,48,1792]{2,1,0:T(8,128)(2,1)S(1)}, u32[]{:S(2)}, u32[]{:S(2)}) collective-permute-start(bf16[2,48,1792]{2,1,0:T(8,128)(2,1)S(1)} %get-tuple-element.171), channel_id=1, source_target_pairs={{0,4},{4,0},{8,12},{12,8},{16,20},{20,16},{24,28},{28,24},{1,5},{5... | collective-permute-start | bytes 1032200 | tf_op jit(solution)/shard_map/ppermute | solution.py:621
  48.8 3.2 %collective-permute-done.18.arrived = bf16[4,48,1536]{2,1,0:T(8,128)(2,1)S(1)} collective-permute-done((bf16[4,48,1536]{2,1,0:T(8,128)(2,1)S(1)}, bf16[4,48,1536]{2,1,0:T(8,128)(2,1)S(1)}, u32[]{:S(2)}, u32[]{:S(2)}) %collective-permute-start.18) | collective-permute-done | bytes 589856 | tf_op jit(solution)/shard_map/ppermute | solution.py:621
  52.0 0.1 shard_map.301
  52.1 1.9 %collective-permute-start.19 = (bf16[2,48,1536]{2,1,0:T(8,128)(2,1)S(1)}, bf16[2,48,1536]{2,1,0:T(8,128)(2,1)S(1)}, u32[]{:S(2)}, u32[]{:S(2)}) collective-permute-start(bf16[2,48,1536]{2,1,0:T(8,128)(2,1)S(1)} %get-tuple-element.183), channel_id=1, source_target_pairs={{0,8},{4,12},{8,0},{12,4},{16,24},{20,28},{24,16},{28,20},{1,9},{5... | collective-permute-start | bytes 884744 | tf_op jit(solution)/shard_map/ppermute | solution.py:625
  54.0 4.6 %collective-permute-done.17.arrived = bf16[4,96,768]{2,1,0:T(8,128)(2,1)S(1)} collective-permute-done((bf16[4,96,768]{2,1,0:T(8,128)(2,1)S(1)}, bf16[4,96,768]{2,1,0:T(8,128)(2,1)S(1)}, u32[]{:S(2)}, u32[]{:S(2)}) %collective-permute-start.17) | collective-permute-done | bytes 589856 | tf_op jit(solution)/shard_map/ppermute | solution.py:630
  58.6 0.1 shard_map.302
  58.7 0.1 shard_map.303
  58.8 1.7 %collective-permute-start.21 = (bf16[2,48,128]{2,1,0:T(8,128)(2,1)S(1)}, bf16[2,48,128]{2,1,0:T(8,128)(2,1)S(1)}, u32[]{:S(2)}, u32[]{:S(2)}) collective-permute-start(bf16[2,48,128]{2,1,0:T(8,128)(2,1)S(1)} %get-tuple-element.188), channel_id=1, source_target_pairs={{0,8},{4,12},{8,0},{12,4},{16,24},{20,28},{24,16},{28,20},{1,9},{5... | collective-permute-start | bytes 73736 | tf_op jit(solution)/shard_map/ppermute | solution.py:625
  60.5 2.6 %collective-permute-start.24 = (bf16[1,48,1536]{2,1,0:T(8,128)(2,1)S(1)}, bf16[1,48,1536]{2,1,0:T(8,128)(2,1)S(1)}, u32[]{:S(2)}, u32[]{:S(2)}) collective-permute-start(bf16[1,48,1536]{2,1,0:T(8,128)(2,1)S(1)} %get-tuple-element.195), channel_id=1, source_target_pairs={{0,16},{4,20},{8,24},{12,28},{16,0},{20,4},{24,8},{28,12},{1,17},{... | collective-permute-start | bytes 442376 | tf_op jit(solution)/shard_map/ppermute | solution.py:625
  63.1 2.3 %collective-permute-start.23 = (bf16[2,96,768]{2,1,0:T(8,128)(2,1)S(1)}, bf16[2,96,768]{2,1,0:T(8,128)(2,1)S(1)}, u32[]{:S(2)}, u32[]{:S(2)}) collective-permute-start(bf16[2,96,768]{2,1,0:T(8,128)(2,1)S(1)} %get-tuple-element.193), channel_id=1, source_target_pairs={{0,8},{2,10},{4,12},{6,14},{8,0},{10,2},{12,4},{14,6},{17,25},{19,... | collective-permute-start | bytes 884744 | tf_op jit(solution)/shard_map/ppermute | solution.py:630
  65.5 1.8 %shard_map.304 = (bf16[3,64,768]{2,1,0:T(8,128)(2,1)}, bf16[3,64,768]{2,1,0:T(8,128)(2,1)}, f32[8,128]{1,0:T(8,128)S(1)}) custom-call(bf16[2,3,64,768]{3,2,1,0:T(8,128)(2,1)S(1)} %get-tuple-element.163.gb_a, bf16[2,3,64,768]{3,2,1,0:T(8,128)(2,1)S(1)} %collective-permute-done.14.gb_b, bf16[208,768]{1,0:T(8,128)(2,1)S(1)} %get-tuple-element.119.t0.tok, ...), custom_call_target="tpu_custom_call" | custom-call | bytes 1000000 | tf_op jit(solution)/shard_map/pallas_call | solution.py:752
  67.5 3.0 %collective-permute-start.22 = (bf16[1,48,128]{2,1,0:T(8,128)(2,1)S(1)}, bf16[1,48,128]{2,1,0:T(8,128)(2,1)S(1)}, u32[]{:S(2)}, u32[]{:S(2)}) collective-permute-start(bf16[1,48,128]{2,1,0:T(8,128)(2,1)S(1)} %get-tuple-element.191), channel_id=1, source_target_pairs={{0,16},{4,20},{8,24},{12,28},{16,0},{20,4},{24,8},{28,12},{1,17},{... | collective-permute-start | bytes 36872 | tf_op jit(solution)/shard_map/ppermute | solution.py:625
  70.4 4.0 %collective-permute-done.23.wr_a = bf16[2,96,768]{2,1,0:T(8,128)(2,1)S(1)} collective-permute-done((bf16[2,96,768]{2,1,0:T(8,128)(2,1)S(1)}, bf16[2,96,768]{2,1,0:T(8,128)(2,1)S(1)}, u32[]{:S(2)}, u32[]{:S(2)}) %collective-permute-start.23) | collective-permute-done | bytes 294944 | tf_op jit(solution)/shard_map/ppermute | solution.py:630
  74.4 0.1 shard_map.307
  74.6 0.5 collective-permute-start.27
  75.1 1.1 %collective-permute-done.22.vec_a = bf16[1,48,128]{2,1,0:T(8,128)(2,1)S(1)} collective-permute-done((bf16[1,48,128]{2,1,0:T(8,128)(2,1)S(1)}, bf16[1,48,128]{2,1,0:T(8,128)(2,1)S(1)}, u32[]{:S(2)}, u32[]{:S(2)}) %collective-permute-start.22) | collective-permute-done | bytes 12320 | tf_op jit(solution)/shard_map/ppermute | solution.py:625
  76.4 0.9 %shard_map.309 = (f32[24,3072]{1,0:T(8,128)}, f32[96,768]{1,0:T(8,128)}, f32[8,128]{1,0:T(8,128)S(1)}) custom-call(f32[24,1536]{1,0:T(8,128)S(1)} %get-tuple-element.202.we_keep, f32[24,1536]{1,0:T(8,128)S(1)} %collective-permute-done.26.we_arrived, f32[96,768]{1,0:T(8,128)S(1)} %get-tuple-element.204.wr_keep, ...), custom_call_target="tpu_custom_call" | custom-call | tf_op jit(solution)/shard_map/pallas_call | solution.py:775
  77.3 0.5 collective-permute-done.25.arrived
  77.7 0.7 shard_map.310
  (31 shorter events, 0.7 us)
Async XLA Ops:
  0.6 11.0 %collective-permute-start.1 = (bf16[3,64,768]{2,1,0:T(8,128)(2,1)}, bf16[3,64,768]{2,1,0:T(8,128)(2,1)S(1)}, u32[]{:S(2)}, u32[]{:S(2)}) collective-permute-start(bf16[3,64,768]{2,1,0:T(8,128)(2,1)} %tok.1), channel_id=1, source_target_pairs={{0,2},{1,3},{2,0},{3,1},{4,6},{5,7},{6,4},{7,5},{8,10},{9,11},{10,... | collective-permute-start | bytes 884744 | tf_op jit(solution)/shard_map/ppermute | solution.py:617
  7.4 5.0 %collective-permute-start = (bf16[208,768]{1,0:T(8,128)(2,1)S(1)}, bf16[208,768]{1,0:T(8,128)(2,1)S(1)}, u32[]{:S(2)}, u32[]{:S(2)}) collective-permute-start(bf16[208,768]{1,0:T(8,128)(2,1)S(1)} %get-tuple-element.119.t0.tok), channel_id=1, source_target_pairs={{0,1},{1,0},{2,3},{3,2},{4,5},{5,4},{6,7},{7,6},{8,9},{9,8},{10,11... | collective-permute-start | bytes 958472 | tf_op jit(solution)/shard_map/ppermute | solution.py:613
  7.4 4.2 %collective-permute-start.2 = (bf16[16,768]{1,0:T(8,128)(2,1)S(1)}, bf16[16,768]{1,0:T(8,128)(2,1)S(1)}, u32[]{:S(2)}, u32[]{:S(2)}) collective-permute-start(bf16[16,768]{1,0:T(8,128)(2,1)S(1)} %get-tuple-element.120), channel_id=1, source_target_pairs={{0,2},{1,3},{2,0},{3,1},{4,6},{5,7},{6,4},{7,5},{8,10},{9,11},{10,... | collective-permute-start | bytes 73736 | tf_op jit(solution)/shard_map/ppermute | solution.py:617
  7.5 10.2 %collective-permute-start.6 = (bf16[3,64,768]{2,1,0:T(8,128)(2,1)S(1)}, bf16[3,64,768]{2,1,0:T(8,128)(2,1)S(1)}, u32[]{:S(2)}, u32[]{:S(2)}) collective-permute-start(bf16[3,64,768]{2,1,0:T(8,128)(2,1)S(1)} %get-tuple-element.128.c0), channel_id=1, source_target_pairs={{0,2},{1,3},{2,0},{3,1},{4,6},{5,7},{6,4},{7,5},{8,10},{9,11},{10,... | collective-permute-start | bytes 884744 | tf_op jit(solution)/shard_map/ppermute | solution.py:617
  11.7 2.1 %collective-permute-start.3 = (bf16[160,768]{1,0:T(8,128)(2,1)S(1)}, bf16[160,768]{1,0:T(8,128)(2,1)S(1)}, u32[]{:S(2)}, u32[]{:S(2)}) collective-permute-start(bf16[160,768]{1,0:T(8,128)(2,1)S(1)} %get-tuple-element.122.x_a), channel_id=1, source_target_pairs={{0,1},{1,0},{2,3},{3,2},{4,5},{5,4},{6,7},{7,6},{8,9},{9,8},{10,11... | collective-permute-start | bytes 737288 | tf_op jit(solution)/shard_map/ppermute | solution.py:613
  11.8 6.6 %collective-permute-start.5 = (bf16[3,64,768]{2,1,0:T(8,128)(2,1)S(1)}, bf16[3,64,768]{2,1,0:T(8,128)(2,1)S(1)}, u32[]{:S(2)}, u32[]{:S(2)}) collective-permute-start(bf16[3,64,768]{2,1,0:T(8,128)(2,1)S(1)} %get-tuple-element.128.c0), channel_id=1, source_target_pairs={{0,1},{1,0},{2,3},{3,2},{4,5},{5,4},{6,7},{7,6},{8,9},{9,8},{10,11... | collective-permute-start | bytes 884744 | tf_op jit(solution)/shard_map/ppermute | solution.py:613
  12.3 1.5 %collective-permute-start.4 = (bf16[48,768]{1,0:T(8,128)(2,1)S(1)}, bf16[48,768]{1,0:T(8,128)(2,1)S(1)}, u32[]{:S(2)}, u32[]{:S(2)}) collective-permute-start(bf16[48,768]{1,0:T(8,128)(2,1)S(1)} %get-tuple-element.123.x_b), channel_id=1, source_target_pairs={{0,1},{1,0},{2,3},{3,2},{4,5},{5,4},{6,7},{7,6},{8,9},{9,8},{10,11... | collective-permute-start | bytes 221192 | tf_op jit(solution)/shard_map/ppermute | solution.py:613
  16.9 2.2 %collective-permute-start.9 = (bf16[224,384]{1,0:T(8,128)(2,1)S(1)}, bf16[224,384]{1,0:T(8,128)(2,1)S(1)}, u32[]{:S(2)}, u32[]{:S(2)}) collective-permute-start(bf16[224,384]{1,0:T(8,128)(2,1)S(1)} %get-tuple-element.125.mix_a), channel_id=1, source_target_pairs={{0,1},{1,0},{2,3},{3,2},{4,5},{5,4},{6,7},{7,6},{8,9},{9,8},{10,11... | collective-permute-start | bytes 516104 | tf_op jit(solution)/shard_map/ppermute | solution.py:613
  17.1 2.0 %collective-permute-start.10 = (bf16[208,384]{1,0:T(8,128)(2,1)S(1)}, bf16[208,384]{1,0:T(8,128)(2,1)S(1)}, u32[]{:S(2)}, u32[]{:S(2)}) collective-permute-start(bf16[208,384]{1,0:T(8,128)(2,1)S(1)} %get-tuple-element.126.mix2_a), channel_id=1, source_target_pairs={{0,1},{1,0},{2,3},{3,2},{4,5},{5,4},{6,7},{7,6},{8,9},{9,8},{10,11... | collective-permute-start | bytes 479240 | tf_op jit(solution)/shard_map/ppermute | solution.py:613
  17.7 3.7 %collective-permute-start.7 = (bf16[96,768]{1,0:T(8,128)(2,1)S(1)}, bf16[96,768]{1,0:T(8,128)(2,1)S(1)}, u32[]{:S(2)}, u32[]{:S(2)}) collective-permute-start(bf16[96,768]{1,0:T(8,128)(2,1)S(1)} %get-tuple-element.129.x_a), channel_id=1, source_target_pairs={{0,1},{1,0},{2,3},{3,2},{4,5},{5,4},{6,7},{7,6},{8,9},{9,8},{10,11... | collective-permute-start | bytes 442376 | tf_op jit(solution)/shard_map/ppermute | solution.py:613
  17.8 3.6 %collective-permute-start.8 = (bf16[96,768]{1,0:T(8,128)(2,1)S(1)}, bf16[96,768]{1,0:T(8,128)(2,1)S(1)}, u32[]{:S(2)}, u32[]{:S(2)}) collective-permute-start(bf16[96,768]{1,0:T(8,128)(2,1)S(1)} %get-tuple-element.130.x_b), channel_id=1, source_target_pairs={{0,1},{1,0},{2,3},{3,2},{4,5},{5,4},{6,7},{7,6},{8,9},{9,8},{10,11... | collective-permute-start | bytes 442376 | tf_op jit(solution)/shard_map/ppermute | solution.py:613
  23.1 16.2 %collective-permute-start.13 = (bf16[4,96,768]{2,1,0:T(8,128)(2,1)S(1)}, bf16[4,96,768]{2,1,0:T(8,128)(2,1)S(1)}, u32[]{:S(2)}, u32[]{:S(2)}) collective-permute-start(bf16[4,96,768]{2,1,0:T(8,128)(2,1)S(1)} %get-tuple-element.160), channel_id=1, source_target_pairs={{0,4},{4,0},{8,12},{12,8},{16,20},{20,16},{24,28},{28,24},{1,5},{5... | collective-permute-start | bytes 1769480 | tf_op jit(solution)/shard_map/ppermute | solution.py:621
  27.3 3.4 %collective-permute-start.11 = (bf16[432,384]{1,0:T(8,128)(2,1)S(1)}, bf16[432,384]{1,0:T(8,128)(2,1)S(1)}, u32[]{:S(2)}, u32[]{:S(2)}) collective-permute-start(bf16[432,384]{1,0:T(8,128)(2,1)S(1)} %get-tuple-element.143.l_a), channel_id=1, source_target_pairs={{0,1},{1,0},{2,3},{3,2},{4,5},{5,4},{6,7},{7,6},{8,9},{9,8},{10,11... | collective-permute-start | bytes 995336 | tf_op jit(solution)/shard_map/ppermute | solution.py:613
  27.4 3.4 %collective-permute-start.12 = (bf16[432,384]{1,0:T(8,128)(2,1)S(1)}, bf16[432,384]{1,0:T(8,128)(2,1)S(1)}, u32[]{:S(2)}, u32[]{:S(2)}) collective-permute-start(bf16[432,384]{1,0:T(8,128)(2,1)S(1)} %get-tuple-element.144.r_a), channel_id=1, source_target_pairs={{0,1},{1,0},{2,3},{3,2},{4,5},{5,4},{6,7},{7,6},{8,9},{9,8},{10,11... | collective-permute-start | bytes 995336 | tf_op jit(solution)/shard_map/ppermute | solution.py:613
  29.1 18.0 %collective-permute-start.15 = (bf16[4,48,1536]{2,1,0:T(8,128)(2,1)S(1)}, bf16[4,48,1536]{2,1,0:T(8,128)(2,1)S(1)}, u32[]{:S(2)}, u32[]{:S(2)}) collective-permute-start(bf16[4,48,1536]{2,1,0:T(8,128)(2,1)S(1)} %get-tuple-element.166), channel_id=1, source_target_pairs={{0,8},{4,12},{8,0},{12,4},{16,24},{20,28},{24,16},{28,20},{1,9},{5... | collective-permute-start | bytes 1769480 | tf_op jit(solution)/shard_map/ppermute | solution.py:625
  35.0 17.0 %collective-permute-start.18 = (bf16[4,48,1536]{2,1,0:T(8,128)(2,1)S(1)}, bf16[4,48,1536]{2,1,0:T(8,128)(2,1)S(1)}, u32[]{:S(2)}, u32[]{:S(2)}) collective-permute-start(bf16[4,48,1536]{2,1,0:T(8,128)(2,1)S(1)} %get-tuple-element.175), channel_id=1, source_target_pairs={{0,4},{4,0},{8,12},{12,8},{16,20},{20,16},{24,28},{28,24},{1,5},{5... | collective-permute-start | bytes 1769480 | tf_op jit(solution)/shard_map/ppermute | solution.py:621
  39.5 19.1 %collective-permute-start.17 = (bf16[4,96,768]{2,1,0:T(8,128)(2,1)S(1)}, bf16[4,96,768]{2,1,0:T(8,128)(2,1)S(1)}, u32[]{:S(2)}, u32[]{:S(2)}) collective-permute-start(bf16[4,96,768]{2,1,0:T(8,128)(2,1)S(1)} %get-tuple-element.173), channel_id=1, source_target_pairs={{1,17},{3,19},{5,21},{7,23},{9,25},{11,27},{13,29},{15,31},{16,0},... | collective-permute-start | bytes 1769480 | tf_op jit(solution)/shard_map/ppermute | solution.py:630
  45.3 20.2 %collective-permute-start.14 = (bf16[2,3,64,768]{3,2,1,0:T(8,128)(2,1)S(1)}, bf16[2,3,64,768]{3,2,1,0:T(8,128)(2,1)S(1)}, u32[]{:S(2)}, u32[]{:S(2)}) collective-permute-start(bf16[2,3,64,768]{3,2,1,0:T(8,128)(2,1)S(1)} %get-tuple-element.164), channel_id=1, source_target_pairs={{0,1},{1,0},{2,3},{3,2},{4,5},{5,4},{6,7},{7,6},{8,9},{9,8},{10,11... | collective-permute-start | bytes 1769480 | tf_op jit(solution)/shard_map/ppermute | solution.py:613
  47.1 11.6 %collective-permute-start.16 = (bf16[2,48,1792]{2,1,0:T(8,128)(2,1)S(1)}, bf16[2,48,1792]{2,1,0:T(8,128)(2,1)S(1)}, u32[]{:S(2)}, u32[]{:S(2)}) collective-permute-start(bf16[2,48,1792]{2,1,0:T(8,128)(2,1)S(1)} %get-tuple-element.171), channel_id=1, source_target_pairs={{0,4},{4,0},{8,12},{12,8},{16,20},{20,16},{24,28},{28,24},{1,5},{5... | collective-permute-start | bytes 1032200 | tf_op jit(solution)/shard_map/ppermute | solution.py:621
  52.1 15.2 %collective-permute-start.19 = (bf16[2,48,1536]{2,1,0:T(8,128)(2,1)S(1)}, bf16[2,48,1536]{2,1,0:T(8,128)(2,1)S(1)}, u32[]{:S(2)}, u32[]{:S(2)}) collective-permute-start(bf16[2,48,1536]{2,1,0:T(8,128)(2,1)S(1)} %get-tuple-element.183), channel_id=1, source_target_pairs={{0,8},{4,12},{8,0},{12,4},{16,24},{20,28},{24,16},{28,20},{1,9},{5... | collective-permute-start | bytes 884744 | tf_op jit(solution)/shard_map/ppermute | solution.py:625
  58.8 8.6 %collective-permute-start.21 = (bf16[2,48,128]{2,1,0:T(8,128)(2,1)S(1)}, bf16[2,48,128]{2,1,0:T(8,128)(2,1)S(1)}, u32[]{:S(2)}, u32[]{:S(2)}) collective-permute-start(bf16[2,48,128]{2,1,0:T(8,128)(2,1)S(1)} %get-tuple-element.188), channel_id=1, source_target_pairs={{0,8},{4,12},{8,0},{12,4},{16,24},{20,28},{24,16},{28,20},{1,9},{5... | collective-permute-start | bytes 73736 | tf_op jit(solution)/shard_map/ppermute | solution.py:625
  60.5 9.9 %collective-permute-start.24 = (bf16[1,48,1536]{2,1,0:T(8,128)(2,1)S(1)}, bf16[1,48,1536]{2,1,0:T(8,128)(2,1)S(1)}, u32[]{:S(2)}, u32[]{:S(2)}) collective-permute-start(bf16[1,48,1536]{2,1,0:T(8,128)(2,1)S(1)} %get-tuple-element.195), channel_id=1, source_target_pairs={{0,16},{4,20},{8,24},{12,28},{16,0},{20,4},{24,8},{28,12},{1,17},{... | collective-permute-start | bytes 442376 | tf_op jit(solution)/shard_map/ppermute | solution.py:625
  63.1 11.3 %collective-permute-start.23 = (bf16[2,96,768]{2,1,0:T(8,128)(2,1)S(1)}, bf16[2,96,768]{2,1,0:T(8,128)(2,1)S(1)}, u32[]{:S(2)}, u32[]{:S(2)}) collective-permute-start(bf16[2,96,768]{2,1,0:T(8,128)(2,1)S(1)} %get-tuple-element.193), channel_id=1, source_target_pairs={{0,8},{2,10},{4,12},{6,14},{8,0},{10,2},{12,4},{14,6},{17,25},{19,... | collective-permute-start | bytes 884744 | tf_op jit(solution)/shard_map/ppermute | solution.py:630
  67.4 8.9 %collective-permute-start.20 = (bf16[1,48,1536]{2,1,0:T(8,128)(2,1)S(1)}, bf16[1,48,1536]{2,1,0:T(8,128)(2,1)S(1)}, u32[]{:S(2)}, u32[]{:S(2)}) collective-permute-start(bf16[1,48,1536]{2,1,0:T(8,128)(2,1)S(1)} %get-tuple-element.186), channel_id=1, source_target_pairs={{0,16},{4,20},{8,24},{12,28},{16,0},{20,4},{24,8},{28,12},{1,17},{... | collective-permute-start | bytes 442376 | tf_op jit(solution)/shard_map/ppermute | solution.py:625
  67.5 8.8 %collective-permute-start.22 = (bf16[1,48,128]{2,1,0:T(8,128)(2,1)S(1)}, bf16[1,48,128]{2,1,0:T(8,128)(2,1)S(1)}, u32[]{:S(2)}, u32[]{:S(2)}) collective-permute-start(bf16[1,48,128]{2,1,0:T(8,128)(2,1)S(1)} %get-tuple-element.191), channel_id=1, source_target_pairs={{0,16},{4,20},{8,24},{12,28},{16,0},{20,4},{24,8},{28,12},{1,17},{... | collective-permute-start | bytes 36872 | tf_op jit(solution)/shard_map/ppermute | solution.py:625
  74.5 1.8 %collective-permute-start.26 = (f32[24,1536]{1,0:T(8,128)S(1)}, f32[24,1536]{1,0:T(8,128)S(1)}, u32[]{:S(2)}, u32[]{:S(2)}) collective-permute-start(f32[24,1536]{1,0:T(8,128)S(1)} %get-tuple-element.203), channel_id=1, source_target_pairs={{0,1},{1,0},{2,3},{3,2},{4,5},{5,4},{6,7},{7,6},{8,9},{9,8},{10,11... | collective-permute-start | bytes 442376 | tf_op jit(solution)/shard_map/ppermute | solution.py:613
  74.6 1.8 %collective-permute-start.27 = (bf16[96,768]{1,0:T(8,128)(2,1)S(1)}, bf16[96,768]{1,0:T(8,128)(2,1)S(1)}, u32[]{:S(2)}, u32[]{:S(2)}) collective-permute-start(bf16[96,768]{1,0:T(8,128)(2,1)S(1)} %get-tuple-element.205), channel_id=1, source_target_pairs={{0,1},{1,0},{2,3},{3,2},{4,5},{5,4},{6,7},{7,6},{8,9},{9,8},{10,11... | collective-permute-start | bytes 442376 | tf_op jit(solution)/shard_map/ppermute | solution.py:613
  76.3 1.4 %collective-permute-start.25 = (f32[24,1408]{1,0:T(8,128)S(1)}, f32[24,1408]{1,0:T(8,128)S(1)}, u32[]{:S(2)}, u32[]{:S(2)}) collective-permute-start(f32[24,1408]{1,0:T(8,128)S(1)} %get-tuple-element.201), channel_id=1, source_target_pairs={{0,1},{1,0},{2,3},{3,2},{4,5},{5,4},{6,7},{7,6},{8,9},{9,8},{10,11... | collective-permute-start | bytes 405512 | tf_op jit(solution)/shard_map/ppermute | solution.py:613

commit v7 on v6

--- a/solution.py
+++ b/solution.py
@@ -521,74 +521,81 @@
         out[...] = (wr_k[at] + wr_a[at].astype(F32)).astype(out.dtype)
     both[...] = we_k[0] + we_a[0].astype(F32)
     we_ko[...] = both[pl.ds(pl.multiple_of(c * 24, 8), 24), :]
-    we_so[...] = both[pl.ds(pl.multiple_of(24 - c * 24, 8), 24), :]
-
-
-def early_out_kernel(we_keep, we_arrived, wr_keep, wr_arrived, after, we_o, wr_o, tick):
-    tick[...] = jnp.zeros_like(tick)
+    we_so[...] = both[pl.ds(pl.multiple_of(24 - c * 24, 8), 24), :].astype(BF)
+
+
+USED = 16
+NEAR = QC + D
+
+
+def cut_kernel(keep, arrived, after, mine_o, hop_o, near_o, far_o, tick, both):
+    tick[...] = jnp.zeros_like(tick)
+    c = lax.axis_index("band") & 1
+    mine, theirs = pl.multiple_of(c * 24, 8), pl.multiple_of(24 - c * 24, 8)
+    for n, own_o, other_o in ((0, mine_o, hop_o), (1, near_o, far_o)):
+        both[...] = keep[n].astype(F32) + arrived[n].astype(F32)
+        own_o[:, 0:QC] = both[pl.ds(mine, 24), 0:QC].astype(own_o.dtype)
+        other_o[...] = both[pl.ds(theirs, 24), 0:QC].astype(own_o.dtype)
+        own_o[:, QC : QC + HALF] = both[0:24, QC:QW].astype(own_o.dtype)
+        own_o[:, QC + HALF :] = both[24:48, QC:QW].astype(own_o.dtype)
+
+
+def cores_kernel(vec_a, vec_b, hop, after, keep_o, send_o, other_o, tick):
+    tick[...] = jnp.zeros_like(tick)
+    keep_o[...] = jnp.zeros_like(keep_o)
+    keep_o[:, 0:USED] = vec_a[0, :, 0:USED] + vec_b[0].astype(F32)
+    send_o[...] = (vec_a[1, :, 0:USED] + vec_b[1].astype(F32)).astype(BF)
+    other_o[...] = hop[...]
+
+
+def vector_fold_kernel(keep, arrived, after, out, send_o, tick):
+    tick[...] = jnp.zeros_like(tick)
+    total = keep[...] + arrived[...].astype(F32)
+    out[...] = total
+    send_o[...] = total[:, :, 0:USED].astype(BF)
+
+
+def total_kernel(mine, near, hop, far, vec_k, vec_a, after, own_o, other_o, vec_o, tick):
+    tick[...] = jnp.zeros_like(tick)
+    own_o[...] = mine[...] + near[...].astype(F32)
+    other_o[...] = hop[...] + far[...].astype(F32)
+    vec_o[...] = vec_k[...]
+    vec_o[:, 0:USED] = vec_k[:, 0:USED] + vec_a[...].astype(F32)
+
+
+def out_kernel(
+    own, other, vec_r, we_keep, we_arrived, wr_keep, wr_arrived, after,
+    qkv_o, first_o, bias_o, qv_o, bp_o, asc_o, gain2_o, bias2_o, br_o, msc_o, eb_o, proj_o, we_o, wr_o,
+):
     _, c, z, _ = place()
     wr_o[...] = jnp.where((z >> 1) == c, wr_keep[...], wr_arrived[...].astype(F32))
     we_o[:, pl.ds(pl.multiple_of(c * FH, 128), FH)] = we_keep[...]
-    we_o[:, pl.ds(pl.multiple_of((1 - c) * FH, 128), FH)] = we_arrived[...]
-
-
-def finish_kernel(qp_k, qp_a, vec_k, vec_a, after, keep_o, send_o, vec_o, proj_o, tick, sums):
-    tick[...] = jnp.zeros_like(tick)
-    c = lax.axis_index("band") & 1
-    sums[...] = qp_k[0] + qp_a[0].astype(F32)
-    keep_o[...] = sums[pl.ds(pl.multiple_of(c * 24, 8), 24), 0:QC]
-    send_o[:, 0:QC] = sums[pl.ds(pl.multiple_of(24 - c * 24, 8), 24), 0:QC]
-    vec = vec_k[0] + vec_a[0].astype(F32)
-    vec_o[...] = vec
-    send_o[:, QC : QC + SMALL] = vec[0:24]
-    send_o[:, QC + SMALL :] = vec[24:48]
-    proj_o[:, 0:HALF] = sums[0:24, QC:QW]
-    proj_o[:, HALF:] = sums[24:48, QC:QW]
-
-
-def out_kernel(
-    keep, vec, proj, arrived, after,
-    qkv_o, first_o, bias_o, qv_o, bp_o, asc_o, gain2_o, bias2_o, br_o, msc_o, eb_o, proj_o, both,
-):
-    c = lax.axis_index("band") & 1
-    proj_o[...] = proj[...]
+    we_o[:, pl.ds(pl.multiple_of((1 - c) * FH, 128), FH)] = we_arrived[...].astype(F32)
+    proj_o[...] = own[:, QC:NEAR]
     for m in range(3):
-        mine = pl.multiple_of(m * D + c * HALF, 128)
-        other = pl.multiple_of(m * D + (1 - c) * HALF, 128)
-        qkv_o[:, pl.ds(mine, HALF)] = keep[:, m * HALF : (m + 1) * HALF]
-        qkv_o[:, pl.ds(other, HALF)] = arrived[:, m * HALF : (m + 1) * HALF]
-    both[0:24] = vec[0:24] + arrived[:, QC : QC + SMALL]
-    both[24:48] = vec[24:48] + arrived[:, QC + SMALL :]
-    own = both[pl.ds(pl.multiple_of(c * 24, 8), 24), :].T
+        cols = slice(m * HALF, (m + 1) * HALF)
+        qkv_o[:, pl.ds(pl.multiple_of(m * D + c * HALF, 128), HALF)] = own[:, cols]
+        qkv_o[:, pl.ds(pl.multiple_of(m * D + (1 - c) * HALF, 128), HALF)] = other[:, cols]
+    vec = vec_r[pl.ds(pl.multiple_of(c * 24, 8), 24), :].T
     outs = (first_o, bias_o, None, None, bp_o, asc_o, gain2_o, bias2_o, br_o, msc_o)
     for r, out in enumerate(outs):
         if out is not None:
-            out[...] = own[r]
-    qv_o[...] = own[2:4]
-    units = both[...].T
+            out[...] = vec[r]
+    qv_o[...] = vec[2:4]
+    units = vec_r[...].T
     units = jnp.where(c == 0, units[10:12], units[12:14])
     eb_o[...] = jnp.concatenate([units[0:1], units[1:2]], axis=1).reshape(96)
 
 
 COSTS = {
-    "first_kernel": (0, 0),
-    "pick_kernel": (0, 0),
-    "hidden_kernel": (0, 0),
-    "reduce_grad_kernel": (0, 0),
-    "back_kernel": (0, 0),
-    "expand_grad_kernel": (0, 0),
-    "attention_back_kernel": (0, 0),
     "vectors_kernel": (8000000000, 20000000),
-    "fold_kernel": (0, 0),
     "second_fold_kernel": (0, 2000000),
     "last_kernel": (0, 1000000),
     "spread_kernel": (0, 2000000),
     "finish_kernel": (0, 1000000),
     "out_kernel": (0, 1000000),
     "prepare_kernel": (0, 9000000),
-    "hold_kernel": (0, 0),
-    "home_kernel": (0, 0),
-    "half_kernel": (0, 0),
+    "total_kernel": (4000000000, 0),
 }
 
 
@@ -623,6 +630,10 @@
 
 def by_z(value, dz):
     return lax.ppermute(value, "batch", [(i, i ^ (2 * dz)) for i in range(8)])
+
+
+def across(value):
+    return lax.ppermute(value, ("batch", "band"), [(d, d ^ 17) for d in range(32)])
 
 
 def homeward(value, dz):
@@ -738,9 +749,9 @@
         join_kernel, (vm((2, 48, FS), F32), vm((2, 48, FS), BF), TICK), [VM] * 4 + [ANY]
     )(we_keep, we_z, vec_keep, vec_send, tick)
     we_y = by_y(we_send)
-    qp_keep, qp_send, tick = fold_call(qp_keep, qp_y, tick)
+    qp_keep, qp_send, tick = fold_call(qp_keep, qp_y, tick, cost=0)
     qp_z = by_z(qp_send, 1)
-    wr_keep, wr_send, tick = fold_call(wr_keep, wr_z, tick)
+    wr_keep, wr_send, tick = fold_call(wr_keep, wr_z, tick, cost=0)
     wr_z = homeward(wr_send, 1)
     we_keep, we_send, vec_keep, vec_send, tick = call(
         part_kernel,
@@ -749,42 +760,50 @@
     )(we_keep, we_y, tick)
     vec_z = by_z(vec_send, 1)
     we_z = by_z(we_send, 2)
+    mine, hop, near, far, tick = call(
+        cut_kernel,
+        (vm((24, NEAR), F32), vm((24, QC), F32), vm((24, NEAR), BF), vm((24, QC), BF), TICK),
+        [VM] * 2 + [ANY],
+        [pltpu.VMEM((48, QW), F32)],
+        cost=0,
+    )(qp_keep, qp_z, tick)
+    near, far, hop = by_z(near, 2), across(far), by_core(hop)
+    vec, vec_send, tick = call(
+        vector_fold_kernel, (vm((2, 48, SMALL), F32), vm((2, 48, USED), BF), TICK), [VM] * 2 + [ANY], cost=4000000000
+    )(vec_keep, vec_z, tick)
+    vec_other = by_core(vec_send)
     layer_out, grad_tokens, tick = call(
         last_kernel,
         (sds(tokens.shape, BF), sds(tokens.shape, BF), TICK),
         [VM] * 7 + [ANY],
     )(gb_keep, gb_other, tok_own, gres, res, pos_mine, par, tick)
-    qp_keep, qp_send, tick = fold_call(qp_keep, qp_z, tick)
-    qp_z = by_z(qp_send, 2)
-    vec_keep, vec_send, tick = fold_call(vec_keep, vec_z, tick, cost=4000000000)
+    vec_keep, vec_send, hop, tick = call(
+        cores_kernel,
+        (vm((48, SMALL), F32), vm((48, USED), BF), vm((24, QC), F32), TICK),
+        [VM] * 3 + [ANY],
+    )(vec, vec_other, hop, tick)
     vec_z = by_z(vec_send, 2)
     wr_keep, wr_send, we_keep, we_send, tick = call(
         settle_kernel,
-        (vm((96, D), F32), vm((96, D), BF), vm((24, FH), F32), vm((24, FH), F32), TICK),
+        (vm((96, D), F32), vm((96, D), BF), vm((24, FH), F32), vm((24, FH), BF), TICK),
         [VM] * 4 + [ANY],
         [pltpu.VMEM((48, FH), F32)],
     )(wr_keep, wr_z, we_keep, we_z, tick)
     we_other, wr_other = by_core(we_send), by_core(wr_send)
-    qp_keep, qp_send, vec, proj, tick = call(
-        finish_kernel,
-        (vm((24, QC), F32), vm((24, QC + 2 * SMALL), F32), vm((48, SMALL), F32), vm((24, D), F32), TICK),
-        [VM] * 4 + [ANY],
-        [pltpu.VMEM((48, QW), F32)],
-    )(qp_keep, qp_z, vec_keep, vec_z, tick)
-    qp_other = by_core(qp_send)
-    grad_expand, grad_reduce, tick = call(
-        early_out_kernel, (sds((24, FF), F32), sds((96, D), F32), TICK), [VM] * 4 + [ANY]
-    )(we_keep, we_other, wr_keep, wr_other, tick)
+    own, other, vec, tick = call(
+        total_kernel,
+        (vm((24, NEAR), F32), vm((24, QC), F32), vm((48, SMALL), F32), TICK),
+        [VM] * 6 + [ANY],
+    )(mine, near, hop, far, vec_keep, vec_z, tick)
     vector = sds((24,), F32)
-    grad_qkv, gg1, gb1, gqv, gbp, gas, gg2, gb2, gbr, gms, geb, grad_proj = call(
+    grad_qkv, gg1, gb1, gqv, gbp, gas, gg2, gb2, gbr, gms, geb, grad_proj, grad_expand, grad_reduce = call(
         out_kernel,
         (
             sds((24, 3 * D), F32), vector, vector, sds((2, 24), F32), vector, vector, vector, vector, vector, vector,
-            sds((96,), F32), sds((24, D), F32),
+            sds((96,), F32), sds((24, D), F32), sds((24, FF), F32), sds((96, D), F32),
         ),
-        [VM] * 4 + [ANY],
-        [pltpu.VMEM((48, SMALL), F32)],
-    )(qp_keep, vec, proj, qp_other, tick)
+        [VM] * 7 + [ANY],
+    )(own, other, vec, we_keep, we_other, wr_keep, wr_other, tick)
     return (
         layer_out, grad_tokens, gg1, gb1, grad_qkv, gqv, grad_proj, gbp, gas, gg2, gb2, grad_expand, geb, grad_reduce,
         gbr, gms,

time: 78.8 us -> 77.8 us (0.987)
  starting transfers between devices: 28.7 us -> 27.7 us
    ppermute x6, starting transfers between devices: 10.9 us -> 8.12 us  [by_z(): return lax.ppermute(value, 'batch', [(i, i ^ 2 * dz) for i in range(8)])]
    ppermute x0 -> x1, starting transfers between devices: none -> 2.79 us  [across(): lax.ppermute(value, ('batch', 'band'), [(d, d ^ 17) for d in range(32)])]
    ppermute x2, waiting for transfers between devices: 8.57 us -> 6.74 us  [homeward(): return lax.ppermute(value, ('batch', 'band'), pairs)]
    ppermute x3, waiting for transfers between devices: 7.05 us -> 8.55 us  [by_y(): return lax.ppermute(value, 'batch', [(i, i ^ 1) for i in range(8)])]
    ppermute x14 -> x15, starting transfers between devices: 4.8 us -> 3.63 us  [by_core(): return lax.ppermute(value, 'band', [(i, i ^ 1) for i in range(4)])]
    ppermute x14 -> x15, waiting for transfers between devices: 1.93 us -> 2.33 us  [by_core(): return lax.ppermute(value, 'band', [(i, i ^ 1) for i in range(4)])]
  transfers between devices with their start and end apart: 28 -> 30, of which waited for: 9 -> 10; matrix products, arithmetic and copies ran while one was open for 0% -> 0% of each run, Pallas kernels for 32% -> 32%
where the time goes in v7:
time: 77.8 us; the launch traced here: 77.6 us
  starting transfers between devices  27.7 us (36%)
  Pallas kernels  27.2 us (35%)
  waiting for transfers between devices  21.7 us (28%)
  between operations  1.06 us (1%)
    ppermute x3, waiting for transfers between devices, by_y(): return lax.ppermute(value, 'batch', [(i, i ^ 1) for i in range(8)])  8.55 us
    ppermute x6, starting transfers between devices, by_z(): return lax.ppermute(value, 'batch', [(i, i ^ 2 * dz) for i in range(8)])  8.12 us
    ppermute x2, waiting for transfers between devices, homeward(): return lax.ppermute(value, ('batch', 'band'), pairs)  6.74 us
    ppermute x3, starting transfers between devices, by_x(): return lax.ppermute(value, 'band', [(i, i ^ 2) for i in range(4)])  5.09 us
    pallas_call x1, Pallas kernels, packed_body(): call(vectors_kernel, (vm((2, *tokens.shape), BF), vm((2, *tokens.shape),...  4.25 us
    pallas_call x1, Pallas kernels, packed_body(): call(attention_back_kernel, (rows_f, vm((ROWS, QC), BF), vm((4, 48, QW),...  4.21 us
    ppermute x3, starting transfers between devices, by_y(): return lax.ppermute(value, 'batch', [(i, i ^ 1) for i in range(8)])  4.2 us
    ppermute x2, starting transfers between devices, homeward(): return lax.ppermute(value, ('batch', 'band'), pairs)  3.85 us
  transfers between devices with their start and end apart: 30, of which 10 were waited for; matrix products, arithmetic and copies ran while one was open for 0% of the time, Pallas kernels for 32%

profile of v7, /device:TPU:0, one launch (start us, length us, event | category | flops | bytes accessed | tf_op | source)
XLA Modules:
  0.0 77.6 jit_solution(10695983924587122450)
XLA Ops:
  0.6 3.0 %collective-permute-start.1 = (bf16[3,64,768]{2,1,0:T(8,128)(2,1)}, bf16[3,64,768]{2,1,0:T(8,128)(2,1)S(1)}, u32[]{:S(2)}, u32[]{:S(2)}) collective-permute-start(bf16[3,64,768]{2,1,0:T(8,128)(2,1)} %tok.1), channel_id=1, source_target_pairs={{0,2},{1,3},{2,0},{3,1},{4,6},{5,7},{6,4},{7,5},{8,10},{9,11},{10,... | collective-permute-start | bytes 884744 | tf_op jit(solution)/shard_map/ppermute | solution.py:624
  3.7 3.7 %shard_map.288 = (bf16[3,64,768]{2,1,0:T(8,128)(2,1)S(1)}, bf16[208,768]{1,0:T(8,128)(2,1)S(1)}, f32[16,768]{1,0:T(8,128)S(1)}, f32[8,1536]{1,0:T(8,128)S(1)}, b...) custom-call(bf16[3,64,768]{2,1,0:T(8,128)(2,1)} %cot.1, ...), custom_call_target="tpu_custom_call" | custom-call | bytes 9000000 | tf_op jit(solution)/shard_map/pallas_call | solution.py:652
  7.4 0.1 collective-permute-start.2
  7.5 2.0 %collective-permute-start.6 = (bf16[3,64,768]{2,1,0:T(8,128)(2,1)S(1)}, bf16[3,64,768]{2,1,0:T(8,128)(2,1)S(1)}, u32[]{:S(2)}, u32[]{:S(2)}) collective-permute-start(bf16[3,64,768]{2,1,0:T(8,128)(2,1)S(1)} %get-tuple-element.132.c0), channel_id=1, source_target_pairs={{0,2},{1,3},{2,0},{3,1},{4,6},{5,7},{6,4},{7,5},{8,10},{9,11},{10,... | collective-permute-start | bytes 884744 | tf_op jit(solution)/shard_map/ppermute | solution.py:624
  9.5 2.1 %collective-permute-done.2.vis = bf16[16,768]{1,0:T(8,128)(2,1)S(1)} collective-permute-done((bf16[16,768]{1,0:T(8,128)(2,1)S(1)}, bf16[16,768]{1,0:T(8,128)(2,1)S(1)}, u32[]{:S(2)}, u32[]{:S(2)}) %collective-permute-start.2) | collective-permute-done | bytes 24608 | tf_op jit(solution)/shard_map/ppermute | solution.py:624
  11.8 0.5 collective-permute-start.5
  12.3 1.4 %collective-permute-done.4.d_b = bf16[48,768]{1,0:T(8,128)(2,1)S(1)} collective-permute-done((bf16[48,768]{1,0:T(8,128)(2,1)S(1)}, bf16[48,768]{1,0:T(8,128)(2,1)S(1)}, u32[]{:S(2)}, u32[]{:S(2)}) %collective-permute-start.4) | collective-permute-done | bytes 73760 | tf_op jit(solution)/shard_map/ppermute | solution.py:620
  13.8 3.1 %shard_map.290 = (bf16[432,768]{1,0:T(8,128)(2,1)S(1)}, bf16[432,768]{1,0:T(8,128)(2,1)S(1)}, bf16[3,432,384]{2,1,0:T(8,128)(2,1)S(1)}, bf16[224,384]{1,0:T(8,12...) custom-call(bf16[208,768]{1,0:T(8,128)(2,1)S(1)} %get-tuple-element., ...), custom_call_target="tpu_custom_call" | custom-call | tf_op jit(solution)/shard_map/pallas_call | solution.py:687
  16.9 0.2 collective-permute-start.9
  17.1 0.4 collective-permute-start.10
  17.4 0.3 collective-permute-done.6.v
  17.8 0.5 collective-permute-start.8
  18.3 0.7 shard_map.292
  19.1 2.3 %shard_map.293 = (f32[432,768]{1,0:T(8,128)S(1)}, f32[432,768]{1,0:T(8,128)S(1)}, bf16[432,768]{1,0:T(8,128)(2,1)S(1)}, bf16[432,1536]{1,0:T(8,128)(2,1)S(1)}, f32[432,1536]{1,0:T(8,128)S(1)}) custom-call(f32[432,768]{1,0:T(8,128)S(1)} %get-tuple-element.138.half, bf16[224,384]{1,0:T(8,128)(2,1)S(1)} %collective-permute-done.9.mix_b, ...), custom_call_target="tpu_custom_call" | custom-call | tf_op jit(solution)/shard_map/pallas_call | solution.py:708
  21.4 1.7 %shard_map.294 = (bf16[432,768]{1,0:T(8,128)(2,1)S(1)}, bf16[432,768]{1,0:T(8,128)(2,1)S(1)}, bf16[4,96,768]{2,1,0:T(8,128)(2,1)S(1)}, bf16[4,96,768]{2,1,0:T(8,128)(2,1)S(1)}) custom-call(f32[432,768]{1,0:T(8,128)S(1)} %get-tuple-element.136.part, bf16[96,768]{1,0:T(8,128)(2,1)S(1)} %collective-permute-done.7.d_a, ...), custom_call_target="tpu_custom_call" | custom-call | tf_op jit(solution)/shard_map/pallas_call | solution.py:713
  23.1 1.8 %collective-permute-start.13 = (bf16[4,96,768]{2,1,0:T(8,128)(2,1)S(1)}, bf16[4,96,768]{2,1,0:T(8,128)(2,1)S(1)}, u32[]{:S(2)}, u32[]{:S(2)}) collective-permute-start(bf16[4,96,768]{2,1,0:T(8,128)(2,1)S(1)} %get-tuple-element.164), channel_id=1, source_target_pairs={{0,4},{4,0},{8,12},{12,8},{16,20},{20,16},{24,28},{28,24},{1,5},{5... | collective-permute-start | bytes 1769480 | tf_op jit(solution)/shard_map/ppermute | solution.py:628
  24.9 2.4 %shard_map.295 = (bf16[432,1536]{1,0:T(8,128)(2,1)S(1)}, bf16[432,384]{1,0:T(8,128)(2,1)S(1)}, bf16[432,384]{1,0:T(8,128)(2,1)S(1)}) custom-call(bf16[432,768]{1,0:T(8,128)(2,1)S(1)} %get-tuple-element.144.gb2, bf16[1536,768]{1,0:T(8,128)(2,1)S(1)} %get-tuple-element.145.wr, f32[432,1536]{1,0:T(8,128)S(1)} %get-tuple-element.146.slope, ...), custom_call_target="tpu_custom_call" | custom-call | tf_op jit(solution)/shard_map/pallas_call | solution.py:721
  27.4 0.5 collective-permute-start.12
  27.9 1.2 %shard_map.296 = (bf16[4,48,1536]{2,1,0:T(8,128)(2,1)S(1)}, bf16[4,48,1536]{2,1,0:T(8,128)(2,1)S(1)}, f32[8,128]{1,0:T(8,128)S(1)}) custom-call(bf16[432,768]{1,0:T(8,128)(2,1)S(1)} %get-tuple-element.156.n2, bf16[432,1536]{1,0:T(8,128)(2,1)S(1)} %get-tuple-element.157.gh, bf16[384,768]{1,0:T(8,128)(2,1)S(1)} %get-tuple-element.142.after.pick), custom_call_target="tpu_custom_call" | custom-call | tf_op jit(solution)/shard_map/pallas_call | solution.py:723
  29.1 1.7 %collective-permute-start.15 = (bf16[4,48,1536]{2,1,0:T(8,128)(2,1)S(1)}, bf16[4,48,1536]{2,1,0:T(8,128)(2,1)S(1)}, u32[]{:S(2)}, u32[]{:S(2)}) collective-permute-start(bf16[4,48,1536]{2,1,0:T(8,128)(2,1)S(1)} %get-tuple-element.170), channel_id=1, source_target_pairs={{0,8},{4,12},{8,0},{12,4},{16,24},{20,28},{24,16},{28,20},{1,9},{5... | collective-permute-start | bytes 1769480 | tf_op jit(solution)/shard_map/ppermute | solution.py:632
  30.7 4.2 %shard_map.297 = (f32[432,768]{1,0:T(8,128)S(1)}, bf16[432,1152]{1,0:T(8,128)(2,1)S(1)}, bf16[4,48,1536]{2,1,0:T(8,128)(2,1)S(1)}, bf16[4,48,1536]{2,1,0:T(8,128)(2,1)S(1)}, f32[8,128]{1,0:T(8,128)S(1)}) custom-call(bf16[432,384]{1,0:T(8,128)(2,1)S(1)} %get-tuple-element.147.l_a, bf16[432,384]{1,0:T(8,128)(2,1)S(1)} %collective-permute-done.11.l_b, ...), custom_call_target="tpu_custom_call" | custom-call | tf_op jit(solution)/shard_map/pallas_call | solution.py:730
  35.0 0.5 collective-permute-start.18
  35.5 3.8 %collective-permute-done.13.arrived = bf16[4,96,768]{2,1,0:T(8,128)(2,1)S(1)} collective-permute-done((bf16[4,96,768]{2,1,0:T(8,128)(2,1)S(1)}, bf16[4,96,768]{2,1,0:T(8,128)(2,1)S(1)}, u32[]{:S(2)}, u32[]{:S(2)}) %collective-permute-start.13) | collective-permute-done | bytes 589856 | tf_op jit(solution)/shard_map/ppermute | solution.py:628
  39.3 0.2 shard_map.298
  39.5 1.5 %collective-permute-start.17 = (bf16[4,96,768]{2,1,0:T(8,128)(2,1)S(1)}, bf16[4,96,768]{2,1,0:T(8,128)(2,1)S(1)}, u32[]{:S(2)}, u32[]{:S(2)}) collective-permute-start(bf16[4,96,768]{2,1,0:T(8,128)(2,1)S(1)} %get-tuple-element.177), channel_id=1, source_target_pairs={{1,17},{3,19},{5,21},{7,23},{9,25},{11,27},{13,29},{15,31},{16,0},... | collective-permute-start | bytes 1769480 | tf_op jit(solution)/shard_map/ppermute | solution.py:641
  41.0 4.3 %shard_map.299 = (bf16[2,3,64,768]{3,2,1,0:T(8,128)(2,1)S(1)}, bf16[2,3,64,768]{3,2,1,0:T(8,128)(2,1)S(1)}, bf16[2,48,256]{2,1,0:T(8,128)(2,1)S(1)}, bf16[2,48,256]{2,1,0:T(8,128)(2,1)S(1)}, f32[8,128]{1,0:T(8,128)S(1)}) custom-call(bf16[432,384]{1,0:T(8,128)(2,1)S(1)} %get-tuple-element.147.l_a, bf16[432,384]{1,0:T(8,128)(2,1)S(1)} %collective-permute-done.11.l_b, ...), custom_call_target="tpu_custom_call" | custom-call | flops 8000000000 | bytes 20000000 | tf_op jit(solution)/shard_map/pallas_call | solution.py:741
  45.3 0.1 shard_map.300
  45.4 1.8 %collective-permute-start.16 = (bf16[2,48,1792]{2,1,0:T(8,128)(2,1)S(1)}, bf16[2,48,1792]{2,1,0:T(8,128)(2,1)S(1)}, u32[]{:S(2)}, u32[]{:S(2)}) collective-permute-start(bf16[2,48,1792]{2,1,0:T(8,128)(2,1)S(1)} %get-tuple-element.175), channel_id=1, source_target_pairs={{0,4},{4,0},{8,12},{12,8},{16,20},{20,16},{24,28},{28,24},{1,5},{5... | collective-permute-start | bytes 1032200 | tf_op jit(solution)/shard_map/ppermute | solution.py:628
  47.3 4.7 %collective-permute-done.18.arrived = bf16[4,48,1536]{2,1,0:T(8,128)(2,1)S(1)} collective-permute-done((bf16[4,48,1536]{2,1,0:T(8,128)(2,1)S(1)}, bf16[4,48,1536]{2,1,0:T(8,128)(2,1)S(1)}, u32[]{:S(2)}, u32[]{:S(2)}) %collective-permute-start.18) | collective-permute-done | bytes 589856 | tf_op jit(solution)/shard_map/ppermute | solution.py:628
  52.0 0.1 shard_map.301
  52.1 1.9 %collective-permute-start.20 = (bf16[2,48,1536]{2,1,0:T(8,128)(2,1)S(1)}, bf16[2,48,1536]{2,1,0:T(8,128)(2,1)S(1)}, u32[]{:S(2)}, u32[]{:S(2)}) collective-permute-start(bf16[2,48,1536]{2,1,0:T(8,128)(2,1)S(1)} %get-tuple-element.186), channel_id=1, source_target_pairs={{0,8},{4,12},{8,0},{12,4},{16,24},{20,28},{24,16},{28,20},{1,9},{5... | collective-permute-start | bytes 884744 | tf_op jit(solution)/shard_map/ppermute | solution.py:632
  54.0 4.6 %collective-permute-done.17.arrived = bf16[4,96,768]{2,1,0:T(8,128)(2,1)S(1)} collective-permute-done((bf16[4,96,768]{2,1,0:T(8,128)(2,1)S(1)}, bf16[4,96,768]{2,1,0:T(8,128)(2,1)S(1)}, u32[]{:S(2)}, u32[]{:S(2)}) %collective-permute-start.17) | collective-permute-done | bytes 589856 | tf_op jit(solution)/shard_map/ppermute | solution.py:641
  58.6 0.1 shard_map.302
  58.8 1.7 %collective-permute-start.19 = (bf16[2,48,128]{2,1,0:T(8,128)(2,1)S(1)}, bf16[2,48,128]{2,1,0:T(8,128)(2,1)S(1)}, u32[]{:S(2)}, u32[]{:S(2)}) collective-permute-start(bf16[2,48,128]{2,1,0:T(8,128)(2,1)S(1)} %get-tuple-element.184), channel_id=1, source_target_pairs={{0,8},{4,12},{8,0},{12,4},{16,24},{20,28},{24,16},{28,20},{1,9},{5... | collective-permute-start | bytes 73736 | tf_op jit(solution)/shard_map/ppermute | solution.py:632
  60.5 2.6 %collective-permute-start.27 = (bf16[1,48,1536]{2,1,0:T(8,128)(2,1)S(1)}, bf16[1,48,1536]{2,1,0:T(8,128)(2,1)S(1)}, u32[]{:S(2)}, u32[]{:S(2)}) collective-permute-start(bf16[1,48,1536]{2,1,0:T(8,128)(2,1)S(1)} %get-tuple-element.205), channel_id=1, source_target_pairs={{0,16},{4,20},{8,24},{12,28},{16,0},{20,4},{24,8},{28,12},{1,17},{... | collective-permute-start | bytes 442376 | tf_op jit(solution)/shard_map/ppermute | solution.py:632
  63.1 2.3 %collective-permute-start.26 = (bf16[2,96,768]{2,1,0:T(8,128)(2,1)S(1)}, bf16[2,96,768]{2,1,0:T(8,128)(2,1)S(1)}, u32[]{:S(2)}, u32[]{:S(2)}) collective-permute-start(bf16[2,96,768]{2,1,0:T(8,128)(2,1)S(1)} %get-tuple-element.203), channel_id=1, source_target_pairs={{0,8},{2,10},{4,12},{6,14},{8,0},{10,2},{12,4},{14,6},{17,25},{19,... | collective-permute-start | bytes 884744 | tf_op jit(solution)/shard_map/ppermute | solution.py:641
  65.5 0.1 shard_map.304
  65.8 0.6 collective-permute-start.22
  66.3 0.8 %collective-permute-done.22.vec_b = bf16[2,48,16]{2,1,0:T(8,128)(2,1)S(1)} collective-permute-done((bf16[2,48,16]{2,1,0:T(8,128)(2,1)S(1)}, bf16[2,48,16]{2,1,0:T(8,128)(2,1)S(1)}, u32[]{:S(2)}, u32[]{:S(2)}) %collective-permute-start.22) | collective-permute-done | bytes 3104 | tf_op jit(solution)/shard_map/ppermute | solution.py:620
  67.2 2.8 %collective-permute-start.24 = (bf16[24,1152]{1,0:T(8,128)(2,1)S(1)}, bf16[24,1152]{1,0:T(8,128)(2,1)S(1)}, u32[]{:S(2)}, u32[]{:S(2)}) collective-permute-start(bf16[24,1152]{1,0:T(8,128)(2,1)S(1)} %get-tuple-element.199), channel_id=1, source_target_pairs={{0,17},{1,16},{2,19},{3,18},{4,21},{5,20},{6,23},{7,22},{8,25},{9,... | collective-permute-start | bytes 165896 | tf_op jit(solution)/shard_map/ppermute | solution.py:636
  70.0 1.8 %shard_map.306 = (bf16[3,64,768]{2,1,0:T(8,128)(2,1)}, bf16[3,64,768]{2,1,0:T(8,128)(2,1)}, f32[8,128]{1,0:T(8,128)S(1)}) custom-call(bf16[2,3,64,768]{3,2,1,0:T(8,128)(2,1)S(1)} %get-tuple-element.167.gb_a, bf16[2,3,64,768]{3,2,1,0:T(8,128)(2,1)S(1)} %collective-permute-done.14.gb_b, bf16[208,768]{1,0:T(8,128)(2,1)S(1)} %get-tuple-element.123.t0.tok, ...), custom_call_target="tpu_custom_call" | custom-call | bytes 1000000 | tf_op jit(solution)/shard_map/pallas_call | solution.py:775
  71.8 0.2 collective-permute-start.25
  72.0 2.2 %collective-permute-done.26.wr_a = bf16[2,96,768]{2,1,0:T(8,128)(2,1)S(1)} collective-permute-done((bf16[2,96,768]{2,1,0:T(8,128)(2,1)S(1)}, bf16[2,96,768]{2,1,0:T(8,128)(2,1)S(1)}, u32[]{:S(2)}, u32[]{:S(2)}) %collective-permute-start.26) | collective-permute-done | bytes 294944 | tf_op jit(solution)/shard_map/ppermute | solution.py:641
  74.1 0.1 shard_map.308
  74.3 0.5 collective-permute-start.29
  74.8 0.3 collective-permute-done.24.far
  75.1 1.3 %collective-permute-done.25.vec_a = bf16[48,16]{1,0:T(8,128)(2,1)S(1)} collective-permute-done((bf16[48,16]{1,0:T(8,128)(2,1)S(1)}, bf16[48,16]{1,0:T(8,128)(2,1)S(1)}, u32[]{:S(2)}, u32[]{:S(2)}) %collective-permute-start.25) | collective-permute-done | bytes 1568 | tf_op jit(solution)/shard_map/ppermute | solution.py:632
  76.5 1.0 %shard_map.310 = (f32[24,2304]{1,0:T(8,128)}, f32[24]{0:T(128)}, f32[24]{0:T(128)}, f32[2,24]{1,0:T(2,128)}, f32[24]{0:T(128)}, /*index=5*/f32[24]{0:T(128)}, f3...) custom-call(f32[24,1920]{1,0:T(8,128)S(1)} %get-tuple-element.208.ow, ...), custom_call_target="tpu_custom_call" | custom-call | bytes 1000000 | tf_op jit(solution)/shard_map/pallas_call | solution.py:799
  (35 shorter events, 0.8 us)
Async XLA Ops:
  0.6 11.0 %collective-permute-start.1 = (bf16[3,64,768]{2,1,0:T(8,128)(2,1)}, bf16[3,64,768]{2,1,0:T(8,128)(2,1)S(1)}, u32[]{:S(2)}, u32[]{:S(2)}) collective-permute-start(bf16[3,64,768]{2,1,0:T(8,128)(2,1)} %tok.1), channel_id=1, source_target_pairs={{0,2},{1,3},{2,0},{3,1},{4,6},{5,7},{6,4},{7,5},{8,10},{9,11},{10,... | collective-permute-start | bytes 884744 | tf_op jit(solution)/shard_map/ppermute | solution.py:624
  7.4 5.0 %collective-permute-start = (bf16[208,768]{1,0:T(8,128)(2,1)S(1)}, bf16[208,768]{1,0:T(8,128)(2,1)S(1)}, u32[]{:S(2)}, u32[]{:S(2)}) collective-permute-start(bf16[208,768]{1,0:T(8,128)(2,1)S(1)} %get-tuple-element.123.t0.tok), channel_id=1, source_target_pairs={{0,1},{1,0},{2,3},{3,2},{4,5},{5,4},{6,7},{7,6},{8,9},{9,8},{10,11... | collective-permute-start | bytes 958472 | tf_op jit(solution)/shard_map/ppermute | solution.py:620
  7.4 4.2 %collective-permute-start.2 = (bf16[16,768]{1,0:T(8,128)(2,1)S(1)}, bf16[16,768]{1,0:T(8,128)(2,1)S(1)}, u32[]{:S(2)}, u32[]{:S(2)}) collective-permute-start(bf16[16,768]{1,0:T(8,128)(2,1)S(1)} %get-tuple-element.124), channel_id=1, source_target_pairs={{0,2},{1,3},{2,0},{3,1},{4,6},{5,7},{6,4},{7,5},{8,10},{9,11},{10,... | collective-permute-start | bytes 73736 | tf_op jit(solution)/shard_map/ppermute | solution.py:624
  7.5 10.2 %collective-permute-start.6 = (bf16[3,64,768]{2,1,0:T(8,128)(2,1)S(1)}, bf16[3,64,768]{2,1,0:T(8,128)(2,1)S(1)}, u32[]{:S(2)}, u32[]{:S(2)}) collective-permute-start(bf16[3,64,768]{2,1,0:T(8,128)(2,1)S(1)} %get-tuple-element.132.c0), channel_id=1, source_target_pairs={{0,2},{1,3},{2,0},{3,1},{4,6},{5,7},{6,4},{7,5},{8,10},{9,11},{10,... | collective-permute-start | bytes 884744 | tf_op jit(solution)/shard_map/ppermute | solution.py:624
  11.7 2.1 %collective-permute-start.3 = (bf16[160,768]{1,0:T(8,128)(2,1)S(1)}, bf16[160,768]{1,0:T(8,128)(2,1)S(1)}, u32[]{:S(2)}, u32[]{:S(2)}) collective-permute-start(bf16[160,768]{1,0:T(8,128)(2,1)S(1)} %get-tuple-element.126.x_a), channel_id=1, source_target_pairs={{0,1},{1,0},{2,3},{3,2},{4,5},{5,4},{6,7},{7,6},{8,9},{9,8},{10,11... | collective-permute-start | bytes 737288 | tf_op jit(solution)/shard_map/ppermute | solution.py:620
  11.8 6.6 %collective-permute-start.5 = (bf16[3,64,768]{2,1,0:T(8,128)(2,1)S(1)}, bf16[3,64,768]{2,1,0:T(8,128)(2,1)S(1)}, u32[]{:S(2)}, u32[]{:S(2)}) collective-permute-start(bf16[3,64,768]{2,1,0:T(8,128)(2,1)S(1)} %get-tuple-element.132.c0), channel_id=1, source_target_pairs={{0,1},{1,0},{2,3},{3,2},{4,5},{5,4},{6,7},{7,6},{8,9},{9,8},{10,11... | collective-permute-start | bytes 884744 | tf_op jit(solution)/shard_map/ppermute | solution.py:620
  12.3 1.5 %collective-permute-start.4 = (bf16[48,768]{1,0:T(8,128)(2,1)S(1)}, bf16[48,768]{1,0:T(8,128)(2,1)S(1)}, u32[]{:S(2)}, u32[]{:S(2)}) collective-permute-start(bf16[48,768]{1,0:T(8,128)(2,1)S(1)} %get-tuple-element.127.x_b), channel_id=1, source_target_pairs={{0,1},{1,0},{2,3},{3,2},{4,5},{5,4},{6,7},{7,6},{8,9},{9,8},{10,11... | collective-permute-start | bytes 221192 | tf_op jit(solution)/shard_map/ppermute | solution.py:620
  16.9 2.2 %collective-permute-start.9 = (bf16[224,384]{1,0:T(8,128)(2,1)S(1)}, bf16[224,384]{1,0:T(8,128)(2,1)S(1)}, u32[]{:S(2)}, u32[]{:S(2)}) collective-permute-start(bf16[224,384]{1,0:T(8,128)(2,1)S(1)} %get-tuple-element.129.mix_a), channel_id=1, source_target_pairs={{0,1},{1,0},{2,3},{3,2},{4,5},{5,4},{6,7},{7,6},{8,9},{9,8},{10,11... | collective-permute-start | bytes 516104 | tf_op jit(solution)/shard_map/ppermute | solution.py:620
  17.1 2.0 %collective-permute-start.10 = (bf16[208,384]{1,0:T(8,128)(2,1)S(1)}, bf16[208,384]{1,0:T(8,128)(2,1)S(1)}, u32[]{:S(2)}, u32[]{:S(2)}) collective-permute-start(bf16[208,384]{1,0:T(8,128)(2,1)S(1)} %get-tuple-element.130.mix2_a), channel_id=1, source_target_pairs={{0,1},{1,0},{2,3},{3,2},{4,5},{5,4},{6,7},{7,6},{8,9},{9,8},{10,11... | collective-permute-start | bytes 479240 | tf_op jit(solution)/shard_map/ppermute | solution.py:620
  17.7 3.7 %collective-permute-start.7 = (bf16[96,768]{1,0:T(8,128)(2,1)S(1)}, bf16[96,768]{1,0:T(8,128)(2,1)S(1)}, u32[]{:S(2)}, u32[]{:S(2)}) collective-permute-start(bf16[96,768]{1,0:T(8,128)(2,1)S(1)} %get-tuple-element.133.x_a), channel_id=1, source_target_pairs={{0,1},{1,0},{2,3},{3,2},{4,5},{5,4},{6,7},{7,6},{8,9},{9,8},{10,11... | collective-permute-start | bytes 442376 | tf_op jit(solution)/shard_map/ppermute | solution.py:620
  17.8 3.6 %collective-permute-start.8 = (bf16[96,768]{1,0:T(8,128)(2,1)S(1)}, bf16[96,768]{1,0:T(8,128)(2,1)S(1)}, u32[]{:S(2)}, u32[]{:S(2)}) collective-permute-start(bf16[96,768]{1,0:T(8,128)(2,1)S(1)} %get-tuple-element.134.x_b), channel_id=1, source_target_pairs={{0,1},{1,0},{2,3},{3,2},{4,5},{5,4},{6,7},{7,6},{8,9},{9,8},{10,11... | collective-permute-start | bytes 442376 | tf_op jit(solution)/shard_map/ppermute | solution.py:620
  23.1 16.2 %collective-permute-start.13 = (bf16[4,96,768]{2,1,0:T(8,128)(2,1)S(1)}, bf16[4,96,768]{2,1,0:T(8,128)(2,1)S(1)}, u32[]{:S(2)}, u32[]{:S(2)}) collective-permute-start(bf16[4,96,768]{2,1,0:T(8,128)(2,1)S(1)} %get-tuple-element.164), channel_id=1, source_target_pairs={{0,4},{4,0},{8,12},{12,8},{16,20},{20,16},{24,28},{28,24},{1,5},{5... | collective-permute-start | bytes 1769480 | tf_op jit(solution)/shard_map/ppermute | solution.py:628
  27.3 3.4 %collective-permute-start.11 = (bf16[432,384]{1,0:T(8,128)(2,1)S(1)}, bf16[432,384]{1,0:T(8,128)(2,1)S(1)}, u32[]{:S(2)}, u32[]{:S(2)}) collective-permute-start(bf16[432,384]{1,0:T(8,128)(2,1)S(1)} %get-tuple-element.147.l_a), channel_id=1, source_target_pairs={{0,1},{1,0},{2,3},{3,2},{4,5},{5,4},{6,7},{7,6},{8,9},{9,8},{10,11... | collective-permute-start | bytes 995336 | tf_op jit(solution)/shard_map/ppermute | solution.py:620
  27.4 3.4 %collective-permute-start.12 = (bf16[432,384]{1,0:T(8,128)(2,1)S(1)}, bf16[432,384]{1,0:T(8,128)(2,1)S(1)}, u32[]{:S(2)}, u32[]{:S(2)}) collective-permute-start(bf16[432,384]{1,0:T(8,128)(2,1)S(1)} %get-tuple-element.148.r_a), channel_id=1, source_target_pairs={{0,1},{1,0},{2,3},{3,2},{4,5},{5,4},{6,7},{7,6},{8,9},{9,8},{10,11... | collective-permute-start | bytes 995336 | tf_op jit(solution)/shard_map/ppermute | solution.py:620
  29.1 16.2 %collective-permute-start.15 = (bf16[4,48,1536]{2,1,0:T(8,128)(2,1)S(1)}, bf16[4,48,1536]{2,1,0:T(8,128)(2,1)S(1)}, u32[]{:S(2)}, u32[]{:S(2)}) collective-permute-start(bf16[4,48,1536]{2,1,0:T(8,128)(2,1)S(1)} %get-tuple-element.170), channel_id=1, source_target_pairs={{0,8},{4,12},{8,0},{12,4},{16,24},{20,28},{24,16},{28,20},{1,9},{5... | collective-permute-start | bytes 1769480 | tf_op jit(solution)/shard_map/ppermute | solution.py:632
  35.0 17.0 %collective-permute-start.18 = (bf16[4,48,1536]{2,1,0:T(8,128)(2,1)S(1)}, bf16[4,48,1536]{2,1,0:T(8,128)(2,1)S(1)}, u32[]{:S(2)}, u32[]{:S(2)}) collective-permute-start(bf16[4,48,1536]{2,1,0:T(8,128)(2,1)S(1)} %get-tuple-element.179), channel_id=1, source_target_pairs={{0,4},{4,0},{8,12},{12,8},{16,20},{20,16},{24,28},{28,24},{1,5},{5... | collective-permute-start | bytes 1769480 | tf_op jit(solution)/shard_map/ppermute | solution.py:628
  39.5 19.1 %collective-permute-start.17 = (bf16[4,96,768]{2,1,0:T(8,128)(2,1)S(1)}, bf16[4,96,768]{2,1,0:T(8,128)(2,1)S(1)}, u32[]{:S(2)}, u32[]{:S(2)}) collective-permute-start(bf16[4,96,768]{2,1,0:T(8,128)(2,1)S(1)} %get-tuple-element.177), channel_id=1, source_target_pairs={{1,17},{3,19},{5,21},{7,23},{9,25},{11,27},{13,29},{15,31},{16,0},... | collective-permute-start | bytes 1769480 | tf_op jit(solution)/shard_map/ppermute | solution.py:641
  45.4 13.3 %collective-permute-start.16 = (bf16[2,48,1792]{2,1,0:T(8,128)(2,1)S(1)}, bf16[2,48,1792]{2,1,0:T(8,128)(2,1)S(1)}, u32[]{:S(2)}, u32[]{:S(2)}) collective-permute-start(bf16[2,48,1792]{2,1,0:T(8,128)(2,1)S(1)} %get-tuple-element.175), channel_id=1, source_target_pairs={{0,4},{4,0},{8,12},{12,8},{16,20},{20,16},{24,28},{28,24},{1,5},{5... | collective-permute-start | bytes 1032200 | tf_op jit(solution)/shard_map/ppermute | solution.py:628
  52.1 13.3 %collective-permute-start.20 = (bf16[2,48,1536]{2,1,0:T(8,128)(2,1)S(1)}, bf16[2,48,1536]{2,1,0:T(8,128)(2,1)S(1)}, u32[]{:S(2)}, u32[]{:S(2)}) collective-permute-start(bf16[2,48,1536]{2,1,0:T(8,128)(2,1)S(1)} %get-tuple-element.186), channel_id=1, source_target_pairs={{0,8},{4,12},{8,0},{12,4},{16,24},{20,28},{24,16},{28,20},{1,9},{5... | collective-permute-start | bytes 884744 | tf_op jit(solution)/shard_map/ppermute | solution.py:632
  54.0 11.7 %collective-permute-start.14 = (bf16[2,3,64,768]{3,2,1,0:T(8,128)(2,1)S(1)}, bf16[2,3,64,768]{3,2,1,0:T(8,128)(2,1)S(1)}, u32[]{:S(2)}, u32[]{:S(2)}) collective-permute-start(bf16[2,3,64,768]{3,2,1,0:T(8,128)(2,1)S(1)} %get-tuple-element.168), channel_id=1, source_target_pairs={{0,1},{1,0},{2,3},{3,2},{4,5},{5,4},{6,7},{7,6},{8,9},{9,8},{10,11... | collective-permute-start | bytes 1769480 | tf_op jit(solution)/shard_map/ppermute | solution.py:620
  58.8 6.8 %collective-permute-start.19 = (bf16[2,48,128]{2,1,0:T(8,128)(2,1)S(1)}, bf16[2,48,128]{2,1,0:T(8,128)(2,1)S(1)}, u32[]{:S(2)}, u32[]{:S(2)}) collective-permute-start(bf16[2,48,128]{2,1,0:T(8,128)(2,1)S(1)} %get-tuple-element.184), channel_id=1, source_target_pairs={{0,8},{4,12},{8,0},{12,4},{16,24},{20,28},{24,16},{28,20},{1,9},{5... | collective-permute-start | bytes 73736 | tf_op jit(solution)/shard_map/ppermute | solution.py:632
  60.5 11.4 %collective-permute-start.27 = (bf16[1,48,1536]{2,1,0:T(8,128)(2,1)S(1)}, bf16[1,48,1536]{2,1,0:T(8,128)(2,1)S(1)}, u32[]{:S(2)}, u32[]{:S(2)}) collective-permute-start(bf16[1,48,1536]{2,1,0:T(8,128)(2,1)S(1)} %get-tuple-element.205), channel_id=1, source_target_pairs={{0,16},{4,20},{8,24},{12,28},{16,0},{20,4},{24,8},{28,12},{1,17},{... | collective-permute-start | bytes 442376 | tf_op jit(solution)/shard_map/ppermute | solution.py:632
  63.1 11.0 %collective-permute-start.26 = (bf16[2,96,768]{2,1,0:T(8,128)(2,1)S(1)}, bf16[2,96,768]{2,1,0:T(8,128)(2,1)S(1)}, u32[]{:S(2)}, u32[]{:S(2)}) collective-permute-start(bf16[2,96,768]{2,1,0:T(8,128)(2,1)S(1)} %get-tuple-element.203), channel_id=1, source_target_pairs={{0,8},{2,10},{4,12},{6,14},{8,0},{10,2},{12,4},{14,6},{17,25},{19,... | collective-permute-start | bytes 884744 | tf_op jit(solution)/shard_map/ppermute | solution.py:641
  65.6 9.6 %collective-permute-start.21 = (bf16[24,1920]{1,0:T(8,128)(2,1)S(1)}, bf16[24,1920]{1,0:T(8,128)(2,1)S(1)}, u32[]{:S(2)}, u32[]{:S(2)}) collective-permute-start(bf16[24,1920]{1,0:T(8,128)(2,1)S(1)} %get-tuple-element.193), channel_id=1, source_target_pairs={{0,16},{4,20},{8,24},{12,28},{16,0},{20,4},{24,8},{28,12},{1,17},{... | collective-permute-start | bytes 276488 | tf_op jit(solution)/shard_map/ppermute | solution.py:632
  65.6 6.1 %collective-permute-start.23 = (f32[24,1152]{1,0:T(8,128)S(1)}, f32[24,1152]{1,0:T(8,128)S(1)}, u32[]{:S(2)}, u32[]{:S(2)}) collective-permute-start(f32[24,1152]{1,0:T(8,128)S(1)} %get-tuple-element.196), channel_id=1, source_target_pairs={{0,1},{1,0},{2,3},{3,2},{4,5},{5,4},{6,7},{7,6},{8,9},{9,8},{10,11... | collective-permute-start | bytes 331784 | tf_op jit(solution)/shard_map/ppermute | solution.py:620
  65.8 1.4 %collective-permute-start.22 = (bf16[2,48,16]{2,1,0:T(8,128)(2,1)S(1)}, bf16[2,48,16]{2,1,0:T(8,128)(2,1)S(1)}, u32[]{:S(2)}, u32[]{:S(2)}) collective-permute-start(bf16[2,48,16]{2,1,0:T(8,128)(2,1)S(1)} %get-tuple-element.195), channel_id=1, source_target_pairs={{0,1},{1,0},{2,3},{3,2},{4,5},{5,4},{6,7},{7,6},{8,9},{9,8},{10,11... | collective-permute-start | bytes 9224 | tf_op jit(solution)/shard_map/ppermute | solution.py:620
  67.2 8.0 %collective-permute-start.24 = (bf16[24,1152]{1,0:T(8,128)(2,1)S(1)}, bf16[24,1152]{1,0:T(8,128)(2,1)S(1)}, u32[]{:S(2)}, u32[]{:S(2)}) collective-permute-start(bf16[24,1152]{1,0:T(8,128)(2,1)S(1)} %get-tuple-element.199), channel_id=1, source_target_pairs={{0,17},{1,16},{2,19},{3,18},{4,21},{5,20},{6,23},{7,22},{8,25},{9,... | collective-permute-start | bytes 165896 | tf_op jit(solution)/shard_map/ppermute | solution.py:636
  71.8 4.7 %collective-permute-start.25 = (bf16[48,16]{1,0:T(8,128)(2,1)S(1)}, bf16[48,16]{1,0:T(8,128)(2,1)S(1)}, u32[]{:S(2)}, u32[]{:S(2)}) collective-permute-start(bf16[48,16]{1,0:T(8,128)(2,1)S(1)} %get-tuple-element.201), channel_id=1, source_target_pairs={{0,16},{4,20},{8,24},{12,28},{16,0},{20,4},{24,8},{28,12},{1,17},{... | collective-permute-start | bytes 4616 | tf_op jit(solution)/shard_map/ppermute | solution.py:632
  74.2 2.3 %collective-permute-start.28 = (bf16[24,1536]{1,0:T(8,128)(2,1)S(1)}, bf16[24,1536]{1,0:T(8,128)(2,1)S(1)}, u32[]{:S(2)}, u32[]{:S(2)}) collective-permute-start(bf16[24,1536]{1,0:T(8,128)(2,1)S(1)} %get-tuple-element.212), channel_id=1, source_target_pairs={{0,1},{1,0},{2,3},{3,2},{4,5},{5,4},{6,7},{7,6},{8,9},{9,8},{10,11... | collective-permute-start | bytes 221192 | tf_op jit(solution)/shard_map/ppermute | solution.py:620
  74.3 2.2 %collective-permute-start.29 = (bf16[96,768]{1,0:T(8,128)(2,1)S(1)}, bf16[96,768]{1,0:T(8,128)(2,1)S(1)}, u32[]{:S(2)}, u32[]{:S(2)}) collective-permute-start(bf16[96,768]{1,0:T(8,128)(2,1)S(1)} %get-tuple-element.214), channel_id=1, source_target_pairs={{0,1},{1,0},{2,3},{3,2},{4,5},{5,4},{6,7},{7,6},{8,9},{9,8},{10,11... | collective-permute-start | bytes 442376 | tf_op jit(solution)/shard_map/ppermute | solution.py:620

commit v8 on v7

--- a/solution.py
+++ b/solution.py
@@ -438,13 +438,13 @@
             out[dz >> 1, :, SMALL * (dz & 1) : SMALL * (dz & 1) + SMALL] = block.astype(BF)
 
 
-def last_kernel(gb_a, gb_b, tok, gres, res, mine, par, after, out_o, gtok_o, tick):
-    tick[...] = jnp.zeros_like(tick)
-
-    def own_rows(pack, value):
-        high = value.astype(BF)
-        return dot_tn(pack, high) + dot_tn(pack, (value - high.astype(F32)).astype(BF))
-
+def own_rows(pack, value):
+    high = value.astype(BF)
+    return dot_tn(pack, high) + dot_tn(pack, (value - high.astype(F32)).astype(BF))
+
+
+def token_grad_kernel(gb_a, gb_b, tok, gres, mine, par, after, gtok_o, tick):
+    tick[...] = jnp.zeros_like(tick)
     for i in range(IMGS):
         rows = slice(i * PACK, (i + 1) * PACK)
         pack = one_hot_pack(mine[...], i)
@@ -452,6 +452,13 @@
         gnp = gb_a[0, i].astype(F32) + gb_b[0, i].astype(F32)
         gtok = own_rows(pack, gres[rows, :]) + norm_back(gnp * par[GAIN1 : GAIN1 + 1, :], z1, rstd1)
         gtok_o[i] = gtok.astype(BF)
+
+
+def layer_out_kernel(gb_a, gb_b, res, mine, par, after, out_o, tick):
+    tick[...] = jnp.zeros_like(tick)
+    for i in range(IMGS):
+        rows = slice(i * PACK, (i + 1) * PACK)
+        pack = one_hot_pack(mine[...], i)
         ones = dot_tn(pack, jnp.ones((PACK, D), BF))
         two = gb_a[1, i].astype(F32) + gb_b[1, i].astype(F32) + ones * par[RB : RB + 1, :]
         out_o[i] = (own_rows(pack, res[rows, :]) + par[MSC : MSC + 1, :] * two).astype(BF)
@@ -772,17 +779,18 @@
         vector_fold_kernel, (vm((2, 48, SMALL), F32), vm((2, 48, USED), BF), TICK), [VM] * 2 + [ANY], cost=4000000000
     )(vec_keep, vec_z, tick)
     vec_other = by_core(vec_send)
-    layer_out, grad_tokens, tick = call(
-        last_kernel,
-        (sds(tokens.shape, BF), sds(tokens.shape, BF), TICK),
-        [VM] * 7 + [ANY],
-    )(gb_keep, gb_other, tok_own, gres, res, pos_mine, par, tick)
+    layer_out, tick = call(layer_out_kernel, (sds(tokens.shape, BF), TICK), [VM] * 5 + [ANY])(
+        gb_keep, gb_other, res, pos_mine, par, tick
+    )
     vec_keep, vec_send, hop, tick = call(
         cores_kernel,
         (vm((48, SMALL), F32), vm((48, USED), BF), vm((24, QC), F32), TICK),
         [VM] * 3 + [ANY],
     )(vec, vec_other, hop, tick)
     vec_z = by_z(vec_send, 2)
+    grad_tokens, tick = call(token_grad_kernel, (sds(tokens.shape, BF), TICK), [VM] * 6 + [ANY])(
+        gb_keep, gb_other, tok_own, gres, pos_mine, par, tick
+    )
     wr_keep, wr_send, we_keep, we_send, tick = call(
         settle_kernel,
         (vm((96, D), F32), vm((96, D), BF), vm((24, FH), F32), vm((24, FH), BF), TICK),

time: 77.8 us -> 77.3 us (level)
  waiting for transfers between devices: 21.7 us -> 20.5 us
    pallas_call x1 -> x2, Pallas kernels: 1.82 us -> 2.53 us  [the longest x1 1.37 us: packed_body(): call(token_grad_kernel, (sds(tokens.shape, BF), TICK), [VM] * 6 + [ANY])]
  transfers between devices with their start and end apart: 30 -> 30, of which waited for: 10 -> 10; matrix products, arithmetic and copies ran while one was open for 0% -> 0% of each run, Pallas kernels for 32% -> 33%
where the time goes in v8:
time: 77.3 us; the launch traced here: 77.1 us
  Pallas kernels  27.9 us (36%)
  starting transfers between devices  27.6 us (36%)
  waiting for transfers between devices  20.5 us (27%)
  between operations  1.07 us (1%)
    ppermute x3, waiting for transfers between devices, by_y(): return lax.ppermute(value, 'batch', [(i, i ^ 1) for i in range(8)])  8.53 us
    ppermute x6, starting transfers between devices, by_z(): return lax.ppermute(value, 'batch', [(i, i ^ 2 * dz) for i in range(8)])  8.04 us
    ppermute x2, waiting for transfers between devices, homeward(): return lax.ppermute(value, ('batch', 'band'), pairs)  6.04 us
    ppermute x3, starting transfers between devices, by_x(): return lax.ppermute(value, 'band', [(i, i ^ 2) for i in range(4)])  5.09 us
    pallas_call x1, Pallas kernels, packed_body(): call(vectors_kernel, (vm((2, *tokens.shape), BF), vm((2, *tokens.shape),...  4.26 us
    ppermute x3, starting transfers between devices, by_y(): return lax.ppermute(value, 'batch', [(i, i ^ 1) for i in range(8)])  4.22 us
    pallas_call x1, Pallas kernels, packed_body(): call(attention_back_kernel, (rows_f, vm((ROWS, QC), BF), vm((4, 48, QW),...  4.21 us
    ppermute x2, starting transfers between devices, homeward(): return lax.ppermute(value, ('batch', 'band'), pairs)  3.86 us
  transfers between devices with their start and end apart: 30, of which 10 were waited for; matrix products, arithmetic and copies ran while one was open for 0% of the time, Pallas kernels for 33%

profile of v8, /device:TPU:0, one launch (start us, length us, event | category | flops | bytes accessed | tf_op | source)
XLA Modules:
  0.0 77.1 jit_solution(9678497943525070679)
XLA Ops:
  0.6 3.0 %collective-permute-start.1 = (bf16[3,64,768]{2,1,0:T(8,128)(2,1)}, bf16[3,64,768]{2,1,0:T(8,128)(2,1)S(1)}, u32[]{:S(2)}, u32[]{:S(2)}) collective-permute-start(bf16[3,64,768]{2,1,0:T(8,128)(2,1)} %tok.1), channel_id=1, source_target_pairs={{0,2},{1,3},{2,0},{3,1},{4,6},{5,7},{6,4},{7,5},{8,10},{9,11},{10,... | collective-permute-start | bytes 884744 | tf_op jit(solution)/shard_map/ppermute | solution.py:631
  3.7 3.7 %shard_map.288 = (bf16[3,64,768]{2,1,0:T(8,128)(2,1)S(1)}, bf16[208,768]{1,0:T(8,128)(2,1)S(1)}, f32[16,768]{1,0:T(8,128)S(1)}, f32[8,1536]{1,0:T(8,128)S(1)}, b...) custom-call(bf16[3,64,768]{2,1,0:T(8,128)(2,1)} %cot.1, ...), custom_call_target="tpu_custom_call" | custom-call | bytes 9000000 | tf_op jit(solution)/shard_map/pallas_call | solution.py:659
  7.4 0.1 collective-permute-start.2
  7.5 2.0 %collective-permute-start.6 = (bf16[3,64,768]{2,1,0:T(8,128)(2,1)S(1)}, bf16[3,64,768]{2,1,0:T(8,128)(2,1)S(1)}, u32[]{:S(2)}, u32[]{:S(2)}) collective-permute-start(bf16[3,64,768]{2,1,0:T(8,128)(2,1)S(1)} %get-tuple-element.133.c0), channel_id=1, source_target_pairs={{0,2},{1,3},{2,0},{3,1},{4,6},{5,7},{6,4},{7,5},{8,10},{9,11},{10,... | collective-permute-start | bytes 884744 | tf_op jit(solution)/shard_map/ppermute | solution.py:631
  9.5 2.1 %collective-permute-done.2.vis = bf16[16,768]{1,0:T(8,128)(2,1)S(1)} collective-permute-done((bf16[16,768]{1,0:T(8,128)(2,1)S(1)}, bf16[16,768]{1,0:T(8,128)(2,1)S(1)}, u32[]{:S(2)}, u32[]{:S(2)}) %collective-permute-start.2) | collective-permute-done | bytes 24608 | tf_op jit(solution)/shard_map/ppermute | solution.py:631
  11.8 0.5 collective-permute-start.5
  12.3 1.4 %collective-permute-done.4.d_b = bf16[48,768]{1,0:T(8,128)(2,1)S(1)} collective-permute-done((bf16[48,768]{1,0:T(8,128)(2,1)S(1)}, bf16[48,768]{1,0:T(8,128)(2,1)S(1)}, u32[]{:S(2)}, u32[]{:S(2)}) %collective-permute-start.4) | collective-permute-done | bytes 73760 | tf_op jit(solution)/shard_map/ppermute | solution.py:627
  13.8 3.1 %shard_map.290 = (bf16[432,768]{1,0:T(8,128)(2,1)S(1)}, bf16[432,768]{1,0:T(8,128)(2,1)S(1)}, bf16[3,432,384]{2,1,0:T(8,128)(2,1)S(1)}, bf16[224,384]{1,0:T(8,12...) custom-call(bf16[208,768]{1,0:T(8,128)(2,1)S(1)} %get-tuple-element., ...), custom_call_target="tpu_custom_call" | custom-call | tf_op jit(solution)/shard_map/pallas_call | solution.py:694
  16.9 0.2 collective-permute-start.9
  17.1 0.4 collective-permute-start.10
  17.4 0.3 collective-permute-done.6.v
  17.8 0.5 collective-permute-start.8
  18.3 0.7 shard_map.292
  19.1 2.3 %shard_map.293 = (f32[432,768]{1,0:T(8,128)S(1)}, f32[432,768]{1,0:T(8,128)S(1)}, bf16[432,768]{1,0:T(8,128)(2,1)S(1)}, bf16[432,1536]{1,0:T(8,128)(2,1)S(1)}, f32[432,1536]{1,0:T(8,128)S(1)}) custom-call(f32[432,768]{1,0:T(8,128)S(1)} %get-tuple-element.139.half, bf16[224,384]{1,0:T(8,128)(2,1)S(1)} %collective-permute-done.9.mix_b, ...), custom_call_target="tpu_custom_call" | custom-call | tf_op jit(solution)/shard_map/pallas_call | solution.py:715
  21.4 1.7 %shard_map.294 = (bf16[432,768]{1,0:T(8,128)(2,1)S(1)}, bf16[432,768]{1,0:T(8,128)(2,1)S(1)}, bf16[4,96,768]{2,1,0:T(8,128)(2,1)S(1)}, bf16[4,96,768]{2,1,0:T(8,128)(2,1)S(1)}) custom-call(f32[432,768]{1,0:T(8,128)S(1)} %get-tuple-element.137.part, bf16[96,768]{1,0:T(8,128)(2,1)S(1)} %collective-permute-done.7.d_a, ...), custom_call_target="tpu_custom_call" | custom-call | tf_op jit(solution)/shard_map/pallas_call | solution.py:720
  23.1 1.8 %collective-permute-start.13 = (bf16[4,96,768]{2,1,0:T(8,128)(2,1)S(1)}, bf16[4,96,768]{2,1,0:T(8,128)(2,1)S(1)}, u32[]{:S(2)}, u32[]{:S(2)}) collective-permute-start(bf16[4,96,768]{2,1,0:T(8,128)(2,1)S(1)} %get-tuple-element.165), channel_id=1, source_target_pairs={{0,4},{4,0},{8,12},{12,8},{16,20},{20,16},{24,28},{28,24},{1,5},{5... | collective-permute-start | bytes 1769480 | tf_op jit(solution)/shard_map/ppermute | solution.py:635
  24.9 2.4 %shard_map.295 = (bf16[432,1536]{1,0:T(8,128)(2,1)S(1)}, bf16[432,384]{1,0:T(8,128)(2,1)S(1)}, bf16[432,384]{1,0:T(8,128)(2,1)S(1)}) custom-call(bf16[432,768]{1,0:T(8,128)(2,1)S(1)} %get-tuple-element.145.gb2, bf16[1536,768]{1,0:T(8,128)(2,1)S(1)} %get-tuple-element.146.wr, f32[432,1536]{1,0:T(8,128)S(1)} %get-tuple-element.147.slope, ...), custom_call_target="tpu_custom_call" | custom-call | tf_op jit(solution)/shard_map/pallas_call | solution.py:728
  27.4 0.5 collective-permute-start.12
  27.9 1.2 %shard_map.296 = (bf16[4,48,1536]{2,1,0:T(8,128)(2,1)S(1)}, bf16[4,48,1536]{2,1,0:T(8,128)(2,1)S(1)}, f32[8,128]{1,0:T(8,128)S(1)}) custom-call(bf16[432,768]{1,0:T(8,128)(2,1)S(1)} %get-tuple-element.157.n2, bf16[432,1536]{1,0:T(8,128)(2,1)S(1)} %get-tuple-element.158.gh, bf16[384,768]{1,0:T(8,128)(2,1)S(1)} %get-tuple-element.143.after.pick), custom_call_target="tpu_custom_call" | custom-call | tf_op jit(solution)/shard_map/pallas_call | solution.py:730
  29.1 1.7 %collective-permute-start.15 = (bf16[4,48,1536]{2,1,0:T(8,128)(2,1)S(1)}, bf16[4,48,1536]{2,1,0:T(8,128)(2,1)S(1)}, u32[]{:S(2)}, u32[]{:S(2)}) collective-permute-start(bf16[4,48,1536]{2,1,0:T(8,128)(2,1)S(1)} %get-tuple-element.171), channel_id=1, source_target_pairs={{0,8},{4,12},{8,0},{12,4},{16,24},{20,28},{24,16},{28,20},{1,9},{5... | collective-permute-start | bytes 1769480 | tf_op jit(solution)/shard_map/ppermute | solution.py:639
  30.7 4.2 %shard_map.297 = (f32[432,768]{1,0:T(8,128)S(1)}, bf16[432,1152]{1,0:T(8,128)(2,1)S(1)}, bf16[4,48,1536]{2,1,0:T(8,128)(2,1)S(1)}, bf16[4,48,1536]{2,1,0:T(8,128)(2,1)S(1)}, f32[8,128]{1,0:T(8,128)S(1)}) custom-call(bf16[432,384]{1,0:T(8,128)(2,1)S(1)} %get-tuple-element.148.l_a, bf16[432,384]{1,0:T(8,128)(2,1)S(1)} %collective-permute-done.11.l_b, ...), custom_call_target="tpu_custom_call" | custom-call | tf_op jit(solution)/shard_map/pallas_call | solution.py:737
  35.0 0.5 collective-permute-start.18
  35.5 3.8 %collective-permute-done.13.arrived = bf16[4,96,768]{2,1,0:T(8,128)(2,1)S(1)} collective-permute-done((bf16[4,96,768]{2,1,0:T(8,128)(2,1)S(1)}, bf16[4,96,768]{2,1,0:T(8,128)(2,1)S(1)}, u32[]{:S(2)}, u32[]{:S(2)}) %collective-permute-start.13) | collective-permute-done | bytes 589856 | tf_op jit(solution)/shard_map/ppermute | solution.py:635
  39.3 0.2 shard_map.298
  39.5 1.5 %collective-permute-start.17 = (bf16[4,96,768]{2,1,0:T(8,128)(2,1)S(1)}, bf16[4,96,768]{2,1,0:T(8,128)(2,1)S(1)}, u32[]{:S(2)}, u32[]{:S(2)}) collective-permute-start(bf16[4,96,768]{2,1,0:T(8,128)(2,1)S(1)} %get-tuple-element.178), channel_id=1, source_target_pairs={{1,17},{3,19},{5,21},{7,23},{9,25},{11,27},{13,29},{15,31},{16,0},... | collective-permute-start | bytes 1769480 | tf_op jit(solution)/shard_map/ppermute | solution.py:648
  41.0 4.3 %shard_map.299 = (bf16[2,3,64,768]{3,2,1,0:T(8,128)(2,1)S(1)}, bf16[2,3,64,768]{3,2,1,0:T(8,128)(2,1)S(1)}, bf16[2,48,256]{2,1,0:T(8,128)(2,1)S(1)}, bf16[2,48,256]{2,1,0:T(8,128)(2,1)S(1)}, f32[8,128]{1,0:T(8,128)S(1)}) custom-call(bf16[432,384]{1,0:T(8,128)(2,1)S(1)} %get-tuple-element.148.l_a, bf16[432,384]{1,0:T(8,128)(2,1)S(1)} %collective-permute-done.11.l_b, ...), custom_call_target="tpu_custom_call" | custom-call | flops 8000000000 | bytes 20000000 | tf_op jit(solution)/shard_map/pallas_call | solution.py:748
  45.3 0.1 shard_map.300
  45.4 1.8 %collective-permute-start.16 = (bf16[2,48,1792]{2,1,0:T(8,128)(2,1)S(1)}, bf16[2,48,1792]{2,1,0:T(8,128)(2,1)S(1)}, u32[]{:S(2)}, u32[]{:S(2)}) collective-permute-start(bf16[2,48,1792]{2,1,0:T(8,128)(2,1)S(1)} %get-tuple-element.176), channel_id=1, source_target_pairs={{0,4},{4,0},{8,12},{12,8},{16,20},{20,16},{24,28},{28,24},{1,5},{5... | collective-permute-start | bytes 1032200 | tf_op jit(solution)/shard_map/ppermute | solution.py:635
  47.3 4.7 %collective-permute-done.18.arrived = bf16[4,48,1536]{2,1,0:T(8,128)(2,1)S(1)} collective-permute-done((bf16[4,48,1536]{2,1,0:T(8,128)(2,1)S(1)}, bf16[4,48,1536]{2,1,0:T(8,128)(2,1)S(1)}, u32[]{:S(2)}, u32[]{:S(2)}) %collective-permute-start.18) | collective-permute-done | bytes 589856 | tf_op jit(solution)/shard_map/ppermute | solution.py:635
  52.0 0.1 shard_map.301
  52.1 1.9 %collective-permute-start.20 = (bf16[2,48,1536]{2,1,0:T(8,128)(2,1)S(1)}, bf16[2,48,1536]{2,1,0:T(8,128)(2,1)S(1)}, u32[]{:S(2)}, u32[]{:S(2)}) collective-permute-start(bf16[2,48,1536]{2,1,0:T(8,128)(2,1)S(1)} %get-tuple-element.187), channel_id=1, source_target_pairs={{0,8},{4,12},{8,0},{12,4},{16,24},{20,28},{24,16},{28,20},{1,9},{5... | collective-permute-start | bytes 884744 | tf_op jit(solution)/shard_map/ppermute | solution.py:639
  54.0 4.6 %collective-permute-done.17.arrived = bf16[4,96,768]{2,1,0:T(8,128)(2,1)S(1)} collective-permute-done((bf16[4,96,768]{2,1,0:T(8,128)(2,1)S(1)}, bf16[4,96,768]{2,1,0:T(8,128)(2,1)S(1)}, u32[]{:S(2)}, u32[]{:S(2)}) %collective-permute-start.17) | collective-permute-done | bytes 589856 | tf_op jit(solution)/shard_map/ppermute | solution.py:648
  58.6 0.1 shard_map.302
  58.8 1.7 %collective-permute-start.19 = (bf16[2,48,128]{2,1,0:T(8,128)(2,1)S(1)}, bf16[2,48,128]{2,1,0:T(8,128)(2,1)S(1)}, u32[]{:S(2)}, u32[]{:S(2)}) collective-permute-start(bf16[2,48,128]{2,1,0:T(8,128)(2,1)S(1)} %get-tuple-element.185), channel_id=1, source_target_pairs={{0,8},{4,12},{8,0},{12,4},{16,24},{20,28},{24,16},{28,20},{1,9},{5... | collective-permute-start | bytes 73736 | tf_op jit(solution)/shard_map/ppermute | solution.py:639
  60.5 2.6 %collective-permute-start.27 = (bf16[1,48,1536]{2,1,0:T(8,128)(2,1)S(1)}, bf16[1,48,1536]{2,1,0:T(8,128)(2,1)S(1)}, u32[]{:S(2)}, u32[]{:S(2)}) collective-permute-start(bf16[1,48,1536]{2,1,0:T(8,128)(2,1)S(1)} %get-tuple-element.207), channel_id=1, source_target_pairs={{0,16},{4,20},{8,24},{12,28},{16,0},{20,4},{24,8},{28,12},{1,17},{... | collective-permute-start | bytes 442376 | tf_op jit(solution)/shard_map/ppermute | solution.py:639
  63.1 2.3 %collective-permute-start.26 = (bf16[2,96,768]{2,1,0:T(8,128)(2,1)S(1)}, bf16[2,96,768]{2,1,0:T(8,128)(2,1)S(1)}, u32[]{:S(2)}, u32[]{:S(2)}) collective-permute-start(bf16[2,96,768]{2,1,0:T(8,128)(2,1)S(1)} %get-tuple-element.205), channel_id=1, source_target_pairs={{0,8},{2,10},{4,12},{6,14},{8,0},{10,2},{12,4},{14,6},{17,25},{19,... | collective-permute-start | bytes 884744 | tf_op jit(solution)/shard_map/ppermute | solution.py:648
  65.7 0.6 collective-permute-start.21
  66.3 0.8 %collective-permute-done.21.vec_b = bf16[2,48,16]{2,1,0:T(8,128)(2,1)S(1)} collective-permute-done((bf16[2,48,16]{2,1,0:T(8,128)(2,1)S(1)}, bf16[2,48,16]{2,1,0:T(8,128)(2,1)S(1)}, u32[]{:S(2)}, u32[]{:S(2)}) %collective-permute-start.21) | collective-permute-done | bytes 3104 | tf_op jit(solution)/shard_map/ppermute | solution.py:627
  67.1 2.8 %collective-permute-start.24 = (bf16[24,1152]{1,0:T(8,128)(2,1)S(1)}, bf16[24,1152]{1,0:T(8,128)(2,1)S(1)}, u32[]{:S(2)}, u32[]{:S(2)}) collective-permute-start(bf16[24,1152]{1,0:T(8,128)(2,1)S(1)} %get-tuple-element.201), channel_id=1, source_target_pairs={{0,17},{1,16},{2,19},{3,18},{4,21},{5,20},{6,23},{7,22},{8,25},{9,... | collective-permute-start | bytes 165896 | tf_op jit(solution)/shard_map/ppermute | solution.py:643
  69.9 1.2 %shard_map.306 = (bf16[3,64,768]{2,1,0:T(8,128)(2,1)}, f32[8,128]{1,0:T(8,128)S(1)}) custom-call(bf16[2,3,64,768]{3,2,1,0:T(8,128)(2,1)S(1)} %get-tuple-element.168.gb_a, bf16[2,3,64,768]{3,2,1,0:T(8,128)(2,1)S(1)} %collective-permute-done.14.gb_b, f32[432,768]{1,0:T(8,128)S(1)} %get-tuple-element.150.res, f32[16,64]{1,0:T(8,128)S(1)} %get-tuple-element.162.mine, ...), custom_call_target="tpu_custom_call" | custom-call | tf_op jit(solution)/shard_map/pallas_call | solution.py:782
  71.1 0.2 collective-permute-start.25
  71.3 1.4 %shard_map.308 = (bf16[3,64,768]{2,1,0:T(8,128)(2,1)}, f32[8,128]{1,0:T(8,128)S(1)}) custom-call(bf16[2,3,64,768]{3,2,1,0:T(8,128)(2,1)S(1)} %get-tuple-element.168.gb_a, bf16[2,3,64,768]{3,2,1,0:T(8,128)(2,1)S(1)} %collective-permute-done.14.gb_b, bf16[208,768]{1,0:T(8,128)(2,1)S(1)} %get-tuple-element.124.t0.tok, f32[432,768]{1,0:T(8,128)S(1)} %get-tuple-element.160.gres, ...), custom_call_target="tpu_custom_call" | custom-call | tf_op jit(solution)/shard_map/pallas_call | solution.py:791
  72.6 1.4 %collective-permute-done.26.wr_a = bf16[2,96,768]{2,1,0:T(8,128)(2,1)S(1)} collective-permute-done((bf16[2,96,768]{2,1,0:T(8,128)(2,1)S(1)}, bf16[2,96,768]{2,1,0:T(8,128)(2,1)S(1)}, u32[]{:S(2)}, u32[]{:S(2)}) %collective-permute-start.26) | collective-permute-done | bytes 294944 | tf_op jit(solution)/shard_map/ppermute | solution.py:648
  74.1 0.1 shard_map.309
  74.3 0.5 collective-permute-start.29
  74.8 0.3 collective-permute-done.24.far
  75.1 0.8 %collective-permute-done.25.vec_a = bf16[48,16]{1,0:T(8,128)(2,1)S(1)} collective-permute-done((bf16[48,16]{1,0:T(8,128)(2,1)S(1)}, bf16[48,16]{1,0:T(8,128)(2,1)S(1)}, u32[]{:S(2)}, u32[]{:S(2)}) %collective-permute-start.25) | collective-permute-done | bytes 1568 | tf_op jit(solution)/shard_map/ppermute | solution.py:639
  76.0 1.0 %shard_map.311 = (f32[24,2304]{1,0:T(8,128)}, f32[24]{0:T(128)}, f32[24]{0:T(128)}, f32[2,24]{1,0:T(2,128)}, f32[24]{0:T(128)}, /*index=5*/f32[24]{0:T(128)}, f3...) custom-call(f32[24,1920]{1,0:T(8,128)S(1)} %get-tuple-element.210.ow, ...), custom_call_target="tpu_custom_call" | custom-call | bytes 1000000 | tf_op jit(solution)/shard_map/pallas_call | solution.py:807
  (36 shorter events, 0.9 us)
Async XLA Ops:
  0.6 11.0 %collective-permute-start.1 = (bf16[3,64,768]{2,1,0:T(8,128)(2,1)}, bf16[3,64,768]{2,1,0:T(8,128)(2,1)S(1)}, u32[]{:S(2)}, u32[]{:S(2)}) collective-permute-start(bf16[3,64,768]{2,1,0:T(8,128)(2,1)} %tok.1), channel_id=1, source_target_pairs={{0,2},{1,3},{2,0},{3,1},{4,6},{5,7},{6,4},{7,5},{8,10},{9,11},{10,... | collective-permute-start | bytes 884744 | tf_op jit(solution)/shard_map/ppermute | solution.py:631
  7.4 5.0 %collective-permute-start = (bf16[208,768]{1,0:T(8,128)(2,1)S(1)}, bf16[208,768]{1,0:T(8,128)(2,1)S(1)}, u32[]{:S(2)}, u32[]{:S(2)}) collective-permute-start(bf16[208,768]{1,0:T(8,128)(2,1)S(1)} %get-tuple-element.124.t0.tok), channel_id=1, source_target_pairs={{0,1},{1,0},{2,3},{3,2},{4,5},{5,4},{6,7},{7,6},{8,9},{9,8},{10,11... | collective-permute-start | bytes 958472 | tf_op jit(solution)/shard_map/ppermute | solution.py:627
  7.4 4.2 %collective-permute-start.2 = (bf16[16,768]{1,0:T(8,128)(2,1)S(1)}, bf16[16,768]{1,0:T(8,128)(2,1)S(1)}, u32[]{:S(2)}, u32[]{:S(2)}) collective-permute-start(bf16[16,768]{1,0:T(8,128)(2,1)S(1)} %get-tuple-element.125), channel_id=1, source_target_pairs={{0,2},{1,3},{2,0},{3,1},{4,6},{5,7},{6,4},{7,5},{8,10},{9,11},{10,... | collective-permute-start | bytes 73736 | tf_op jit(solution)/shard_map/ppermute | solution.py:631
  7.5 10.2 %collective-permute-start.6 = (bf16[3,64,768]{2,1,0:T(8,128)(2,1)S(1)}, bf16[3,64,768]{2,1,0:T(8,128)(2,1)S(1)}, u32[]{:S(2)}, u32[]{:S(2)}) collective-permute-start(bf16[3,64,768]{2,1,0:T(8,128)(2,1)S(1)} %get-tuple-element.133.c0), channel_id=1, source_target_pairs={{0,2},{1,3},{2,0},{3,1},{4,6},{5,7},{6,4},{7,5},{8,10},{9,11},{10,... | collective-permute-start | bytes 884744 | tf_op jit(solution)/shard_map/ppermute | solution.py:631
  11.7 2.1 %collective-permute-start.3 = (bf16[160,768]{1,0:T(8,128)(2,1)S(1)}, bf16[160,768]{1,0:T(8,128)(2,1)S(1)}, u32[]{:S(2)}, u32[]{:S(2)}) collective-permute-start(bf16[160,768]{1,0:T(8,128)(2,1)S(1)} %get-tuple-element.127.x_a), channel_id=1, source_target_pairs={{0,1},{1,0},{2,3},{3,2},{4,5},{5,4},{6,7},{7,6},{8,9},{9,8},{10,11... | collective-permute-start | bytes 737288 | tf_op jit(solution)/shard_map/ppermute | solution.py:627
  11.8 6.6 %collective-permute-start.5 = (bf16[3,64,768]{2,1,0:T(8,128)(2,1)S(1)}, bf16[3,64,768]{2,1,0:T(8,128)(2,1)S(1)}, u32[]{:S(2)}, u32[]{:S(2)}) collective-permute-start(bf16[3,64,768]{2,1,0:T(8,128)(2,1)S(1)} %get-tuple-element.133.c0), channel_id=1, source_target_pairs={{0,1},{1,0},{2,3},{3,2},{4,5},{5,4},{6,7},{7,6},{8,9},{9,8},{10,11... | collective-permute-start | bytes 884744 | tf_op jit(solution)/shard_map/ppermute | solution.py:627
  12.3 1.5 %collective-permute-start.4 = (bf16[48,768]{1,0:T(8,128)(2,1)S(1)}, bf16[48,768]{1,0:T(8,128)(2,1)S(1)}, u32[]{:S(2)}, u32[]{:S(2)}) collective-permute-start(bf16[48,768]{1,0:T(8,128)(2,1)S(1)} %get-tuple-element.128.x_b), channel_id=1, source_target_pairs={{0,1},{1,0},{2,3},{3,2},{4,5},{5,4},{6,7},{7,6},{8,9},{9,8},{10,11... | collective-permute-start | bytes 221192 | tf_op jit(solution)/shard_map/ppermute | solution.py:627
  16.9 2.2 %collective-permute-start.9 = (bf16[224,384]{1,0:T(8,128)(2,1)S(1)}, bf16[224,384]{1,0:T(8,128)(2,1)S(1)}, u32[]{:S(2)}, u32[]{:S(2)}) collective-permute-start(bf16[224,384]{1,0:T(8,128)(2,1)S(1)} %get-tuple-element.130.mix_a), channel_id=1, source_target_pairs={{0,1},{1,0},{2,3},{3,2},{4,5},{5,4},{6,7},{7,6},{8,9},{9,8},{10,11... | collective-permute-start | bytes 516104 | tf_op jit(solution)/shard_map/ppermute | solution.py:627
  17.1 2.0 %collective-permute-start.10 = (bf16[208,384]{1,0:T(8,128)(2,1)S(1)}, bf16[208,384]{1,0:T(8,128)(2,1)S(1)}, u32[]{:S(2)}, u32[]{:S(2)}) collective-permute-start(bf16[208,384]{1,0:T(8,128)(2,1)S(1)} %get-tuple-element.131.mix2_a), channel_id=1, source_target_pairs={{0,1},{1,0},{2,3},{3,2},{4,5},{5,4},{6,7},{7,6},{8,9},{9,8},{10,11... | collective-permute-start | bytes 479240 | tf_op jit(solution)/shard_map/ppermute | solution.py:627
  17.7 3.7 %collective-permute-start.7 = (bf16[96,768]{1,0:T(8,128)(2,1)S(1)}, bf16[96,768]{1,0:T(8,128)(2,1)S(1)}, u32[]{:S(2)}, u32[]{:S(2)}) collective-permute-start(bf16[96,768]{1,0:T(8,128)(2,1)S(1)} %get-tuple-element.134.x_a), channel_id=1, source_target_pairs={{0,1},{1,0},{2,3},{3,2},{4,5},{5,4},{6,7},{7,6},{8,9},{9,8},{10,11... | collective-permute-start | bytes 442376 | tf_op jit(solution)/shard_map/ppermute | solution.py:627
  17.8 3.6 %collective-permute-start.8 = (bf16[96,768]{1,0:T(8,128)(2,1)S(1)}, bf16[96,768]{1,0:T(8,128)(2,1)S(1)}, u32[]{:S(2)}, u32[]{:S(2)}) collective-permute-start(bf16[96,768]{1,0:T(8,128)(2,1)S(1)} %get-tuple-element.135.x_b), channel_id=1, source_target_pairs={{0,1},{1,0},{2,3},{3,2},{4,5},{5,4},{6,7},{7,6},{8,9},{9,8},{10,11... | collective-permute-start | bytes 442376 | tf_op jit(solution)/shard_map/ppermute | solution.py:627
  23.1 16.2 %collective-permute-start.13 = (bf16[4,96,768]{2,1,0:T(8,128)(2,1)S(1)}, bf16[4,96,768]{2,1,0:T(8,128)(2,1)S(1)}, u32[]{:S(2)}, u32[]{:S(2)}) collective-permute-start(bf16[4,96,768]{2,1,0:T(8,128)(2,1)S(1)} %get-tuple-element.165), channel_id=1, source_target_pairs={{0,4},{4,0},{8,12},{12,8},{16,20},{20,16},{24,28},{28,24},{1,5},{5... | collective-permute-start | bytes 1769480 | tf_op jit(solution)/shard_map/ppermute | solution.py:635
  27.3 3.4 %collective-permute-start.11 = (bf16[432,384]{1,0:T(8,128)(2,1)S(1)}, bf16[432,384]{1,0:T(8,128)(2,1)S(1)}, u32[]{:S(2)}, u32[]{:S(2)}) collective-permute-start(bf16[432,384]{1,0:T(8,128)(2,1)S(1)} %get-tuple-element.148.l_a), channel_id=1, source_target_pairs={{0,1},{1,0},{2,3},{3,2},{4,5},{5,4},{6,7},{7,6},{8,9},{9,8},{10,11... | collective-permute-start | bytes 995336 | tf_op jit(solution)/shard_map/ppermute | solution.py:627
  27.4 3.3 %collective-permute-start.12 = (bf16[432,384]{1,0:T(8,128)(2,1)S(1)}, bf16[432,384]{1,0:T(8,128)(2,1)S(1)}, u32[]{:S(2)}, u32[]{:S(2)}) collective-permute-start(bf16[432,384]{1,0:T(8,128)(2,1)S(1)} %get-tuple-element.149.r_a), channel_id=1, source_target_pairs={{0,1},{1,0},{2,3},{3,2},{4,5},{5,4},{6,7},{7,6},{8,9},{9,8},{10,11... | collective-permute-start | bytes 995336 | tf_op jit(solution)/shard_map/ppermute | solution.py:627
  29.1 16.2 %collective-permute-start.15 = (bf16[4,48,1536]{2,1,0:T(8,128)(2,1)S(1)}, bf16[4,48,1536]{2,1,0:T(8,128)(2,1)S(1)}, u32[]{:S(2)}, u32[]{:S(2)}) collective-permute-start(bf16[4,48,1536]{2,1,0:T(8,128)(2,1)S(1)} %get-tuple-element.171), channel_id=1, source_target_pairs={{0,8},{4,12},{8,0},{12,4},{16,24},{20,28},{24,16},{28,20},{1,9},{5... | collective-permute-start | bytes 1769480 | tf_op jit(solution)/shard_map/ppermute | solution.py:639
  35.0 17.0 %collective-permute-start.18 = (bf16[4,48,1536]{2,1,0:T(8,128)(2,1)S(1)}, bf16[4,48,1536]{2,1,0:T(8,128)(2,1)S(1)}, u32[]{:S(2)}, u32[]{:S(2)}) collective-permute-start(bf16[4,48,1536]{2,1,0:T(8,128)(2,1)S(1)} %get-tuple-element.180), channel_id=1, source_target_pairs={{0,4},{4,0},{8,12},{12,8},{16,20},{20,16},{24,28},{28,24},{1,5},{5... | collective-permute-start | bytes 1769480 | tf_op jit(solution)/shard_map/ppermute | solution.py:635
  39.5 19.1 %collective-permute-start.17 = (bf16[4,96,768]{2,1,0:T(8,128)(2,1)S(1)}, bf16[4,96,768]{2,1,0:T(8,128)(2,1)S(1)}, u32[]{:S(2)}, u32[]{:S(2)}) collective-permute-start(bf16[4,96,768]{2,1,0:T(8,128)(2,1)S(1)} %get-tuple-element.178), channel_id=1, source_target_pairs={{1,17},{3,19},{5,21},{7,23},{9,25},{11,27},{13,29},{15,31},{16,0},... | collective-permute-start | bytes 1769480 | tf_op jit(solution)/shard_map/ppermute | solution.py:648
  45.4 13.3 %collective-permute-start.16 = (bf16[2,48,1792]{2,1,0:T(8,128)(2,1)S(1)}, bf16[2,48,1792]{2,1,0:T(8,128)(2,1)S(1)}, u32[]{:S(2)}, u32[]{:S(2)}) collective-permute-start(bf16[2,48,1792]{2,1,0:T(8,128)(2,1)S(1)} %get-tuple-element.176), channel_id=1, source_target_pairs={{0,4},{4,0},{8,12},{12,8},{16,20},{20,16},{24,28},{28,24},{1,5},{5... | collective-permute-start | bytes 1032200 | tf_op jit(solution)/shard_map/ppermute | solution.py:635
  52.1 13.3 %collective-permute-start.20 = (bf16[2,48,1536]{2,1,0:T(8,128)(2,1)S(1)}, bf16[2,48,1536]{2,1,0:T(8,128)(2,1)S(1)}, u32[]{:S(2)}, u32[]{:S(2)}) collective-permute-start(bf16[2,48,1536]{2,1,0:T(8,128)(2,1)S(1)} %get-tuple-element.187), channel_id=1, source_target_pairs={{0,8},{4,12},{8,0},{12,4},{16,24},{20,28},{24,16},{28,20},{1,9},{5... | collective-permute-start | bytes 884744 | tf_op jit(solution)/shard_map/ppermute | solution.py:639
  54.0 11.7 %collective-permute-start.14 = (bf16[2,3,64,768]{3,2,1,0:T(8,128)(2,1)S(1)}, bf16[2,3,64,768]{3,2,1,0:T(8,128)(2,1)S(1)}, u32[]{:S(2)}, u32[]{:S(2)}) collective-permute-start(bf16[2,3,64,768]{3,2,1,0:T(8,128)(2,1)S(1)} %get-tuple-element.169), channel_id=1, source_target_pairs={{0,1},{1,0},{2,3},{3,2},{4,5},{5,4},{6,7},{7,6},{8,9},{9,8},{10,11... | collective-permute-start | bytes 1769480 | tf_op jit(solution)/shard_map/ppermute | solution.py:627
  58.8 6.8 %collective-permute-start.19 = (bf16[2,48,128]{2,1,0:T(8,128)(2,1)S(1)}, bf16[2,48,128]{2,1,0:T(8,128)(2,1)S(1)}, u32[]{:S(2)}, u32[]{:S(2)}) collective-permute-start(bf16[2,48,128]{2,1,0:T(8,128)(2,1)S(1)} %get-tuple-element.185), channel_id=1, source_target_pairs={{0,8},{4,12},{8,0},{12,4},{16,24},{20,28},{24,16},{28,20},{1,9},{5... | collective-permute-start | bytes 73736 | tf_op jit(solution)/shard_map/ppermute | solution.py:639
  60.5 12.2 %collective-permute-start.27 = (bf16[1,48,1536]{2,1,0:T(8,128)(2,1)S(1)}, bf16[1,48,1536]{2,1,0:T(8,128)(2,1)S(1)}, u32[]{:S(2)}, u32[]{:S(2)}) collective-permute-start(bf16[1,48,1536]{2,1,0:T(8,128)(2,1)S(1)} %get-tuple-element.207), channel_id=1, source_target_pairs={{0,16},{4,20},{8,24},{12,28},{16,0},{20,4},{24,8},{28,12},{1,17},{... | collective-permute-start | bytes 442376 | tf_op jit(solution)/shard_map/ppermute | solution.py:639
  63.1 11.0 %collective-permute-start.26 = (bf16[2,96,768]{2,1,0:T(8,128)(2,1)S(1)}, bf16[2,96,768]{2,1,0:T(8,128)(2,1)S(1)}, u32[]{:S(2)}, u32[]{:S(2)}) collective-permute-start(bf16[2,96,768]{2,1,0:T(8,128)(2,1)S(1)} %get-tuple-element.205), channel_id=1, source_target_pairs={{0,8},{2,10},{4,12},{6,14},{8,0},{10,2},{12,4},{14,6},{17,25},{19,... | collective-permute-start | bytes 884744 | tf_op jit(solution)/shard_map/ppermute | solution.py:648
  65.5 9.5 %collective-permute-start.23 = (bf16[24,1920]{1,0:T(8,128)(2,1)S(1)}, bf16[24,1920]{1,0:T(8,128)(2,1)S(1)}, u32[]{:S(2)}, u32[]{:S(2)}) collective-permute-start(bf16[24,1920]{1,0:T(8,128)(2,1)S(1)} %get-tuple-element.199), channel_id=1, source_target_pairs={{0,16},{4,20},{8,24},{12,28},{16,0},{20,4},{24,8},{28,12},{1,17},{... | collective-permute-start | bytes 276488 | tf_op jit(solution)/shard_map/ppermute | solution.py:639
  65.6 5.5 %collective-permute-start.22 = (f32[24,1152]{1,0:T(8,128)S(1)}, f32[24,1152]{1,0:T(8,128)S(1)}, u32[]{:S(2)}, u32[]{:S(2)}) collective-permute-start(f32[24,1152]{1,0:T(8,128)S(1)} %get-tuple-element.194), channel_id=1, source_target_pairs={{0,1},{1,0},{2,3},{3,2},{4,5},{5,4},{6,7},{7,6},{8,9},{9,8},{10,11... | collective-permute-start | bytes 331784 | tf_op jit(solution)/shard_map/ppermute | solution.py:627
  65.7 1.4 %collective-permute-start.21 = (bf16[2,48,16]{2,1,0:T(8,128)(2,1)S(1)}, bf16[2,48,16]{2,1,0:T(8,128)(2,1)S(1)}, u32[]{:S(2)}, u32[]{:S(2)}) collective-permute-start(bf16[2,48,16]{2,1,0:T(8,128)(2,1)S(1)} %get-tuple-element.193), channel_id=1, source_target_pairs={{0,1},{1,0},{2,3},{3,2},{4,5},{5,4},{6,7},{7,6},{8,9},{9,8},{10,11... | collective-permute-start | bytes 9224 | tf_op jit(solution)/shard_map/ppermute | solution.py:627
  67.1 7.9 %collective-permute-start.24 = (bf16[24,1152]{1,0:T(8,128)(2,1)S(1)}, bf16[24,1152]{1,0:T(8,128)(2,1)S(1)}, u32[]{:S(2)}, u32[]{:S(2)}) collective-permute-start(bf16[24,1152]{1,0:T(8,128)(2,1)S(1)} %get-tuple-element.201), channel_id=1, source_target_pairs={{0,17},{1,16},{2,19},{3,18},{4,21},{5,20},{6,23},{7,22},{8,25},{9,... | collective-permute-start | bytes 165896 | tf_op jit(solution)/shard_map/ppermute | solution.py:643
  71.1 4.8 %collective-permute-start.25 = (bf16[48,16]{1,0:T(8,128)(2,1)S(1)}, bf16[48,16]{1,0:T(8,128)(2,1)S(1)}, u32[]{:S(2)}, u32[]{:S(2)}) collective-permute-start(bf16[48,16]{1,0:T(8,128)(2,1)S(1)} %get-tuple-element.203), channel_id=1, source_target_pairs={{0,16},{4,20},{8,24},{12,28},{16,0},{20,4},{24,8},{28,12},{1,17},{... | collective-permute-start | bytes 4616 | tf_op jit(solution)/shard_map/ppermute | solution.py:639
  74.2 1.7 %collective-permute-start.28 = (bf16[24,1536]{1,0:T(8,128)(2,1)S(1)}, bf16[24,1536]{1,0:T(8,128)(2,1)S(1)}, u32[]{:S(2)}, u32[]{:S(2)}) collective-permute-start(bf16[24,1536]{1,0:T(8,128)(2,1)S(1)} %get-tuple-element.214), channel_id=1, source_target_pairs={{0,1},{1,0},{2,3},{3,2},{4,5},{5,4},{6,7},{7,6},{8,9},{9,8},{10,11... | collective-permute-start | bytes 221192 | tf_op jit(solution)/shard_map/ppermute | solution.py:627
  74.3 1.7 %collective-permute-start.29 = (bf16[96,768]{1,0:T(8,128)(2,1)S(1)}, bf16[96,768]{1,0:T(8,128)(2,1)S(1)}, u32[]{:S(2)}, u32[]{:S(2)}) collective-permute-start(bf16[96,768]{1,0:T(8,128)(2,1)S(1)} %get-tuple-element.216), channel_id=1, source_target_pairs={{0,1},{1,0},{2,3},{3,2},{4,5},{5,4},{6,7},{7,6},{8,9},{9,8},{10,11... | collective-permute-start | bytes 442376 | tf_op jit(solution)/shard_map/ppermute | solution.py:627

commit v9 on v8

--- a/solution.py
+++ b/solution.py
@@ -595,6 +595,8 @@
 
 
 COSTS = {
+    "back_kernel": (2000000000, 0),
+    "expand_grad_kernel": (1000000000, 0),
     "vectors_kernel": (8000000000, 20000000),
     "second_fold_kernel": (0, 2000000),
     "last_kernel": (0, 1000000),

time: 77.3 us -> 77.2 us (level)
  no operation moved by 1% of the time
where the time goes in v9:
time: 77.2 us; the launch traced here: 77 us
  Pallas kernels  27.9 us (36%)
  starting transfers between devices  27.6 us (36%)
  waiting for transfers between devices  20.4 us (26%)
  between operations  1.06 us (1%)
    ppermute x3, waiting for transfers between devices, by_y(): return lax.ppermute(value, 'batch', [(i, i ^ 1) for i in range(8)])  8.53 us
    ppermute x6, starting transfers between devices, by_z(): return lax.ppermute(value, 'batch', [(i, i ^ 2 * dz) for i in range(8)])  8.01 us
    ppermute x2, waiting for transfers between devices, homeward(): return lax.ppermute(value, ('batch', 'band'), pairs)  6 us
    ppermute x3, starting transfers between devices, by_x(): return lax.ppermute(value, 'band', [(i, i ^ 2) for i in range(4)])  5.09 us
    ppermute x3, starting transfers between devices, by_y(): return lax.ppermute(value, 'batch', [(i, i ^ 1) for i in range(8)])  4.23 us
    pallas_call x1, Pallas kernels, packed_body(): call(attention_back_kernel, (rows_f, vm((ROWS, QC), BF), vm((4, 48, QW),...  4.22 us
    pallas_call x1, Pallas kernels, packed_body(): call(vectors_kernel, (vm((2, *tokens.shape), BF), vm((2, *tokens.shape),...  4.21 us
    ppermute x2, starting transfers between devices, homeward(): return lax.ppermute(value, ('batch', 'band'), pairs)  3.87 us
  transfers between devices with their start and end apart: 30, of which 10 were waited for; matrix products, arithmetic and copies ran while one was open for 0% of the time, Pallas kernels for 33%

profile of v9, /device:TPU:0, one launch (start us, length us, event | category | flops | bytes accessed | tf_op | source)
XLA Modules:
  0.0 77.0 jit_solution(14403573901145044994)
XLA Ops:
  0.6 3.0 %collective-permute-start.1 = (bf16[3,64,768]{2,1,0:T(8,128)(2,1)}, bf16[3,64,768]{2,1,0:T(8,128)(2,1)S(1)}, u32[]{:S(2)}, u32[]{:S(2)}) collective-permute-start(bf16[3,64,768]{2,1,0:T(8,128)(2,1)} %tok.1), channel_id=1, source_target_pairs={{0,2},{1,3},{2,0},{3,1},{4,6},{5,7},{6,4},{7,5},{8,10},{9,11},{10,... | collective-permute-start | bytes 884744 | tf_op jit(solution)/shard_map/ppermute | solution.py:633
  3.7 3.7 %shard_map.288 = (bf16[3,64,768]{2,1,0:T(8,128)(2,1)S(1)}, bf16[208,768]{1,0:T(8,128)(2,1)S(1)}, f32[16,768]{1,0:T(8,128)S(1)}, f32[8,1536]{1,0:T(8,128)S(1)}, b...) custom-call(bf16[3,64,768]{2,1,0:T(8,128)(2,1)} %cot.1, ...), custom_call_target="tpu_custom_call" | custom-call | bytes 9000000 | tf_op jit(solution)/shard_map/pallas_call | solution.py:661
  7.5 2.0 %collective-permute-start.6 = (bf16[3,64,768]{2,1,0:T(8,128)(2,1)S(1)}, bf16[3,64,768]{2,1,0:T(8,128)(2,1)S(1)}, u32[]{:S(2)}, u32[]{:S(2)}) collective-permute-start(bf16[3,64,768]{2,1,0:T(8,128)(2,1)S(1)} %get-tuple-element.133.c0), channel_id=1, source_target_pairs={{0,2},{1,3},{2,0},{3,1},{4,6},{5,7},{6,4},{7,5},{8,10},{9,11},{10,... | collective-permute-start | bytes 884744 | tf_op jit(solution)/shard_map/ppermute | solution.py:633
  9.5 2.1 %collective-permute-done.2.vis = bf16[16,768]{1,0:T(8,128)(2,1)S(1)} collective-permute-done((bf16[16,768]{1,0:T(8,128)(2,1)S(1)}, bf16[16,768]{1,0:T(8,128)(2,1)S(1)}, u32[]{:S(2)}, u32[]{:S(2)}) %collective-permute-start.2) | collective-permute-done | bytes 24608 | tf_op jit(solution)/shard_map/ppermute | solution.py:633
  11.8 0.5 collective-permute-start.5
  12.3 1.4 %collective-permute-done.4.d_b = bf16[48,768]{1,0:T(8,128)(2,1)S(1)} collective-permute-done((bf16[48,768]{1,0:T(8,128)(2,1)S(1)}, bf16[48,768]{1,0:T(8,128)(2,1)S(1)}, u32[]{:S(2)}, u32[]{:S(2)}) %collective-permute-start.4) | collective-permute-done | bytes 73760 | tf_op jit(solution)/shard_map/ppermute | solution.py:629
  13.8 3.0 %shard_map.290 = (bf16[432,768]{1,0:T(8,128)(2,1)S(1)}, bf16[432,768]{1,0:T(8,128)(2,1)S(1)}, bf16[3,432,384]{2,1,0:T(8,128)(2,1)S(1)}, bf16[224,384]{1,0:T(8,12...) custom-call(bf16[208,768]{1,0:T(8,128)(2,1)S(1)} %get-tuple-element., ...), custom_call_target="tpu_custom_call" | custom-call | tf_op jit(solution)/shard_map/pallas_call | solution.py:696
  16.8 0.2 collective-permute-start.9
  17.0 0.3 collective-permute-start.10
  17.4 0.3 collective-permute-done.6.v
  17.8 0.5 collective-permute-start.8
  18.3 0.7 shard_map.292
  19.1 2.3 %shard_map.293 = (f32[432,768]{1,0:T(8,128)S(1)}, f32[432,768]{1,0:T(8,128)S(1)}, bf16[432,768]{1,0:T(8,128)(2,1)S(1)}, bf16[432,1536]{1,0:T(8,128)(2,1)S(1)}, f32[432,1536]{1,0:T(8,128)S(1)}) custom-call(f32[432,768]{1,0:T(8,128)S(1)} %get-tuple-element.139.half, bf16[224,384]{1,0:T(8,128)(2,1)S(1)} %collective-permute-done.9.mix_b, ...), custom_call_target="tpu_custom_call" | custom-call | tf_op jit(solution)/shard_map/pallas_call | solution.py:717
  21.4 1.7 %shard_map.294 = (bf16[432,768]{1,0:T(8,128)(2,1)S(1)}, bf16[432,768]{1,0:T(8,128)(2,1)S(1)}, bf16[4,96,768]{2,1,0:T(8,128)(2,1)S(1)}, bf16[4,96,768]{2,1,0:T(8,128)(2,1)S(1)}) custom-call(f32[432,768]{1,0:T(8,128)S(1)} %get-tuple-element.137.part, bf16[96,768]{1,0:T(8,128)(2,1)S(1)} %collective-permute-done.7.d_a, ...), custom_call_target="tpu_custom_call" | custom-call | tf_op jit(solution)/shard_map/pallas_call | solution.py:722
  23.1 1.8 %collective-permute-start.13 = (bf16[4,96,768]{2,1,0:T(8,128)(2,1)S(1)}, bf16[4,96,768]{2,1,0:T(8,128)(2,1)S(1)}, u32[]{:S(2)}, u32[]{:S(2)}) collective-permute-start(bf16[4,96,768]{2,1,0:T(8,128)(2,1)S(1)} %get-tuple-element.165), channel_id=1, source_target_pairs={{0,4},{4,0},{8,12},{12,8},{16,20},{20,16},{24,28},{28,24},{1,5},{5... | collective-permute-start | bytes 1769480 | tf_op jit(solution)/shard_map/ppermute | solution.py:637
  24.9 2.4 %shard_map.295 = (bf16[432,1536]{1,0:T(8,128)(2,1)S(1)}, bf16[432,384]{1,0:T(8,128)(2,1)S(1)}, bf16[432,384]{1,0:T(8,128)(2,1)S(1)}) custom-call(bf16[432,768]{1,0:T(8,128)(2,1)S(1)} %get-tuple-element.145.gb2, bf16[1536,768]{1,0:T(8,128)(2,1)S(1)} %get-tuple-element.146.wr, f32[432,1536]{1,0:T(8,128)S(1)} %get-tuple-element.147.slope, ...), custom_call_target="tpu_custom_call" | custom-call | flops 2000000000 | tf_op jit(solution)/shard_map/pallas_call | solution.py:730
  27.4 0.5 collective-permute-start.12
  27.9 1.2 %shard_map.296 = (bf16[4,48,1536]{2,1,0:T(8,128)(2,1)S(1)}, bf16[4,48,1536]{2,1,0:T(8,128)(2,1)S(1)}, f32[8,128]{1,0:T(8,128)S(1)}) custom-call(bf16[432,768]{1,0:T(8,128)(2,1)S(1)} %get-tuple-element.157.n2, bf16[432,1536]{1,0:T(8,128)(2,1)S(1)} %get-tuple-element.158.gh, bf16[384,768]{1,0:T(8,128)(2,1)S(1)} %get-tuple-element.143.after.pick), custom_call_target="tpu_custom_call" | custom-call | flops 1000000000 | tf_op jit(solution)/shard_map/pallas_call | solution.py:732
  29.1 1.7 %collective-permute-start.15 = (bf16[4,48,1536]{2,1,0:T(8,128)(2,1)S(1)}, bf16[4,48,1536]{2,1,0:T(8,128)(2,1)S(1)}, u32[]{:S(2)}, u32[]{:S(2)}) collective-permute-start(bf16[4,48,1536]{2,1,0:T(8,128)(2,1)S(1)} %get-tuple-element.171), channel_id=1, source_target_pairs={{0,8},{4,12},{8,0},{12,4},{16,24},{20,28},{24,16},{28,20},{1,9},{5... | collective-permute-start | bytes 1769480 | tf_op jit(solution)/shard_map/ppermute | solution.py:641
  30.8 4.2 %shard_map.297 = (f32[432,768]{1,0:T(8,128)S(1)}, bf16[432,1152]{1,0:T(8,128)(2,1)S(1)}, bf16[4,48,1536]{2,1,0:T(8,128)(2,1)S(1)}, bf16[4,48,1536]{2,1,0:T(8,128)(2,1)S(1)}, f32[8,128]{1,0:T(8,128)S(1)}) custom-call(bf16[432,384]{1,0:T(8,128)(2,1)S(1)} %get-tuple-element.148.l_a, bf16[432,384]{1,0:T(8,128)(2,1)S(1)} %collective-permute-done.11.l_b, ...), custom_call_target="tpu_custom_call" | custom-call | tf_op jit(solution)/shard_map/pallas_call | solution.py:739
  35.0 0.5 collective-permute-start.18
  35.6 3.8 %collective-permute-done.13.arrived = bf16[4,96,768]{2,1,0:T(8,128)(2,1)S(1)} collective-permute-done((bf16[4,96,768]{2,1,0:T(8,128)(2,1)S(1)}, bf16[4,96,768]{2,1,0:T(8,128)(2,1)S(1)}, u32[]{:S(2)}, u32[]{:S(2)}) %collective-permute-start.13) | collective-permute-done | bytes 589856 | tf_op jit(solution)/shard_map/ppermute | solution.py:637
  39.4 0.2 shard_map.298
  39.5 1.5 %collective-permute-start.17 = (bf16[4,96,768]{2,1,0:T(8,128)(2,1)S(1)}, bf16[4,96,768]{2,1,0:T(8,128)(2,1)S(1)}, u32[]{:S(2)}, u32[]{:S(2)}) collective-permute-start(bf16[4,96,768]{2,1,0:T(8,128)(2,1)S(1)} %get-tuple-element.178), channel_id=1, source_target_pairs={{1,17},{3,19},{5,21},{7,23},{9,25},{11,27},{13,29},{15,31},{16,0},... | collective-permute-start | bytes 1769480 | tf_op jit(solution)/shard_map/ppermute | solution.py:650
  41.0 4.2 %shard_map.299 = (bf16[2,3,64,768]{3,2,1,0:T(8,128)(2,1)S(1)}, bf16[2,3,64,768]{3,2,1,0:T(8,128)(2,1)S(1)}, bf16[2,48,256]{2,1,0:T(8,128)(2,1)S(1)}, bf16[2,48,256]{2,1,0:T(8,128)(2,1)S(1)}, f32[8,128]{1,0:T(8,128)S(1)}) custom-call(bf16[432,384]{1,0:T(8,128)(2,1)S(1)} %get-tuple-element.148.l_a, bf16[432,384]{1,0:T(8,128)(2,1)S(1)} %collective-permute-done.11.l_b, ...), custom_call_target="tpu_custom_call" | custom-call | flops 8000000000 | bytes 20000000 | tf_op jit(solution)/shard_map/pallas_call | solution.py:750
  45.3 0.1 shard_map.300
  45.4 1.8 %collective-permute-start.16 = (bf16[2,48,1792]{2,1,0:T(8,128)(2,1)S(1)}, bf16[2,48,1792]{2,1,0:T(8,128)(2,1)S(1)}, u32[]{:S(2)}, u32[]{:S(2)}) collective-permute-start(bf16[2,48,1792]{2,1,0:T(8,128)(2,1)S(1)} %get-tuple-element.176), channel_id=1, source_target_pairs={{0,4},{4,0},{8,12},{12,8},{16,20},{20,16},{24,28},{28,24},{1,5},{5... | collective-permute-start | bytes 1032200 | tf_op jit(solution)/shard_map/ppermute | solution.py:637
  47.3 4.7 %collective-permute-done.18.arrived = bf16[4,48,1536]{2,1,0:T(8,128)(2,1)S(1)} collective-permute-done((bf16[4,48,1536]{2,1,0:T(8,128)(2,1)S(1)}, bf16[4,48,1536]{2,1,0:T(8,128)(2,1)S(1)}, u32[]{:S(2)}, u32[]{:S(2)}) %collective-permute-start.18) | collective-permute-done | bytes 589856 | tf_op jit(solution)/shard_map/ppermute | solution.py:637
  52.0 0.1 shard_map.301
  52.1 1.9 %collective-permute-start.20 = (bf16[2,48,1536]{2,1,0:T(8,128)(2,1)S(1)}, bf16[2,48,1536]{2,1,0:T(8,128)(2,1)S(1)}, u32[]{:S(2)}, u32[]{:S(2)}) collective-permute-start(bf16[2,48,1536]{2,1,0:T(8,128)(2,1)S(1)} %get-tuple-element.187), channel_id=1, source_target_pairs={{0,8},{4,12},{8,0},{12,4},{16,24},{20,28},{24,16},{28,20},{1,9},{5... | collective-permute-start | bytes 884744 | tf_op jit(solution)/shard_map/ppermute | solution.py:641
  54.0 4.6 %collective-permute-done.17.arrived = bf16[4,96,768]{2,1,0:T(8,128)(2,1)S(1)} collective-permute-done((bf16[4,96,768]{2,1,0:T(8,128)(2,1)S(1)}, bf16[4,96,768]{2,1,0:T(8,128)(2,1)S(1)}, u32[]{:S(2)}, u32[]{:S(2)}) %collective-permute-start.17) | collective-permute-done | bytes 589856 | tf_op jit(solution)/shard_map/ppermute | solution.py:650
  58.6 0.1 shard_map.302
  58.9 1.6 %collective-permute-start.19 = (bf16[2,48,128]{2,1,0:T(8,128)(2,1)S(1)}, bf16[2,48,128]{2,1,0:T(8,128)(2,1)S(1)}, u32[]{:S(2)}, u32[]{:S(2)}) collective-permute-start(bf16[2,48,128]{2,1,0:T(8,128)(2,1)S(1)} %get-tuple-element.185), channel_id=1, source_target_pairs={{0,8},{4,12},{8,0},{12,4},{16,24},{20,28},{24,16},{28,20},{1,9},{5... | collective-permute-start | bytes 73736 | tf_op jit(solution)/shard_map/ppermute | solution.py:641
  60.5 2.6 %collective-permute-start.27 = (bf16[1,48,1536]{2,1,0:T(8,128)(2,1)S(1)}, bf16[1,48,1536]{2,1,0:T(8,128)(2,1)S(1)}, u32[]{:S(2)}, u32[]{:S(2)}) collective-permute-start(bf16[1,48,1536]{2,1,0:T(8,128)(2,1)S(1)} %get-tuple-element.207), channel_id=1, source_target_pairs={{0,16},{4,20},{8,24},{12,28},{16,0},{20,4},{24,8},{28,12},{1,17},{... | collective-permute-start | bytes 442376 | tf_op jit(solution)/shard_map/ppermute | solution.py:641
  63.1 2.4 %collective-permute-start.26 = (bf16[2,96,768]{2,1,0:T(8,128)(2,1)S(1)}, bf16[2,96,768]{2,1,0:T(8,128)(2,1)S(1)}, u32[]{:S(2)}, u32[]{:S(2)}) collective-permute-start(bf16[2,96,768]{2,1,0:T(8,128)(2,1)S(1)} %get-tuple-element.205), channel_id=1, source_target_pairs={{0,8},{2,10},{4,12},{6,14},{8,0},{10,2},{12,4},{14,6},{17,25},{19,... | collective-permute-start | bytes 884744 | tf_op jit(solution)/shard_map/ppermute | solution.py:650
  65.4 0.1 shard_map.304
  65.7 0.6 collective-permute-start.21
  66.3 0.8 %collective-permute-done.21.vec_b = bf16[2,48,16]{2,1,0:T(8,128)(2,1)S(1)} collective-permute-done((bf16[2,48,16]{2,1,0:T(8,128)(2,1)S(1)}, bf16[2,48,16]{2,1,0:T(8,128)(2,1)S(1)}, u32[]{:S(2)}, u32[]{:S(2)}) %collective-permute-start.21) | collective-permute-done | bytes 3104 | tf_op jit(solution)/shard_map/ppermute | solution.py:629
  67.2 2.8 %collective-permute-start.24 = (bf16[24,1152]{1,0:T(8,128)(2,1)S(1)}, bf16[24,1152]{1,0:T(8,128)(2,1)S(1)}, u32[]{:S(2)}, u32[]{:S(2)}) collective-permute-start(bf16[24,1152]{1,0:T(8,128)(2,1)S(1)} %get-tuple-element.201), channel_id=1, source_target_pairs={{0,17},{1,16},{2,19},{3,18},{4,21},{5,20},{6,23},{7,22},{8,25},{9,... | collective-permute-start | bytes 165896 | tf_op jit(solution)/shard_map/ppermute | solution.py:645
  69.9 1.2 %shard_map.306 = (bf16[3,64,768]{2,1,0:T(8,128)(2,1)}, f32[8,128]{1,0:T(8,128)S(1)}) custom-call(bf16[2,3,64,768]{3,2,1,0:T(8,128)(2,1)S(1)} %get-tuple-element.168.gb_a, bf16[2,3,64,768]{3,2,1,0:T(8,128)(2,1)S(1)} %collective-permute-done.14.gb_b, f32[432,768]{1,0:T(8,128)S(1)} %get-tuple-element.150.res, f32[16,64]{1,0:T(8,128)S(1)} %get-tuple-element.162.mine, ...), custom_call_target="tpu_custom_call" | custom-call | tf_op jit(solution)/shard_map/pallas_call | solution.py:784
  71.1 0.2 collective-permute-start.25
  71.3 1.4 %shard_map.308 = (bf16[3,64,768]{2,1,0:T(8,128)(2,1)}, f32[8,128]{1,0:T(8,128)S(1)}) custom-call(bf16[2,3,64,768]{3,2,1,0:T(8,128)(2,1)S(1)} %get-tuple-element.168.gb_a, bf16[2,3,64,768]{3,2,1,0:T(8,128)(2,1)S(1)} %collective-permute-done.14.gb_b, bf16[208,768]{1,0:T(8,128)(2,1)S(1)} %get-tuple-element.124.t0.tok, f32[432,768]{1,0:T(8,128)S(1)} %get-tuple-element.160.gres, ...), custom_call_target="tpu_custom_call" | custom-call | tf_op jit(solution)/shard_map/pallas_call | solution.py:793
  72.7 1.4 %collective-permute-done.26.wr_a = bf16[2,96,768]{2,1,0:T(8,128)(2,1)S(1)} collective-permute-done((bf16[2,96,768]{2,1,0:T(8,128)(2,1)S(1)}, bf16[2,96,768]{2,1,0:T(8,128)(2,1)S(1)}, u32[]{:S(2)}, u32[]{:S(2)}) %collective-permute-start.26) | collective-permute-done | bytes 294944 | tf_op jit(solution)/shard_map/ppermute | solution.py:650
  74.0 0.1 shard_map.309
  74.2 0.5 collective-permute-start.29
  74.7 0.3 collective-permute-done.24.far
  75.0 0.8 %collective-permute-done.25.vec_a = bf16[48,16]{1,0:T(8,128)(2,1)S(1)} collective-permute-done((bf16[48,16]{1,0:T(8,128)(2,1)S(1)}, bf16[48,16]{1,0:T(8,128)(2,1)S(1)}, u32[]{:S(2)}, u32[]{:S(2)}) %collective-permute-start.25) | collective-permute-done | bytes 1568 | tf_op jit(solution)/shard_map/ppermute | solution.py:641
  75.9 1.0 %shard_map.311 = (f32[24,2304]{1,0:T(8,128)}, f32[24]{0:T(128)}, f32[24]{0:T(128)}, f32[2,24]{1,0:T(2,128)}, f32[24]{0:T(128)}, /*index=5*/f32[24]{0:T(128)}, f3...) custom-call(f32[24,1920]{1,0:T(8,128)S(1)} %get-tuple-element.210.ow, ...), custom_call_target="tpu_custom_call" | custom-call | bytes 1000000 | tf_op jit(solution)/shard_map/pallas_call | solution.py:809
  (36 shorter events, 0.9 us)
Async XLA Ops:
  0.6 11.0 %collective-permute-start.1 = (bf16[3,64,768]{2,1,0:T(8,128)(2,1)}, bf16[3,64,768]{2,1,0:T(8,128)(2,1)S(1)}, u32[]{:S(2)}, u32[]{:S(2)}) collective-permute-start(bf16[3,64,768]{2,1,0:T(8,128)(2,1)} %tok.1), channel_id=1, source_target_pairs={{0,2},{1,3},{2,0},{3,1},{4,6},{5,7},{6,4},{7,5},{8,10},{9,11},{10,... | collective-permute-start | bytes 884744 | tf_op jit(solution)/shard_map/ppermute | solution.py:633
  7.4 5.0 %collective-permute-start = (bf16[208,768]{1,0:T(8,128)(2,1)S(1)}, bf16[208,768]{1,0:T(8,128)(2,1)S(1)}, u32[]{:S(2)}, u32[]{:S(2)}) collective-permute-start(bf16[208,768]{1,0:T(8,128)(2,1)S(1)} %get-tuple-element.124.t0.tok), channel_id=1, source_target_pairs={{0,1},{1,0},{2,3},{3,2},{4,5},{5,4},{6,7},{7,6},{8,9},{9,8},{10,11... | collective-permute-start | bytes 958472 | tf_op jit(solution)/shard_map/ppermute | solution.py:629
  7.4 4.2 %collective-permute-start.2 = (bf16[16,768]{1,0:T(8,128)(2,1)S(1)}, bf16[16,768]{1,0:T(8,128)(2,1)S(1)}, u32[]{:S(2)}, u32[]{:S(2)}) collective-permute-start(bf16[16,768]{1,0:T(8,128)(2,1)S(1)} %get-tuple-element.125), channel_id=1, source_target_pairs={{0,2},{1,3},{2,0},{3,1},{4,6},{5,7},{6,4},{7,5},{8,10},{9,11},{10,... | collective-permute-start | bytes 73736 | tf_op jit(solution)/shard_map/ppermute | solution.py:633
  7.5 10.2 %collective-permute-start.6 = (bf16[3,64,768]{2,1,0:T(8,128)(2,1)S(1)}, bf16[3,64,768]{2,1,0:T(8,128)(2,1)S(1)}, u32[]{:S(2)}, u32[]{:S(2)}) collective-permute-start(bf16[3,64,768]{2,1,0:T(8,128)(2,1)S(1)} %get-tuple-element.133.c0), channel_id=1, source_target_pairs={{0,2},{1,3},{2,0},{3,1},{4,6},{5,7},{6,4},{7,5},{8,10},{9,11},{10,... | collective-permute-start | bytes 884744 | tf_op jit(solution)/shard_map/ppermute | solution.py:633
  11.7 2.1 %collective-permute-start.3 = (bf16[160,768]{1,0:T(8,128)(2,1)S(1)}, bf16[160,768]{1,0:T(8,128)(2,1)S(1)}, u32[]{:S(2)}, u32[]{:S(2)}) collective-permute-start(bf16[160,768]{1,0:T(8,128)(2,1)S(1)} %get-tuple-element.127.x_a), channel_id=1, source_target_pairs={{0,1},{1,0},{2,3},{3,2},{4,5},{5,4},{6,7},{7,6},{8,9},{9,8},{10,11... | collective-permute-start | bytes 737288 | tf_op jit(solution)/shard_map/ppermute | solution.py:629
  11.8 6.6 %collective-permute-start.5 = (bf16[3,64,768]{2,1,0:T(8,128)(2,1)S(1)}, bf16[3,64,768]{2,1,0:T(8,128)(2,1)S(1)}, u32[]{:S(2)}, u32[]{:S(2)}) collective-permute-start(bf16[3,64,768]{2,1,0:T(8,128)(2,1)S(1)} %get-tuple-element.133.c0), channel_id=1, source_target_pairs={{0,1},{1,0},{2,3},{3,2},{4,5},{5,4},{6,7},{7,6},{8,9},{9,8},{10,11... | collective-permute-start | bytes 884744 | tf_op jit(solution)/shard_map/ppermute | solution.py:629
  12.3 1.5 %collective-permute-start.4 = (bf16[48,768]{1,0:T(8,128)(2,1)S(1)}, bf16[48,768]{1,0:T(8,128)(2,1)S(1)}, u32[]{:S(2)}, u32[]{:S(2)}) collective-permute-start(bf16[48,768]{1,0:T(8,128)(2,1)S(1)} %get-tuple-element.128.x_b), channel_id=1, source_target_pairs={{0,1},{1,0},{2,3},{3,2},{4,5},{5,4},{6,7},{7,6},{8,9},{9,8},{10,11... | collective-permute-start | bytes 221192 | tf_op jit(solution)/shard_map/ppermute | solution.py:629
  16.8 2.2 %collective-permute-start.9 = (bf16[224,384]{1,0:T(8,128)(2,1)S(1)}, bf16[224,384]{1,0:T(8,128)(2,1)S(1)}, u32[]{:S(2)}, u32[]{:S(2)}) collective-permute-start(bf16[224,384]{1,0:T(8,128)(2,1)S(1)} %get-tuple-element.130.mix_a), channel_id=1, source_target_pairs={{0,1},{1,0},{2,3},{3,2},{4,5},{5,4},{6,7},{7,6},{8,9},{9,8},{10,11... | collective-permute-start | bytes 516104 | tf_op jit(solution)/shard_map/ppermute | solution.py:629
  17.0 2.0 %collective-permute-start.10 = (bf16[208,384]{1,0:T(8,128)(2,1)S(1)}, bf16[208,384]{1,0:T(8,128)(2,1)S(1)}, u32[]{:S(2)}, u32[]{:S(2)}) collective-permute-start(bf16[208,384]{1,0:T(8,128)(2,1)S(1)} %get-tuple-element.131.mix2_a), channel_id=1, source_target_pairs={{0,1},{1,0},{2,3},{3,2},{4,5},{5,4},{6,7},{7,6},{8,9},{9,8},{10,11... | collective-permute-start | bytes 479240 | tf_op jit(solution)/shard_map/ppermute | solution.py:629
  17.7 3.7 %collective-permute-start.7 = (bf16[96,768]{1,0:T(8,128)(2,1)S(1)}, bf16[96,768]{1,0:T(8,128)(2,1)S(1)}, u32[]{:S(2)}, u32[]{:S(2)}) collective-permute-start(bf16[96,768]{1,0:T(8,128)(2,1)S(1)} %get-tuple-element.134.x_a), channel_id=1, source_target_pairs={{0,1},{1,0},{2,3},{3,2},{4,5},{5,4},{6,7},{7,6},{8,9},{9,8},{10,11... | collective-permute-start | bytes 442376 | tf_op jit(solution)/shard_map/ppermute | solution.py:629
  17.8 3.6 %collective-permute-start.8 = (bf16[96,768]{1,0:T(8,128)(2,1)S(1)}, bf16[96,768]{1,0:T(8,128)(2,1)S(1)}, u32[]{:S(2)}, u32[]{:S(2)}) collective-permute-start(bf16[96,768]{1,0:T(8,128)(2,1)S(1)} %get-tuple-element.135.x_b), channel_id=1, source_target_pairs={{0,1},{1,0},{2,3},{3,2},{4,5},{5,4},{6,7},{7,6},{8,9},{9,8},{10,11... | collective-permute-start | bytes 442376 | tf_op jit(solution)/shard_map/ppermute | solution.py:629
  23.1 16.2 %collective-permute-start.13 = (bf16[4,96,768]{2,1,0:T(8,128)(2,1)S(1)}, bf16[4,96,768]{2,1,0:T(8,128)(2,1)S(1)}, u32[]{:S(2)}, u32[]{:S(2)}) collective-permute-start(bf16[4,96,768]{2,1,0:T(8,128)(2,1)S(1)} %get-tuple-element.165), channel_id=1, source_target_pairs={{0,4},{4,0},{8,12},{12,8},{16,20},{20,16},{24,28},{28,24},{1,5},{5... | collective-permute-start | bytes 1769480 | tf_op jit(solution)/shard_map/ppermute | solution.py:637
  27.4 3.4 %collective-permute-start.11 = (bf16[432,384]{1,0:T(8,128)(2,1)S(1)}, bf16[432,384]{1,0:T(8,128)(2,1)S(1)}, u32[]{:S(2)}, u32[]{:S(2)}) collective-permute-start(bf16[432,384]{1,0:T(8,128)(2,1)S(1)} %get-tuple-element.148.l_a), channel_id=1, source_target_pairs={{0,1},{1,0},{2,3},{3,2},{4,5},{5,4},{6,7},{7,6},{8,9},{9,8},{10,11... | collective-permute-start | bytes 995336 | tf_op jit(solution)/shard_map/ppermute | solution.py:629
  27.4 3.3 %collective-permute-start.12 = (bf16[432,384]{1,0:T(8,128)(2,1)S(1)}, bf16[432,384]{1,0:T(8,128)(2,1)S(1)}, u32[]{:S(2)}, u32[]{:S(2)}) collective-permute-start(bf16[432,384]{1,0:T(8,128)(2,1)S(1)} %get-tuple-element.149.r_a), channel_id=1, source_target_pairs={{0,1},{1,0},{2,3},{3,2},{4,5},{5,4},{6,7},{7,6},{8,9},{9,8},{10,11... | collective-permute-start | bytes 995336 | tf_op jit(solution)/shard_map/ppermute | solution.py:629
  29.1 16.2 %collective-permute-start.15 = (bf16[4,48,1536]{2,1,0:T(8,128)(2,1)S(1)}, bf16[4,48,1536]{2,1,0:T(8,128)(2,1)S(1)}, u32[]{:S(2)}, u32[]{:S(2)}) collective-permute-start(bf16[4,48,1536]{2,1,0:T(8,128)(2,1)S(1)} %get-tuple-element.171), channel_id=1, source_target_pairs={{0,8},{4,12},{8,0},{12,4},{16,24},{20,28},{24,16},{28,20},{1,9},{5... | collective-permute-start | bytes 1769480 | tf_op jit(solution)/shard_map/ppermute | solution.py:641
  35.0 17.0 %collective-permute-start.18 = (bf16[4,48,1536]{2,1,0:T(8,128)(2,1)S(1)}, bf16[4,48,1536]{2,1,0:T(8,128)(2,1)S(1)}, u32[]{:S(2)}, u32[]{:S(2)}) collective-permute-start(bf16[4,48,1536]{2,1,0:T(8,128)(2,1)S(1)} %get-tuple-element.180), channel_id=1, source_target_pairs={{0,4},{4,0},{8,12},{12,8},{16,20},{20,16},{24,28},{28,24},{1,5},{5... | collective-permute-start | bytes 1769480 | tf_op jit(solution)/shard_map/ppermute | solution.py:637
  39.5 19.1 %collective-permute-start.17 = (bf16[4,96,768]{2,1,0:T(8,128)(2,1)S(1)}, bf16[4,96,768]{2,1,0:T(8,128)(2,1)S(1)}, u32[]{:S(2)}, u32[]{:S(2)}) collective-permute-start(bf16[4,96,768]{2,1,0:T(8,128)(2,1)S(1)} %get-tuple-element.178), channel_id=1, source_target_pairs={{1,17},{3,19},{5,21},{7,23},{9,25},{11,27},{13,29},{15,31},{16,0},... | collective-permute-start | bytes 1769480 | tf_op jit(solution)/shard_map/ppermute | solution.py:650
  45.4 13.3 %collective-permute-start.16 = (bf16[2,48,1792]{2,1,0:T(8,128)(2,1)S(1)}, bf16[2,48,1792]{2,1,0:T(8,128)(2,1)S(1)}, u32[]{:S(2)}, u32[]{:S(2)}) collective-permute-start(bf16[2,48,1792]{2,1,0:T(8,128)(2,1)S(1)} %get-tuple-element.176), channel_id=1, source_target_pairs={{0,4},{4,0},{8,12},{12,8},{16,20},{20,16},{24,28},{28,24},{1,5},{5... | collective-permute-start | bytes 1032200 | tf_op jit(solution)/shard_map/ppermute | solution.py:637
  52.1 13.3 %collective-permute-start.20 = (bf16[2,48,1536]{2,1,0:T(8,128)(2,1)S(1)}, bf16[2,48,1536]{2,1,0:T(8,128)(2,1)S(1)}, u32[]{:S(2)}, u32[]{:S(2)}) collective-permute-start(bf16[2,48,1536]{2,1,0:T(8,128)(2,1)S(1)} %get-tuple-element.187), channel_id=1, source_target_pairs={{0,8},{4,12},{8,0},{12,4},{16,24},{20,28},{24,16},{28,20},{1,9},{5... | collective-permute-start | bytes 884744 | tf_op jit(solution)/shard_map/ppermute | solution.py:641
  54.0 11.7 %collective-permute-start.14 = (bf16[2,3,64,768]{3,2,1,0:T(8,128)(2,1)S(1)}, bf16[2,3,64,768]{3,2,1,0:T(8,128)(2,1)S(1)}, u32[]{:S(2)}, u32[]{:S(2)}) collective-permute-start(bf16[2,3,64,768]{3,2,1,0:T(8,128)(2,1)S(1)} %get-tuple-element.169), channel_id=1, source_target_pairs={{0,1},{1,0},{2,3},{3,2},{4,5},{5,4},{6,7},{7,6},{8,9},{9,8},{10,11... | collective-permute-start | bytes 1769480 | tf_op jit(solution)/shard_map/ppermute | solution.py:629
  58.9 6.8 %collective-permute-start.19 = (bf16[2,48,128]{2,1,0:T(8,128)(2,1)S(1)}, bf16[2,48,128]{2,1,0:T(8,128)(2,1)S(1)}, u32[]{:S(2)}, u32[]{:S(2)}) collective-permute-start(bf16[2,48,128]{2,1,0:T(8,128)(2,1)S(1)} %get-tuple-element.185), channel_id=1, source_target_pairs={{0,8},{4,12},{8,0},{12,4},{16,24},{20,28},{24,16},{28,20},{1,9},{5... | collective-permute-start | bytes 73736 | tf_op jit(solution)/shard_map/ppermute | solution.py:641
  60.5 12.2 %collective-permute-start.27 = (bf16[1,48,1536]{2,1,0:T(8,128)(2,1)S(1)}, bf16[1,48,1536]{2,1,0:T(8,128)(2,1)S(1)}, u32[]{:S(2)}, u32[]{:S(2)}) collective-permute-start(bf16[1,48,1536]{2,1,0:T(8,128)(2,1)S(1)} %get-tuple-element.207), channel_id=1, source_target_pairs={{0,16},{4,20},{8,24},{12,28},{16,0},{20,4},{24,8},{28,12},{1,17},{... | collective-permute-start | bytes 442376 | tf_op jit(solution)/shard_map/ppermute | solution.py:641
  63.1 11.0 %collective-permute-start.26 = (bf16[2,96,768]{2,1,0:T(8,128)(2,1)S(1)}, bf16[2,96,768]{2,1,0:T(8,128)(2,1)S(1)}, u32[]{:S(2)}, u32[]{:S(2)}) collective-permute-start(bf16[2,96,768]{2,1,0:T(8,128)(2,1)S(1)} %get-tuple-element.205), channel_id=1, source_target_pairs={{0,8},{2,10},{4,12},{6,14},{8,0},{10,2},{12,4},{14,6},{17,25},{19,... | collective-permute-start | bytes 884744 | tf_op jit(solution)/shard_map/ppermute | solution.py:650
  65.5 9.4 %collective-permute-start.23 = (bf16[24,1920]{1,0:T(8,128)(2,1)S(1)}, bf16[24,1920]{1,0:T(8,128)(2,1)S(1)}, u32[]{:S(2)}, u32[]{:S(2)}) collective-permute-start(bf16[24,1920]{1,0:T(8,128)(2,1)S(1)} %get-tuple-element.199), channel_id=1, source_target_pairs={{0,16},{4,20},{8,24},{12,28},{16,0},{20,4},{24,8},{28,12},{1,17},{... | collective-permute-start | bytes 276488 | tf_op jit(solution)/shard_map/ppermute | solution.py:641
  65.6 5.5 %collective-permute-start.22 = (f32[24,1152]{1,0:T(8,128)S(1)}, f32[24,1152]{1,0:T(8,128)S(1)}, u32[]{:S(2)}, u32[]{:S(2)}) collective-permute-start(f32[24,1152]{1,0:T(8,128)S(1)} %get-tuple-element.194), channel_id=1, source_target_pairs={{0,1},{1,0},{2,3},{3,2},{4,5},{5,4},{6,7},{7,6},{8,9},{9,8},{10,11... | collective-permute-start | bytes 331784 | tf_op jit(solution)/shard_map/ppermute | solution.py:629
  65.7 1.4 %collective-permute-start.21 = (bf16[2,48,16]{2,1,0:T(8,128)(2,1)S(1)}, bf16[2,48,16]{2,1,0:T(8,128)(2,1)S(1)}, u32[]{:S(2)}, u32[]{:S(2)}) collective-permute-start(bf16[2,48,16]{2,1,0:T(8,128)(2,1)S(1)} %get-tuple-element.193), channel_id=1, source_target_pairs={{0,1},{1,0},{2,3},{3,2},{4,5},{5,4},{6,7},{7,6},{8,9},{9,8},{10,11... | collective-permute-start | bytes 9224 | tf_op jit(solution)/shard_map/ppermute | solution.py:629
  67.2 7.8 %collective-permute-start.24 = (bf16[24,1152]{1,0:T(8,128)(2,1)S(1)}, bf16[24,1152]{1,0:T(8,128)(2,1)S(1)}, u32[]{:S(2)}, u32[]{:S(2)}) collective-permute-start(bf16[24,1152]{1,0:T(8,128)(2,1)S(1)} %get-tuple-element.201), channel_id=1, source_target_pairs={{0,17},{1,16},{2,19},{3,18},{4,21},{5,20},{6,23},{7,22},{8,25},{9,... | collective-permute-start | bytes 165896 | tf_op jit(solution)/shard_map/ppermute | solution.py:645
  71.1 4.7 %collective-permute-start.25 = (bf16[48,16]{1,0:T(8,128)(2,1)S(1)}, bf16[48,16]{1,0:T(8,128)(2,1)S(1)}, u32[]{:S(2)}, u32[]{:S(2)}) collective-permute-start(bf16[48,16]{1,0:T(8,128)(2,1)S(1)} %get-tuple-element.203), channel_id=1, source_target_pairs={{0,16},{4,20},{8,24},{12,28},{16,0},{20,4},{24,8},{28,12},{1,17},{... | collective-permute-start | bytes 4616 | tf_op jit(solution)/shard_map/ppermute | solution.py:641
  74.2 1.7 %collective-permute-start.28 = (bf16[24,1536]{1,0:T(8,128)(2,1)S(1)}, bf16[24,1536]{1,0:T(8,128)(2,1)S(1)}, u32[]{:S(2)}, u32[]{:S(2)}) collective-permute-start(bf16[24,1536]{1,0:T(8,128)(2,1)S(1)} %get-tuple-element.214), channel_id=1, source_target_pairs={{0,1},{1,0},{2,3},{3,2},{4,5},{5,4},{6,7},{7,6},{8,9},{9,8},{10,11... | collective-permute-start | bytes 221192 | tf_op jit(solution)/shard_map/ppermute | solution.py:629
  74.2 1.7 %collective-permute-start.29 = (bf16[96,768]{1,0:T(8,128)(2,1)S(1)}, bf16[96,768]{1,0:T(8,128)(2,1)S(1)}, u32[]{:S(2)}, u32[]{:S(2)}) collective-permute-start(bf16[96,768]{1,0:T(8,128)(2,1)S(1)} %get-tuple-element.216), channel_id=1, source_target_pairs={{0,1},{1,0},{2,3},{3,2},{4,5},{5,4},{6,7},{7,6},{8,9},{9,8},{10,11... | collective-permute-start | bytes 442376 | tf_op jit(solution)/shard_map/ppermute | solution.py:629
